TPU v7x, 256 devices: a whole 4x4x8 slice. The times are simulated.
256 devices in a mesh: dp: 16 (over x, y_hi, core), seq: 16 (over y_lo, z).
Axes of the slice: x: 4, y: 4 (y_hi: 2, y_lo: 2; y = y_hi * 2 + y_lo), z: 8, core: 2. Of those that a mesh axis runs over, the one named last changes fastest.
Arguments:
- activations: bfloat16 [16, 20480, 768], P('dp', 'seq'), may hold values from -400 to 400
- nucleotides: int32 [16, 20480], P('dp', 'seq'), may hold values from 0 to 3
- base_table: float32 [4, 768], replicated, may hold values from -4 to 4
- norm_gain: float32 [768], replicated, may hold values from 0.1 to 1.9
- filter_weight: bfloat16 [3, 768, 768], P(None, 'dp'), may hold values from -0.125 to 0.125
- upstream: bfloat16 [16, 20480, 768], P('dp', 'seq'), may hold values from -6 to 6
Outputs:
- input_grad: bfloat16 [16, 20480, 768], P('dp', 'seq')
- weight_grad: float32 [3, 768, 768], P(None, 'dp')
All inputs are finite; a program needn't handle non-finite values.
Results may differ from a plain program's by a relative error of at most 0.0056.
Values may be sent and summed in bfloat16 or wider, within the bound.
No kernel may reach another device: no remote copies, remote signals or barrier semaphores. Data moves between devices by JAX's collectives and lax.ppermute only.
A program may use at most 64 MiB of HBM per device.

v0:
```python
import math

import jax
import jax.numpy as jnp
from jax import lax
from jax.sharding import PartitionSpec as P

FILTER_TAPS = 3
DILATION_STEP = 32


def with_halo(block, sides, width):
    for axis, dim in sides:
        count = lax.axis_size(axis)
        forward = [(i, i + 1) for i in range(count - 1)]
        backward = [(target, source) for source, target in forward]
        low = lax.ppermute(
            lax.slice_in_dim(block, block.shape[dim] - width, None, axis=dim), axis, forward
        )
        high = lax.ppermute(lax.slice_in_dim(block, 0, width, axis=dim), axis, backward)
        block = jnp.concatenate([low, block, high], axis=dim)
    return block


def gelu_slope(value):
    coeff = math.sqrt(2.0 / math.pi)
    inner = coeff * (value + 0.044715 * value * value * value)
    tangent = jnp.tanh(inner)
    return 0.5 * (1.0 + tangent) + 0.5 * value * (1.0 - tangent * tangent) * coeff * (
        1.0 + 3.0 * 0.044715 * value * value
    )


def on_device(activations, nucleotides, base_table, norm_gain, filter_weight, upstream):
    receptive_reach = DILATION_STEP * (FILTER_TAPS // 2)
    filter_kernel = lax.all_gather(filter_weight, "dp", axis=1, tiled=True)
    tokens = activations[0]
    element_count = tokens.shape[0]
    hot = (nucleotides[0][:, None] == jnp.arange(4, dtype=jnp.int32)[None, :]).astype(jnp.float32)
    inputs = tokens.astype(jnp.float32) + jnp.dot(hot, base_table, precision=lax.Precision.HIGHEST)
    scale_inv = lax.rsqrt(jnp.mean(inputs * inputs, axis=-1, keepdims=True) + 1e-06)
    normed = (inputs * scale_inv * norm_gain).astype(jnp.bfloat16)
    padded_input = with_halo(normed, (("seq", 0),), receptive_reach)
    channels = filter_kernel.shape[2]
    convolve_block = jnp.zeros((element_count, channels), jnp.float32)
    for filter_tap in range(FILTER_TAPS):
        convolve_block = convolve_block + jnp.dot(
            padded_input[filter_tap * DILATION_STEP : filter_tap * DILATION_STEP + element_count],
            filter_kernel[filter_tap],
            preferred_element_type=jnp.float32,
        )
    incoming = upstream[0].astype(jnp.float32)
    backward_pass = (incoming * gelu_slope(convolve_block)).astype(jnp.bfloat16)
    back_pad = with_halo(backward_pass, (("seq", 0),), receptive_reach)
    gradient_list = []
    for filter_tap in range(FILTER_TAPS):
        gradient_list.append(
            lax.dot_general(
                padded_input[
                    filter_tap * DILATION_STEP : filter_tap * DILATION_STEP + element_count
                ],
                backward_pass,
                (((0,), (0,)), ((), ())),
                preferred_element_type=jnp.float32,
            )
        )
    local_grad = jnp.stack(gradient_list)
    normed_grad = jnp.zeros((element_count, channels), jnp.float32)
    for filter_tap in range(FILTER_TAPS):
        start_offset = (FILTER_TAPS - 1 - filter_tap) * DILATION_STEP
        normed_grad = normed_grad + lax.dot_general(
            back_pad[start_offset : start_offset + element_count],
            filter_kernel[filter_tap],
            (((1,), (1,)), ((), ())),
            preferred_element_type=jnp.float32,
        )
    scaled = norm_gain * normed_grad
    spread = jnp.mean(scaled * inputs, axis=-1, keepdims=True)
    result = incoming + scale_inv * scaled - inputs * scale_inv * scale_inv * scale_inv * spread
    summed = lax.psum(local_grad, "seq")
    owned = lax.psum_scatter(summed, "dp", scatter_dimension=1, tiled=True)
    total_rows = lax.axis_size("dp") * activations.shape[0] * lax.axis_size("seq") * element_count
    weight_grad = owned / math.sqrt(total_rows)
    return (result.astype(jnp.bfloat16)[None], weight_grad)


def solution(mesh):
    in_specs = (
        P("dp", "seq", None),
        P("dp", "seq"),
        P(),
        P(),
        P(None, "dp", None),
        P("dp", "seq", None),
    )
    out_specs = (P("dp", "seq", None), P(None, "dp", None))
    return jax.shard_map(
        on_device, mesh=mesh, in_specs=in_specs, out_specs=out_specs, check_vma=False
    )
```

profile of v0, /device:TPU:2, one launch (start us, length us, event | category | flops | bytes accessed | tf_op | source)
XLA Modules:
  0.0 334.4 jit_solution(242663913550230027)
XLA Ops:
  7.2 0.0 copy-start
  7.2 0.0 copy-start.8
  7.2 0.0 all-gather.2.cloned.1.call-start
  7.2 0.7 all-gather.2.cloned.1.call-update
  7.9 0.0 reduce-scatter.2.cloned.1.call-start
  8.0 0.7 reduce
  8.7 0.0 copy-done
  8.7 3.7 %multiply_reduce_fusion.1 = (f32[1280]{0:T(1024)S(1)}, f32[1280,768]{1,0:T(8,128)S(1)}) fusion(f32[4,768]{1,0:T(4,128)S(1)} %copy-done, s32[1280]{0:T(1024)S(1)} %reduce, bf16[1,1280,768]{2,1,0:T(8,128)(2,1)} %param.6), kind=kOutput, calls=%fused_computation.17 | convolution fusion | flops 51121920 | bytes 5920768 | tf_op jit(solution)/shard_map/dot_general | solution.py:40
  12.4 0.0 copy-start.1
  12.4 2.0 copy-done.1
  14.4 0.0 copy-done.8
  14.4 0.4 multiply_convert_fusion
  14.8 3.8 %collective-permute-start = (bf16[32,768]{1,0:T(8,128)(2,1)S(1)}, bf16[32,768]{1,0:T(8,128)(2,1)S(1)}, u32[]{:S(2)}, u32[]{:S(2)}) collective-permute-start(bf16[32,768]{1,0:T(8,128)(2,1)S(1)} %get-tuple-element.5), channel_id=1, source_target_pairs={{0,1},{1,2},{2,3},{3,4},{4,5},{5,6},{6,7},{7,8},{8,9},{9,10},{10,1... | collective-permute-start | bytes 147464 | tf_op jit(solution)/shard_map/ppermute | solution.py:17
  18.6 1.5 collective-permute-start.1
  20.1 52.2 %all-gather.2.cloned.1.call-done = bf16[3,768,768]{2,1,0:T(8,128)(2,1)} async-done(((bf16[3,48,768]{2,1,0:T(8,128)(2,1)}), bf16[3,768,768]{2,1,0:T(8,128)(2,1)}) %all-gather.2.cloned.1.call-update) | async-done | bytes 3538960 | tf_op jit(solution)/shard_map/all_gather | solution.py:36
  72.3 0.0 copy-start.6
  72.3 3.2 fusion.16
  75.5 0.0 copy-start.5
  75.5 0.0 collective-permute-done
  75.5 0.0 copy-done.6
  75.5 1.7 fusion.13
  77.2 0.0 collective-permute-done.1
  77.2 0.0 copy-done.5
  77.3 4.4 %fusion = bf16[1280,768]{1,0:T(8,128)(2,1)S(1)} fusion(f32[1280,768]{1,0:T(8,128)S(1)} %fusion.13, f32[1280,768]{1,0:T(8,128)S(1)} %fusion.16, bf16[1,1280,768]{2,1,0:T(8,128)(2,1)S(1)} %copy-done.5, bf16[32,768]{1,0:T(8,128)(2,1)S(1)} %collective-permute-done.1, bf16[1280,768]{1,0:T(8,128)(2,1)S(1)} %multiply_convert_fusion, ...), kind=kOutput, calls=%fused_computation.6 | convolution fusion | flops 1535508480 | bytes 14991360 | tf_op jit(solution)/shard_map/dot_general | solution.py:47
  81.7 0.0 copy-start.3
  81.7 1.8 convolution_bitcast_fusion.1
  83.5 1.8 convolution_bitcast_fusion
  85.2 0.0 copy-done.3
  85.3 1.8 convolution_bitcast_fusion.2
  87.0 3.4 %pad_maximum_fusion = f32[3,768,768]{2,1,0:T(8,128)} fusion(f32[1,768,768]{2,1,0:T(8,128)S(1)} %convolution_bitcast_fusion, f32[1,768,768]{2,1,0:T(8,128)S(1)} %convolution_bitcast_fusion.1, f32[1,768,768]{2,1,0:T(8,128)S(1)} %convolution_bitcast_fusion.2), kind=kLoop, calls=%fused_computation | loop fusion | flops 3538944 | bytes 14155776 | tf_op jit(solution)/shard_map/stack | solution.py:67
  90.4 0.0 copy-start.4
  90.4 0.0 reduce-scatter.2.cloned.1.call-update
  90.4 0.0 all-reduce.2.cloned.1.call-start
  90.5 1.5 copy-done.4
  92.0 3.5 %collective-permute-start.3 = (bf16[32,768]{1,0:T(8,128)(2,1)S(1)}, bf16[32,768]{1,0:T(8,128)(2,1)S(1)}, u32[]{:S(2)}, u32[]{:S(2)}) collective-permute-start(bf16[32,768]{1,0:T(8,128)(2,1)S(1)} %get-tuple-element.2), channel_id=1, source_target_pairs={{0,1},{1,2},{2,3},{3,4},{4,5},{5,6},{6,7},{7,8},{8,9},{9,10},{10,1... | collective-permute-start | bytes 147464 | tf_op jit(solution)/shard_map/ppermute | solution.py:17
  95.4 0.0 copy-start.7
  95.4 1.8 collective-permute-start.2
  97.2 3.0 fusion.15
  100.3 0.0 copy-start.2
  100.3 1.4 collective-permute-done.2
  101.7 0.0 copy-done.7
  101.7 1.8 fusion.11
  103.5 0.0 collective-permute-done.3
  103.5 0.0 copy-done.2
  103.5 4.4 %multiply_reduce_fusion = (f32[1280]{0:T(1024)S(1)}, f32[1280,768]{1,0:T(8,128)}) fusion(f32[1280,768]{1,0:T(8,128)S(1)} %copy-done.2, bf16[3,768,768]{2,1,0:T(8,128)(2,1)S(1)} %copy-done.7, bf16[1280,768]{1,0:T(8,128)(2,1)S(1)} %copy-done.4, bf16[32,768]{1,0:T(8,128)(2,1)S(1)} %collective-permute-done.3, f32[1280,768]{1,0:T(8,128)S(1)} %fusion.11, ...), kind=kOutput, calls=%fused_computation.14 | convolution fusion | flops 1518795520 | bytes 18932736 | tf_op jit(solution)/shard_map/dot_general | solution.py:71
  107.9 82.3 %reduce-scatter.2.cloned.1.call-done = f32[3,48,768]{2,1,0:T(8,128)} async-done(((f32[3,768,768]{2,1,0:T(8,128)}), f32[3,48,768]{2,1,0:T(8,128)}) %reduce-scatter.2.cloned.1.call-update) | async-done | bytes 442384 | tf_op jit(solution)/shard_map/reduce_scatter | solution.py:81
  190.2 0.0 all-reduce.2.cloned.1.call-update
  190.2 5.4 %fusion.8 = bf16[1,1280,768]{2,1,0:T(8,128)(2,1)} fusion(f32[1280,768]{1,0:T(8,128)} %copy-done.1, f32[1280,768]{1,0:T(8,128)} %get-tuple-element.9, bf16[1,1280,768]{2,1,0:T(8,128)(2,1)} %param.11, f32[1280]{0:T(1024)S(1)} %broadcast_multiply_fusion.1, f32[1280]{0:T(1024)S(1)} %add_rsqrt_fusion), kind=kLoop, calls=%fused_computation.18 | loop fusion | flops 8847360 | bytes 11806720 | tf_op jit(solution)/shard_map/broadcast_in_dim | solution.py:84
  195.6 130.5 %all-reduce.2.cloned.1.call-done = f32[3,48,768]{2,1,0:T(8,128)} async-done(((f32[3,48,768]{2,1,0:T(8,128)}), f32[3,48,768]{2,1,0:T(8,128)}) %all-reduce.2.cloned.1.call-update) | async-done | bytes 442384 | tf_op jit(solution)/shard_map/psum | solution.py:80
  326.1 1.8 broadcast_multiply_fusion
  (4 shorter events, 0.0 us)
Async XLA Ops:
  7.2 1.5 copy-start
  7.2 7.2 %copy-start.8 = (f32[768]{0:T(1024)S(1)}, f32[768]{0:T(1024)}, u32[]{:S(2)}) copy-start(f32[768]{0:T(1024)} %param.9) | copy-start | bytes 9220
  7.2 65.1 %all-gather.2.cloned.1.call-start = ((), (), s32[]{:S(2)}) async-start(), calls=%async_computation.1 | async-start | bytes 3760128 | tf_op jit(solution)/shard_map/all_gather | solution.py:36
  7.9 182.3 %reduce-scatter.2.cloned.1.call-start = ((), (), s32[]{:S(2)}) async-start(), calls=%async_computation.2 | async-start | bytes 7520256 | tf_op jit(solution)/shard_map/reduce_scatter | solution.py:81
  12.4 2.0 copy-start.1
  14.8 60.7 %collective-permute-start = (bf16[32,768]{1,0:T(8,128)(2,1)S(1)}, bf16[32,768]{1,0:T(8,128)(2,1)S(1)}, u32[]{:S(2)}, u32[]{:S(2)}) collective-permute-start(bf16[32,768]{1,0:T(8,128)(2,1)S(1)} %get-tuple-element.5), channel_id=1, source_target_pairs={{0,1},{1,2},{2,3},{3,4},{4,5},{5,6},{6,7},{7,8},{8,9},{9,10},{10,1... | collective-permute-start | bytes 147464 | tf_op jit(solution)/shard_map/ppermute | solution.py:17
  18.6 58.6 %collective-permute-start.1 = (bf16[32,768]{1,0:T(8,128)(2,1)S(1)}, bf16[32,768]{1,0:T(8,128)(2,1)S(1)}, u32[]{:S(2)}, u32[]{:S(2)}) collective-permute-start(bf16[32,768]{1,0:T(8,128)(2,1)S(1)} %get-tuple-element.4), channel_id=1, source_target_pairs={{1,0},{2,1},{3,2},{4,3},{5,4},{6,5},{7,6},{8,7},{9,8},{10,9},{11,1... | collective-permute-start | bytes 147464 | tf_op jit(solution)/shard_map/ppermute | solution.py:20
  72.3 3.2 copy-start.6
  75.5 1.8 copy-start.5
  81.7 3.6 %copy-start.3 = (bf16[1280,768]{1,0:T(8,128)(2,1)}, bf16[1280,768]{1,0:T(8,128)(2,1)S(1)}, u32[]{:S(2)}) copy-start(bf16[1280,768]{1,0:T(8,128)(2,1)S(1)} %fusion) | copy-start | bytes 5898244
  90.4 1.5 copy-start.4
  90.4 235.7 %all-reduce.2.cloned.1.call-start = ((), (), s32[]{:S(2)}) async-start(), calls=%async_computation.3 | async-start | bytes 884736 | tf_op jit(solution)/shard_map/psum | solution.py:80
  92.0 11.5 %collective-permute-start.3 = (bf16[32,768]{1,0:T(8,128)(2,1)S(1)}, bf16[32,768]{1,0:T(8,128)(2,1)S(1)}, u32[]{:S(2)}, u32[]{:S(2)}) collective-permute-start(bf16[32,768]{1,0:T(8,128)(2,1)S(1)} %get-tuple-element.2), channel_id=1, source_target_pairs={{0,1},{1,2},{2,3},{3,4},{4,5},{5,6},{6,7},{7,8},{8,9},{9,10},{10,1... | collective-permute-start | bytes 147464 | tf_op jit(solution)/shard_map/ppermute | solution.py:17
  95.4 6.3 %copy-start.7 = (bf16[3,768,768]{2,1,0:T(8,128)(2,1)S(1)}, bf16[3,768,768]{2,1,0:T(8,128)(2,1)}, u32[]{:S(2)}) copy-start(bf16[3,768,768]{2,1,0:T(8,128)(2,1)} %all-gather.2.cloned.1.call-done) | copy-start | bytes 10616836
  95.4 6.2 %collective-permute-start.2 = (bf16[32,768]{1,0:T(8,128)(2,1)S(1)}, bf16[32,768]{1,0:T(8,128)(2,1)S(1)}, u32[]{:S(2)}, u32[]{:S(2)}) collective-permute-start(bf16[32,768]{1,0:T(8,128)(2,1)S(1)} %get-tuple-element.3), channel_id=1, source_target_pairs={{1,0},{2,1},{3,2},{4,3},{5,4},{6,5},{7,6},{8,7},{9,8},{10,9},{11,1... | collective-permute-start | bytes 147464 | tf_op jit(solution)/shard_map/ppermute | solution.py:20
  100.3 3.2 copy-start.2
Sparse Core Ops, SparseCore 0:
  10.8 61.4 all-gather.1
  90.6 99.5 reduce-scatter.1
  192.8 133.2 all-reduce.1
where the time goes:
time: 335 us; the launch traced here: 334 us
  waiting for transfers between devices  267 us (80%)
  matrix products  27.5 us (8%)
  between operations  14 us (4%)
  other arithmetic  11.7 us (3%)
  starting transfers between devices  10.7 us (3%)
  local copies, waits for them, and re-layouts  3.51 us (1%)
    psum x1, waiting for transfers between devices, on_device(): summed = lax.psum(local_grad, 'seq')  130 us
    reduce_scatter x1, waiting for transfers between devices, on_device(): owned = lax.psum_scatter(summed, 'dp', scatter_dimension=1, tiled=True)  82.3 us
    all_gather x1, waiting for transfers between devices, on_device(): filter_kernel = lax.all_gather(filter_weight, 'dp', axis=1, tiled=True)  52.2 us
    dot_general x3, matrix products, on_device(): jnp.dot(padded_input[filter_tap * DILATION_STEP:filter_tap * DILATION_STE...  9.3 us
    dot_general x3, matrix products, on_device(): lax.dot_general(back_pad[start_offset:start_offset + element_count], filt...  9.21 us
    ppermute x2, starting transfers between devices, with_halo(): lax.ppermute(lax.slice_in_dim(block, block.shape[dim] - width, None, axis...  7.29 us
  transfers between devices with their start and end apart: 7, of which 4 were waited for; matrix products, arithmetic and copies ran while one was open for 7% of the time, Pallas kernels for 0%

commit v1 on v0

v1 whole, which is shorter than its diff:
```python
import functools
import math

import jax
import jax.numpy as jnp
from jax import lax
from jax.experimental import pallas as pl
from jax.experimental.pallas import tpu as pltpu
from jax.sharding import Mesh, PartitionSpec as P

FILTER_TAPS = 3
DILATION_STEP = 32
REACH = 32
AXES = ("x", "yh", "core", "yl", "z")
SIZES = (4, 2, 2, 2, 8)
SEQ = ("yl", "z")
RING_Y = ("yh", "yl")
BF16 = jnp.bfloat16
F32 = jnp.float32


def shift(value, axis, count, step):
    pairs = [(i, (i + step) % count) for i in range(count)]
    return lax.ppermute(value, axis, pairs)


def swap(value, axis, count, mask):
    return lax.ppermute(value, axis, [(i, i ^ mask) for i in range(count)])


def gelu_slope(value):
    coeff = math.sqrt(2.0 / math.pi)
    square = value * value
    tangent = jnp.tanh(value * (coeff + coeff * 0.044715 * square))
    return (0.5 + 0.5 * tangent) * (
        1.0 + value * (1.0 - tangent) * (coeff + coeff * 3.0 * 0.044715 * square)
    )


def gather_weight(weight, x, yh, core):
    half = weight.shape[2] // 2
    mine = lax.dynamic_slice_in_dim(weight, core * half, half, axis=2)
    other = lax.dynamic_slice_in_dim(weight, (1 - core) * half, half, axis=2)
    arrived = swap(other, "core", 2, 1)
    own = jnp.where(
        core == 0,
        jnp.concatenate([mine, arrived], axis=1),
        jnp.concatenate([arrived, mine], axis=1),
    )
    rows = weight.shape[1]
    across = swap(own, RING_Y, 4, 3)
    up_own = shift(own, "x", 4, 1)
    down_own = shift(own, "x", 4, -1)
    up_across = shift(across, "x", 4, 1)
    down_across = shift(across, "x", 4, -1)
    far = [
        shift(up_own[:, :rows], "x", 4, 1),
        shift(down_own[:, rows:], "x", 4, -1),
        shift(up_across[:, :rows], "x", 4, 1),
        shift(down_across[:, rows:], "x", 4, -1),
    ]
    return [own, across, up_own, up_across, down_own, down_across] + far


def forward_kernel(position, *refs):
    pieces, refs = refs[:10], refs[10:]
    normed_hbm, turned_hbm, upstream_hbm = refs[0:2], refs[2:4], refs[4:6]
    weight_out, back_out, grad_out = refs[6], refs[7:9], refs[9:12]
    weight, normed, turned, upstream, back, grad = refs[12:18]
    piece_sem, normed_sem, turned_sem, upstream_sem, back_sem, grad_sem, weight_sem = refs[18:]
    x, yh = position[0], position[1]
    wide = pieces[0].shape[1]
    rows = wide // 2

    def at(step_x, step_y, low):
        place = ((x + step_x) % 4) * (2 * wide) + ((yh + step_y) % 2) * wide + low
        return pl.multiple_of(place, 16)

    places = [at(0, 0, 0), at(0, 1, 0), at(3, 0, 0), at(3, 1, 0), at(1, 0, 0), at(1, 1, 0)]
    places += [at(2, 0, 0), at(2, 0, rows), at(2, 1, 0), at(2, 1, rows)]
    copies = []
    for index, (piece, place) in enumerate(zip(pieces, places)):
        copies.append(
            pltpu.make_async_copy(
                piece, weight.at[:, pl.ds(place, piece.shape[1]), :], piece_sem.at[index]
            )
        )
    loads = []
    for index in range(2):
        loads.append(
            (
                pltpu.make_async_copy(normed_hbm[index], normed.at[index], normed_sem.at[index]),
                pltpu.make_async_copy(
                    upstream_hbm[index], upstream.at[index], upstream_sem.at[index]
                ),
                pltpu.make_async_copy(turned_hbm[index], turned.at[index], turned_sem.at[index]),
            )
        )
    for copy in copies:
        copy.start()
    for load in loads:
        load[0].start()
        load[1].start()
    for load in loads:
        load[2].start()
    for copy in copies:
        copy.wait()
    save = pltpu.make_async_copy(weight, weight_out, weight_sem)
    save.start()
    length = back.shape[1]
    block = length // 3
    back_saves = []
    for index in range(2):
        loads[index][0].wait()
        loads[index][1].wait()
        for start in range(0, length, block):
            conv = jnp.zeros((block, weight.shape[2]), F32)
            for tap in range(FILTER_TAPS):
                low = start + tap * DILATION_STEP
                conv = conv + jnp.dot(
                    normed[index, low : low + block, :], weight[tap], preferred_element_type=F32
                )
            incoming = upstream[index, start : start + block, :].astype(F32)
            back[index, start : start + block, :] = (incoming * gelu_slope(conv)).astype(BF16)
        back_save = pltpu.make_async_copy(back.at[index], back_out[index], back_sem.at[index])
        back_save.start()
        back_saves.append(back_save)
    for load in loads:
        load[2].wait()
    count = turned.shape[2]
    saves = []
    for tap in range(FILTER_TAPS):
        low = 2 * REACH - tap * DILATION_STEP
        total = jnp.dot(turned[0], back[0, low : low + count, :], preferred_element_type=F32)
        total = total + jnp.dot(
            turned[1], back[1, low : low + count, :], preferred_element_type=F32
        )
        grad[tap] = total.astype(BF16)
        grad_save = pltpu.make_async_copy(grad.at[tap], grad_out[tap], grad_sem.at[tap])
        grad_save.start()
        saves.append(grad_save)
    for copy in [save] + back_saves + saves:
        copy.wait()


def forward(position, pieces, normed, turned, upstream):
    channels = normed[0].shape[1]
    half = channels // 2
    length = upstream[0].shape[0]
    count = turned[0].shape[1]
    anywhere = pl.BlockSpec(memory_space=pl.ANY)
    dma = pltpu.SemaphoreType.DMA
    return pl.pallas_call(
        forward_kernel,
        out_shape=[jax.ShapeDtypeStruct((FILTER_TAPS, channels, half), BF16)]
        + [jax.ShapeDtypeStruct((length, half), BF16)] * 2
        + [jax.ShapeDtypeStruct((channels, half), BF16)] * 3,
        in_specs=[pl.BlockSpec(memory_space=pltpu.SMEM)] + [anywhere] * 16,
        out_specs=[anywhere] * 6,
        scratch_shapes=[
            pltpu.VMEM((FILTER_TAPS, channels, half), BF16),
            pltpu.VMEM((2,) + normed[0].shape, BF16),
            pltpu.VMEM((2,) + turned[0].shape, BF16),
            pltpu.VMEM((2, length, half), BF16),
            pltpu.VMEM((2, length, half), BF16),
            pltpu.VMEM((FILTER_TAPS, channels, half), BF16),
            dma((10,)),
            dma((2,)),
            dma((2,)),
            dma((2,)),
            dma((2,)),
            dma((3,)),
            dma,
        ],
        compiler_params=pltpu.CompilerParams(vmem_limit_bytes=56 * 1024 * 1024),
        name="forward",
    )(position, *pieces, *normed, *turned, *upstream)


def backward_kernel(back_a, back_b, weight_a, weight_b, inputs, scale, gain, incoming, out):
    block = out.shape[0]
    start = pl.program_id(0) * block
    grad = jnp.zeros(out.shape, F32)
    for back, weight in ((back_a, weight_a), (back_b, weight_b)):
        for tap in range(FILTER_TAPS):
            low = start + (FILTER_TAPS - 1 - tap) * DILATION_STEP
            grad = grad + lax.dot_general(
                back[pl.ds(pl.multiple_of(low, 32), block), :],
                weight[tap],
                (((1,), (1,)), ((), ())),
                preferred_element_type=F32,
            )
    scaled = grad * gain[...]
    value = inputs[...]
    factor = scale[...]
    spread = jnp.mean(scaled * value, axis=-1, keepdims=True)
    result = incoming[...].astype(F32) + factor * scaled - value * (factor * factor * factor * spread)
    out[...] = result.astype(BF16)


def backward(back, weight, inputs, scale, gain, incoming):
    count, channels = inputs.shape
    block = 256
    whole = lambda array: pl.BlockSpec(array.shape, lambda i: (0,) * array.ndim)
    part = pl.BlockSpec((block, channels), lambda i: (i, 0))
    return pl.pallas_call(
        backward_kernel,
        grid=(count // block,),
        out_shape=jax.ShapeDtypeStruct((count, channels), BF16),
        in_specs=[whole(back[0]), whole(back[1]), whole(weight[0]), whole(weight[1]), part]
        + [pl.BlockSpec((block, 1), lambda i: (i, 0)), whole(gain), part],
        out_specs=part,
        compiler_params=pltpu.CompilerParams(vmem_limit_bytes=56 * 1024 * 1024),
        name="backward",
    )(*back, *weight, inputs, scale, gain, incoming)


def reduce_weight_grad(grads, x, y):
    quarter = grads[0].shape[0] // 4
    rows = quarter // 4

    def along_x(step):
        start = ((x + step) % 4) * quarter
        return jnp.stack(
            [lax.dynamic_slice_in_dim(grad, start, quarter, axis=0) for grad in grads[:2]]
        )

    def along_y(step):
        start = ((y + step) % 4) * rows
        tall = grads[2].reshape(4, quarter, -1)
        return lax.dynamic_slice_in_dim(tall, start, rows, axis=1)

    first = [along_x(0)] + [shift(along_x(step), "x", 4, step) for step in (1, 3, 2)]
    second = [along_y(0)] + [shift(along_y(step), RING_Y, 4, step) for step in (1, 3, 2)]

    def over_y(step):
        start = ((y + step) % 4) * rows
        return sum(
            lax.dynamic_slice_in_dim(part, start, rows, axis=1).astype(F32) for part in first
        )

    def over_x(step):
        start = (x + step) % 4
        return sum(
            lax.dynamic_slice_in_dim(part, start, 1, axis=0).astype(F32) for part in second
        )

    total_y = over_y(0) + sum(
        shift(over_y(step).astype(BF16), RING_Y, 4, step).astype(F32) for step in (1, 3, 2)
    )
    total_x = over_x(0) + sum(
        shift(over_x(step).astype(BF16), "x", 4, step).astype(F32) for step in (1, 3, 2)
    )
    return jnp.concatenate([total_y, total_x], axis=0)


def share_weight_grad(total, yl, core):
    for mask in (1, 2, 4):
        sent = total.astype(BF16)
        total = sent.astype(F32) + swap(sent, "z", 8, mask).astype(F32)
    mine = total.astype(BF16)
    other = swap(mine, "yl", 2, 1)
    by_core = [jnp.where(yl == rows, mine, other) for rows in range(2)]
    kept = jnp.where(core == 0, by_core[0], by_core[1])
    sent = jnp.where(core == 0, by_core[1], by_core[0])
    arrived = swap(sent, "core", 2, 1)
    low = jnp.where(core == 0, kept, arrived)
    high = jnp.where(core == 0, arrived, kept)
    return jnp.concatenate([low, high], axis=2).astype(F32)


def on_device(activations, nucleotides, base_table, norm_gain, filter_weight, upstream):
    x, yh, core, yl = (lax.axis_index(name) for name in ("x", "yh", "core", "yl"))
    pieces = gather_weight(filter_weight, x, yh, core)
    tokens = activations[0]
    count, channels = tokens.shape
    half = channels // 2
    bases = nucleotides[0][:, None]
    row = base_table[3][None]
    for base in (2, 1, 0):
        row = jnp.where(bases == base, base_table[base][None], row)
    inputs = tokens.astype(F32) + row
    scale_inv = lax.rsqrt(jnp.mean(inputs * inputs, axis=-1, keepdims=True) + 1e-06)
    normed = (inputs * scale_inv * norm_gain).astype(BF16)
    incoming = upstream[0]
    last = jnp.concatenate([normed[count - 2 * REACH :], incoming[count - REACH :]])
    first = jnp.concatenate([normed[: 2 * REACH], incoming[:REACH]])
    low = lax.ppermute(last, SEQ, [(i, i + 1) for i in range(15)])
    high = lax.ppermute(first, SEQ, [(i + 1, i) for i in range(15)])
    normed_wide = jnp.concatenate([low[: 2 * REACH], normed, high[: 2 * REACH]])
    upstream_wide = jnp.concatenate([low[2 * REACH :], incoming, high[2 * REACH :]])
    upstream_mine = lax.dynamic_slice_in_dim(upstream_wide, core * half, half, axis=1)
    upstream_sent = lax.dynamic_slice_in_dim(upstream_wide, (1 - core) * half, half, axis=1)
    normed_other = swap(normed_wide, "core", 2, 1)
    upstream_other = swap(upstream_sent, "core", 2, 1)
    turned = normed.T
    turned_other = swap(turned, "core", 2, 1)
    position = jnp.stack([x, yh]).astype(jnp.int32)
    weight, back, back_other, *grads = forward(
        position,
        pieces,
        (normed_wide, normed_other),
        (turned, turned_other),
        (upstream_mine, upstream_other),
    )
    total = reduce_weight_grad(grads, x, yh * 2 + yl)
    back_rest = swap(back_other, "core", 2, 1)
    weight_rest = swap(weight, "core", 2, 1)
    result = backward(
        (back, back_rest), (weight, weight_rest), inputs, scale_inv, norm_gain[None], incoming
    )
    weight_grad = share_weight_grad(total, yl, core)
    total_rows = 16 * 16 * count
    return (result[None], weight_grad / math.sqrt(total_rows))


def solution(mesh):
    grid = Mesh(mesh.devices.reshape(SIZES), AXES)
    dp, seq = ("x", "yh", "core"), SEQ
    in_specs = (
        P(dp, seq, None),
        P(dp, seq),
        P(),
        P(),
        P(None, dp, None),
        P(dp, seq, None),
    )
    out_specs = (P(dp, seq, None), P(None, dp, None))
    return jax.shard_map(
        on_device, mesh=grid, in_specs=in_specs, out_specs=out_specs, check_vma=False
    )
```

time: 335 us -> 172 us (0.51)
  the two profiles are of different devices: /device:TPU:2 before, /device:TPU:1 now
where the time goes in v1:
time: 172 us; the launch traced here: 171 us
  starting transfers between devices  62.9 us (37%)
  waiting for transfers between devices  35.5 us (21%)
  Pallas kernels  31 us (18%)
  local copies, waits for them, and re-layouts  25.8 us (15%)
  other arithmetic  14.7 us (9%)
    ppermute x12, starting transfers between devices, swap(): return lax.ppermute(value, axis, [(i, i ^ mask) for i in range(count)])  33.8 us
    ppermute x20, starting transfers between devices, shift(): return lax.ppermute(value, axis, pairs)  23.4 us
    pallas_call x1, Pallas kernels, forward(): pl.pallas_call(forward_kernel, out_shape=[jax.ShapeDtypeStruct((FILTER_TA...  19 us
    ppermute x20, waiting for transfers between devices, shift(): return lax.ppermute(value, axis, pairs)  16.4 us
    ppermute x12, waiting for transfers between devices, swap(): return lax.ppermute(value, axis, [(i, i ^ mask) for i in range(count)])  13.7 us
    pallas_call x1, Pallas kernels, backward(): pl.pallas_call(backward_kernel, grid=(count // block,), out_shape=jax.Sha...  12 us
    ppermute x1, starting transfers between devices, on_device(): low = lax.ppermute(last, SEQ, [(i, i + 1) for i in range(15)])  4.38 us
    ppermute x1, waiting for transfers between devices, on_device(): high = lax.ppermute(first, SEQ, [(i + 1, i) for i in range(15)])  4.19 us
  transfers between devices with their start and end apart: 34, of which 13 were waited for; matrix products, arithmetic and copies ran while one was open for 16% of the time, Pallas kernels for 0%

profile of v1, /device:TPU:1, one launch (start us, length us, event | category | flops | bytes accessed | tf_op | source)
XLA Modules:
  0.0 170.8 jit_solution(3663076632379921009)
XLA Ops:
  0.6 0.9 slice_reduce_fusion.3
  1.5 0.7 compare_reduce_fusion.2
  2.3 3.7 %multiply_reduce_fusion = (f32[1280]{0:T(1024)S(1)}, f32[1280,768]{1,0:T(8,128)S(1)}) fusion(f32[768]{0:T(1024)S(1)} %get-tuple-element.16, f32[768]{0:T(1024)S(1)} %get-tuple-element.17, pred[1280]{0:T(1024)(128)(4,1)S(1)} %get-tuple-element.19, f32[768]{0:T(1024)S(1)} %get-tuple-element.15, pred[1280]{0:T(1024)(128)(4,1)S(1)} %get-tuple-element.20, ...), kind=kLoop, calls=%fused_computation.2 | loop fusion | flops 6880000 | bytes 5919488 | tf_op jit(solution)/shard_map/reduce_sum | solution.py:283
  6.1 0.4 multiply_convert_fusion
  6.5 0.9 slice_bitcast_fusion.1
  7.4 4.4 %collective-permute-start.10 = (bf16[96,768]{1,0:T(8,128)(2,1)S(1)}, bf16[96,768]{1,0:T(8,128)(2,1)S(1)}, u32[]{:S(2)}, u32[]{:S(2)}) collective-permute-start(bf16[96,768]{1,0:T(8,128)(2,1)S(1)} %pad_maximum_fusion.5), channel_id=1, source_target_pairs={{0,1},{1,2},{2,3},{3,4},{4,5},{5,6},{6,7},{7,8},{8,9},{9,10},{10,1... | collective-permute-start | bytes 442376 | tf_op jit(solution)/shard_map/ppermute | solution.py:288
  11.9 1.3 collective-permute-start.11
  13.2 1.2 collective-permute-done.10
  14.3 4.2 %collective-permute-done.11 = bf16[96,768]{1,0:T(8,128)(2,1)S(1)} collective-permute-done((bf16[96,768]{1,0:T(8,128)(2,1)S(1)}, bf16[96,768]{1,0:T(8,128)(2,1)S(1)}, u32[]{:S(2)}, u32[]{:S(2)}) %collective-permute-start.11) | collective-permute-done | bytes 147488 | tf_op jit(solution)/shard_map/ppermute | solution.py:289
  18.7 1.8 %collective-permute-start.12 = (bf16[1408,768]{1,0:T(8,128)(2,1)S(1)}, bf16[1408,768]{1,0:T(8,128)(2,1)}, u32[]{:S(2)}, u32[]{:S(2)}) collective-permute-start(bf16[1408,768]{1,0:T(8,128)(2,1)S(1)} %pad_maximum_fusion.refs_10_), channel_id=1, source_target_pairs={{0,16},{16,0},{1,17},{17,1},{2,18},{18,2},{3,19},{19,3},{4,20},{20... | collective-permute-start | bytes 6488072 | tf_op jit(solution)/shard_map/ppermute | solution.py:28
  20.5 1.7 fusion.5
  22.4 1.7 %pad_maximum_fusion.1 = bf16[1344,768]{1,0:T(8,128)(2,1)S(1)} fusion(bf16[32,768]{1,0:T(8,128)(2,1)S(1)} %slice.81, bf16[1280,768]{1,0:T(8,128)(2,1)} %bitcast.31, bf16[32,768]{1,0:T(8,128)(2,1)S(1)} %slice.80), kind=kLoop, calls=%fused_computation.4 | loop fusion | flops 6193152 | bytes 4128768 | tf_op jit(solution)/shard_map/concatenate | solution.py:291
  24.1 1.6 constant_dynamic-slice_fusion.3
  25.7 0.4 collective-permute-start.14
  26.1 0.7 constant_dynamic-slice_fusion.6
  26.9 2.1 %collective-permute-done = bf16[3,48,384]{2,1,0:T(8,128)(2,1)S(1)} collective-permute-done((bf16[3,48,384]{2,1,0:T(8,128)(2,1)}, bf16[3,48,384]{2,1,0:T(8,128)(2,1)S(1)}, u32[]{:S(2)}, u32[]{:S(2)}) %collective-permute-start) | collective-permute-done | bytes 110624 | tf_op jit(solution)/shard_map/ppermute | solution.py:28
  29.0 0.6 copy-done.10
  29.6 1.0 maximum_select_fusion.refs_0_
  30.7 4.6 %collective-permute-start.1 = (bf16[3,96,384]{2,1,0:T(8,128)(2,1)S(1)}, bf16[3,96,384]{2,1,0:T(8,128)(2,1)}, u32[]{:S(2)}, u32[]{:S(2)}) collective-permute-start(bf16[3,96,384]{2,1,0:T(8,128)(2,1)S(1)} %maximum_select_fusion.refs_0_), channel_id=1, source_target_pairs={{0,40},{8,32},{32,8},{40,0},{1,41},{9,33},{33,9},{41,1},{2,42},{10... | collective-permute-start | bytes 663560 | tf_op jit(solution)/shard_map/ppermute | solution.py:28
  35.2 1.2 collective-permute-start.2
  36.5 4.4 %collective-permute-done.1.refs_1_ = bf16[3,96,384]{2,1,0:T(8,128)(2,1)} collective-permute-done((bf16[3,96,384]{2,1,0:T(8,128)(2,1)S(1)}, bf16[3,96,384]{2,1,0:T(8,128)(2,1)}, u32[]{:S(2)}, u32[]{:S(2)}) %collective-permute-start.1) | collective-permute-done | bytes 221216 | tf_op jit(solution)/shard_map/ppermute | solution.py:28
  40.9 2.5 %collective-permute-start.4 = (bf16[3,96,384]{2,1,0:T(8,128)(2,1)S(1)}, bf16[3,96,384]{2,1,0:T(8,128)(2,1)S(1)}, u32[]{:S(2)}, u32[]{:S(2)}) collective-permute-start(bf16[3,96,384]{2,1,0:T(8,128)(2,1)S(1)} %maximum_select_fusion.refs_0_), channel_id=1, source_target_pairs={{0,192},{64,0},{128,64},{192,128},{1,193},{65,1},{129,65},{193,129... | collective-permute-start | bytes 663560 | tf_op jit(solution)/shard_map/ppermute | solution.py:24
  43.3 3.8 %collective-permute-done.4.refs_4_ = bf16[3,96,384]{2,1,0:T(8,128)(2,1)S(1)} collective-permute-done((bf16[3,96,384]{2,1,0:T(8,128)(2,1)S(1)}, bf16[3,96,384]{2,1,0:T(8,128)(2,1)S(1)}, u32[]{:S(2)}, u32[]{:S(2)}) %collective-permute-start.4) | collective-permute-done | bytes 221216 | tf_op jit(solution)/shard_map/ppermute | solution.py:24
  47.2 0.7 copy-done.7
  47.9 3.4 %collective-permute-start.5 = (bf16[3,96,384]{2,1,0:T(8,128)(2,1)}, bf16[3,96,384]{2,1,0:T(8,128)(2,1)}, u32[]{:S(2)}, u32[]{:S(2)}) collective-permute-start(bf16[3,96,384]{2,1,0:T(8,128)(2,1)} %collective-permute-done.1.refs_1_), channel_id=1, source_target_pairs={{0,192},{64,0},{128,64},{192,128},{1,193},{65,1},{129,65},{193,129... | collective-permute-start | bytes 663560 | tf_op jit(solution)/shard_map/ppermute | solution.py:24
  51.3 0.7 slice.72
  52.0 4.0 %copy.10.refs_12_ = bf16[768,1280]{1,0:T(8,128)(2,1)} copy(bf16[768,1280]{0,1:T(8,128)(2,1)} %fusion.5) | data formatting | bytes 3932160 | tf_op jit(solution)/shard_map/transpose | solution.py:296
  56.0 1.6 slice.73
  57.5 1.5 slice.74
  59.1 2.7 %collective-permute-start.7 = (bf16[3,48,384]{2,1,0:T(8,128)(2,1)}, bf16[3,48,384]{2,1,0:T(8,128)(2,1)}, u32[]{:S(2)}, u32[]{:S(2)}) collective-permute-start(bf16[3,48,384]{2,1,0:T(8,128)(2,1)} %slice.73), channel_id=1, source_target_pairs={{0,192},{64,0},{128,64},{192,128},{1,193},{65,1},{129,65},{193,129... | collective-permute-start | bytes 331784 | tf_op jit(solution)/shard_map/ppermute | solution.py:24
  61.7 1.5 slice.75
  63.3 2.7 %collective-permute-start.9 = (bf16[3,48,384]{2,1,0:T(8,128)(2,1)}, bf16[3,48,384]{2,1,0:T(8,128)(2,1)}, u32[]{:S(2)}, u32[]{:S(2)}) collective-permute-start(bf16[3,48,384]{2,1,0:T(8,128)(2,1)} %slice.75), channel_id=1, source_target_pairs={{0,192},{64,0},{128,64},{192,128},{1,193},{65,1},{129,65},{193,129... | collective-permute-start | bytes 331784 | tf_op jit(solution)/shard_map/ppermute | solution.py:24
  66.0 0.6 pad_add_fusion.position
  66.5 4.0 %copy.11.refs_13_ = bf16[768,1280]{1,0:T(8,128)(2,1)} copy(bf16[768,1280]{0,1:T(8,128)(2,1)} %collective-permute-done.13) | data formatting | bytes 3932160 | tf_op jit(solution)/shard_map/ppermute | solution.py:28
  70.6 1.0 copy-done.3
  71.6 19.0 %forward.1 = (bf16[3,768,384]{2,1,0:T(8,128)(2,1)}, bf16[1344,384]{1,0:T(8,128)(2,1)}, bf16[1344,384]{1,0:T(8,128)(2,1)}, bf16[768,384]{1,0:T(8,128)(2,1)}, bf16...) custom-call(s32[2]{0:T(128)} %pad_add_fusion.position, bf16[3,96,384]{2,1,0:T(8,128)(2,1)} %copy-done.5, ...), custom_call_target="tpu_custom_call" | custom-call | tf_op jit(solution)/shard_map/forward/pallas_call | solution.py:153
  90.6 1.6 dynamic-slice_bitcast_fusion.4
  92.2 0.8 pad_maximum_fusion.2
  93.0 2.8 %collective-permute-start.18 = (bf16[2,192,384]{2,1,0:T(8,128)(2,1)S(1)}, bf16[2,192,384]{2,1,0:T(8,128)(2,1)S(1)}, u32[]{:S(2)}, u32[]{:S(2)}) collective-permute-start(bf16[2,192,384]{2,1,0:T(8,128)(2,1)S(1)} %pad_maximum_fusion.3), channel_id=1, source_target_pairs={{0,192},{64,0},{128,64},{192,128},{1,193},{65,1},{129,65},{193,129... | collective-permute-start | bytes 884744 | tf_op jit(solution)/shard_map/ppermute | solution.py:24
  95.7 1.8 %constant_dynamic-slice_fusion.1 = (bf16[4,48,384]{2,1,0:T(8,128)(2,1)S(1)}, bf16[4,48,384]{2,1,0:T(8,128)(2,1)}, bf16[4,48,384]{2,1,0:T(8,128)(2,1)}) fusion(bf16[4,192,384]{2,1,0:T(8,128)(2,1)} %bitcast.34, s32[]{:T(128)S(6)} %select_n.208, s32[]{:T(128)S(6)} %select_n.212, s32[]{:T(128)S(6)} %select_n.210), kind=kLoop, calls=%fused_computation.56 | loop fusion | bytes 884748 | tf_op jit(solution)/shard_map/dynamic_slice | solution.py:231
  97.5 0.7 pad_maximum_fusion.4
  98.3 2.7 %collective-permute-start.24 = (bf16[4,48,384]{2,1,0:T(8,128)(2,1)}, bf16[4,48,384]{2,1,0:T(8,128)(2,1)}, u32[]{:S(2)}, u32[]{:S(2)}) collective-permute-start(bf16[4,48,384]{2,1,0:T(8,128)(2,1)} %get-tuple-element.48), channel_id=1, source_target_pairs={{0,40},{8,0},{32,8},{40,32},{1,41},{9,1},{33,9},{41,33},{2,42},{10... | collective-permute-start | bytes 442376 | tf_op jit(solution)/shard_map/ppermute | solution.py:24
  100.9 2.1 %collective-permute-done.23 = bf16[4,48,384]{2,1,0:T(8,128)(2,1)S(1)} collective-permute-done((bf16[4,48,384]{2,1,0:T(8,128)(2,1)S(1)}, bf16[4,48,384]{2,1,0:T(8,128)(2,1)S(1)}, u32[]{:S(2)}, u32[]{:S(2)}) %collective-permute-start.23) | collective-permute-done | bytes 147488 | tf_op jit(solution)/shard_map/ppermute | solution.py:24
  103.0 0.3 collective-permute-done.24
  103.4 6.3 %collective-permute-done.25 = bf16[4,48,384]{2,1,0:T(8,128)(2,1)} collective-permute-done((bf16[4,48,384]{2,1,0:T(8,128)(2,1)}, bf16[4,48,384]{2,1,0:T(8,128)(2,1)}, u32[]{:S(2)}, u32[]{:S(2)}) %collective-permute-start.25) | collective-permute-done | bytes 147488 | tf_op jit(solution)/shard_map/ppermute | solution.py:24
  109.7 1.0 add_convert_fusion.10
  110.8 2.7 %collective-permute-start.27 = (bf16[1,48,384]{2,1,0:T(8,128)(2,1)S(1)}, bf16[1,48,384]{2,1,0:T(8,128)(2,1)S(1)}, u32[]{:S(2)}, u32[]{:S(2)}) collective-permute-start(bf16[1,48,384]{2,1,0:T(8,128)(2,1)S(1)} %get-tuple-element.37), channel_id=1, source_target_pairs={{0,192},{64,0},{128,64},{192,128},{1,193},{65,1},{129,65},{193,129... | collective-permute-start | bytes 110600 | tf_op jit(solution)/shard_map/ppermute | solution.py:24
  113.7 2.7 %collective-permute-start.21 = (bf16[2,48,384]{2,1,0:T(8,128)(2,1)S(1)}, bf16[2,48,384]{2,1,0:T(8,128)(2,1)S(1)}, u32[]{:S(2)}, u32[]{:S(2)}) collective-permute-start(bf16[2,48,384]{2,1,0:T(8,128)(2,1)S(1)} %get-tuple-element.33), channel_id=1, source_target_pairs={{0,40},{8,0},{32,8},{40,32},{1,41},{9,1},{33,9},{41,33},{2,42},{10... | collective-permute-start | bytes 221192 | tf_op jit(solution)/shard_map/ppermute | solution.py:24
  116.4 1.4 collective-permute-done.28
  117.7 0.9 add_convert_fusion.7
  118.6 2.4 %collective-permute-done.22 = bf16[2,48,384]{2,1,0:T(8,128)(2,1)S(1)} collective-permute-done((bf16[2,48,384]{2,1,0:T(8,128)(2,1)S(1)}, bf16[2,48,384]{2,1,0:T(8,128)(2,1)S(1)}, u32[]{:S(2)}, u32[]{:S(2)}) %collective-permute-start.22) | collective-permute-done | bytes 73760 | tf_op jit(solution)/shard_map/ppermute | solution.py:24
  121.3 7.3 %collective-permute-start.16 = (bf16[3,768,384]{2,1,0:T(8,128)(2,1)S(1)}, bf16[3,768,384]{2,1,0:T(8,128)(2,1)}, u32[]{:S(2)}, u32[]{:S(2)}) collective-permute-start(bf16[3,768,384]{2,1,0:T(8,128)(2,1)S(1)} %copy-done.2), channel_id=1, source_target_pairs={{0,16},{16,0},{1,17},{17,1},{2,18},{18,2},{3,19},{19,3},{4,20},{20... | collective-permute-start | bytes 5308424 | tf_op jit(solution)/shard_map/ppermute | solution.py:28
  128.6 5.1 %collective-permute-start.30 = (bf16[3,48,384]{2,1,0:T(8,128)(2,1)S(1)}, bf16[3,48,384]{2,1,0:T(8,128)(2,1)S(1)}, u32[]{:S(2)}, u32[]{:S(2)}) collective-permute-start(bf16[3,48,384]{2,1,0:T(8,128)(2,1)S(1)} %add_convert_fusion.2), channel_id=1, source_target_pairs={{0,2},{1,3},{2,0},{3,1},{4,6},{5,7},{6,4},{7,5},{8,10},{9,11},{10,... | collective-permute-start | bytes 331784 | tf_op jit(solution)/shard_map/ppermute | solution.py:28
  133.7 3.1 %collective-permute-done.30 = bf16[3,48,384]{2,1,0:T(8,128)(2,1)S(1)} collective-permute-done((bf16[3,48,384]{2,1,0:T(8,128)(2,1)S(1)}, bf16[3,48,384]{2,1,0:T(8,128)(2,1)S(1)}, u32[]{:S(2)}, u32[]{:S(2)}) %collective-permute-start.30) | collective-permute-done | bytes 110624 | tf_op jit(solution)/shard_map/ppermute | solution.py:28
  136.9 3.8 %collective-permute-start.31 = (bf16[3,48,384]{2,1,0:T(8,128)(2,1)S(1)}, bf16[3,48,384]{2,1,0:T(8,128)(2,1)S(1)}, u32[]{:S(2)}, u32[]{:S(2)}) collective-permute-start(bf16[3,48,384]{2,1,0:T(8,128)(2,1)S(1)} %add_convert_fusion.1), channel_id=1, source_target_pairs={{0,4},{1,5},{2,6},{3,7},{4,0},{5,1},{6,2},{7,3},{8,12},{9,13},{10,... | collective-permute-start | bytes 331784 | tf_op jit(solution)/shard_map/ppermute | solution.py:28
  140.7 4.3 %collective-permute-start.15 = (bf16[1344,384]{1,0:T(8,128)(2,1)}, bf16[1344,384]{1,0:T(8,128)(2,1)S(1)}, u32[]{:S(2)}, u32[]{:S(2)}) collective-permute-start(bf16[1344,384]{1,0:T(8,128)(2,1)} %get-tuple-element.9), channel_id=1, source_target_pairs={{0,16},{16,0},{1,17},{17,1},{2,18},{18,2},{3,19},{19,3},{4,20},{20... | collective-permute-start | bytes 3096584 | tf_op jit(solution)/shard_map/ppermute | solution.py:28
  144.9 0.3 collective-permute-done.31
  145.3 3.9 %collective-permute-done.32 = bf16[3,48,384]{2,1,0:T(8,128)(2,1)S(1)} collective-permute-done((bf16[3,48,384]{2,1,0:T(8,128)(2,1)S(1)}, bf16[3,48,384]{2,1,0:T(8,128)(2,1)S(1)}, u32[]{:S(2)}, u32[]{:S(2)}) %collective-permute-start.32) | collective-permute-done | bytes 110624 | tf_op jit(solution)/shard_map/ppermute | solution.py:28
  149.2 6.1 %collective-permute-start.33 = (bf16[3,48,384]{2,1,0:T(8,128)(2,1)S(1)}, bf16[3,48,384]{2,1,0:T(8,128)(2,1)S(1)}, u32[]{:S(2)}, u32[]{:S(2)}) collective-permute-start(bf16[3,48,384]{2,1,0:T(8,128)(2,1)S(1)} %get-tuple-element.21), channel_id=1, source_target_pairs={{0,16},{16,0},{1,17},{17,1},{2,18},{18,2},{3,19},{19,3},{4,20},{20... | collective-permute-start | bytes 331784 | tf_op jit(solution)/shard_map/ppermute | solution.py:28
  155.3 1.1 rsqrt.7.scale
  156.4 0.6 broadcast_in_dim.77.gain
  157.0 0.8 convert_multiply_fusion
  157.9 1.0 copy-done.4
  158.8 12.0 %backward.1 = bf16[1280,768]{1,0:T(8,128)(2,1)} custom-call(bf16[1344,384]{1,0:T(8,128)(2,1)} %get-tuple-element.8.back_a, bf16[1344,384]{1,0:T(8,128)(2,1)} %copy-done.4, bf16[3,768,384]{2,1,0:T(8,128)(2,1)} %get-tuple-element.10.weight_a, bf16[3,768,384]{2,1,0:T(8,128)(2,1)} %collective-permute-done.16.weight_b, f32[1280,768]{1,0:T(8,128)} %copy-done, ...), custom_call_target="tpu_custom_call" | custom-call | tf_op jit(solution)/shard_map/backward/pallas_call | solution.py:206
  (74 shorter events, 1.5 us)
Async XLA Ops:
  0.6 5.4 %copy-start.11 = (f32[768]{0:T(1024)S(1)}, f32[768]{0:T(1024)}, u32[]{:S(2)}) copy-start(f32[768]{0:T(1024)} %param.9) | copy-start | bytes 9220
  6.0 14.4 %copy-start = (f32[1280,768]{1,0:T(8,128)}, f32[1280,768]{1,0:T(8,128)S(1)}, u32[]{:S(2)}) copy-start(f32[1280,768]{1,0:T(8,128)S(1)} %get-tuple-element.25.inputs) | copy-start | bytes 11796484
  7.4 6.9 %collective-permute-start.10 = (bf16[96,768]{1,0:T(8,128)(2,1)S(1)}, bf16[96,768]{1,0:T(8,128)(2,1)S(1)}, u32[]{:S(2)}, u32[]{:S(2)}) collective-permute-start(bf16[96,768]{1,0:T(8,128)(2,1)S(1)} %pad_maximum_fusion.5), channel_id=1, source_target_pairs={{0,1},{1,2},{2,3},{3,4},{4,5},{5,6},{6,7},{7,8},{8,9},{9,10},{10,1... | collective-permute-start | bytes 442376 | tf_op jit(solution)/shard_map/ppermute | solution.py:288
  11.9 6.7 %collective-permute-start.11 = (bf16[96,768]{1,0:T(8,128)(2,1)S(1)}, bf16[96,768]{1,0:T(8,128)(2,1)S(1)}, u32[]{:S(2)}, u32[]{:S(2)}) collective-permute-start(bf16[96,768]{1,0:T(8,128)(2,1)S(1)} %pad_maximum_fusion.6), channel_id=1, source_target_pairs={{1,0},{2,1},{3,2},{4,3},{5,4},{6,5},{7,6},{8,7},{9,8},{10,9},{11,1... | collective-permute-start | bytes 442376 | tf_op jit(solution)/shard_map/ppermute | solution.py:289
  18.7 5.4 %copy-start.1 = (bf16[1408,768]{1,0:T(8,128)(2,1)}, bf16[1408,768]{1,0:T(8,128)(2,1)S(1)}, u32[]{:S(2)}) copy-start(bf16[1408,768]{1,0:T(8,128)(2,1)S(1)} %pad_maximum_fusion.refs_10_) | copy-start | bytes 6488068
  18.7 51.9 %collective-permute-start.12 = (bf16[1408,768]{1,0:T(8,128)(2,1)S(1)}, bf16[1408,768]{1,0:T(8,128)(2,1)}, u32[]{:S(2)}, u32[]{:S(2)}) collective-permute-start(bf16[1408,768]{1,0:T(8,128)(2,1)S(1)} %pad_maximum_fusion.refs_10_), channel_id=1, source_target_pairs={{0,16},{16,0},{1,17},{17,1},{2,18},{18,2},{3,19},{19,3},{4,20},{20... | collective-permute-start | bytes 6488072 | tf_op jit(solution)/shard_map/ppermute | solution.py:28
  22.1 41.2 %collective-permute-start.13 = (bf16[768,1280]{0,1:T(8,128)(2,1)}, bf16[768,1280]{0,1:T(8,128)(2,1)}, u32[]{:S(2)}, u32[]{:S(2)}) collective-permute-start(bf16[768,1280]{0,1:T(8,128)(2,1)} %fusion.5), channel_id=1, source_target_pairs={{0,16},{16,0},{1,17},{17,1},{2,18},{18,2},{3,19},{19,3},{4,20},{20... | collective-permute-start | bytes 5898248 | tf_op jit(solution)/shard_map/ppermute | solution.py:28
  22.3 3.7 %copy-start.8 = (bf16[3,48,768]{2,1,0:T(8,128)(2,1)S(1)}, bf16[3,48,768]{2,1,0:T(8,128)(2,1)}, u32[]{:S(2)}) copy-start(bf16[3,48,768]{2,1,0:T(8,128)(2,1)} %param.10) | copy-start | bytes 663556
  25.7 44.8 %collective-permute-start.14 = (bf16[1344,384]{1,0:T(8,128)(2,1)}, bf16[1344,384]{1,0:T(8,128)(2,1)S(1)}, u32[]{:S(2)}, u32[]{:S(2)}) collective-permute-start(bf16[1344,384]{1,0:T(8,128)(2,1)} %get-tuple-element.26), channel_id=1, source_target_pairs={{0,16},{16,0},{1,17},{17,1},{2,18},{18,2},{3,19},{19,3},{4,20},{20... | collective-permute-start | bytes 3096584 | tf_op jit(solution)/shard_map/ppermute | solution.py:28
  26.8 2.2 %collective-permute-start = (bf16[3,48,384]{2,1,0:T(8,128)(2,1)}, bf16[3,48,384]{2,1,0:T(8,128)(2,1)S(1)}, u32[]{:S(2)}, u32[]{:S(2)}) collective-permute-start(bf16[3,48,384]{2,1,0:T(8,128)(2,1)} %get-tuple-element.52), channel_id=1, source_target_pairs={{0,16},{16,0},{1,17},{17,1},{2,18},{18,2},{3,19},{19,3},{4,20},{20... | collective-permute-start | bytes 331784 | tf_op jit(solution)/shard_map/ppermute | solution.py:28
  29.0 0.6 copy-start.10
  30.7 39.8 %copy-start.5 = (bf16[3,96,384]{2,1,0:T(8,128)(2,1)}, bf16[3,96,384]{2,1,0:T(8,128)(2,1)S(1)}, u32[]{:S(2)}) copy-start(bf16[3,96,384]{2,1,0:T(8,128)(2,1)S(1)} %maximum_select_fusion.refs_0_) | copy-start | bytes 663556
  30.7 10.2 %collective-permute-start.1 = (bf16[3,96,384]{2,1,0:T(8,128)(2,1)S(1)}, bf16[3,96,384]{2,1,0:T(8,128)(2,1)}, u32[]{:S(2)}, u32[]{:S(2)}) collective-permute-start(bf16[3,96,384]{2,1,0:T(8,128)(2,1)S(1)} %maximum_select_fusion.refs_0_), channel_id=1, source_target_pairs={{0,40},{8,32},{32,8},{40,0},{1,41},{9,33},{33,9},{41,1},{2,42},{10... | collective-permute-start | bytes 663560 | tf_op jit(solution)/shard_map/ppermute | solution.py:28
  35.2 8.1 %collective-permute-start.2 = (bf16[3,96,384]{2,1,0:T(8,128)(2,1)S(1)}, bf16[3,96,384]{2,1,0:T(8,128)(2,1)S(1)}, u32[]{:S(2)}, u32[]{:S(2)}) collective-permute-start(bf16[3,96,384]{2,1,0:T(8,128)(2,1)S(1)} %maximum_select_fusion.refs_0_), channel_id=1, source_target_pairs={{0,64},{64,128},{128,192},{192,0},{1,65},{65,129},{129,193},{193,1... | collective-permute-start | bytes 663560 | tf_op jit(solution)/shard_map/ppermute | solution.py:24
  40.9 6.3 %collective-permute-start.4 = (bf16[3,96,384]{2,1,0:T(8,128)(2,1)S(1)}, bf16[3,96,384]{2,1,0:T(8,128)(2,1)S(1)}, u32[]{:S(2)}, u32[]{:S(2)}) collective-permute-start(bf16[3,96,384]{2,1,0:T(8,128)(2,1)S(1)} %maximum_select_fusion.refs_0_), channel_id=1, source_target_pairs={{0,192},{64,0},{128,64},{192,128},{1,193},{65,1},{129,65},{193,129... | collective-permute-start | bytes 663560 | tf_op jit(solution)/shard_map/ppermute | solution.py:24
  43.3 8.0 %copy-start.6 = (bf16[3,96,384]{2,1,0:T(8,128)(2,1)}, bf16[3,96,384]{2,1,0:T(8,128)(2,1)S(1)}, u32[]{:S(2)}) copy-start(bf16[3,96,384]{2,1,0:T(8,128)(2,1)S(1)} %collective-permute-done.2.refs_2_) | copy-start | bytes 663556
  43.3 8.6 %collective-permute-start.3 = (bf16[3,96,384]{2,1,0:T(8,128)(2,1)}, bf16[3,96,384]{2,1,0:T(8,128)(2,1)}, u32[]{:S(2)}, u32[]{:S(2)}) collective-permute-start(bf16[3,96,384]{2,1,0:T(8,128)(2,1)} %collective-permute-done.1.refs_1_), channel_id=1, source_target_pairs={{0,64},{64,128},{128,192},{192,0},{1,65},{65,129},{129,193},{193,1... | collective-permute-start | bytes 663560 | tf_op jit(solution)/shard_map/ppermute | solution.py:24
  47.2 0.7 copy-start.7
  47.9 11.2 %collective-permute-start.5 = (bf16[3,96,384]{2,1,0:T(8,128)(2,1)}, bf16[3,96,384]{2,1,0:T(8,128)(2,1)}, u32[]{:S(2)}, u32[]{:S(2)}) collective-permute-start(bf16[3,96,384]{2,1,0:T(8,128)(2,1)} %collective-permute-done.1.refs_1_), channel_id=1, source_target_pairs={{0,192},{64,0},{128,64},{192,128},{1,193},{65,1},{129,65},{193,129... | collective-permute-start | bytes 663560 | tf_op jit(solution)/shard_map/ppermute | solution.py:24
  52.0 11.3 %collective-permute-start.6 = (bf16[3,48,384]{2,1,0:T(8,128)(2,1)}, bf16[3,48,384]{2,1,0:T(8,128)(2,1)S(1)}, u32[]{:S(2)}, u32[]{:S(2)}) collective-permute-start(bf16[3,48,384]{2,1,0:T(8,128)(2,1)} %slice.72), channel_id=1, source_target_pairs={{0,64},{64,128},{128,192},{192,0},{1,65},{65,129},{129,193},{193,1... | collective-permute-start | bytes 331784 | tf_op jit(solution)/shard_map/ppermute | solution.py:24
  59.1 11.4 %collective-permute-start.7 = (bf16[3,48,384]{2,1,0:T(8,128)(2,1)}, bf16[3,48,384]{2,1,0:T(8,128)(2,1)}, u32[]{:S(2)}, u32[]{:S(2)}) collective-permute-start(bf16[3,48,384]{2,1,0:T(8,128)(2,1)} %slice.73), channel_id=1, source_target_pairs={{0,192},{64,0},{128,64},{192,128},{1,193},{65,1},{129,65},{193,129... | collective-permute-start | bytes 331784 | tf_op jit(solution)/shard_map/ppermute | solution.py:24
  63.3 7.3 %copy-start.9 = (bf16[3,48,384]{2,1,0:T(8,128)(2,1)}, bf16[3,48,384]{2,1,0:T(8,128)(2,1)S(1)}, u32[]{:S(2)}) copy-start(bf16[3,48,384]{2,1,0:T(8,128)(2,1)S(1)} %collective-permute-done.6.refs_6_) | copy-start | bytes 331780
  63.3 7.2 %collective-permute-start.8 = (bf16[3,48,384]{2,1,0:T(8,128)(2,1)}, bf16[3,48,384]{2,1,0:T(8,128)(2,1)}, u32[]{:S(2)}, u32[]{:S(2)}) collective-permute-start(bf16[3,48,384]{2,1,0:T(8,128)(2,1)} %slice.74), channel_id=1, source_target_pairs={{0,64},{64,128},{128,192},{192,0},{1,65},{65,129},{129,193},{193,1... | collective-permute-start | bytes 331784 | tf_op jit(solution)/shard_map/ppermute | solution.py:24
  63.3 7.2 %collective-permute-start.9 = (bf16[3,48,384]{2,1,0:T(8,128)(2,1)}, bf16[3,48,384]{2,1,0:T(8,128)(2,1)}, u32[]{:S(2)}, u32[]{:S(2)}) collective-permute-start(bf16[3,48,384]{2,1,0:T(8,128)(2,1)} %slice.75), channel_id=1, source_target_pairs={{0,192},{64,0},{128,64},{192,128},{1,193},{65,1},{129,65},{193,129... | collective-permute-start | bytes 331784 | tf_op jit(solution)/shard_map/ppermute | solution.py:24
  70.5 1.0 copy-start.3
  90.6 30.7 %copy-start.2 = (bf16[3,768,384]{2,1,0:T(8,128)(2,1)S(1)}, bf16[3,768,384]{2,1,0:T(8,128)(2,1)}, u32[]{:S(2)}) copy-start(bf16[3,768,384]{2,1,0:T(8,128)(2,1)} %get-tuple-element.10.weight_a) | copy-start | bytes 5308420
  92.9 20.5 %collective-permute-start.17 = (bf16[2,192,384]{2,1,0:T(8,128)(2,1)}, bf16[2,192,384]{2,1,0:T(8,128)(2,1)S(1)}, u32[]{:S(2)}, u32[]{:S(2)}) collective-permute-start(bf16[2,192,384]{2,1,0:T(8,128)(2,1)} %pad_maximum_fusion.2), channel_id=1, source_target_pairs={{0,64},{64,128},{128,192},{192,0},{1,65},{65,129},{129,193},{193,1... | collective-permute-start | bytes 884744 | tf_op jit(solution)/shard_map/ppermute | solution.py:24
  93.0 20.5 %collective-permute-start.18 = (bf16[2,192,384]{2,1,0:T(8,128)(2,1)S(1)}, bf16[2,192,384]{2,1,0:T(8,128)(2,1)S(1)}, u32[]{:S(2)}, u32[]{:S(2)}) collective-permute-start(bf16[2,192,384]{2,1,0:T(8,128)(2,1)S(1)} %pad_maximum_fusion.3), channel_id=1, source_target_pairs={{0,192},{64,0},{128,64},{192,128},{1,193},{65,1},{129,65},{193,129... | collective-permute-start | bytes 884744 | tf_op jit(solution)/shard_map/ppermute | solution.py:24
  97.5 5.5 %collective-permute-start.23 = (bf16[4,48,384]{2,1,0:T(8,128)(2,1)S(1)}, bf16[4,48,384]{2,1,0:T(8,128)(2,1)S(1)}, u32[]{:S(2)}, u32[]{:S(2)}) collective-permute-start(bf16[4,48,384]{2,1,0:T(8,128)(2,1)S(1)} %get-tuple-element.46), channel_id=1, source_target_pairs={{0,8},{8,32},{32,40},{40,0},{1,9},{9,33},{33,41},{41,1},{2,10},{10... | collective-permute-start | bytes 442376 | tf_op jit(solution)/shard_map/ppermute | solution.py:24
  98.3 15.2 %collective-permute-start.19 = (bf16[2,192,384]{2,1,0:T(8,128)(2,1)}, bf16[2,192,384]{2,1,0:T(8,128)(2,1)S(1)}, u32[]{:S(2)}, u32[]{:S(2)}) collective-permute-start(bf16[2,192,384]{2,1,0:T(8,128)(2,1)} %pad_maximum_fusion.4), channel_id=1, source_target_pairs={{0,128},{64,192},{128,0},{192,64},{1,129},{65,193},{129,1},{193,65... | collective-permute-start | bytes 884744 | tf_op jit(solution)/shard_map/ppermute | solution.py:24
  98.3 5.1 %collective-permute-start.24 = (bf16[4,48,384]{2,1,0:T(8,128)(2,1)}, bf16[4,48,384]{2,1,0:T(8,128)(2,1)}, u32[]{:S(2)}, u32[]{:S(2)}) collective-permute-start(bf16[4,48,384]{2,1,0:T(8,128)(2,1)} %get-tuple-element.48), channel_id=1, source_target_pairs={{0,40},{8,0},{32,8},{40,32},{1,41},{9,1},{33,9},{41,33},{2,42},{10... | collective-permute-start | bytes 442376 | tf_op jit(solution)/shard_map/ppermute | solution.py:24
  103.0 6.6 %collective-permute-start.25 = (bf16[4,48,384]{2,1,0:T(8,128)(2,1)}, bf16[4,48,384]{2,1,0:T(8,128)(2,1)}, u32[]{:S(2)}, u32[]{:S(2)}) collective-permute-start(bf16[4,48,384]{2,1,0:T(8,128)(2,1)} %get-tuple-element.47), channel_id=1, source_target_pairs={{0,32},{8,40},{32,0},{40,8},{1,33},{9,41},{33,1},{41,9},{2,34},{10... | collective-permute-start | bytes 442376 | tf_op jit(solution)/shard_map/ppermute | solution.py:24
  110.7 5.7 %collective-permute-start.26 = (bf16[1,48,384]{2,1,0:T(8,128)(2,1)S(1)}, bf16[1,48,384]{2,1,0:T(8,128)(2,1)S(1)}, u32[]{:S(2)}, u32[]{:S(2)}) collective-permute-start(bf16[1,48,384]{2,1,0:T(8,128)(2,1)S(1)} %get-tuple-element.35), channel_id=1, source_target_pairs={{0,64},{64,128},{128,192},{192,0},{1,65},{65,129},{129,193},{193,1... | collective-permute-start | bytes 110600 | tf_op jit(solution)/shard_map/ppermute | solution.py:24
  110.8 5.6 %collective-permute-start.27 = (bf16[1,48,384]{2,1,0:T(8,128)(2,1)S(1)}, bf16[1,48,384]{2,1,0:T(8,128)(2,1)S(1)}, u32[]{:S(2)}, u32[]{:S(2)}) collective-permute-start(bf16[1,48,384]{2,1,0:T(8,128)(2,1)S(1)} %get-tuple-element.37), channel_id=1, source_target_pairs={{0,192},{64,0},{128,64},{192,128},{1,193},{65,1},{129,65},{193,129... | collective-permute-start | bytes 110600 | tf_op jit(solution)/shard_map/ppermute | solution.py:24
  113.4 4.3 %collective-permute-start.28 = (bf16[1,48,384]{2,1,0:T(8,128)(2,1)S(1)}, bf16[1,48,384]{2,1,0:T(8,128)(2,1)S(1)}, u32[]{:S(2)}, u32[]{:S(2)}) collective-permute-start(bf16[1,48,384]{2,1,0:T(8,128)(2,1)S(1)} %get-tuple-element.36), channel_id=1, source_target_pairs={{0,128},{64,192},{128,0},{192,64},{1,129},{65,193},{129,1},{193,65... | collective-permute-start | bytes 110600 | tf_op jit(solution)/shard_map/ppermute | solution.py:24
  113.6 5.0 %collective-permute-start.20 = (bf16[2,48,384]{2,1,0:T(8,128)(2,1)S(1)}, bf16[2,48,384]{2,1,0:T(8,128)(2,1)S(1)}, u32[]{:S(2)}, u32[]{:S(2)}) collective-permute-start(bf16[2,48,384]{2,1,0:T(8,128)(2,1)S(1)} %get-tuple-element.32), channel_id=1, source_target_pairs={{0,8},{8,32},{32,40},{40,0},{1,9},{9,33},{33,41},{41,1},{2,10},{10... | collective-permute-start | bytes 221192 | tf_op jit(solution)/shard_map/ppermute | solution.py:24
  113.7 4.9 %collective-permute-start.21 = (bf16[2,48,384]{2,1,0:T(8,128)(2,1)S(1)}, bf16[2,48,384]{2,1,0:T(8,128)(2,1)S(1)}, u32[]{:S(2)}, u32[]{:S(2)}) collective-permute-start(bf16[2,48,384]{2,1,0:T(8,128)(2,1)S(1)} %get-tuple-element.33), channel_id=1, source_target_pairs={{0,40},{8,0},{32,8},{40,32},{1,41},{9,1},{33,9},{41,33},{2,42},{10... | collective-permute-start | bytes 221192 | tf_op jit(solution)/shard_map/ppermute | solution.py:24
  116.3 4.7 %collective-permute-start.22 = (bf16[2,48,384]{2,1,0:T(8,128)(2,1)S(1)}, bf16[2,48,384]{2,1,0:T(8,128)(2,1)S(1)}, u32[]{:S(2)}, u32[]{:S(2)}) collective-permute-start(bf16[2,48,384]{2,1,0:T(8,128)(2,1)S(1)} %get-tuple-element.34), channel_id=1, source_target_pairs={{0,32},{8,40},{32,0},{40,8},{1,33},{9,41},{33,1},{41,9},{2,34},{10... | collective-permute-start | bytes 221192 | tf_op jit(solution)/shard_map/ppermute | solution.py:24
  121.2 7.4 %collective-permute-start.29 = (bf16[3,48,384]{2,1,0:T(8,128)(2,1)S(1)}, bf16[3,48,384]{2,1,0:T(8,128)(2,1)S(1)}, u32[]{:S(2)}, u32[]{:S(2)}) collective-permute-start(bf16[3,48,384]{2,1,0:T(8,128)(2,1)S(1)} %pad_maximum_fusion.7), channel_id=1, source_target_pairs={{0,1},{1,0},{2,3},{3,2},{4,5},{5,4},{6,7},{7,6},{8,9},{9,8},{10,11... | collective-permute-start | bytes 331784 | tf_op jit(solution)/shard_map/ppermute | solution.py:28
  121.3 36.6 %collective-permute-start.16 = (bf16[3,768,384]{2,1,0:T(8,128)(2,1)S(1)}, bf16[3,768,384]{2,1,0:T(8,128)(2,1)}, u32[]{:S(2)}, u32[]{:S(2)}) collective-permute-start(bf16[3,768,384]{2,1,0:T(8,128)(2,1)S(1)} %copy-done.2), channel_id=1, source_target_pairs={{0,16},{16,0},{1,17},{17,1},{2,18},{18,2},{3,19},{19,3},{4,20},{20... | collective-permute-start | bytes 5308424 | tf_op jit(solution)/shard_map/ppermute | solution.py:28
  128.6 8.2 %collective-permute-start.30 = (bf16[3,48,384]{2,1,0:T(8,128)(2,1)S(1)}, bf16[3,48,384]{2,1,0:T(8,128)(2,1)S(1)}, u32[]{:S(2)}, u32[]{:S(2)}) collective-permute-start(bf16[3,48,384]{2,1,0:T(8,128)(2,1)S(1)} %add_convert_fusion.2), channel_id=1, source_target_pairs={{0,2},{1,3},{2,0},{3,1},{4,6},{5,7},{6,4},{7,5},{8,10},{9,11},{10,... | collective-permute-start | bytes 331784 | tf_op jit(solution)/shard_map/ppermute | solution.py:28
  136.9 8.3 %collective-permute-start.31 = (bf16[3,48,384]{2,1,0:T(8,128)(2,1)S(1)}, bf16[3,48,384]{2,1,0:T(8,128)(2,1)S(1)}, u32[]{:S(2)}, u32[]{:S(2)}) collective-permute-start(bf16[3,48,384]{2,1,0:T(8,128)(2,1)S(1)} %add_convert_fusion.1), channel_id=1, source_target_pairs={{0,4},{1,5},{2,6},{3,7},{4,0},{5,1},{6,2},{7,3},{8,12},{9,13},{10,... | collective-permute-start | bytes 331784 | tf_op jit(solution)/shard_map/ppermute | solution.py:28
  140.7 17.2 %collective-permute-start.15 = (bf16[1344,384]{1,0:T(8,128)(2,1)}, bf16[1344,384]{1,0:T(8,128)(2,1)S(1)}, u32[]{:S(2)}, u32[]{:S(2)}) collective-permute-start(bf16[1344,384]{1,0:T(8,128)(2,1)} %get-tuple-element.9), channel_id=1, source_target_pairs={{0,16},{16,0},{1,17},{17,1},{2,18},{18,2},{3,19},{19,3},{4,20},{20... | collective-permute-start | bytes 3096584 | tf_op jit(solution)/shard_map/ppermute | solution.py:28
  145.2 4.0 %collective-permute-start.32 = (bf16[3,48,384]{2,1,0:T(8,128)(2,1)S(1)}, bf16[3,48,384]{2,1,0:T(8,128)(2,1)S(1)}, u32[]{:S(2)}, u32[]{:S(2)}) collective-permute-start(bf16[3,48,384]{2,1,0:T(8,128)(2,1)S(1)} %add_convert_fusion), channel_id=1, source_target_pairs={{0,8},{8,0},{1,9},{9,1},{2,10},{10,2},{3,11},{11,3},{4,12},{12,4},... | collective-permute-start | bytes 331784 | tf_op jit(solution)/shard_map/ppermute | solution.py:28
  149.2 7.8 %collective-permute-start.33 = (bf16[3,48,384]{2,1,0:T(8,128)(2,1)S(1)}, bf16[3,48,384]{2,1,0:T(8,128)(2,1)S(1)}, u32[]{:S(2)}, u32[]{:S(2)}) collective-permute-start(bf16[3,48,384]{2,1,0:T(8,128)(2,1)S(1)} %get-tuple-element.21), channel_id=1, source_target_pairs={{0,16},{16,0},{1,17},{17,1},{2,18},{18,2},{3,19},{19,3},{4,20},{20... | collective-permute-start | bytes 331784 | tf_op jit(solution)/shard_map/ppermute | solution.py:28
  157.9 1.0 copy-start.4

commit v2 on v1

v2 whole, which is shorter than its diff:
```python
import functools
import math

import jax
import jax.numpy as jnp
from jax import lax
from jax.experimental import pallas as pl
from jax.experimental.pallas import tpu as pltpu
from jax.sharding import Mesh, PartitionSpec as P

FILTER_TAPS = 3
DILATION_STEP = 32
REACH = 32
AXES = ("x", "yh", "core", "yl", "z")
SIZES = (4, 2, 2, 2, 8)
SEQ = ("yl", "z")
RING_Y = ("yh", "yl")
BF16 = jnp.bfloat16
F32 = jnp.float32


def shift(value, axis, count, step):
    pairs = [(i, (i + step) % count) for i in range(count)]
    return lax.ppermute(value, axis, pairs)


def swap(value, axis, count, mask):
    return lax.ppermute(value, axis, [(i, i ^ mask) for i in range(count)])


def gelu_slope(value):
    coeff = math.sqrt(2.0 / math.pi)
    square = value * value
    tangent = jnp.tanh(value * (coeff + coeff * 0.044715 * square))
    return (0.5 + 0.5 * tangent) * (
        1.0 + value * (1.0 - tangent) * (coeff + coeff * 3.0 * 0.044715 * square)
    )


def join(*arrays):
    return lax.optimization_barrier(arrays)


def load_weight(position, pieces, weight, sem):
    x, yh, core = position[0], position[1], position[2]
    rows = pieces[0].shape[2]
    steps = [(0, 0), (0, 1), (3, 0), (3, 1), (1, 0), (1, 1)]
    parts = []
    for piece, step in zip(pieces[:6], steps):
        parts += [(piece.at[0], step, 0), (piece.at[1], step, 1)]
    far = [((2, 0), 0), ((2, 0), 1), ((2, 1), 0), ((2, 1), 1)]
    parts += [(piece, step, side) for piece, (step, side) in zip(pieces[6:], far)]
    copies = []
    for index, (part, (step_x, step_y), side) in enumerate(parts):
        owner = ((x + step_x) % 4) * 4 + ((yh + step_y) % 2) * 2 + (core + side) % 2
        place = pl.multiple_of(owner * rows, 16)
        copies.append(
            pltpu.make_async_copy(part, weight.at[:, pl.ds(place, rows), :], sem.at[index])
        )
    return copies


def forward_kernel(position, *refs):
    pieces, refs = refs[:10], refs[10:]
    normed_hbm, edge_hbm, upstream_hbm = refs[0:2], refs[2:6], refs[6:8]
    weight_out, back_out = refs[8], refs[9:11]
    weight, normed, upstream, back = refs[11:15]
    piece_sem, load_sem, back_sem, weight_sem = refs[15:]
    core = position[2]
    half = weight.shape[2]
    count = normed_hbm[0].shape[0]
    lane = pl.multiple_of(core * half, 128)
    copies = load_weight(position, pieces, weight, piece_sem)
    loads = []
    for index in range(2):
        low, high = edge_hbm[2 * index], edge_hbm[2 * index + 1]
        center = upstream_hbm[index]
        if index == 0:
            center = center.at[:, pl.ds(lane, half)]
        moves = [
            (low.at[: 2 * REACH], normed.at[index, : 2 * REACH]),
            (normed_hbm[index], normed.at[index, 2 * REACH : 2 * REACH + count]),
            (high.at[: 2 * REACH], normed.at[index, 2 * REACH + count :]),
            (low.at[2 * REACH :, pl.ds(lane, half)], upstream.at[index, :REACH]),
            (center, upstream.at[index, REACH : REACH + count]),
            (high.at[2 * REACH :, pl.ds(lane, half)], upstream.at[index, REACH + count :]),
        ]
        loads.append(
            [
                pltpu.make_async_copy(source, target, load_sem.at[index, place])
                for place, (source, target) in enumerate(moves)
            ]
        )
    for copy in copies + loads[0] + loads[1]:
        copy.start()
    for copy in copies:
        copy.wait()
    save = pltpu.make_async_copy(weight, weight_out, weight_sem)
    save.start()
    length = back.shape[1]
    block = length // 3
    saves = [save]
    for index in range(2):
        for copy in loads[index]:
            copy.wait()
        for start in range(0, length, block):
            conv = jnp.dot(
                normed[index, start : start + block, :], weight[0], preferred_element_type=F32
            )
            for tap in range(1, FILTER_TAPS):
                low = start + tap * DILATION_STEP
                conv = conv + jnp.dot(
                    normed[index, low : low + block, :], weight[tap], preferred_element_type=F32
                )
            incoming = upstream[index, start : start + block, :].astype(F32)
            back[index, start : start + block, :] = (incoming * gelu_slope(conv)).astype(BF16)
        back_save = pltpu.make_async_copy(back.at[index], back_out[index], back_sem.at[index])
        back_save.start()
        saves.append(back_save)
    for copy in saves:
        copy.wait()


def forward(position, pieces, normed, edges, upstream):
    count, channels = normed[0].shape
    half = channels // 2
    length = count + 2 * REACH
    anywhere = pl.BlockSpec(memory_space=pl.ANY)
    dma = pltpu.SemaphoreType.DMA
    return pl.pallas_call(
        forward_kernel,
        out_shape=[jax.ShapeDtypeStruct((FILTER_TAPS, channels, half), BF16)]
        + [jax.ShapeDtypeStruct((length, half), BF16)] * 2,
        in_specs=[pl.BlockSpec(memory_space=pltpu.SMEM)] + [anywhere] * 18,
        out_specs=[anywhere] * 3,
        scratch_shapes=[
            pltpu.VMEM((FILTER_TAPS, channels, half), BF16),
            pltpu.VMEM((2, length + 2 * REACH, channels), BF16),
            pltpu.VMEM((2, length, half), BF16),
            pltpu.VMEM((2, length, half), BF16),
            dma((16,)),
            dma((2, 6)),
            dma((2,)),
            dma,
        ],
        compiler_params=pltpu.CompilerParams(vmem_limit_bytes=56 * 1024 * 1024),
        name="forward",
    )(position, *pieces, *normed, *edges, *upstream)


def weight_grad_kernel(position, *refs):
    normed_hbm, back_hbm = refs[0:2], refs[2:4]
    along_x, along_y = refs[4:8], refs[8:12]
    normed, back, grad, normed_sem, back_sem, x_sem, y_sem = refs[12:]
    x, y = position[0], position[1] * 2 + position[3]
    count, channels = normed.shape[1:]
    half = back.shape[2]
    quarter, rows = channels // 4, channels // 16
    loads = []
    for index in range(2):
        loads.append(pltpu.make_async_copy(normed_hbm[index], normed.at[index], normed_sem.at[index]))
        loads.append(pltpu.make_async_copy(back_hbm[index], back.at[index], back_sem.at[index]))
    for copy in loads:
        copy.start()
    total = None
    for index in range(2):
        loads[2 * index].wait()
        loads[2 * index + 1].wait()
        shifted = jnp.concatenate(
            [
                back[index, 2 * REACH - tap * DILATION_STEP :][:count]
                for tap in range(FILTER_TAPS)
            ],
            axis=1,
        )
        part = lax.dot_general(
            normed[index], shifted, (((0,), (0,)), ((), ())), preferred_element_type=F32
        )
        total = part if total is None else total + part
    for tap in range(FILTER_TAPS):
        grad[tap] = total[:, tap * half : (tap + 1) * half].astype(BF16)
    saves = []
    for step in range(4):
        place = pl.multiple_of(((x + step) % 4) * quarter, 16)
        saves.append(
            pltpu.make_async_copy(
                grad.at[:2, pl.ds(place, quarter), :], along_x[step], x_sem.at[step]
            )
        )
    for step in range(4):
        for owner in range(4):
            place = pl.multiple_of(owner * quarter + ((y + step) % 4) * rows, 16)
            saves.append(
                pltpu.make_async_copy(
                    grad.at[2, pl.ds(place, rows), :],
                    along_y[step].at[owner],
                    y_sem.at[step, owner],
                )
            )
    for copy in saves:
        copy.start()
    for copy in saves:
        copy.wait()


def weight_grads(position, normed, back):
    count, channels = normed[0].shape
    length, half = back[0].shape
    quarter, rows = channels // 4, channels // 16
    anywhere = pl.BlockSpec(memory_space=pl.ANY)
    dma = pltpu.SemaphoreType.DMA
    return pl.pallas_call(
        weight_grad_kernel,
        out_shape=[jax.ShapeDtypeStruct((2, quarter, half), BF16)] * 4
        + [jax.ShapeDtypeStruct((4, rows, half), BF16)] * 4,
        in_specs=[pl.BlockSpec(memory_space=pltpu.SMEM)] + [anywhere] * 4,
        out_specs=[anywhere] * 8,
        scratch_shapes=[
            pltpu.VMEM((2, count, channels), BF16),
            pltpu.VMEM((2, length, half), BF16),
            pltpu.VMEM((FILTER_TAPS, channels, half), BF16),
            dma((2,)),
            dma((2,)),
            dma((4,)),
            dma((4, 4)),
        ],
        compiler_params=pltpu.CompilerParams(vmem_limit_bytes=56 * 1024 * 1024),
        name="weight_grads",
    )(position, *normed, *back)


def backward_kernel(back_a, back_b, weight_a, weight_b, inputs, scale, gain, incoming, out):
    block = out.shape[0]
    start = pl.program_id(0) * block
    grad = jnp.zeros(out.shape, F32)
    for back, weight in ((back_a, weight_a), (back_b, weight_b)):
        for tap in range(FILTER_TAPS):
            low = start + (FILTER_TAPS - 1 - tap) * DILATION_STEP
            grad = grad + lax.dot_general(
                back[pl.ds(pl.multiple_of(low, 32), block), :],
                weight[tap],
                (((1,), (1,)), ((), ())),
                preferred_element_type=F32,
            )
    scaled = grad * gain[...]
    value = inputs[...]
    factor = scale[...]
    spread = jnp.mean(scaled * value, axis=-1, keepdims=True)
    result = incoming[...].astype(F32) + factor * scaled - value * (factor * factor * factor * spread)
    out[...] = result.astype(BF16)


def backward(back, weight, inputs, scale, gain, incoming):
    count, channels = inputs.shape
    block = 256
    whole = lambda array: pl.BlockSpec(array.shape, lambda i: (0,) * array.ndim)
    part = pl.BlockSpec((block, channels), lambda i: (i, 0))
    return pl.pallas_call(
        backward_kernel,
        grid=(count // block,),
        out_shape=jax.ShapeDtypeStruct((count, channels), BF16),
        in_specs=[whole(back[0]), whole(back[1]), whole(weight[0]), whole(weight[1]), part]
        + [pl.BlockSpec((block, 1), lambda i: (i, 0)), whole(gain), part],
        out_specs=part,
        compiler_params=pltpu.CompilerParams(vmem_limit_bytes=56 * 1024 * 1024),
        name="backward",
    )(*back, *weight, inputs, scale, gain, incoming)


def first_sums(along_x, along_y, x, y):
    rows = along_y[0].shape[1]
    by_y = []
    by_x = []
    for step in range(4):
        start = ((y + step) % 4) * rows
        parts = [lax.dynamic_slice_in_dim(part, start, rows, axis=1) for part in along_x]
        by_y.append(sum(part.astype(F32) for part in parts))
        start = (x + step) % 4
        parts = [lax.dynamic_slice_in_dim(part, start, 1, axis=0) for part in along_y]
        by_x.append(sum(part.astype(F32) for part in parts))
    return by_y, by_x


def share_weight_grad(total, yl, core):
    for mask in (1, 2, 4):
        sent = total.astype(BF16)
        total = sent.astype(F32) + swap(sent, "z", 8, mask).astype(F32)
    mine = total.astype(BF16)
    other = swap(mine, "yl", 2, 1)
    by_core = [jnp.where(yl == rows, mine, other) for rows in range(2)]
    kept = jnp.where(core == 0, by_core[0], by_core[1])
    sent = jnp.where(core == 0, by_core[1], by_core[0])
    arrived = swap(sent, "core", 2, 1)
    low = jnp.where(core == 0, kept, arrived)
    high = jnp.where(core == 0, arrived, kept)
    return jnp.concatenate([low, high], axis=2).astype(F32)


def on_device(activations, nucleotides, base_table, norm_gain, filter_weight, upstream):
    x, yh, core, yl = (lax.axis_index(name) for name in ("x", "yh", "core", "yl"))
    y = yh * 2 + yl
    position = jnp.stack([x, yh, core, yl]).astype(jnp.int32)
    tokens, incoming = activations[0], upstream[0]
    count, channels = tokens.shape
    half = channels // 2

    mine = lax.dynamic_slice_in_dim(filter_weight, core * half, half, axis=2)
    other = lax.dynamic_slice_in_dim(filter_weight, (1 - core) * half, half, axis=2)
    own = jnp.stack([mine, swap(other, "core", 2, 1)])
    own, tokens, nucleotides, incoming = join(own, tokens, nucleotides, incoming)

    across = swap(own, RING_Y, 4, 3)
    up_own, down_own = shift(own, "x", 4, 1), shift(own, "x", 4, -1)
    bases = nucleotides[0][:, None]
    row = base_table[3][None]
    for base in (2, 1, 0):
        row = jnp.where(bases == base, base_table[base][None], row)
    inputs = tokens.astype(F32) + row
    scale_inv = lax.rsqrt(jnp.mean(inputs * inputs, axis=-1, keepdims=True) + 1e-06)
    normed = (inputs * scale_inv * norm_gain).astype(BF16)
    last = jnp.concatenate([normed[count - 2 * REACH :], incoming[count - REACH :]])
    first = jnp.concatenate([normed[: 2 * REACH], incoming[:REACH]])
    upstream_sent = lax.dynamic_slice_in_dim(incoming, (1 - core) * half, half, axis=1)
    across, up_own, down_own, normed, last, first, upstream_sent = join(
        across, up_own, down_own, normed, last, first, upstream_sent
    )

    up_across, down_across = shift(across, "x", 4, 1), shift(across, "x", 4, -1)
    far_up, far_down = shift(up_own[0], "x", 4, 1), shift(down_own[1], "x", 4, -1)
    low = lax.ppermute(last, SEQ, [(i, i + 1) for i in range(15)])
    high = lax.ppermute(first, SEQ, [(i + 1, i) for i in range(15)])
    normed_other = swap(normed, "core", 2, 1)
    upstream_other = swap(upstream_sent, "core", 2, 1)
    up_across, down_across, far_up, far_down, low, high, normed_other, upstream_other = join(
        up_across, down_across, far_up, far_down, low, high, normed_other, upstream_other
    )

    far_across_up = shift(up_across[0], "x", 4, 1)
    far_across_down = shift(down_across[1], "x", 4, -1)
    low_other, high_other = swap(low, "core", 2, 1), swap(high, "core", 2, 1)
    pieces = [own, across, up_own, up_across, down_own, down_across]
    pieces += [far_up, far_down, far_across_up, far_across_down]
    weight, back, back_other = forward(
        position,
        pieces,
        (normed, normed_other),
        (low, high, low_other, high_other),
        (incoming, upstream_other),
    )

    back_rest = swap(back_other, "core", 2, 1)
    weight_rest = swap(weight, "core", 2, 1)
    grads = weight_grads(position, (normed, normed_other), (back, back_other))
    back_rest, weight_rest, *grads = join(back_rest, weight_rest, *grads)

    along_x, along_y = [grads[0]], [grads[4]]
    for step in (1, 3, 2):
        along_x.append(shift(grads[step], "x", 4, step))
        along_y.append(shift(grads[4 + step], RING_Y, 4, step))
    result = backward(
        (back, back_rest), (weight, weight_rest), inputs, scale_inv, norm_gain[None], incoming
    )
    joined = join(result, *along_x, *along_y)
    result, along_x, along_y = joined[0], joined[1:5], joined[5:]

    by_y, by_x = first_sums(along_x, along_y, x, y)
    total_y, total_x = by_y[0], by_x[0]
    for step in (1, 3, 2):
        total_y = total_y + shift(by_y[step].astype(BF16), RING_Y, 4, step).astype(F32)
        total_x = total_x + shift(by_x[step].astype(BF16), "x", 4, step).astype(F32)
    total = jnp.concatenate([total_y, total_x], axis=0)
    weight_grad = share_weight_grad(total, yl, core)
    total_rows = 16 * 16 * count
    return (result[None], weight_grad / math.sqrt(total_rows))


def solution(mesh):
    grid = Mesh(mesh.devices.reshape(SIZES), AXES)
    dp, seq = ("x", "yh", "core"), SEQ
    in_specs = (
        P(dp, seq, None),
        P(dp, seq),
        P(),
        P(),
        P(None, dp, None),
        P(dp, seq, None),
    )
    out_specs = (P(dp, seq, None), P(None, dp, None))
    return jax.shard_map(
        on_device, mesh=grid, in_specs=in_specs, out_specs=out_specs, check_vma=False
    )
```

time: 172 us -> 144 us (0.84)
  local copies, waits for them, and re-layouts: 25.8 us -> 10.2 us
  waiting for transfers between devices: 35.5 us -> 28.3 us
  starting transfers between devices: 62.9 us -> 56.5 us
  Pallas kernels: 31 us -> 35.5 us
  other arithmetic: 14.7 us -> 10.4 us
    ppermute x12 -> x13, starting transfers between devices: 33.8 us -> 21.4 us  [swap(): return lax.ppermute(value, axis, [(i, i ^ mask) for i in range(count)])]
    ppermute x20, waiting for transfers between devices: 16.4 us -> 5.62 us  [shift(): return lax.ppermute(value, axis, pairs)]
    pallas_call x0 -> x1, Pallas kernels: none -> 10.1 us  [weight_grads(): pl.pallas_call(weight_grad_kernel, out_shape=[jax.ShapeDtypeStruct((2, qu...]
    ppermute x20, starting transfers between devices: 23.4 us -> 30.2 us  [shift(): return lax.ppermute(value, axis, pairs)]
    slice x10 -> x2, local copies, waits for them, and re-layouts: 6.28 us -> 0.02 us  [on_device(): first = jnp.concatenate([normed[:2 * REACH], incoming[:REACH]])]
    pallas_call x1, Pallas kernels: 19 us -> 13.3 us  [forward(): pl.pallas_call(forward_kernel, out_shape=[jax.ShapeDtypeStruct((FILTER_TA...]
    ppermute x12 -> x13, waiting for transfers between devices: 13.7 us -> 17.8 us  [swap(): return lax.ppermute(value, axis, [(i, i ^ mask) for i in range(count)])]
    transpose x1 -> x0, local copies, waits for them, and re-layouts: 3.99 us -> none  [on_device(): turned = normed.T]
  transfers between devices with their start and end apart: 34 -> 35, of which waited for: 13 -> 10; matrix products, arithmetic and copies ran while one was open for 16% -> 9% of each run, Pallas kernels for 0% -> 16%
where the time goes in v2:
time: 144 us; the launch traced here: 142 us
  starting transfers between devices  56.5 us (39%)
  Pallas kernels  35.5 us (25%)
  waiting for transfers between devices  28.3 us (20%)
  other arithmetic  10.4 us (7%)
  local copies, waits for them, and re-layouts  10.2 us (7%)
    ppermute x20, starting transfers between devices, shift(): return lax.ppermute(value, axis, pairs)  30.2 us
    ppermute x13, starting transfers between devices, swap(): return lax.ppermute(value, axis, [(i, i ^ mask) for i in range(count)])  21.4 us
    ppermute x13, waiting for transfers between devices, swap(): return lax.ppermute(value, axis, [(i, i ^ mask) for i in range(count)])  17.8 us
    pallas_call x1, Pallas kernels, forward(): pl.pallas_call(forward_kernel, out_shape=[jax.ShapeDtypeStruct((FILTER_TA...  13.3 us
    pallas_call x1, Pallas kernels, backward(): pl.pallas_call(backward_kernel, grid=(count // block,), out_shape=jax.Sha...  12.1 us
    pallas_call x1, Pallas kernels, weight_grads(): pl.pallas_call(weight_grad_kernel, out_shape=[jax.ShapeDtypeStruct((2, qu...  10.1 us
    ppermute x20, waiting for transfers between devices, shift(): return lax.ppermute(value, axis, pairs)  5.62 us
    ppermute x1, waiting for transfers between devices, on_device(): high = lax.ppermute(first, SEQ, [(i + 1, i) for i in range(15)])  4.87 us
  transfers between devices with their start and end apart: 35, of which 10 were waited for; matrix products, arithmetic and copies ran while one was open for 9% of the time, Pallas kernels for 16%

profile of v2, /device:TPU:1, one launch (start us, length us, event | category | flops | bytes accessed | tf_op | source)
XLA Modules:
  0.0 141.9 jit_solution(3608669742508675929)
XLA Ops:
  0.6 1.0 dynamic-slice_bitcast_fusion
  1.6 3.3 %collective-permute-start = (bf16[3,48,384]{2,1,0:T(8,128)(2,1)S(1)}, bf16[3,48,384]{2,1,0:T(8,128)(2,1)S(1)}, u32[]{:S(2)}, u32[]{:S(2)}) collective-permute-start(bf16[3,48,384]{2,1,0:T(8,128)(2,1)S(1)} %get-tuple-element.125), channel_id=1, source_target_pairs={{0,16},{16,0},{1,17},{17,1},{2,18},{18,2},{3,19},{19,3},{4,20},{20... | collective-permute-start | bytes 331784 | tf_op jit(solution)/shard_map/ppermute | solution.py:28
  5.0 0.9 slice_reduce_fusion.3
  6.0 1.1 collective-permute-start.1
  7.0 1.2 collective-permute-start.2
  8.3 1.5 %collective-permute-start.3 = (bf16[2,3,48,384]{3,2,1,0:T(8,128)(2,1)S(1)}, bf16[2,3,48,384]{3,2,1,0:T(8,128)(2,1)S(1)}, u32[]{:S(2)}, u32[]{:S(2)}) collective-permute-start(bf16[2,3,48,384]{3,2,1,0:T(8,128)(2,1)S(1)} %pad_maximum_fusion.refs_0_), channel_id=1, source_target_pairs={{0,192},{64,0},{128,64},{192,128},{1,193},{65,1},{129,65},{193,129... | collective-permute-start | bytes 663560 | tf_op jit(solution)/shard_map/ppermute | solution.py:24
  9.7 0.7 compare_reduce_fusion.2
  10.5 3.8 %multiply_reduce_fusion = (f32[1280]{0:T(1024)S(1)}, f32[1280,768]{1,0:T(8,128)S(1)}) fusion(f32[768]{0:T(1024)S(1)} %get-tuple-element.102, f32[768]{0:T(1024)S(1)} %get-tuple-element.103, pred[1280]{0:T(1024)(128)(4,1)S(1)} %get-tuple-element.105, f32[768]{0:T(1024)S(1)} %get-tuple-element.101, pred[1280]{0:T(1024)(128)(4,1)S(1)} %get-tuple-element.106, ...), kind=kLoop, calls=%fused_computation.1 | loop fusion | flops 6880000 | bytes 5919488 | tf_op jit(solution)/shard_map/reduce_sum | solution.py:319
  14.3 0.4 multiply_convert_fusion.refs_10_.refs_0_
  14.7 2.5 %copy-done.2 = bf16[1,1280,768]{2,1,0:T(8,128)(2,1)S(1)} copy-done((bf16[1,1280,768]{2,1,0:T(8,128)(2,1)S(1)}, bf16[1,1280,768]{2,1,0:T(8,128)(2,1)}, u32[]{:S(2)}) %copy-start.2) | copy-done | bytes 1966104
  17.3 1.1 constant_dynamic-slice_fusion
  18.4 1.3 collective-permute-start.10
  19.7 0.1 collective-permute-start.11
  19.8 0.1 collective-permute-start.6
  19.9 2.7 %collective-permute-start.7 = (bf16[3,48,384]{2,1,0:T(8,128)(2,1)S(1)}, bf16[3,48,384]{2,1,0:T(8,128)(2,1)S(1)}, u32[]{:S(2)}, u32[]{:S(2)}) collective-permute-start(bf16[3,48,384]{2,1,0:T(8,128)(2,1)S(1)} %slice_bitcast_fusion.2), channel_id=1, source_target_pairs={{0,192},{64,0},{128,64},{192,128},{1,193},{65,1},{129,65},{193,129... | collective-permute-start | bytes 331784 | tf_op jit(solution)/shard_map/ppermute | solution.py:24
  22.7 3.5 %collective-permute-start.8 = (bf16[96,768]{1,0:T(8,128)(2,1)S(1)}, bf16[96,768]{1,0:T(8,128)(2,1)S(1)}, u32[]{:S(2)}, u32[]{:S(2)}) collective-permute-start(bf16[96,768]{1,0:T(8,128)(2,1)S(1)} %get-tuple-element.58), channel_id=1, source_target_pairs={{0,1},{1,2},{2,3},{3,4},{4,5},{5,6},{6,7},{7,8},{8,9},{9,10},{10,1... | collective-permute-start | bytes 442376 | tf_op jit(solution)/shard_map/ppermute | solution.py:330
  26.2 0.1 collective-permute-start.4
  26.4 2.6 %collective-permute-start.5 = (bf16[2,3,48,384]{3,2,1,0:T(8,128)(2,1)}, bf16[2,3,48,384]{3,2,1,0:T(8,128)(2,1)}, u32[]{:S(2)}, u32[]{:S(2)}) collective-permute-start(bf16[2,3,48,384]{3,2,1,0:T(8,128)(2,1)} %collective-permute-done.1.refs_1_), channel_id=1, source_target_pairs={{0,192},{64,0},{128,64},{192,128},{1,193},{65,1},{129,65},{193,129... | collective-permute-start | bytes 663560 | tf_op jit(solution)/shard_map/ppermute | solution.py:24
  29.0 0.7 copy-done.12
  29.7 1.3 collective-permute-start.9
  31.0 4.9 %collective-permute-done.9.refs_13_ = bf16[96,768]{1,0:T(8,128)(2,1)} collective-permute-done((bf16[96,768]{1,0:T(8,128)(2,1)S(1)}, bf16[96,768]{1,0:T(8,128)(2,1)}, u32[]{:S(2)}, u32[]{:S(2)}) %collective-permute-start.9) | collective-permute-done | bytes 147488 | tf_op jit(solution)/shard_map/ppermute | solution.py:331
  35.9 0.1 collective-permute-start.12
  36.0 2.9 %collective-permute-start.14 = (bf16[96,768]{1,0:T(8,128)(2,1)}, bf16[96,768]{1,0:T(8,128)(2,1)S(1)}, u32[]{:S(2)}, u32[]{:S(2)}) collective-permute-start(bf16[96,768]{1,0:T(8,128)(2,1)} %copy-done.12), channel_id=1, source_target_pairs={{0,16},{16,0},{1,17},{17,1},{2,18},{18,2},{3,19},{19,3},{4,20},{20... | collective-permute-start | bytes 442376 | tf_op jit(solution)/shard_map/ppermute | solution.py:28
  38.9 0.1 collective-permute-start.15
  39.0 0.9 slice_bitcast_fusion
  39.9 3.0 %collective-permute-start.13 = (bf16[3,48,384]{2,1,0:T(8,128)(2,1)S(1)}, bf16[3,48,384]{2,1,0:T(8,128)(2,1)S(1)}, u32[]{:S(2)}, u32[]{:S(2)}) collective-permute-start(bf16[3,48,384]{2,1,0:T(8,128)(2,1)S(1)} %slice_bitcast_fusion), channel_id=1, source_target_pairs={{0,192},{64,0},{128,64},{192,128},{1,193},{65,1},{129,65},{193,129... | collective-permute-start | bytes 331784 | tf_op jit(solution)/shard_map/ppermute | solution.py:24
  42.9 0.7 pad_add_fusion.position
  43.6 1.3 collective-permute-done.13.refs_9_
  44.9 0.6 copy-done.18
  45.5 0.7 copy-done.14
  46.2 13.3 %forward.1 = (bf16[3,768,384]{2,1,0:T(8,128)(2,1)}, bf16[1344,384]{1,0:T(8,128)(2,1)}, bf16[1344,384]{1,0:T(8,128)(2,1)}) custom-call(s32[4]{0:T(128)} %pad_add_fusion.position, bf16[2,3,48,384]{3,2,1,0:T(8,128)(2,1)} %copy-done.6, bf16[2,3,48,384]{3,2,1,0:T(8,128)(2,1)} %collective-permute-done.1.refs_1_, bf16[2,3,48,384]{3,2,1,0:T(8,128)(2,1)} %copy-done.7, ...), custom_call_target="tpu_custom_call" | custom-call | tf_op jit(solution)/shard_map/forward/pallas_call | solution.py:130
  59.5 1.4 %collective-permute-start.17 = (bf16[3,768,384]{2,1,0:T(8,128)(2,1)}, bf16[3,768,384]{2,1,0:T(8,128)(2,1)S(1)}, u32[]{:S(2)}, u32[]{:S(2)}) collective-permute-start(bf16[3,768,384]{2,1,0:T(8,128)(2,1)} %get-tuple-element.72.weight_a), channel_id=1, source_target_pairs={{0,16},{16,0},{1,17},{17,1},{2,18},{18,2},{3,19},{19,3},{4,20},{20... | collective-permute-start | bytes 5308424 | tf_op jit(solution)/shard_map/ppermute | solution.py:28
  61.0 0.1 collective-permute-start.16
  61.1 10.1 %weight_grads.1 = (bf16[2,192,384]{2,1,0:T(8,128)(2,1)}, bf16[2,192,384]{2,1,0:T(8,128)(2,1)}, bf16[2,192,384]{2,1,0:T(8,128)(2,1)}, bf16[2,192,384]{2,1,0:T(8,1...) custom-call(s32[4]{0:T(128)} %pad_add_fusion.position, ...), custom_call_target="tpu_custom_call" | custom-call | tf_op jit(solution)/shard_map/weight_grads/pallas_call | solution.py:212
  71.2 5.4 %collective-permute-start.21 = (bf16[4,48,384]{2,1,0:T(8,128)(2,1)}, bf16[4,48,384]{2,1,0:T(8,128)(2,1)S(1)}, u32[]{:S(2)}, u32[]{:S(2)}) collective-permute-start(bf16[4,48,384]{2,1,0:T(8,128)(2,1)} %get-tuple-element.88), channel_id=1, source_target_pairs={{0,8},{8,32},{32,40},{40,0},{1,9},{9,33},{33,41},{41,1},{2,10},{10... | collective-permute-start | bytes 442376 | tf_op jit(solution)/shard_map/ppermute | solution.py:24
  76.6 3.4 %collective-permute-start.19 = (bf16[2,192,384]{2,1,0:T(8,128)(2,1)}, bf16[2,192,384]{2,1,0:T(8,128)(2,1)S(1)}, u32[]{:S(2)}, u32[]{:S(2)}) collective-permute-start(bf16[2,192,384]{2,1,0:T(8,128)(2,1)} %get-tuple-element.85), channel_id=1, source_target_pairs={{0,192},{64,0},{128,64},{192,128},{1,193},{65,1},{129,65},{193,129... | collective-permute-start | bytes 884744 | tf_op jit(solution)/shard_map/ppermute | solution.py:24
  80.0 1.2 collective-permute-start.20
  81.2 1.9 %collective-permute-start.23 = (bf16[4,48,384]{2,1,0:T(8,128)(2,1)}, bf16[4,48,384]{2,1,0:T(8,128)(2,1)}, u32[]{:S(2)}, u32[]{:S(2)}) collective-permute-start(bf16[4,48,384]{2,1,0:T(8,128)(2,1)} %get-tuple-element.90), channel_id=1, source_target_pairs={{0,32},{8,40},{32,0},{40,8},{1,33},{9,41},{33,1},{41,9},{2,34},{10... | collective-permute-start | bytes 442376 | tf_op jit(solution)/shard_map/ppermute | solution.py:24
  83.0 0.6 broadcast_in_dim.77.gain
  83.6 1.1 rsqrt.7.scale
  84.7 12.1 %backward.1 = bf16[1280,768]{1,0:T(8,128)(2,1)} custom-call(bf16[1344,384]{1,0:T(8,128)(2,1)} %get-tuple-element.70.refs_2_.back_a, bf16[1344,384]{1,0:T(8,128)(2,1)} %copy-done.4, bf16[3,768,384]{2,1,0:T(8,128)(2,1)} %get-tuple-element.72.weight_a, bf16[3,768,384]{2,1,0:T(8,128)(2,1)} %copy-done.3, f32[1280,768]{1,0:T(8,128)} %copy-done, ...), custom_call_target="tpu_custom_call" | custom-call | tf_op jit(solution)/shard_map/backward/pallas_call | solution.py:258
  96.9 0.9 add_convert_fusion.10
  97.8 0.9 collective-permute-start.27
  98.7 2.0 %collective-permute-start.28 = (bf16[1,48,384]{2,1,0:T(8,128)(2,1)S(1)}, bf16[1,48,384]{2,1,0:T(8,128)(2,1)S(1)}, u32[]{:S(2)}, u32[]{:S(2)}) collective-permute-start(bf16[1,48,384]{2,1,0:T(8,128)(2,1)S(1)} %get-tuple-element.121), channel_id=1, source_target_pairs={{0,192},{64,0},{128,64},{192,128},{1,193},{65,1},{129,65},{193,129... | collective-permute-start | bytes 110600 | tf_op jit(solution)/shard_map/ppermute | solution.py:24
  100.8 1.1 collective-permute-start.29
  101.9 1.1 add_convert_fusion.6
  103.0 0.1 collective-permute-start.24
  103.0 2.7 %collective-permute-start.25 = (bf16[2,48,384]{2,1,0:T(8,128)(2,1)S(1)}, bf16[2,48,384]{2,1,0:T(8,128)(2,1)S(1)}, u32[]{:S(2)}, u32[]{:S(2)}) collective-permute-start(bf16[2,48,384]{2,1,0:T(8,128)(2,1)S(1)} %get-tuple-element.118), channel_id=1, source_target_pairs={{0,40},{8,0},{32,8},{40,32},{1,41},{9,1},{33,9},{41,33},{2,42},{10... | collective-permute-start | bytes 221192 | tf_op jit(solution)/shard_map/ppermute | solution.py:24
  105.7 0.3 collective-permute-start.26
  106.0 0.8 add_convert_fusion.7
  106.8 0.9 collective-permute-done.24
  107.7 3.4 %collective-permute-done.26 = bf16[2,48,384]{2,1,0:T(8,128)(2,1)S(1)} collective-permute-done((bf16[2,48,384]{2,1,0:T(8,128)(2,1)S(1)}, bf16[2,48,384]{2,1,0:T(8,128)(2,1)S(1)}, u32[]{:S(2)}, u32[]{:S(2)}) %collective-permute-start.26) | collective-permute-done | bytes 73760 | tf_op jit(solution)/shard_map/ppermute | solution.py:24
  111.1 1.0 add_convert_fusion.3
  112.1 0.1 collective-permute-start.30
  112.2 3.6 %collective-permute-done.30 = bf16[3,48,384]{2,1,0:T(8,128)(2,1)S(1)} collective-permute-done((bf16[3,48,384]{2,1,0:T(8,128)(2,1)S(1)}, bf16[3,48,384]{2,1,0:T(8,128)(2,1)S(1)}, u32[]{:S(2)}, u32[]{:S(2)}) %collective-permute-start.30) | collective-permute-done | bytes 110624 | tf_op jit(solution)/shard_map/ppermute | solution.py:28
  115.8 0.7 collective-permute-start.31
  116.5 5.0 %collective-permute-done.31 = bf16[3,48,384]{2,1,0:T(8,128)(2,1)S(1)} collective-permute-done((bf16[3,48,384]{2,1,0:T(8,128)(2,1)S(1)}, bf16[3,48,384]{2,1,0:T(8,128)(2,1)S(1)}, u32[]{:S(2)}, u32[]{:S(2)}) %collective-permute-start.31) | collective-permute-done | bytes 110624 | tf_op jit(solution)/shard_map/ppermute | solution.py:28
  121.5 3.4 %collective-permute-start.32 = (bf16[3,48,384]{2,1,0:T(8,128)(2,1)S(1)}, bf16[3,48,384]{2,1,0:T(8,128)(2,1)S(1)}, u32[]{:S(2)}, u32[]{:S(2)}) collective-permute-start(bf16[3,48,384]{2,1,0:T(8,128)(2,1)S(1)} %add_convert_fusion.1), channel_id=1, source_target_pairs={{0,4},{1,5},{2,6},{3,7},{4,0},{5,1},{6,2},{7,3},{8,12},{9,13},{10,... | collective-permute-start | bytes 331784 | tf_op jit(solution)/shard_map/ppermute | solution.py:28
  124.9 4.3 %collective-permute-done.32 = bf16[3,48,384]{2,1,0:T(8,128)(2,1)S(1)} collective-permute-done((bf16[3,48,384]{2,1,0:T(8,128)(2,1)S(1)}, bf16[3,48,384]{2,1,0:T(8,128)(2,1)S(1)}, u32[]{:S(2)}, u32[]{:S(2)}) %collective-permute-start.32) | collective-permute-done | bytes 110624 | tf_op jit(solution)/shard_map/ppermute | solution.py:28
  129.2 0.1 collective-permute-start.33
  129.3 3.9 %collective-permute-done.33 = bf16[3,48,384]{2,1,0:T(8,128)(2,1)S(1)} collective-permute-done((bf16[3,48,384]{2,1,0:T(8,128)(2,1)S(1)}, bf16[3,48,384]{2,1,0:T(8,128)(2,1)S(1)}, u32[]{:S(2)}, u32[]{:S(2)}) %collective-permute-start.33) | collective-permute-done | bytes 110624 | tf_op jit(solution)/shard_map/ppermute | solution.py:28
  133.2 6.9 %collective-permute-start.34 = (bf16[3,48,384]{2,1,0:T(8,128)(2,1)S(1)}, bf16[3,48,384]{2,1,0:T(8,128)(2,1)S(1)}, u32[]{:S(2)}, u32[]{:S(2)}) collective-permute-start(bf16[3,48,384]{2,1,0:T(8,128)(2,1)S(1)} %get-tuple-element.107), channel_id=1, source_target_pairs={{0,16},{16,0},{1,17},{17,1},{2,18},{18,2},{3,19},{19,3},{4,20},{20... | collective-permute-start | bytes 331784 | tf_op jit(solution)/shard_map/ppermute | solution.py:28
  140.1 1.0 collective-permute-done.34
  141.1 0.8 convert_multiply_fusion
  (78 shorter events, 0.6 us)
Async XLA Ops:
  0.6 13.6 %copy-start.19 = (f32[768]{0:T(1024)S(1)}, f32[768]{0:T(1024)}, u32[]{:S(2)}) copy-start(f32[768]{0:T(1024)} %param.9) | copy-start | bytes 9220
  1.6 4.3 %collective-permute-start = (bf16[3,48,384]{2,1,0:T(8,128)(2,1)S(1)}, bf16[3,48,384]{2,1,0:T(8,128)(2,1)S(1)}, u32[]{:S(2)}, u32[]{:S(2)}) collective-permute-start(bf16[3,48,384]{2,1,0:T(8,128)(2,1)S(1)} %get-tuple-element.125), channel_id=1, source_target_pairs={{0,16},{16,0},{1,17},{17,1},{2,18},{18,2},{3,19},{19,3},{4,20},{20... | collective-permute-start | bytes 331784 | tf_op jit(solution)/shard_map/ppermute | solution.py:28
  5.9 8.7 %copy-start.6 = (bf16[2,3,48,384]{3,2,1,0:T(8,128)(2,1)}, bf16[2,3,48,384]{3,2,1,0:T(8,128)(2,1)S(1)}, u32[]{:S(2)}) copy-start(bf16[2,3,48,384]{3,2,1,0:T(8,128)(2,1)S(1)} %pad_maximum_fusion.refs_0_) | copy-start | bytes 663556
  6.0 12.4 %collective-permute-start.1 = (bf16[2,3,48,384]{3,2,1,0:T(8,128)(2,1)S(1)}, bf16[2,3,48,384]{3,2,1,0:T(8,128)(2,1)}, u32[]{:S(2)}, u32[]{:S(2)}) collective-permute-start(bf16[2,3,48,384]{3,2,1,0:T(8,128)(2,1)S(1)} %pad_maximum_fusion.refs_0_), channel_id=1, source_target_pairs={{0,40},{8,32},{32,8},{40,0},{1,41},{9,33},{33,9},{41,1},{2,42},{10... | collective-permute-start | bytes 663560 | tf_op jit(solution)/shard_map/ppermute | solution.py:28
  7.0 11.3 %collective-permute-start.2 = (bf16[2,3,48,384]{3,2,1,0:T(8,128)(2,1)S(1)}, bf16[2,3,48,384]{3,2,1,0:T(8,128)(2,1)S(1)}, u32[]{:S(2)}, u32[]{:S(2)}) collective-permute-start(bf16[2,3,48,384]{3,2,1,0:T(8,128)(2,1)S(1)} %pad_maximum_fusion.refs_0_), channel_id=1, source_target_pairs={{0,64},{64,128},{128,192},{192,0},{1,65},{65,129},{129,193},{193,1... | collective-permute-start | bytes 663560 | tf_op jit(solution)/shard_map/ppermute | solution.py:24
  8.3 10.1 %collective-permute-start.3 = (bf16[2,3,48,384]{3,2,1,0:T(8,128)(2,1)S(1)}, bf16[2,3,48,384]{3,2,1,0:T(8,128)(2,1)S(1)}, u32[]{:S(2)}, u32[]{:S(2)}) collective-permute-start(bf16[2,3,48,384]{3,2,1,0:T(8,128)(2,1)S(1)} %pad_maximum_fusion.refs_0_), channel_id=1, source_target_pairs={{0,192},{64,0},{128,64},{192,128},{1,193},{65,1},{129,65},{193,129... | collective-permute-start | bytes 663560 | tf_op jit(solution)/shard_map/ppermute | solution.py:24
  14.2 4.1 %copy-start = (f32[1280,768]{1,0:T(8,128)}, f32[1280,768]{1,0:T(8,128)S(1)}, u32[]{:S(2)}) copy-start(f32[1280,768]{1,0:T(8,128)S(1)} %get-tuple-element.111.inputs) | copy-start | bytes 11796484
  14.2 3.0 %copy-start.2 = (bf16[1,1280,768]{2,1,0:T(8,128)(2,1)S(1)}, bf16[1,1280,768]{2,1,0:T(8,128)(2,1)}, u32[]{:S(2)}) copy-start(bf16[1,1280,768]{2,1,0:T(8,128)(2,1)} %param.11) | copy-start | bytes 5898244
  14.7 30.1 %copy-start.1 = (bf16[1280,768]{1,0:T(8,128)(2,1)}, bf16[1280,768]{1,0:T(8,128)(2,1)S(1)}, u32[]{:S(2)}) copy-start(bf16[1280,768]{1,0:T(8,128)(2,1)S(1)} %multiply_convert_fusion.refs_10_.refs_0_) | copy-start | bytes 5898244
  18.4 26.4 %copy-start.7 = (bf16[2,3,48,384]{3,2,1,0:T(8,128)(2,1)}, bf16[2,3,48,384]{3,2,1,0:T(8,128)(2,1)S(1)}, u32[]{:S(2)}) copy-start(bf16[2,3,48,384]{3,2,1,0:T(8,128)(2,1)S(1)} %collective-permute-done.2.refs_2_) | copy-start | bytes 663556
  18.4 1.5 %copy-start.8 = (bf16[2,3,48,384]{3,2,1,0:T(8,128)(2,1)}, bf16[2,3,48,384]{3,2,1,0:T(8,128)(2,1)S(1)}, u32[]{:S(2)}) copy-start(bf16[2,3,48,384]{3,2,1,0:T(8,128)(2,1)S(1)} %collective-permute-done.3.refs_4_) | copy-start | bytes 663556
  18.4 17.5 %collective-permute-start.10 = (bf16[1280,768]{1,0:T(8,128)(2,1)S(1)}, bf16[1280,768]{1,0:T(8,128)(2,1)}, u32[]{:S(2)}, u32[]{:S(2)}) collective-permute-start(bf16[1280,768]{1,0:T(8,128)(2,1)S(1)} %multiply_convert_fusion.refs_10_.refs_0_), channel_id=1, source_target_pairs={{0,16},{16,0},{1,17},{17,1},{2,18},{18,2},{3,19},{19,3},{4,20},{20... | collective-permute-start | bytes 5898248 | tf_op jit(solution)/shard_map/ppermute | solution.py:28
  19.7 16.1 %collective-permute-start.11 = (bf16[1280,384]{1,0:T(8,128)(2,1)}, bf16[1280,384]{1,0:T(8,128)(2,1)S(1)}, u32[]{:S(2)}, u32[]{:S(2)}) collective-permute-start(bf16[1280,384]{1,0:T(8,128)(2,1)} %constant_dynamic-slice_fusion), channel_id=1, source_target_pairs={{0,16},{16,0},{1,17},{17,1},{2,18},{18,2},{3,19},{19,3},{4,20},{20... | collective-permute-start | bytes 2949128 | tf_op jit(solution)/shard_map/ppermute | solution.py:28
  19.8 6.4 %collective-permute-start.6 = (bf16[3,48,384]{2,1,0:T(8,128)(2,1)S(1)}, bf16[3,48,384]{2,1,0:T(8,128)(2,1)S(1)}, u32[]{:S(2)}, u32[]{:S(2)}) collective-permute-start(bf16[3,48,384]{2,1,0:T(8,128)(2,1)S(1)} %slice_bitcast_fusion.3), channel_id=1, source_target_pairs={{0,64},{64,128},{128,192},{192,0},{1,65},{65,129},{129,193},{193,1... | collective-permute-start | bytes 331784 | tf_op jit(solution)/shard_map/ppermute | solution.py:24
  19.9 6.4 %collective-permute-start.7 = (bf16[3,48,384]{2,1,0:T(8,128)(2,1)S(1)}, bf16[3,48,384]{2,1,0:T(8,128)(2,1)S(1)}, u32[]{:S(2)}, u32[]{:S(2)}) collective-permute-start(bf16[3,48,384]{2,1,0:T(8,128)(2,1)S(1)} %slice_bitcast_fusion.2), channel_id=1, source_target_pairs={{0,192},{64,0},{128,64},{192,128},{1,193},{65,1},{129,65},{193,129... | collective-permute-start | bytes 331784 | tf_op jit(solution)/shard_map/ppermute | solution.py:24
  22.7 6.3 %collective-permute-start.8 = (bf16[96,768]{1,0:T(8,128)(2,1)S(1)}, bf16[96,768]{1,0:T(8,128)(2,1)S(1)}, u32[]{:S(2)}, u32[]{:S(2)}) collective-permute-start(bf16[96,768]{1,0:T(8,128)(2,1)S(1)} %get-tuple-element.58), channel_id=1, source_target_pairs={{0,1},{1,2},{2,3},{3,4},{4,5},{5,6},{6,7},{7,8},{8,9},{9,10},{10,1... | collective-permute-start | bytes 442376 | tf_op jit(solution)/shard_map/ppermute | solution.py:330
  26.2 2.8 %copy-start.15 = (bf16[3,48,384]{2,1,0:T(8,128)(2,1)}, bf16[3,48,384]{2,1,0:T(8,128)(2,1)S(1)}, u32[]{:S(2)}) copy-start(bf16[3,48,384]{2,1,0:T(8,128)(2,1)S(1)} %collective-permute-done.6.refs_6_) | copy-start | bytes 331780
  26.2 9.6 %collective-permute-start.4 = (bf16[2,3,48,384]{3,2,1,0:T(8,128)(2,1)}, bf16[2,3,48,384]{3,2,1,0:T(8,128)(2,1)S(1)}, u32[]{:S(2)}, u32[]{:S(2)}) collective-permute-start(bf16[2,3,48,384]{3,2,1,0:T(8,128)(2,1)} %collective-permute-done.1.refs_1_), channel_id=1, source_target_pairs={{0,64},{64,128},{128,192},{192,0},{1,65},{65,129},{129,193},{193,1... | collective-permute-start | bytes 663560 | tf_op jit(solution)/shard_map/ppermute | solution.py:24
  26.3 2.7 %copy-start.16 = (bf16[3,48,384]{2,1,0:T(8,128)(2,1)}, bf16[3,48,384]{2,1,0:T(8,128)(2,1)S(1)}, u32[]{:S(2)}) copy-start(bf16[3,48,384]{2,1,0:T(8,128)(2,1)S(1)} %collective-permute-done.7.refs_7_) | copy-start | bytes 331780
  26.4 9.5 %collective-permute-start.5 = (bf16[2,3,48,384]{3,2,1,0:T(8,128)(2,1)}, bf16[2,3,48,384]{3,2,1,0:T(8,128)(2,1)}, u32[]{:S(2)}, u32[]{:S(2)}) collective-permute-start(bf16[2,3,48,384]{3,2,1,0:T(8,128)(2,1)} %collective-permute-done.1.refs_1_), channel_id=1, source_target_pairs={{0,192},{64,0},{128,64},{192,128},{1,193},{65,1},{129,65},{193,129... | collective-permute-start | bytes 663560 | tf_op jit(solution)/shard_map/ppermute | solution.py:24
  29.0 0.7 copy-start.12
  29.7 6.2 %collective-permute-start.9 = (bf16[96,768]{1,0:T(8,128)(2,1)S(1)}, bf16[96,768]{1,0:T(8,128)(2,1)}, u32[]{:S(2)}, u32[]{:S(2)}) collective-permute-start(bf16[96,768]{1,0:T(8,128)(2,1)S(1)} %get-tuple-element.59), channel_id=1, source_target_pairs={{1,0},{2,1},{3,2},{4,3},{5,4},{6,5},{7,6},{8,7},{9,8},{10,9},{11,1... | collective-permute-start | bytes 442376 | tf_op jit(solution)/shard_map/ppermute | solution.py:331
  35.8 9.0 %copy-start.9 = (bf16[2,3,48,384]{3,2,1,0:T(8,128)(2,1)}, bf16[2,3,48,384]{3,2,1,0:T(8,128)(2,1)S(1)}, u32[]{:S(2)}) copy-start(bf16[2,3,48,384]{3,2,1,0:T(8,128)(2,1)S(1)} %collective-permute-done.4.refs_3_) | copy-start | bytes 663556
  35.9 9.0 %copy-start.5 = (bf16[1280,384]{1,0:T(8,128)(2,1)}, bf16[1280,384]{1,0:T(8,128)(2,1)S(1)}, u32[]{:S(2)}) copy-start(bf16[1280,384]{1,0:T(8,128)(2,1)S(1)} %collective-permute-done.11.refs_17_) | copy-start | bytes 2949124
  35.9 7.6 %collective-permute-start.12 = (bf16[3,48,384]{2,1,0:T(8,128)(2,1)S(1)}, bf16[3,48,384]{2,1,0:T(8,128)(2,1)S(1)}, u32[]{:S(2)}, u32[]{:S(2)}) collective-permute-start(bf16[3,48,384]{2,1,0:T(8,128)(2,1)S(1)} %slice_bitcast_fusion.1), channel_id=1, source_target_pairs={{0,64},{64,128},{128,192},{192,0},{1,65},{65,129},{129,193},{193,1... | collective-permute-start | bytes 331784 | tf_op jit(solution)/shard_map/ppermute | solution.py:24
  36.0 8.8 %collective-permute-start.14 = (bf16[96,768]{1,0:T(8,128)(2,1)}, bf16[96,768]{1,0:T(8,128)(2,1)S(1)}, u32[]{:S(2)}, u32[]{:S(2)}) collective-permute-start(bf16[96,768]{1,0:T(8,128)(2,1)} %copy-done.12), channel_id=1, source_target_pairs={{0,16},{16,0},{1,17},{17,1},{2,18},{18,2},{3,19},{19,3},{4,20},{20... | collective-permute-start | bytes 442376 | tf_op jit(solution)/shard_map/ppermute | solution.py:28
  38.9 6.0 %collective-permute-start.15 = (bf16[96,768]{1,0:T(8,128)(2,1)}, bf16[96,768]{1,0:T(8,128)(2,1)S(1)}, u32[]{:S(2)}, u32[]{:S(2)}) collective-permute-start(bf16[96,768]{1,0:T(8,128)(2,1)} %collective-permute-done.9.refs_13_), channel_id=1, source_target_pairs={{0,16},{16,0},{1,17},{17,1},{2,18},{18,2},{3,19},{19,3},{4,20},{20... | collective-permute-start | bytes 442376 | tf_op jit(solution)/shard_map/ppermute | solution.py:28
  39.9 4.9 %collective-permute-start.13 = (bf16[3,48,384]{2,1,0:T(8,128)(2,1)S(1)}, bf16[3,48,384]{2,1,0:T(8,128)(2,1)S(1)}, u32[]{:S(2)}, u32[]{:S(2)}) collective-permute-start(bf16[3,48,384]{2,1,0:T(8,128)(2,1)S(1)} %slice_bitcast_fusion), channel_id=1, source_target_pairs={{0,192},{64,0},{128,64},{192,128},{1,193},{65,1},{129,65},{193,129... | collective-permute-start | bytes 331784 | tf_op jit(solution)/shard_map/ppermute | solution.py:24
  43.5 1.3 copy-start.17
  44.8 0.6 copy-start.18
  44.8 0.7 copy-start.13
  45.5 0.7 copy-start.14
  59.5 11.6 %collective-permute-start.17 = (bf16[3,768,384]{2,1,0:T(8,128)(2,1)}, bf16[3,768,384]{2,1,0:T(8,128)(2,1)S(1)}, u32[]{:S(2)}, u32[]{:S(2)}) collective-permute-start(bf16[3,768,384]{2,1,0:T(8,128)(2,1)} %get-tuple-element.72.weight_a), channel_id=1, source_target_pairs={{0,16},{16,0},{1,17},{17,1},{2,18},{18,2},{3,19},{19,3},{4,20},{20... | collective-permute-start | bytes 5308424 | tf_op jit(solution)/shard_map/ppermute | solution.py:28
  61.0 10.2 %collective-permute-start.16 = (bf16[1344,384]{1,0:T(8,128)(2,1)}, bf16[1344,384]{1,0:T(8,128)(2,1)S(1)}, u32[]{:S(2)}, u32[]{:S(2)}) collective-permute-start(bf16[1344,384]{1,0:T(8,128)(2,1)} %get-tuple-element.71.refs_3_), channel_id=1, source_target_pairs={{0,16},{16,0},{1,17},{17,1},{2,18},{18,2},{3,19},{19,3},{4,20},{20... | collective-permute-start | bytes 3096584 | tf_op jit(solution)/shard_map/ppermute | solution.py:28
  71.1 13.6 %copy-start.4 = (bf16[1344,384]{1,0:T(8,128)(2,1)}, bf16[1344,384]{1,0:T(8,128)(2,1)S(1)}, u32[]{:S(2)}) copy-start(bf16[1344,384]{1,0:T(8,128)(2,1)S(1)} %collective-permute-done.16.back_b) | copy-start | bytes 3096580
  71.2 13.6 %copy-start.3 = (bf16[3,768,384]{2,1,0:T(8,128)(2,1)}, bf16[3,768,384]{2,1,0:T(8,128)(2,1)S(1)}, u32[]{:S(2)}) copy-start(bf16[3,768,384]{2,1,0:T(8,128)(2,1)S(1)} %collective-permute-done.17.weight_b) | copy-start | bytes 5308420
  71.2 10.0 %collective-permute-start.21 = (bf16[4,48,384]{2,1,0:T(8,128)(2,1)}, bf16[4,48,384]{2,1,0:T(8,128)(2,1)S(1)}, u32[]{:S(2)}, u32[]{:S(2)}) collective-permute-start(bf16[4,48,384]{2,1,0:T(8,128)(2,1)} %get-tuple-element.88), channel_id=1, source_target_pairs={{0,8},{8,32},{32,40},{40,0},{1,9},{9,33},{33,41},{41,1},{2,10},{10... | collective-permute-start | bytes 442376 | tf_op jit(solution)/shard_map/ppermute | solution.py:24
  76.6 20.3 %collective-permute-start.18 = (bf16[2,192,384]{2,1,0:T(8,128)(2,1)}, bf16[2,192,384]{2,1,0:T(8,128)(2,1)S(1)}, u32[]{:S(2)}, u32[]{:S(2)}) collective-permute-start(bf16[2,192,384]{2,1,0:T(8,128)(2,1)} %get-tuple-element.84), channel_id=1, source_target_pairs={{0,64},{64,128},{128,192},{192,0},{1,65},{65,129},{129,193},{193,1... | collective-permute-start | bytes 884744 | tf_op jit(solution)/shard_map/ppermute | solution.py:24
  76.6 20.3 %collective-permute-start.19 = (bf16[2,192,384]{2,1,0:T(8,128)(2,1)}, bf16[2,192,384]{2,1,0:T(8,128)(2,1)S(1)}, u32[]{:S(2)}, u32[]{:S(2)}) collective-permute-start(bf16[2,192,384]{2,1,0:T(8,128)(2,1)} %get-tuple-element.85), channel_id=1, source_target_pairs={{0,192},{64,0},{128,64},{192,128},{1,193},{65,1},{129,65},{193,129... | collective-permute-start | bytes 884744 | tf_op jit(solution)/shard_map/ppermute | solution.py:24
  80.0 16.9 %collective-permute-start.20 = (bf16[2,192,384]{2,1,0:T(8,128)(2,1)}, bf16[2,192,384]{2,1,0:T(8,128)(2,1)}, u32[]{:S(2)}, u32[]{:S(2)}) collective-permute-start(bf16[2,192,384]{2,1,0:T(8,128)(2,1)} %get-tuple-element.86), channel_id=1, source_target_pairs={{0,128},{64,192},{128,0},{192,64},{1,129},{65,193},{129,1},{193,65... | collective-permute-start | bytes 884744 | tf_op jit(solution)/shard_map/ppermute | solution.py:24
  81.2 15.7 %collective-permute-start.22 = (bf16[4,48,384]{2,1,0:T(8,128)(2,1)}, bf16[4,48,384]{2,1,0:T(8,128)(2,1)}, u32[]{:S(2)}, u32[]{:S(2)}) collective-permute-start(bf16[4,48,384]{2,1,0:T(8,128)(2,1)} %get-tuple-element.89), channel_id=1, source_target_pairs={{0,40},{8,0},{32,8},{40,32},{1,41},{9,1},{33,9},{41,33},{2,42},{10... | collective-permute-start | bytes 442376 | tf_op jit(solution)/shard_map/ppermute | solution.py:24
  81.2 15.7 %collective-permute-start.23 = (bf16[4,48,384]{2,1,0:T(8,128)(2,1)}, bf16[4,48,384]{2,1,0:T(8,128)(2,1)}, u32[]{:S(2)}, u32[]{:S(2)}) collective-permute-start(bf16[4,48,384]{2,1,0:T(8,128)(2,1)} %get-tuple-element.90), channel_id=1, source_target_pairs={{0,32},{8,40},{32,0},{40,8},{1,33},{9,41},{33,1},{41,9},{2,34},{10... | collective-permute-start | bytes 442376 | tf_op jit(solution)/shard_map/ppermute | solution.py:24
  84.7 12.1 %copy-start.11 = (bf16[4,48,384]{2,1,0:T(8,128)(2,1)S(1)}, bf16[4,48,384]{2,1,0:T(8,128)(2,1)}, u32[]{:S(2)}) copy-start(bf16[4,48,384]{2,1,0:T(8,128)(2,1)} %get-tuple-element.96) | copy-start | bytes 442372
  84.7 17.1 %copy-start.10 = (bf16[2,192,384]{2,1,0:T(8,128)(2,1)S(1)}, bf16[2,192,384]{2,1,0:T(8,128)(2,1)}, u32[]{:S(2)}) copy-start(bf16[2,192,384]{2,1,0:T(8,128)(2,1)} %get-tuple-element.92) | copy-start | bytes 884740
  97.8 7.9 %collective-permute-start.27 = (bf16[1,48,384]{2,1,0:T(8,128)(2,1)S(1)}, bf16[1,48,384]{2,1,0:T(8,128)(2,1)S(1)}, u32[]{:S(2)}, u32[]{:S(2)}) collective-permute-start(bf16[1,48,384]{2,1,0:T(8,128)(2,1)S(1)} %get-tuple-element.119), channel_id=1, source_target_pairs={{0,64},{64,128},{128,192},{192,0},{1,65},{65,129},{129,193},{193,1... | collective-permute-start | bytes 110600 | tf_op jit(solution)/shard_map/ppermute | solution.py:24
  98.7 7.2 %collective-permute-start.28 = (bf16[1,48,384]{2,1,0:T(8,128)(2,1)S(1)}, bf16[1,48,384]{2,1,0:T(8,128)(2,1)S(1)}, u32[]{:S(2)}, u32[]{:S(2)}) collective-permute-start(bf16[1,48,384]{2,1,0:T(8,128)(2,1)S(1)} %get-tuple-element.121), channel_id=1, source_target_pairs={{0,192},{64,0},{128,64},{192,128},{1,193},{65,1},{129,65},{193,129... | collective-permute-start | bytes 110600 | tf_op jit(solution)/shard_map/ppermute | solution.py:24
  100.8 5.2 %collective-permute-start.29 = (bf16[1,48,384]{2,1,0:T(8,128)(2,1)S(1)}, bf16[1,48,384]{2,1,0:T(8,128)(2,1)S(1)}, u32[]{:S(2)}, u32[]{:S(2)}) collective-permute-start(bf16[1,48,384]{2,1,0:T(8,128)(2,1)S(1)} %get-tuple-element.120), channel_id=1, source_target_pairs={{0,128},{64,192},{128,0},{192,64},{1,129},{65,193},{129,1},{193,65... | collective-permute-start | bytes 110600 | tf_op jit(solution)/shard_map/ppermute | solution.py:24
  103.0 4.8 %collective-permute-start.24 = (bf16[2,48,384]{2,1,0:T(8,128)(2,1)S(1)}, bf16[2,48,384]{2,1,0:T(8,128)(2,1)S(1)}, u32[]{:S(2)}, u32[]{:S(2)}) collective-permute-start(bf16[2,48,384]{2,1,0:T(8,128)(2,1)S(1)} %get-tuple-element.116), channel_id=1, source_target_pairs={{0,8},{8,32},{32,40},{40,0},{1,9},{9,33},{33,41},{41,1},{2,10},{10... | collective-permute-start | bytes 221192 | tf_op jit(solution)/shard_map/ppermute | solution.py:24
  103.0 4.7 %collective-permute-start.25 = (bf16[2,48,384]{2,1,0:T(8,128)(2,1)S(1)}, bf16[2,48,384]{2,1,0:T(8,128)(2,1)S(1)}, u32[]{:S(2)}, u32[]{:S(2)}) collective-permute-start(bf16[2,48,384]{2,1,0:T(8,128)(2,1)S(1)} %get-tuple-element.118), channel_id=1, source_target_pairs={{0,40},{8,0},{32,8},{40,32},{1,41},{9,1},{33,9},{41,33},{2,42},{10... | collective-permute-start | bytes 221192 | tf_op jit(solution)/shard_map/ppermute | solution.py:24
  105.7 5.4 %collective-permute-start.26 = (bf16[2,48,384]{2,1,0:T(8,128)(2,1)S(1)}, bf16[2,48,384]{2,1,0:T(8,128)(2,1)S(1)}, u32[]{:S(2)}, u32[]{:S(2)}) collective-permute-start(bf16[2,48,384]{2,1,0:T(8,128)(2,1)S(1)} %get-tuple-element.117), channel_id=1, source_target_pairs={{0,32},{8,40},{32,0},{40,8},{1,33},{9,41},{33,1},{41,9},{2,34},{10... | collective-permute-start | bytes 221192 | tf_op jit(solution)/shard_map/ppermute | solution.py:24
  112.1 3.7 %collective-permute-start.30 = (bf16[3,48,384]{2,1,0:T(8,128)(2,1)S(1)}, bf16[3,48,384]{2,1,0:T(8,128)(2,1)S(1)}, u32[]{:S(2)}, u32[]{:S(2)}) collective-permute-start(bf16[3,48,384]{2,1,0:T(8,128)(2,1)S(1)} %pad_maximum_fusion.3), channel_id=1, source_target_pairs={{0,1},{1,0},{2,3},{3,2},{4,5},{5,4},{6,7},{7,6},{8,9},{9,8},{10,11... | collective-permute-start | bytes 331784 | tf_op jit(solution)/shard_map/ppermute | solution.py:28
  115.8 5.6 %collective-permute-start.31 = (bf16[3,48,384]{2,1,0:T(8,128)(2,1)S(1)}, bf16[3,48,384]{2,1,0:T(8,128)(2,1)S(1)}, u32[]{:S(2)}, u32[]{:S(2)}) collective-permute-start(bf16[3,48,384]{2,1,0:T(8,128)(2,1)S(1)} %add_convert_fusion.2), channel_id=1, source_target_pairs={{0,2},{1,3},{2,0},{3,1},{4,6},{5,7},{6,4},{7,5},{8,10},{9,11},{10,... | collective-permute-start | bytes 331784 | tf_op jit(solution)/shard_map/ppermute | solution.py:28
  121.5 7.7 %collective-permute-start.32 = (bf16[3,48,384]{2,1,0:T(8,128)(2,1)S(1)}, bf16[3,48,384]{2,1,0:T(8,128)(2,1)S(1)}, u32[]{:S(2)}, u32[]{:S(2)}) collective-permute-start(bf16[3,48,384]{2,1,0:T(8,128)(2,1)S(1)} %add_convert_fusion.1), channel_id=1, source_target_pairs={{0,4},{1,5},{2,6},{3,7},{4,0},{5,1},{6,2},{7,3},{8,12},{9,13},{10,... | collective-permute-start | bytes 331784 | tf_op jit(solution)/shard_map/ppermute | solution.py:28
  129.2 4.0 %collective-permute-start.33 = (bf16[3,48,384]{2,1,0:T(8,128)(2,1)S(1)}, bf16[3,48,384]{2,1,0:T(8,128)(2,1)S(1)}, u32[]{:S(2)}, u32[]{:S(2)}) collective-permute-start(bf16[3,48,384]{2,1,0:T(8,128)(2,1)S(1)} %add_convert_fusion), channel_id=1, source_target_pairs={{0,8},{8,0},{1,9},{9,1},{2,10},{10,2},{3,11},{11,3},{4,12},{12,4},... | collective-permute-start | bytes 331784 | tf_op jit(solution)/shard_map/ppermute | solution.py:28
  133.2 7.9 %collective-permute-start.34 = (bf16[3,48,384]{2,1,0:T(8,128)(2,1)S(1)}, bf16[3,48,384]{2,1,0:T(8,128)(2,1)S(1)}, u32[]{:S(2)}, u32[]{:S(2)}) collective-permute-start(bf16[3,48,384]{2,1,0:T(8,128)(2,1)S(1)} %get-tuple-element.107), channel_id=1, source_target_pairs={{0,16},{16,0},{1,17},{17,1},{2,18},{18,2},{3,19},{19,3},{4,20},{20... | collective-permute-start | bytes 331784 | tf_op jit(solution)/shard_map/ppermute | solution.py:28

commit v3 on v2

v3 whole, which is shorter than its diff:
```python
import functools
import math

import jax
import jax.numpy as jnp
from jax import lax
from jax.experimental import pallas as pl
from jax.experimental.pallas import tpu as pltpu
from jax.sharding import Mesh, PartitionSpec as P

FILTER_TAPS = 3
DILATION_STEP = 32
REACH = 32
AXES = ("x", "yh", "core", "yl", "z")
SIZES = (4, 2, 2, 2, 8)
SEQ = ("yl", "z")
RING_Y = ("yh", "yl")
BF16 = jnp.bfloat16
F32 = jnp.float32


def shift(value, axis, count, step):
    pairs = [(i, (i + step) % count) for i in range(count)]
    return lax.ppermute(value, axis, pairs)


def swap(value, axis, count, mask):
    return lax.ppermute(value, axis, [(i, i ^ mask) for i in range(count)])


def gelu_slope(value):
    coeff = math.sqrt(2.0 / math.pi)
    square = value * value
    tangent = jnp.tanh(value * (coeff + coeff * 0.044715 * square))
    return (0.5 + 0.5 * tangent) * (
        1.0 + value * (1.0 - tangent) * (coeff + coeff * 3.0 * 0.044715 * square)
    )


def join(*arrays):
    return lax.optimization_barrier(arrays)


def load_weight(position, pieces, weight, sem):
    x, yh, core = position[0], position[1], position[2]
    rows = pieces[0].shape[2]
    own, across, up_own, up_across, down_own, down_across, far = pieces
    blocks = [(own, 0, 0), (across, 0, 1), (up_own, 3, 0), (up_across, 3, 1)]
    blocks += [(down_own, 1, 0), (down_across, 1, 1), (far.at[0], 2, 0), (far.at[1], 2, 1)]
    copies = []
    for block, step_x, step_y in blocks:
        for side in range(2):
            owner = ((x + step_x) % 4) * 4 + ((yh + step_y) % 2) * 2 + (core + side) % 2
            place = pl.multiple_of(owner * rows, 16)
            copies.append(
                pltpu.make_async_copy(
                    block.at[side], weight.at[:, pl.ds(place, rows), :], sem.at[len(copies)]
                )
            )
    return copies


def forward_kernel(position, *refs):
    pieces, refs = refs[:7], refs[7:]
    normed_hbm, edges, upstream_hbm = refs[0:2], refs[2:4], refs[4:6]
    weight_out, back_out, along_x = refs[6], refs[7:9], refs[9:13]
    weight, normed, upstream, back, grad = refs[13:18]
    piece_sem, load_sem, back_sem, weight_sem, grad_sem = refs[18:]
    x, core = position[0], position[2]
    channels, half = weight.shape[1:]
    count = normed_hbm[0].shape[0]
    lane = pl.multiple_of(core * half, 128)
    copies = load_weight(position, pieces, weight, piece_sem)
    wide = 2 * REACH
    loads = []
    for index in range(2):
        center = upstream_hbm[index]
        if index == 0:
            center = center.at[:, pl.ds(lane, half)]
        rows, lanes = slice(index * wide, (index + 1) * wide), slice(index * half, (index + 1) * half)
        moves = [
            (normed_hbm[index], normed.at[index, wide : wide + count]),
            (center, upstream.at[index, REACH : REACH + count]),
        ]
        for edge, place in zip(edges, (0, wide + count)):
            moves.append((edge.at[rows], normed.at[index, place : place + wide]))
        for edge, place in zip(edges, (0, REACH + count)):
            moves.append((edge.at[2 * wide :, lanes], upstream.at[index, place : place + REACH]))
        loads.append(
            [
                pltpu.make_async_copy(source, target, load_sem.at[index, place])
                for place, (source, target) in enumerate(moves)
            ]
        )
    for copy in copies + loads[0] + loads[1]:
        copy.start()
    for copy in copies:
        copy.wait()
    save = pltpu.make_async_copy(weight, weight_out, weight_sem)
    save.start()
    length = back.shape[1]
    block = length // 3
    saves = [save]
    for index in range(2):
        for copy in loads[index]:
            copy.wait()
        for start in range(0, length, block):
            conv = jnp.dot(
                normed[index, start : start + block, :], weight[0], preferred_element_type=F32
            )
            for tap in range(1, FILTER_TAPS):
                low = start + tap * DILATION_STEP
                conv = conv + jnp.dot(
                    normed[index, low : low + block, :], weight[tap], preferred_element_type=F32
                )
            incoming = upstream[index, start : start + block, :].astype(F32)
            back[index, start : start + block, :] = (incoming * gelu_slope(conv)).astype(BF16)
        back_save = pltpu.make_async_copy(back.at[index], back_out[index], back_sem.at[index])
        back_save.start()
        saves.append(back_save)
    total = None
    for index in range(2):
        shifted = jnp.concatenate(
            [
                back[index, wide - tap * DILATION_STEP : wide - tap * DILATION_STEP + count, :]
                for tap in range(FILTER_TAPS)
            ],
            axis=1,
        )
        part = lax.dot_general(
            normed[index, wide : wide + count, :],
            shifted,
            (((0,), (0,)), ((), ())),
            preferred_element_type=F32,
        )
        total = part if total is None else total + part
    for tap in range(FILTER_TAPS):
        grad[tap] = total[:, tap * half : (tap + 1) * half].astype(BF16)
    quarter = channels // 4
    for step in range(4):
        place = pl.multiple_of(((x + step) % 4) * quarter, 16)
        grad_save = pltpu.make_async_copy(
            grad.at[:, pl.ds(place, quarter), :], along_x[step], grad_sem.at[step]
        )
        grad_save.start()
        saves.append(grad_save)
    for copy in saves:
        copy.wait()


def forward(position, pieces, normed, edges, upstream):
    count, channels = normed[0].shape
    half = channels // 2
    length = count + 2 * REACH
    anywhere = pl.BlockSpec(memory_space=pl.ANY)
    dma = pltpu.SemaphoreType.DMA
    return pl.pallas_call(
        forward_kernel,
        out_shape=[jax.ShapeDtypeStruct((FILTER_TAPS, channels, half), BF16)]
        + [jax.ShapeDtypeStruct((length, half), BF16)] * 2
        + [jax.ShapeDtypeStruct((FILTER_TAPS, channels // 4, half), BF16)] * 4,
        in_specs=[pl.BlockSpec(memory_space=pltpu.SMEM)] + [anywhere] * 13,
        out_specs=[anywhere] * 7,
        scratch_shapes=[
            pltpu.VMEM((FILTER_TAPS, channels, half), BF16),
            pltpu.VMEM((2, length + 2 * REACH, channels), BF16),
            pltpu.VMEM((2, length, half), BF16),
            pltpu.VMEM((2, length, half), BF16),
            pltpu.VMEM((FILTER_TAPS, channels, half), BF16),
            dma((16,)),
            dma((2, 6)),
            dma((2,)),
            dma,
            dma((4,)),
        ],
        compiler_params=pltpu.CompilerParams(vmem_limit_bytes=56 * 1024 * 1024),
        name="forward",
    )(position, *pieces, *normed, *edges, *upstream)


def backward_kernel(back_a, back_b, weight_a, weight_b, inputs, scale, gain, incoming, out):
    block = out.shape[0]
    start = pl.program_id(0) * block
    grad = jnp.zeros(out.shape, F32)
    for tap in range(FILTER_TAPS):
        low = pl.multiple_of(start + (FILTER_TAPS - 1 - tap) * DILATION_STEP, 32)
        rows = pl.ds(low, block)
        grad = grad + lax.dot_general(
            jnp.concatenate([back_a[rows, :], back_b[rows, :]], axis=1),
            jnp.concatenate([weight_a[tap], weight_b[tap]], axis=1),
            (((1,), (1,)), ((), ())),
            preferred_element_type=F32,
        )
    scaled = grad * gain[...]
    value = inputs[...]
    factor = scale[...]
    spread = jnp.mean(scaled * value, axis=-1, keepdims=True)
    result = incoming[...].astype(F32) + factor * scaled - value * (factor * factor * factor * spread)
    out[...] = result.astype(BF16)


def backward(back, weight, inputs, scale, gain, incoming):
    count, channels = inputs.shape
    block = 256
    whole = lambda array: pl.BlockSpec(array.shape, lambda i: (0,) * array.ndim)
    part = pl.BlockSpec((block, channels), lambda i: (i, 0))
    return pl.pallas_call(
        backward_kernel,
        grid=(count // block,),
        out_shape=jax.ShapeDtypeStruct((count, channels), BF16),
        in_specs=[whole(back[0]), whole(back[1]), whole(weight[0]), whole(weight[1]), part]
        + [pl.BlockSpec((block, 1), lambda i: (i, 0)), whole(gain), part],
        out_specs=part,
        compiler_params=pltpu.CompilerParams(vmem_limit_bytes=56 * 1024 * 1024),
        name="backward",
    )(*back, *weight, inputs, scale, gain, incoming)


def share_weight_grad(total, yl, core):
    for mask in (1, 2, 4):
        sent = total.astype(BF16)
        total = sent.astype(F32) + swap(sent, "z", 8, mask).astype(F32)
    mine = total.astype(BF16)
    other = swap(mine, "yl", 2, 1)
    by_core = [jnp.where(yl == rows, mine, other) for rows in range(2)]
    kept = jnp.where(core == 0, by_core[0], by_core[1])
    sent = jnp.where(core == 0, by_core[1], by_core[0])
    arrived = swap(sent, "core", 2, 1)
    low = jnp.where(core == 0, kept, arrived)
    high = jnp.where(core == 0, arrived, kept)
    return jnp.concatenate([low, high], axis=2).astype(F32)


def on_device(activations, nucleotides, base_table, norm_gain, filter_weight, upstream):
    x, yh, core, yl = (lax.axis_index(name) for name in ("x", "yh", "core", "yl"))
    y = yh * 2 + yl
    position = jnp.stack([x, yh, core, yl]).astype(jnp.int32)
    tokens, incoming = activations[0], upstream[0]
    count, channels = tokens.shape
    half = channels // 2

    mine = lax.dynamic_slice_in_dim(filter_weight, core * half, half, axis=2)
    other = lax.dynamic_slice_in_dim(filter_weight, (1 - core) * half, half, axis=2)
    own = jnp.stack([mine, swap(other, "core", 2, 1)])
    own, tokens, nucleotides, incoming = join(own, tokens, nucleotides, incoming)

    across = swap(own, RING_Y, 4, 3)
    up_own, down_own = shift(own, "x", 4, 1), shift(own, "x", 4, -1)
    bases = nucleotides[0][:, None]
    row = base_table[3][None]
    for base in (2, 1, 0):
        row = jnp.where(bases == base, base_table[base][None], row)
    inputs = tokens.astype(F32) + row
    scale_inv = lax.rsqrt(jnp.mean(inputs * inputs, axis=-1, keepdims=True) + 1e-06)
    normed = (inputs * scale_inv * norm_gain).astype(BF16)
    across, up_own, down_own, normed, incoming = join(across, up_own, down_own, normed, incoming)

    far = shift(jnp.stack([own, across]), "x", 4, 2)
    up_across, down_across = shift(across, "x", 4, 1), shift(across, "x", 4, -1)
    upstream_sent = lax.dynamic_slice_in_dim(incoming, (1 - core) * half, half, axis=1)
    normed_other = swap(normed, "core", 2, 1)
    upstream_other = swap(upstream_sent, "core", 2, 1)

    def edge(rows, reach_rows):
        upstream_edge = lax.dynamic_slice_in_dim(incoming[reach_rows], core * half, half, axis=1)
        upstream_edge = jnp.concatenate([upstream_edge, upstream_other[reach_rows]], axis=1)
        return jnp.concatenate([normed[rows], normed_other[rows], upstream_edge])

    low = lax.ppermute(
        edge(slice(count - 2 * REACH, count), slice(count - REACH, count)),
        SEQ,
        [(i, i + 1) for i in range(15)],
    )
    high = lax.ppermute(
        edge(slice(0, 2 * REACH), slice(0, REACH)), SEQ, [(i + 1, i) for i in range(15)]
    )
    weight, back, back_other, *grads = forward(
        position,
        [own, across, up_own, up_across, down_own, down_across, far],
        (normed, normed_other),
        (low, high),
        (incoming, upstream_other),
    )

    back_rest = swap(back_other, "core", 2, 1)
    weight_rest = swap(weight, "core", 2, 1)
    along_x = [grads[0]] + [shift(grads[step], "x", 4, step) for step in (1, 3, 2)]
    result = backward(
        (back, back_rest), (weight, weight_rest), inputs, scale_inv, norm_gain[None], incoming
    )
    result, *along_x = join(result, *along_x)

    rows = channels // 16
    by_y = []
    for step in range(4):
        start = ((y + step) % 4) * rows
        parts = [lax.dynamic_slice_in_dim(part, start, rows, axis=1) for part in along_x]
        by_y.append(sum(part.astype(F32) for part in parts))
    total = by_y[0]
    for step in (1, 3, 2):
        total = total + shift(by_y[step].astype(BF16), RING_Y, 4, step).astype(F32)
    weight_grad = share_weight_grad(total, yl, core)
    total_rows = 16 * 16 * count
    return (result[None], weight_grad / math.sqrt(total_rows))


def solution(mesh):
    grid = Mesh(mesh.devices.reshape(SIZES), AXES)
    dp, seq = ("x", "yh", "core"), SEQ
    in_specs = (
        P(dp, seq, None),
        P(dp, seq),
        P(),
        P(),
        P(None, dp, None),
        P(dp, seq, None),
    )
    out_specs = (P(dp, seq, None), P(None, dp, None))
    return jax.shard_map(
        on_device, mesh=grid, in_specs=in_specs, out_specs=out_specs, check_vma=False
    )
```

time: 144 us -> 126 us (0.88)
  starting transfers between devices: 56.5 us -> 42.2 us
  Pallas kernels: 35.5 us -> 29.1 us
  waiting for transfers between devices: 28.3 us -> 34 us
    ppermute x20 -> x11, starting transfers between devices: 30.2 us -> 17.5 us  [shift(): return lax.ppermute(value, axis, pairs)]
    pallas_call x1 -> x0, Pallas kernels: 10.1 us -> none  [weight_grads(): pl.pallas_call(weight_grad_kernel, out_shape=[jax.ShapeDtypeStruct((2, qu...]
    ppermute x20 -> x11, waiting for transfers between devices: 5.62 us -> 14.9 us  [shift(): return lax.ppermute(value, axis, pairs)]
    pallas_call x1, Pallas kernels: 13.3 us -> 18.2 us  [forward(): pl.pallas_call(forward_kernel, out_shape=[jax.ShapeDtypeStruct((FILTER_TA...]
    ppermute x2, waiting for transfers between devices: 4.87 us -> 0.01 us  [the longest x1 0.01 us: on_device(): lax.ppermute(edge(slice(0, 2 * REACH), slice(0, REACH)), SEQ, [(i + 1, i)...]
    ppermute x13 -> x11, starting transfers between devices: 21.4 us -> 19.2 us  [swap(): return lax.ppermute(value, axis, [(i, i ^ mask) for i in range(count)])]
    ppermute x13 -> x11, waiting for transfers between devices: 17.8 us -> 19.1 us  [swap(): return lax.ppermute(value, axis, [(i, i ^ mask) for i in range(count)])]
    unnamed x40 -> x34, local copies, waits for them, and re-layouts: 4.58 us -> 5.41 us
  transfers between devices with their start and end apart: 35 -> 24, of which waited for: 10 -> 12; matrix products, arithmetic and copies ran while one was open for 9% -> 7% of each run, Pallas kernels for 16% -> 9%
where the time goes in v3:
time: 126 us; the launch traced here: 125 us
  starting transfers between devices  42.2 us (33%)
  waiting for transfers between devices  34 us (27%)
  Pallas kernels  29.1 us (23%)
  other arithmetic  9.95 us (8%)
  local copies, waits for them, and re-layouts  9.13 us (7%)
    ppermute x11, starting transfers between devices, swap(): return lax.ppermute(value, axis, [(i, i ^ mask) for i in range(count)])  19.2 us
    ppermute x11, waiting for transfers between devices, swap(): return lax.ppermute(value, axis, [(i, i ^ mask) for i in range(count)])  19.1 us
    pallas_call x1, Pallas kernels, forward(): pl.pallas_call(forward_kernel, out_shape=[jax.ShapeDtypeStruct((FILTER_TA...  18.2 us
    ppermute x11, starting transfers between devices, shift(): return lax.ppermute(value, axis, pairs)  17.5 us
    ppermute x11, waiting for transfers between devices, shift(): return lax.ppermute(value, axis, pairs)  14.9 us
    pallas_call x1, Pallas kernels, backward(): pl.pallas_call(backward_kernel, grid=(count // block,), out_shape=jax.Sha...  10.8 us
    unnamed x34, local copies, waits for them, and re-layouts  5.41 us
    ppermute x1, starting transfers between devices, on_device(): lax.ppermute(edge(slice(count - 2 * REACH, count), slice(count - REACH, c...  4.18 us
  transfers between devices with their start and end apart: 24, of which 12 were waited for; matrix products, arithmetic and copies ran while one was open for 7% of the time, Pallas kernels for 9%

profile of v3, /device:TPU:1, one launch (start us, length us, event | category | flops | bytes accessed | tf_op | source)
XLA Modules:
  0.0 125.3 jit_solution(4310795325093671420)
XLA Ops:
  0.6 1.0 dynamic-slice_bitcast_fusion
  1.6 3.3 %collective-permute-start = (bf16[3,48,384]{2,1,0:T(8,128)(2,1)S(1)}, bf16[3,48,384]{2,1,0:T(8,128)(2,1)S(1)}, u32[]{:S(2)}, u32[]{:S(2)}) collective-permute-start(bf16[3,48,384]{2,1,0:T(8,128)(2,1)S(1)} %get-tuple-element.70), channel_id=1, source_target_pairs={{0,16},{16,0},{1,17},{17,1},{2,18},{18,2},{3,19},{19,3},{4,20},{20... | collective-permute-start | bytes 331784 | tf_op jit(solution)/shard_map/ppermute | solution.py:28
  5.0 0.9 slice_reduce_fusion.3
  5.9 0.1 collective-permute-done
  6.0 1.1 collective-permute-start.1
  7.0 1.2 collective-permute-start.2
  8.3 1.5 %collective-permute-start.3 = (bf16[2,3,48,384]{3,2,1,0:T(8,128)(2,1)S(1)}, bf16[2,3,48,384]{3,2,1,0:T(8,128)(2,1)S(1)}, u32[]{:S(2)}, u32[]{:S(2)}) collective-permute-start(bf16[2,3,48,384]{3,2,1,0:T(8,128)(2,1)S(1)} %pad_maximum_fusion.1.refs_0_), channel_id=1, source_target_pairs={{0,192},{64,0},{128,64},{192,128},{1,193},{65,1},{129,65},{193,129... | collective-permute-start | bytes 663560 | tf_op jit(solution)/shard_map/ppermute | solution.py:24
  9.7 0.7 compare_reduce_fusion.2
  10.5 3.7 %multiply_reduce_fusion = (f32[1280]{0:T(1024)S(1)}, f32[1280,768]{1,0:T(8,128)S(1)}) fusion(f32[768]{0:T(1024)S(1)} %get-tuple-element.46, f32[768]{0:T(1024)S(1)} %get-tuple-element.47, pred[1280]{0:T(1024)(128)(4,1)S(1)} %get-tuple-element.49, f32[768]{0:T(1024)S(1)} %get-tuple-element.45, pred[1280]{0:T(1024)(128)(4,1)S(1)} %get-tuple-element.50, ...), kind=kLoop, calls=%fused_computation.1 | loop fusion | flops 6880000 | bytes 5919488 | tf_op jit(solution)/shard_map/reduce_sum | solution.py:254
  14.2 0.0 copy-start.1
  14.2 0.4 multiply_convert_fusion.refs_7_
  14.6 0.0 copy-start.2
  14.7 0.0 collective-permute-done.1.refs_1_
  14.7 0.0 collective-permute-done.3.refs_4_
  14.7 1.5 %collective-permute-start.7 = (bf16[1280,768]{1,0:T(8,128)(2,1)S(1)}, bf16[1280,768]{1,0:T(8,128)(2,1)S(1)}, u32[]{:S(2)}, u32[]{:S(2)}) collective-permute-start(bf16[1280,768]{1,0:T(8,128)(2,1)S(1)} %multiply_convert_fusion.refs_7_), channel_id=1, source_target_pairs={{0,16},{16,0},{1,17},{17,1},{2,18},{18,2},{3,19},{19,3},{4,20},{20... | collective-permute-start | bytes 5898248 | tf_op jit(solution)/shard_map/ppermute | solution.py:28
  16.2 1.0 copy-done.1
  17.2 0.1 constant_dynamic-slice_fusion.1
  17.3 1.3 %collective-permute-start.8 = (bf16[1280,384]{1,0:T(8,128)(2,1)S(1)}, bf16[1280,384]{1,0:T(8,128)(2,1)S(1)}, u32[]{:S(2)}, u32[]{:S(2)}) collective-permute-start(bf16[1280,384]{1,0:T(8,128)(2,1)S(1)} %constant_dynamic-slice_fusion.1), channel_id=1, source_target_pairs={{0,16},{16,0},{1,17},{17,1},{2,18},{18,2},{3,19},{19,3},{4,20},{20... | collective-permute-start | bytes 2949128 | tf_op jit(solution)/shard_map/ppermute | solution.py:28
  18.6 0.8 pad_maximum_fusion
  19.4 1.5 %collective-permute-start.6 = (bf16[2,2,3,48,384]{4,3,2,1,0:T(8,128)(2,1)}, bf16[2,2,3,48,384]{4,3,2,1,0:T(8,128)(2,1)}, u32[]{:S(2)}, u32[]{:S(2)}) collective-permute-start(bf16[2,2,3,48,384]{4,3,2,1,0:T(8,128)(2,1)} %pad_maximum_fusion), channel_id=1, source_target_pairs={{0,128},{64,192},{128,0},{192,64},{1,129},{65,193},{129,1},{193,65... | collective-permute-start | bytes 1327112 | tf_op jit(solution)/shard_map/ppermute | solution.py:24
  21.0 0.2 collective-permute-done.8.refs_12_
  21.2 1.3 %copy-done.3 = bf16[1280,768]{1,0:T(8,128)(2,1)} copy-done((bf16[1280,768]{1,0:T(8,128)(2,1)}, bf16[1280,768]{1,0:T(8,128)(2,1)S(1)}, u32[]{:S(2)}) %copy-start.3) | copy-done | bytes 1966104
  22.6 1.3 %collective-permute-start.10 = (bf16[160,768]{1,0:T(8,128)(2,1)S(1)}, bf16[160,768]{1,0:T(8,128)(2,1)S(1)}, u32[]{:S(2)}, u32[]{:S(2)}) collective-permute-start(bf16[160,768]{1,0:T(8,128)(2,1)S(1)} %maximum_maximum_fusion.1), channel_id=1, source_target_pairs={{1,0},{2,1},{3,2},{4,3},{5,4},{6,5},{7,6},{8,7},{9,8},{10,9},{11,1... | collective-permute-start | bytes 737288 | tf_op jit(solution)/shard_map/ppermute | solution.py:274
  23.9 4.2 %collective-permute-start.9 = (bf16[160,768]{1,0:T(8,128)(2,1)S(1)}, bf16[160,768]{1,0:T(8,128)(2,1)S(1)}, u32[]{:S(2)}, u32[]{:S(2)}) collective-permute-start(bf16[160,768]{1,0:T(8,128)(2,1)S(1)} %maximum_maximum_fusion), channel_id=1, source_target_pairs={{0,1},{1,2},{2,3},{3,4},{4,5},{5,6},{6,7},{7,8},{8,9},{9,10},{10,1... | collective-permute-start | bytes 737288 | tf_op jit(solution)/shard_map/ppermute | solution.py:269
  28.1 1.2 collective-permute-start.4
  29.3 1.7 %collective-permute-start.5 = (bf16[2,3,48,384]{3,2,1,0:T(8,128)(2,1)S(1)}, bf16[2,3,48,384]{3,2,1,0:T(8,128)(2,1)S(1)}, u32[]{:S(2)}, u32[]{:S(2)}) collective-permute-start(bf16[2,3,48,384]{3,2,1,0:T(8,128)(2,1)S(1)} %collective-permute-done.1.refs_1_), channel_id=1, source_target_pairs={{0,192},{64,0},{128,64},{192,128},{1,193},{65,1},{129,65},{193,129... | collective-permute-start | bytes 663560 | tf_op jit(solution)/shard_map/ppermute | solution.py:24
  31.0 0.7 pad_add_fusion.position
  31.7 6.3 %collective-permute-done.4.refs_3_ = bf16[2,3,48,384]{3,2,1,0:T(8,128)(2,1)S(1)} collective-permute-done((bf16[2,3,48,384]{3,2,1,0:T(8,128)(2,1)S(1)}, bf16[2,3,48,384]{3,2,1,0:T(8,128)(2,1)S(1)}, u32[]{:S(2)}, u32[]{:S(2)}) %collective-permute-start.4) | collective-permute-done | bytes 221216 | tf_op jit(solution)/shard_map/ppermute | solution.py:24
  38.0 0.0 collective-permute-done.5.refs_5_
  38.0 0.0 collective-permute-done.6.refs_6_
  38.0 0.6 copy-done.14
  38.7 0.1 copy-done.15
  38.7 0.1 copy-done.10
  38.8 0.7 copy-done.11
  39.5 18.2 %forward.1 = (bf16[3,768,384]{2,1,0:T(8,128)(2,1)}, bf16[1344,384]{1,0:T(8,128)(2,1)}, bf16[1344,384]{1,0:T(8,128)(2,1)}, bf16[3,192,384]{2,1,0:T(8,128)(2,1)}, ...) custom-call(s32[4]{0:T(128)} %pad_add_fusion.position, ...), custom_call_target="tpu_custom_call" | custom-call | tf_op jit(solution)/shard_map/forward/pallas_call | solution.py:157
  57.8 0.6 collective-permute-start.12
  58.4 0.1 collective-permute-start.11
  58.5 0.0 collective-permute-start.13
  58.5 2.6 %collective-permute-start.14 = (bf16[3,192,384]{2,1,0:T(8,128)(2,1)}, bf16[3,192,384]{2,1,0:T(8,128)(2,1)}, u32[]{:S(2)}, u32[]{:S(2)}) collective-permute-start(bf16[3,192,384]{2,1,0:T(8,128)(2,1)} %get-tuple-element.37), channel_id=1, source_target_pairs={{0,192},{64,0},{128,64},{192,128},{1,193},{65,1},{129,65},{193,129... | collective-permute-start | bytes 1327112 | tf_op jit(solution)/shard_map/ppermute | solution.py:24
  61.1 0.3 collective-permute-start.15
  61.5 0.6 broadcast_in_dim.77.gain
  62.1 1.1 rsqrt.7.scale
  63.2 0.2 collective-permute-done.11.back_b
  63.4 1.0 copy-done.7
  64.3 0.6 copy-done.5
  64.9 10.8 %backward.1 = bf16[1280,768]{1,0:T(8,128)(2,1)} custom-call(bf16[1344,384]{1,0:T(8,128)(2,1)} %get-tuple-element.32.back_a, bf16[1344,384]{1,0:T(8,128)(2,1)} %copy-done.7, bf16[3,768,384]{2,1,0:T(8,128)(2,1)} %get-tuple-element.34.weight_a, bf16[3,768,384]{2,1,0:T(8,128)(2,1)} %copy-done.5, f32[1280,768]{1,0:T(8,128)} %copy-done, f32[1280,1]{1,0:T(8,128)} %rsqrt.7.scale, ...), custom_call_target="tpu_custom_call" | custom-call | tf_op jit(solution)/shard_map/backward/pallas_call | solution.py:207
  75.8 5.1 %collective-permute-done.15 = bf16[3,192,384]{2,1,0:T(8,128)(2,1)} collective-permute-done((bf16[3,192,384]{2,1,0:T(8,128)(2,1)}, bf16[3,192,384]{2,1,0:T(8,128)(2,1)}, u32[]{:S(2)}, u32[]{:S(2)}) %collective-permute-start.15) | collective-permute-done | bytes 442400 | tf_op jit(solution)/shard_map/ppermute | solution.py:24
  80.9 1.5 %add_convert_fusion.6 = (bf16[3,48,384]{2,1,0:T(8,128)(2,1)S(1)}, bf16[3,48,384]{2,1,0:T(8,128)(2,1)S(1)}, bf16[3,48,384]{2,1,0:T(8,128)(2,1)S(1)}) fusion(bf16[3,192,384]{2,1,0:T(8,128)(2,1)} %collective-permute-done.15, s32[]{:T(128)S(6)} %select_n.105, bf16[3,192,384]{2,1,0:T(8,128)(2,1)} %collective-permute-done.14, ...), kind=kLoop, calls=%fused_computation.14 | loop fusion | flops 1327104 | bytes 1658892 | tf_op jit(solution)/shard_map/convert_element_type | solution.py:301
  82.3 5.5 %collective-permute-start.16 = (bf16[3,48,384]{2,1,0:T(8,128)(2,1)S(1)}, bf16[3,48,384]{2,1,0:T(8,128)(2,1)S(1)}, u32[]{:S(2)}, u32[]{:S(2)}) collective-permute-start(bf16[3,48,384]{2,1,0:T(8,128)(2,1)S(1)} %get-tuple-element.62), channel_id=1, source_target_pairs={{0,8},{8,32},{32,40},{40,0},{1,9},{9,33},{33,41},{41,1},{2,10},{10... | collective-permute-start | bytes 331784 | tf_op jit(solution)/shard_map/ppermute | solution.py:24
  87.8 1.9 %collective-permute-start.18 = (bf16[3,48,384]{2,1,0:T(8,128)(2,1)S(1)}, bf16[3,48,384]{2,1,0:T(8,128)(2,1)S(1)}, u32[]{:S(2)}, u32[]{:S(2)}) collective-permute-start(bf16[3,48,384]{2,1,0:T(8,128)(2,1)S(1)} %get-tuple-element.63), channel_id=1, source_target_pairs={{0,32},{8,40},{32,0},{40,8},{1,33},{9,41},{33,1},{41,9},{2,34},{10... | collective-permute-start | bytes 331784 | tf_op jit(solution)/shard_map/ppermute | solution.py:24
  89.7 1.7 %collective-permute-done.17 = bf16[3,48,384]{2,1,0:T(8,128)(2,1)S(1)} collective-permute-done((bf16[3,48,384]{2,1,0:T(8,128)(2,1)S(1)}, bf16[3,48,384]{2,1,0:T(8,128)(2,1)S(1)}, u32[]{:S(2)}, u32[]{:S(2)}) %collective-permute-start.17) | collective-permute-done | bytes 110624 | tf_op jit(solution)/shard_map/ppermute | solution.py:24
  91.4 1.8 %collective-permute-done.18 = bf16[3,48,384]{2,1,0:T(8,128)(2,1)S(1)} collective-permute-done((bf16[3,48,384]{2,1,0:T(8,128)(2,1)S(1)}, bf16[3,48,384]{2,1,0:T(8,128)(2,1)S(1)}, u32[]{:S(2)}, u32[]{:S(2)}) %collective-permute-start.18) | collective-permute-done | bytes 110624 | tf_op jit(solution)/shard_map/ppermute | solution.py:24
  93.2 1.1 add_convert_fusion.3
  94.3 0.1 collective-permute-start.19
  94.4 3.6 %collective-permute-done.19 = bf16[3,48,384]{2,1,0:T(8,128)(2,1)S(1)} collective-permute-done((bf16[3,48,384]{2,1,0:T(8,128)(2,1)S(1)}, bf16[3,48,384]{2,1,0:T(8,128)(2,1)S(1)}, u32[]{:S(2)}, u32[]{:S(2)}) %collective-permute-start.19) | collective-permute-done | bytes 110624 | tf_op jit(solution)/shard_map/ppermute | solution.py:28
  98.0 1.5 %collective-permute-start.20 = (bf16[3,48,384]{2,1,0:T(8,128)(2,1)S(1)}, bf16[3,48,384]{2,1,0:T(8,128)(2,1)S(1)}, u32[]{:S(2)}, u32[]{:S(2)}) collective-permute-start(bf16[3,48,384]{2,1,0:T(8,128)(2,1)S(1)} %add_convert_fusion.2), channel_id=1, source_target_pairs={{0,2},{1,3},{2,0},{3,1},{4,6},{5,7},{6,4},{7,5},{8,10},{9,11},{10,... | collective-permute-start | bytes 331784 | tf_op jit(solution)/shard_map/ppermute | solution.py:28
  99.5 4.3 %collective-permute-done.20 = bf16[3,48,384]{2,1,0:T(8,128)(2,1)S(1)} collective-permute-done((bf16[3,48,384]{2,1,0:T(8,128)(2,1)S(1)}, bf16[3,48,384]{2,1,0:T(8,128)(2,1)S(1)}, u32[]{:S(2)}, u32[]{:S(2)}) %collective-permute-start.20) | collective-permute-done | bytes 110624 | tf_op jit(solution)/shard_map/ppermute | solution.py:28
  103.8 2.9 %collective-permute-start.21 = (bf16[3,48,384]{2,1,0:T(8,128)(2,1)S(1)}, bf16[3,48,384]{2,1,0:T(8,128)(2,1)S(1)}, u32[]{:S(2)}, u32[]{:S(2)}) collective-permute-start(bf16[3,48,384]{2,1,0:T(8,128)(2,1)S(1)} %add_convert_fusion.1), channel_id=1, source_target_pairs={{0,4},{1,5},{2,6},{3,7},{4,0},{5,1},{6,2},{7,3},{8,12},{9,13},{10,... | collective-permute-start | bytes 331784 | tf_op jit(solution)/shard_map/ppermute | solution.py:28
  106.7 5.9 %collective-permute-done.21 = bf16[3,48,384]{2,1,0:T(8,128)(2,1)S(1)} collective-permute-done((bf16[3,48,384]{2,1,0:T(8,128)(2,1)S(1)}, bf16[3,48,384]{2,1,0:T(8,128)(2,1)S(1)}, u32[]{:S(2)}, u32[]{:S(2)}) %collective-permute-start.21) | collective-permute-done | bytes 110624 | tf_op jit(solution)/shard_map/ppermute | solution.py:28
  112.6 0.1 collective-permute-start.22
  112.7 3.9 %collective-permute-done.22 = bf16[3,48,384]{2,1,0:T(8,128)(2,1)S(1)} collective-permute-done((bf16[3,48,384]{2,1,0:T(8,128)(2,1)S(1)}, bf16[3,48,384]{2,1,0:T(8,128)(2,1)S(1)}, u32[]{:S(2)}, u32[]{:S(2)}) %collective-permute-start.22) | collective-permute-done | bytes 110624 | tf_op jit(solution)/shard_map/ppermute | solution.py:28
  116.7 6.8 %collective-permute-start.23 = (bf16[3,48,384]{2,1,0:T(8,128)(2,1)S(1)}, bf16[3,48,384]{2,1,0:T(8,128)(2,1)S(1)}, u32[]{:S(2)}, u32[]{:S(2)}) collective-permute-start(bf16[3,48,384]{2,1,0:T(8,128)(2,1)S(1)} %get-tuple-element.51), channel_id=1, source_target_pairs={{0,16},{16,0},{1,17},{17,1},{2,18},{18,2},{3,19},{19,3},{4,20},{20... | collective-permute-start | bytes 331784 | tf_op jit(solution)/shard_map/ppermute | solution.py:28
  123.5 1.0 collective-permute-done.23
  124.5 0.8 convert_multiply_fusion
  (48 shorter events, 0.4 us)
Async XLA Ops:
  0.6 13.6 %copy-start.16 = (f32[768]{0:T(1024)S(1)}, f32[768]{0:T(1024)}, u32[]{:S(2)}) copy-start(f32[768]{0:T(1024)} %param.9) | copy-start | bytes 9220
  1.6 4.3 %collective-permute-start = (bf16[3,48,384]{2,1,0:T(8,128)(2,1)S(1)}, bf16[3,48,384]{2,1,0:T(8,128)(2,1)S(1)}, u32[]{:S(2)}, u32[]{:S(2)}) collective-permute-start(bf16[3,48,384]{2,1,0:T(8,128)(2,1)S(1)} %get-tuple-element.70), channel_id=1, source_target_pairs={{0,16},{16,0},{1,17},{17,1},{2,18},{18,2},{3,19},{19,3},{4,20},{20... | collective-permute-start | bytes 331784 | tf_op jit(solution)/shard_map/ppermute | solution.py:28
  6.0 12.7 %copy-start.4 = (bf16[2,3,48,384]{3,2,1,0:T(8,128)(2,1)}, bf16[2,3,48,384]{3,2,1,0:T(8,128)(2,1)S(1)}, u32[]{:S(2)}) copy-start(bf16[2,3,48,384]{3,2,1,0:T(8,128)(2,1)S(1)} %pad_maximum_fusion.1.refs_0_) | copy-start | bytes 663556
  6.0 8.7 %collective-permute-start.1 = (bf16[2,3,48,384]{3,2,1,0:T(8,128)(2,1)S(1)}, bf16[2,3,48,384]{3,2,1,0:T(8,128)(2,1)S(1)}, u32[]{:S(2)}, u32[]{:S(2)}) collective-permute-start(bf16[2,3,48,384]{3,2,1,0:T(8,128)(2,1)S(1)} %pad_maximum_fusion.1.refs_0_), channel_id=1, source_target_pairs={{0,40},{8,32},{32,8},{40,0},{1,41},{9,33},{33,9},{41,1},{2,42},{10... | collective-permute-start | bytes 663560 | tf_op jit(solution)/shard_map/ppermute | solution.py:28
  7.0 7.6 %collective-permute-start.2 = (bf16[2,3,48,384]{3,2,1,0:T(8,128)(2,1)S(1)}, bf16[2,3,48,384]{3,2,1,0:T(8,128)(2,1)S(1)}, u32[]{:S(2)}, u32[]{:S(2)}) collective-permute-start(bf16[2,3,48,384]{3,2,1,0:T(8,128)(2,1)S(1)} %pad_maximum_fusion.1.refs_0_), channel_id=1, source_target_pairs={{0,64},{64,128},{128,192},{192,0},{1,65},{65,129},{129,193},{193,1... | collective-permute-start | bytes 663560 | tf_op jit(solution)/shard_map/ppermute | solution.py:24
  8.3 6.4 %collective-permute-start.3 = (bf16[2,3,48,384]{3,2,1,0:T(8,128)(2,1)S(1)}, bf16[2,3,48,384]{3,2,1,0:T(8,128)(2,1)S(1)}, u32[]{:S(2)}, u32[]{:S(2)}) collective-permute-start(bf16[2,3,48,384]{3,2,1,0:T(8,128)(2,1)S(1)} %pad_maximum_fusion.1.refs_0_), channel_id=1, source_target_pairs={{0,192},{64,0},{128,64},{192,128},{1,193},{65,1},{129,65},{193,129... | collective-permute-start | bytes 663560 | tf_op jit(solution)/shard_map/ppermute | solution.py:24
  14.2 3.1 %copy-start = (f32[1280,768]{1,0:T(8,128)}, f32[1280,768]{1,0:T(8,128)S(1)}, u32[]{:S(2)}) copy-start(f32[1280,768]{1,0:T(8,128)S(1)} %get-tuple-element.55.inputs) | copy-start | bytes 11796484
  14.2 3.0 %copy-start.1 = (bf16[1,1280,768]{2,1,0:T(8,128)(2,1)S(1)}, bf16[1,1280,768]{2,1,0:T(8,128)(2,1)}, u32[]{:S(2)}) copy-start(bf16[1,1280,768]{2,1,0:T(8,128)(2,1)} %param.11) | copy-start | bytes 5898244
  14.6 6.4 %copy-start.2 = (bf16[1280,768]{1,0:T(8,128)(2,1)}, bf16[1280,768]{1,0:T(8,128)(2,1)S(1)}, u32[]{:S(2)}) copy-start(bf16[1280,768]{1,0:T(8,128)(2,1)S(1)} %multiply_convert_fusion.refs_7_) | copy-start | bytes 5898244
  14.7 23.3 %copy-start.8 = (bf16[2,3,48,384]{3,2,1,0:T(8,128)(2,1)}, bf16[2,3,48,384]{3,2,1,0:T(8,128)(2,1)S(1)}, u32[]{:S(2)}) copy-start(bf16[2,3,48,384]{3,2,1,0:T(8,128)(2,1)S(1)} %collective-permute-done.1.refs_1_) | copy-start | bytes 663556
  14.7 1.5 %copy-start.12 = (bf16[2,3,48,384]{3,2,1,0:T(8,128)(2,1)}, bf16[2,3,48,384]{3,2,1,0:T(8,128)(2,1)S(1)}, u32[]{:S(2)}) copy-start(bf16[2,3,48,384]{3,2,1,0:T(8,128)(2,1)S(1)} %collective-permute-done.2.refs_2_) | copy-start | bytes 663556
  14.7 1.5 %copy-start.13 = (bf16[2,3,48,384]{3,2,1,0:T(8,128)(2,1)}, bf16[2,3,48,384]{3,2,1,0:T(8,128)(2,1)S(1)}, u32[]{:S(2)}) copy-start(bf16[2,3,48,384]{3,2,1,0:T(8,128)(2,1)S(1)} %collective-permute-done.3.refs_4_) | copy-start | bytes 663556
  14.7 6.5 %collective-permute-start.7 = (bf16[1280,768]{1,0:T(8,128)(2,1)S(1)}, bf16[1280,768]{1,0:T(8,128)(2,1)S(1)}, u32[]{:S(2)}, u32[]{:S(2)}) collective-permute-start(bf16[1280,768]{1,0:T(8,128)(2,1)S(1)} %multiply_convert_fusion.refs_7_), channel_id=1, source_target_pairs={{0,16},{16,0},{1,17},{17,1},{2,18},{18,2},{3,19},{19,3},{4,20},{20... | collective-permute-start | bytes 5898248 | tf_op jit(solution)/shard_map/ppermute | solution.py:28
  17.3 3.9 %collective-permute-start.8 = (bf16[1280,384]{1,0:T(8,128)(2,1)S(1)}, bf16[1280,384]{1,0:T(8,128)(2,1)S(1)}, u32[]{:S(2)}, u32[]{:S(2)}) collective-permute-start(bf16[1280,384]{1,0:T(8,128)(2,1)S(1)} %constant_dynamic-slice_fusion.1), channel_id=1, source_target_pairs={{0,16},{16,0},{1,17},{17,1},{2,18},{18,2},{3,19},{19,3},{4,20},{20... | collective-permute-start | bytes 2949128 | tf_op jit(solution)/shard_map/ppermute | solution.py:28
  19.4 18.6 %collective-permute-start.6 = (bf16[2,2,3,48,384]{4,3,2,1,0:T(8,128)(2,1)}, bf16[2,2,3,48,384]{4,3,2,1,0:T(8,128)(2,1)}, u32[]{:S(2)}, u32[]{:S(2)}) collective-permute-start(bf16[2,2,3,48,384]{4,3,2,1,0:T(8,128)(2,1)} %pad_maximum_fusion), channel_id=1, source_target_pairs={{0,128},{64,192},{128,0},{192,64},{1,129},{65,193},{129,1},{193,65... | collective-permute-start | bytes 1327112 | tf_op jit(solution)/shard_map/ppermute | solution.py:24
  21.2 16.8 %copy-start.6 = (bf16[1280,384]{1,0:T(8,128)(2,1)}, bf16[1280,384]{1,0:T(8,128)(2,1)S(1)}, u32[]{:S(2)}) copy-start(bf16[1280,384]{1,0:T(8,128)(2,1)S(1)} %collective-permute-done.8.refs_12_) | copy-start | bytes 2949124
  21.2 1.3 %copy-start.3 = (bf16[1280,768]{1,0:T(8,128)(2,1)}, bf16[1280,768]{1,0:T(8,128)(2,1)S(1)}, u32[]{:S(2)}) copy-start(bf16[1280,768]{1,0:T(8,128)(2,1)S(1)} %collective-permute-done.7.refs_8_) | copy-start | bytes 5898244
  22.6 15.4 %collective-permute-start.10 = (bf16[160,768]{1,0:T(8,128)(2,1)S(1)}, bf16[160,768]{1,0:T(8,128)(2,1)S(1)}, u32[]{:S(2)}, u32[]{:S(2)}) collective-permute-start(bf16[160,768]{1,0:T(8,128)(2,1)S(1)} %maximum_maximum_fusion.1), channel_id=1, source_target_pairs={{1,0},{2,1},{3,2},{4,3},{5,4},{6,5},{7,6},{8,7},{9,8},{10,9},{11,1... | collective-permute-start | bytes 737288 | tf_op jit(solution)/shard_map/ppermute | solution.py:274
  23.9 14.1 %collective-permute-start.9 = (bf16[160,768]{1,0:T(8,128)(2,1)S(1)}, bf16[160,768]{1,0:T(8,128)(2,1)S(1)}, u32[]{:S(2)}, u32[]{:S(2)}) collective-permute-start(bf16[160,768]{1,0:T(8,128)(2,1)S(1)} %maximum_maximum_fusion), channel_id=1, source_target_pairs={{0,1},{1,2},{2,3},{3,4},{4,5},{5,6},{6,7},{7,8},{8,9},{9,10},{10,1... | collective-permute-start | bytes 737288 | tf_op jit(solution)/shard_map/ppermute | solution.py:269
  28.1 9.9 %collective-permute-start.4 = (bf16[2,3,48,384]{3,2,1,0:T(8,128)(2,1)S(1)}, bf16[2,3,48,384]{3,2,1,0:T(8,128)(2,1)S(1)}, u32[]{:S(2)}, u32[]{:S(2)}) collective-permute-start(bf16[2,3,48,384]{3,2,1,0:T(8,128)(2,1)S(1)} %collective-permute-done.1.refs_1_), channel_id=1, source_target_pairs={{0,64},{64,128},{128,192},{192,0},{1,65},{65,129},{129,193},{193,1... | collective-permute-start | bytes 663560 | tf_op jit(solution)/shard_map/ppermute | solution.py:24
  29.3 8.7 %collective-permute-start.5 = (bf16[2,3,48,384]{3,2,1,0:T(8,128)(2,1)S(1)}, bf16[2,3,48,384]{3,2,1,0:T(8,128)(2,1)S(1)}, u32[]{:S(2)}, u32[]{:S(2)}) collective-permute-start(bf16[2,3,48,384]{3,2,1,0:T(8,128)(2,1)S(1)} %collective-permute-done.1.refs_1_), channel_id=1, source_target_pairs={{0,192},{64,0},{128,64},{192,128},{1,193},{65,1},{129,65},{193,129... | collective-permute-start | bytes 663560 | tf_op jit(solution)/shard_map/ppermute | solution.py:24
  38.0 0.7 copy-start.14
  38.0 0.7 copy-start.15
  38.0 0.8 copy-start.10
  38.8 0.7 copy-start.11
  57.8 5.6 %collective-permute-start.12 = (bf16[3,768,384]{2,1,0:T(8,128)(2,1)}, bf16[3,768,384]{2,1,0:T(8,128)(2,1)S(1)}, u32[]{:S(2)}, u32[]{:S(2)}) collective-permute-start(bf16[3,768,384]{2,1,0:T(8,128)(2,1)} %get-tuple-element.34.weight_a), channel_id=1, source_target_pairs={{0,16},{16,0},{1,17},{17,1},{2,18},{18,2},{3,19},{19,3},{4,20},{20... | collective-permute-start | bytes 5308424 | tf_op jit(solution)/shard_map/ppermute | solution.py:28
  58.4 5.0 %collective-permute-start.11 = (bf16[1344,384]{1,0:T(8,128)(2,1)}, bf16[1344,384]{1,0:T(8,128)(2,1)S(1)}, u32[]{:S(2)}, u32[]{:S(2)}) collective-permute-start(bf16[1344,384]{1,0:T(8,128)(2,1)} %get-tuple-element.33), channel_id=1, source_target_pairs={{0,16},{16,0},{1,17},{17,1},{2,18},{18,2},{3,19},{19,3},{4,20},{20... | collective-permute-start | bytes 3096584 | tf_op jit(solution)/shard_map/ppermute | solution.py:28
  58.5 17.3 %collective-permute-start.13 = (bf16[3,192,384]{2,1,0:T(8,128)(2,1)}, bf16[3,192,384]{2,1,0:T(8,128)(2,1)}, u32[]{:S(2)}, u32[]{:S(2)}) collective-permute-start(bf16[3,192,384]{2,1,0:T(8,128)(2,1)} %get-tuple-element.36), channel_id=1, source_target_pairs={{0,64},{64,128},{128,192},{192,0},{1,65},{65,129},{129,193},{193,1... | collective-permute-start | bytes 1327112 | tf_op jit(solution)/shard_map/ppermute | solution.py:24
  58.5 17.2 %collective-permute-start.14 = (bf16[3,192,384]{2,1,0:T(8,128)(2,1)}, bf16[3,192,384]{2,1,0:T(8,128)(2,1)}, u32[]{:S(2)}, u32[]{:S(2)}) collective-permute-start(bf16[3,192,384]{2,1,0:T(8,128)(2,1)} %get-tuple-element.37), channel_id=1, source_target_pairs={{0,192},{64,0},{128,64},{192,128},{1,193},{65,1},{129,65},{193,129... | collective-permute-start | bytes 1327112 | tf_op jit(solution)/shard_map/ppermute | solution.py:24
  61.1 19.7 %collective-permute-start.15 = (bf16[3,192,384]{2,1,0:T(8,128)(2,1)}, bf16[3,192,384]{2,1,0:T(8,128)(2,1)}, u32[]{:S(2)}, u32[]{:S(2)}) collective-permute-start(bf16[3,192,384]{2,1,0:T(8,128)(2,1)} %get-tuple-element.38), channel_id=1, source_target_pairs={{0,128},{64,192},{128,0},{192,64},{1,129},{65,193},{129,1},{193,65... | collective-permute-start | bytes 1327112 | tf_op jit(solution)/shard_map/ppermute | solution.py:24
  63.4 1.0 copy-start.7
  63.4 1.5 %copy-start.5 = (bf16[3,768,384]{2,1,0:T(8,128)(2,1)}, bf16[3,768,384]{2,1,0:T(8,128)(2,1)S(1)}, u32[]{:S(2)}) copy-start(bf16[3,768,384]{2,1,0:T(8,128)(2,1)S(1)} %collective-permute-done.12.weight_b) | copy-start | bytes 5308420
  64.9 15.9 %copy-start.9 = (bf16[3,192,384]{2,1,0:T(8,128)(2,1)S(1)}, bf16[3,192,384]{2,1,0:T(8,128)(2,1)}, u32[]{:S(2)}) copy-start(bf16[3,192,384]{2,1,0:T(8,128)(2,1)} %get-tuple-element.40) | copy-start | bytes 1327108
  82.3 7.3 %collective-permute-start.16 = (bf16[3,48,384]{2,1,0:T(8,128)(2,1)S(1)}, bf16[3,48,384]{2,1,0:T(8,128)(2,1)S(1)}, u32[]{:S(2)}, u32[]{:S(2)}) collective-permute-start(bf16[3,48,384]{2,1,0:T(8,128)(2,1)S(1)} %get-tuple-element.62), channel_id=1, source_target_pairs={{0,8},{8,32},{32,40},{40,0},{1,9},{9,33},{33,41},{41,1},{2,10},{10... | collective-permute-start | bytes 331784 | tf_op jit(solution)/shard_map/ppermute | solution.py:24
  87.8 3.6 %collective-permute-start.17 = (bf16[3,48,384]{2,1,0:T(8,128)(2,1)S(1)}, bf16[3,48,384]{2,1,0:T(8,128)(2,1)S(1)}, u32[]{:S(2)}, u32[]{:S(2)}) collective-permute-start(bf16[3,48,384]{2,1,0:T(8,128)(2,1)S(1)} %get-tuple-element.64), channel_id=1, source_target_pairs={{0,40},{8,0},{32,8},{40,32},{1,41},{9,1},{33,9},{41,33},{2,42},{10... | collective-permute-start | bytes 331784 | tf_op jit(solution)/shard_map/ppermute | solution.py:24
  87.8 5.4 %collective-permute-start.18 = (bf16[3,48,384]{2,1,0:T(8,128)(2,1)S(1)}, bf16[3,48,384]{2,1,0:T(8,128)(2,1)S(1)}, u32[]{:S(2)}, u32[]{:S(2)}) collective-permute-start(bf16[3,48,384]{2,1,0:T(8,128)(2,1)S(1)} %get-tuple-element.63), channel_id=1, source_target_pairs={{0,32},{8,40},{32,0},{40,8},{1,33},{9,41},{33,1},{41,9},{2,34},{10... | collective-permute-start | bytes 331784 | tf_op jit(solution)/shard_map/ppermute | solution.py:24
  94.3 3.7 %collective-permute-start.19 = (bf16[3,48,384]{2,1,0:T(8,128)(2,1)S(1)}, bf16[3,48,384]{2,1,0:T(8,128)(2,1)S(1)}, u32[]{:S(2)}, u32[]{:S(2)}) collective-permute-start(bf16[3,48,384]{2,1,0:T(8,128)(2,1)S(1)} %add_convert_fusion.3), channel_id=1, source_target_pairs={{0,1},{1,0},{2,3},{3,2},{4,5},{5,4},{6,7},{7,6},{8,9},{9,8},{10,11... | collective-permute-start | bytes 331784 | tf_op jit(solution)/shard_map/ppermute | solution.py:28
  98.0 5.8 %collective-permute-start.20 = (bf16[3,48,384]{2,1,0:T(8,128)(2,1)S(1)}, bf16[3,48,384]{2,1,0:T(8,128)(2,1)S(1)}, u32[]{:S(2)}, u32[]{:S(2)}) collective-permute-start(bf16[3,48,384]{2,1,0:T(8,128)(2,1)S(1)} %add_convert_fusion.2), channel_id=1, source_target_pairs={{0,2},{1,3},{2,0},{3,1},{4,6},{5,7},{6,4},{7,5},{8,10},{9,11},{10,... | collective-permute-start | bytes 331784 | tf_op jit(solution)/shard_map/ppermute | solution.py:28
  103.8 8.8 %collective-permute-start.21 = (bf16[3,48,384]{2,1,0:T(8,128)(2,1)S(1)}, bf16[3,48,384]{2,1,0:T(8,128)(2,1)S(1)}, u32[]{:S(2)}, u32[]{:S(2)}) collective-permute-start(bf16[3,48,384]{2,1,0:T(8,128)(2,1)S(1)} %add_convert_fusion.1), channel_id=1, source_target_pairs={{0,4},{1,5},{2,6},{3,7},{4,0},{5,1},{6,2},{7,3},{8,12},{9,13},{10,... | collective-permute-start | bytes 331784 | tf_op jit(solution)/shard_map/ppermute | solution.py:28
  112.6 4.0 %collective-permute-start.22 = (bf16[3,48,384]{2,1,0:T(8,128)(2,1)S(1)}, bf16[3,48,384]{2,1,0:T(8,128)(2,1)S(1)}, u32[]{:S(2)}, u32[]{:S(2)}) collective-permute-start(bf16[3,48,384]{2,1,0:T(8,128)(2,1)S(1)} %add_convert_fusion), channel_id=1, source_target_pairs={{0,8},{8,0},{1,9},{9,1},{2,10},{10,2},{3,11},{11,3},{4,12},{12,4},... | collective-permute-start | bytes 331784 | tf_op jit(solution)/shard_map/ppermute | solution.py:28
  116.7 7.8 %collective-permute-start.23 = (bf16[3,48,384]{2,1,0:T(8,128)(2,1)S(1)}, bf16[3,48,384]{2,1,0:T(8,128)(2,1)S(1)}, u32[]{:S(2)}, u32[]{:S(2)}) collective-permute-start(bf16[3,48,384]{2,1,0:T(8,128)(2,1)S(1)} %get-tuple-element.51), channel_id=1, source_target_pairs={{0,16},{16,0},{1,17},{17,1},{2,18},{18,2},{3,19},{19,3},{4,20},{20... | collective-permute-start | bytes 331784 | tf_op jit(solution)/shard_map/ppermute | solution.py:28

commit v4 on v3

--- a/solution.py
+++ b/solution.py
@@ -44,11 +44,9 @@
 def load_weight(position, pieces, weight, sem):
     x, yh, core = position[0], position[1], position[2]
     rows = pieces[0].shape[2]
-    own, across, up_own, up_across, down_own, down_across, far = pieces
-    blocks = [(own, 0, 0), (across, 0, 1), (up_own, 3, 0), (up_across, 3, 1)]
-    blocks += [(down_own, 1, 0), (down_across, 1, 1), (far.at[0], 2, 0), (far.at[1], 2, 1)]
+    steps = [(0, 0), (0, 1), (3, 0), (3, 1), (1, 0), (1, 1), (2, 0), (2, 1)]
     copies = []
-    for block, step_x, step_y in blocks:
+    for block, (step_x, step_y) in zip(pieces, steps):
         for side in range(2):
             owner = ((x + step_x) % 4) * 4 + ((yh + step_y) % 2) * 2 + (core + side) % 2
             place = pl.multiple_of(owner * rows, 16)
@@ -61,12 +59,12 @@
 
 
 def forward_kernel(position, *refs):
-    pieces, refs = refs[:7], refs[7:]
+    pieces, refs = refs[:8], refs[8:]
     normed_hbm, edges, upstream_hbm = refs[0:2], refs[2:4], refs[4:6]
-    weight_out, back_out, along_x = refs[6], refs[7:9], refs[9:13]
-    weight, normed, upstream, back, grad = refs[13:18]
-    piece_sem, load_sem, back_sem, weight_sem, grad_sem = refs[18:]
-    x, core = position[0], position[2]
+    weight_out, back_out, grad_out = refs[6], refs[7:9], refs[9]
+    weight, normed, upstream, back, grad = refs[10:15]
+    piece_sem, load_sem, back_sem, weight_sem, grad_sem = refs[15:]
+    core = position[2]
     channels, half = weight.shape[1:]
     count = normed_hbm[0].shape[0]
     lane = pl.multiple_of(core * half, 128)
@@ -136,11 +134,12 @@
         total = part if total is None else total + part
     for tap in range(FILTER_TAPS):
         grad[tap] = total[:, tap * half : (tap + 1) * half].astype(BF16)
-    quarter = channels // 4
-    for step in range(4):
-        place = pl.multiple_of(((x + step) % 4) * quarter, 16)
+    owners, _, rows, _ = grad_out.shape
+    for owner in range(owners):
         grad_save = pltpu.make_async_copy(
-            grad.at[:, pl.ds(place, quarter), :], along_x[step], grad_sem.at[step]
+            grad.at[:, owner * rows : (owner + 1) * rows, :],
+            grad_out.at[owner],
+            grad_sem.at[owner],
         )
         grad_save.start()
         saves.append(grad_save)
@@ -158,9 +157,9 @@
         forward_kernel,
         out_shape=[jax.ShapeDtypeStruct((FILTER_TAPS, channels, half), BF16)]
         + [jax.ShapeDtypeStruct((length, half), BF16)] * 2
-        + [jax.ShapeDtypeStruct((FILTER_TAPS, channels // 4, half), BF16)] * 4,
-        in_specs=[pl.BlockSpec(memory_space=pltpu.SMEM)] + [anywhere] * 13,
-        out_specs=[anywhere] * 7,
+        + [jax.ShapeDtypeStruct((16, FILTER_TAPS, channels // 16, half), BF16)],
+        in_specs=[pl.BlockSpec(memory_space=pltpu.SMEM)] + [anywhere] * 14,
+        out_specs=[anywhere] * 4,
         scratch_shapes=[
             pltpu.VMEM((FILTER_TAPS, channels, half), BF16),
             pltpu.VMEM((2, length + 2 * REACH, channels), BF16),
@@ -171,7 +170,7 @@
             dma((2, 6)),
             dma((2,)),
             dma,
-            dma((4,)),
+            dma((16,)),
         ],
         compiler_params=pltpu.CompilerParams(vmem_limit_bytes=56 * 1024 * 1024),
         name="forward",
@@ -217,23 +216,22 @@
 
 
 def share_weight_grad(total, yl, core):
-    for mask in (1, 2, 4):
-        sent = total.astype(BF16)
-        total = sent.astype(F32) + swap(sent, "z", 8, mask).astype(F32)
-    mine = total.astype(BF16)
-    other = swap(mine, "yl", 2, 1)
-    by_core = [jnp.where(yl == rows, mine, other) for rows in range(2)]
-    kept = jnp.where(core == 0, by_core[0], by_core[1])
-    sent = jnp.where(core == 0, by_core[1], by_core[0])
-    arrived = swap(sent, "core", 2, 1)
-    low = jnp.where(core == 0, kept, arrived)
-    high = jnp.where(core == 0, arrived, kept)
+    sent = total.astype(BF16)
+    near, middle, far = (swap(sent, "z", 8, mask).astype(F32) for mask in (1, 2, 3))
+    sent = ((sent.astype(F32) + near) + (middle + far)).astype(BF16)
+    mine = (sent.astype(F32) + swap(sent, "z", 8, 7).astype(F32)).astype(BF16)
+    pair = ("core", "yl")
+    first = lax.ppermute(mine, pair, [(2, 0), (1, 3), (0, 1), (3, 2)])
+    second = lax.ppermute(mine, pair, [(2, 1), (1, 2)])
+    here = jnp.where(core == yl, mine, first)
+    there = jnp.where(core == yl, first, second)
+    low = jnp.where(core == 0, here, there)
+    high = jnp.where(core == 0, there, here)
     return jnp.concatenate([low, high], axis=2).astype(F32)
 
 
 def on_device(activations, nucleotides, base_table, norm_gain, filter_weight, upstream):
     x, yh, core, yl = (lax.axis_index(name) for name in ("x", "yh", "core", "yl"))
-    y = yh * 2 + yl
     position = jnp.stack([x, yh, core, yl]).astype(jnp.int32)
     tokens, incoming = activations[0], upstream[0]
     count, channels = tokens.shape
@@ -245,21 +243,26 @@
     own, tokens, nucleotides, incoming = join(own, tokens, nucleotides, incoming)
 
     across = swap(own, RING_Y, 4, 3)
-    up_own, down_own = shift(own, "x", 4, 1), shift(own, "x", 4, -1)
+    around_own = [shift(own, "x", 4, step) for step in (1, -1, 2)]
     bases = nucleotides[0][:, None]
     row = base_table[3][None]
     for base in (2, 1, 0):
         row = jnp.where(bases == base, base_table[base][None], row)
     inputs = tokens.astype(F32) + row
-    scale_inv = lax.rsqrt(jnp.mean(inputs * inputs, axis=-1, keepdims=True) + 1e-06)
+    square = jnp.mean(inputs * inputs, axis=-1)
+    across, inputs, square, incoming, *around_own = join(
+        across, inputs, square, incoming, *around_own
+    )
+
+    around_across = [shift(across, "x", 4, step) for step in (1, -1, 2)]
+    scale_inv = lax.rsqrt(square + 1e-06)[:, None]
     normed = (inputs * scale_inv * norm_gain).astype(BF16)
-    across, up_own, down_own, normed, incoming = join(across, up_own, down_own, normed, incoming)
-
-    far = shift(jnp.stack([own, across]), "x", 4, 2)
-    up_across, down_across = shift(across, "x", 4, 1), shift(across, "x", 4, -1)
     upstream_sent = lax.dynamic_slice_in_dim(incoming, (1 - core) * half, half, axis=1)
     normed_other = swap(normed, "core", 2, 1)
     upstream_other = swap(upstream_sent, "core", 2, 1)
+    around_across[0], around_across[1], normed, normed_other, upstream_other, incoming = join(
+        around_across[0], around_across[1], normed, normed_other, upstream_other, incoming
+    )
 
     def edge(rows, reach_rows):
         upstream_edge = lax.dynamic_slice_in_dim(incoming[reach_rows], core * half, half, axis=1)
@@ -274,9 +277,12 @@
     high = lax.ppermute(
         edge(slice(0, 2 * REACH), slice(0, REACH)), SEQ, [(i + 1, i) for i in range(15)]
     )
-    weight, back, back_other, *grads = forward(
+    pieces = [own, across]
+    for pair in zip(around_own, around_across):
+        pieces += pair
+    weight, back, back_other, grads = forward(
         position,
-        [own, across, up_own, up_across, down_own, down_across, far],
+        pieces,
         (normed, normed_other),
         (low, high),
         (incoming, upstream_other),
@@ -284,21 +290,12 @@
 
     back_rest = swap(back_other, "core", 2, 1)
     weight_rest = swap(weight, "core", 2, 1)
-    along_x = [grads[0]] + [shift(grads[step], "x", 4, step) for step in (1, 3, 2)]
+    arrived = lax.all_to_all(grads, ("x", "yh", "yl"), 0, 0, tiled=True)
     result = backward(
         (back, back_rest), (weight, weight_rest), inputs, scale_inv, norm_gain[None], incoming
     )
-    result, *along_x = join(result, *along_x)
-
-    rows = channels // 16
-    by_y = []
-    for step in range(4):
-        start = ((y + step) % 4) * rows
-        parts = [lax.dynamic_slice_in_dim(part, start, rows, axis=1) for part in along_x]
-        by_y.append(sum(part.astype(F32) for part in parts))
-    total = by_y[0]
-    for step in (1, 3, 2):
-        total = total + shift(by_y[step].astype(BF16), RING_Y, 4, step).astype(F32)
+    result, arrived = join(result, arrived)
+    total = jnp.sum(arrived.astype(F32), axis=0)
     weight_grad = share_weight_grad(total, yl, core)
     total_rows = 16 * 16 * count
     return (result[None], weight_grad / math.sqrt(total_rows))

time: 126 us -> 129 us (1.024)
  starting transfers between devices: 42.2 us -> 47.1 us
  other arithmetic: 9.95 us -> 6.75 us
  waiting for transfers between devices: 34 us -> 35.8 us
    ppermute x11 -> x10, waiting for transfers between devices: 19.1 us -> 6.98 us  [swap(): return lax.ppermute(value, axis, [(i, i ^ mask) for i in range(count)])]
    all_to_all x0 -> x1, waiting for transfers between devices: none -> 10.5 us  [on_device(): arrived = lax.all_to_all(grads, ('x', 'yh', 'yl'), 0, 0, tiled=True)]
    ppermute x0 -> x2, starting transfers between devices: none -> 8.99 us  [the longest x1 6.9 us: share_weight_grad(): first = lax.ppermute(mine, pair, [(2, 0), (1, 3), (0, 1), (3, 2)])]
    ppermute x11 -> x6, starting transfers between devices: 17.5 us -> 8.53 us  [shift(): return lax.ppermute(value, axis, pairs)]
    all_to_all x0 -> x1, starting transfers between devices: none -> 8.59 us  [on_device(): arrived = lax.all_to_all(grads, ('x', 'yh', 'yl'), 0, 0, tiled=True)]
    ppermute x0 -> x2, waiting for transfers between devices: none -> 3.95 us  [the longest x1 3.94 us: share_weight_grad(): second = lax.ppermute(mine, pair, [(2, 1), (1, 2)])]
    ppermute x11 -> x10, starting transfers between devices: 19.2 us -> 15.5 us  [swap(): return lax.ppermute(value, axis, [(i, i ^ mask) for i in range(count)])]
    convert_element_type x5 -> x2, other arithmetic: 2.67 us -> 0.09 us  [the longest x1 0.06 us: share_weight_grad(): sent = (sent.astype(F32) + near + (middle + far)).astype(BF16)]
  transfers between devices with their start and end apart: 24 -> 21, of which waited for: 12 -> 10; matrix products, arithmetic and copies ran while one was open for 7% -> 6% of each run, Pallas kernels for 9% -> 8%
where the time goes in v4:
time: 129 us; the launch traced here: 128 us
  starting transfers between devices  47.1 us (37%)
  waiting for transfers between devices  35.8 us (28%)
  Pallas kernels  29.1 us (23%)
  local copies, waits for them, and re-layouts  7.97 us (6%)
  other arithmetic  6.75 us (5%)
    pallas_call x1, Pallas kernels, forward(): pl.pallas_call(forward_kernel, out_shape=[jax.ShapeDtypeStruct((FILTER_TA...  18.4 us
    ppermute x10, starting transfers between devices, swap(): return lax.ppermute(value, axis, [(i, i ^ mask) for i in range(count)])  15.5 us
    ppermute x6, waiting for transfers between devices, shift(): return lax.ppermute(value, axis, pairs)  14.4 us
    pallas_call x1, Pallas kernels, backward(): pl.pallas_call(backward_kernel, grid=(count // block,), out_shape=jax.Sha...  10.8 us
    all_to_all x1, waiting for transfers between devices, on_device(): arrived = lax.all_to_all(grads, ('x', 'yh', 'yl'), 0, 0, tiled=True)  10.5 us
    all_to_all x1, starting transfers between devices, on_device(): arrived = lax.all_to_all(grads, ('x', 'yh', 'yl'), 0, 0, tiled=True)  8.59 us
    ppermute x6, starting transfers between devices, shift(): return lax.ppermute(value, axis, pairs)  8.53 us
    ppermute x10, waiting for transfers between devices, swap(): return lax.ppermute(value, axis, [(i, i ^ mask) for i in range(count)])  6.98 us
  transfers between devices with their start and end apart: 21, of which 10 were waited for; matrix products, arithmetic and copies ran while one was open for 6% of the time, Pallas kernels for 8%

profile of v4, /device:TPU:1, one launch (start us, length us, event | category | flops | bytes accessed | tf_op | source)
XLA Modules:
  0.0 127.8 jit_solution(17367436984147856459)
XLA Ops:
  0.6 1.0 dynamic-slice_bitcast_fusion
  1.6 3.3 %collective-permute-start = (bf16[3,48,384]{2,1,0:T(8,128)(2,1)S(1)}, bf16[3,48,384]{2,1,0:T(8,128)(2,1)S(1)}, u32[]{:S(2)}, u32[]{:S(2)}) collective-permute-start(bf16[3,48,384]{2,1,0:T(8,128)(2,1)S(1)} %get-tuple-element.68), channel_id=1, source_target_pairs={{0,16},{16,0},{1,17},{17,1},{2,18},{18,2},{3,19},{19,3},{4,20},{20... | collective-permute-start | bytes 331784 | tf_op jit(solution)/shard_map/ppermute | solution.py:28
  5.0 0.9 slice_reduce_fusion.3
  5.9 0.1 collective-permute-done
  6.0 1.1 collective-permute-start.1
  7.0 1.2 collective-permute-start.2
  8.3 1.5 %collective-permute-start.3 = (bf16[2,3,48,384]{3,2,1,0:T(8,128)(2,1)S(1)}, bf16[2,3,48,384]{3,2,1,0:T(8,128)(2,1)S(1)}, u32[]{:S(2)}, u32[]{:S(2)}) collective-permute-start(bf16[2,3,48,384]{3,2,1,0:T(8,128)(2,1)S(1)} %pad_maximum_fusion.refs_0_), channel_id=1, source_target_pairs={{0,192},{64,0},{128,64},{192,128},{1,193},{65,1},{129,65},{193,129... | collective-permute-start | bytes 663560 | tf_op jit(solution)/shard_map/ppermute | solution.py:24
  9.7 1.5 %collective-permute-start.4 = (bf16[2,3,48,384]{3,2,1,0:T(8,128)(2,1)S(1)}, bf16[2,3,48,384]{3,2,1,0:T(8,128)(2,1)S(1)}, u32[]{:S(2)}, u32[]{:S(2)}) collective-permute-start(bf16[2,3,48,384]{3,2,1,0:T(8,128)(2,1)S(1)} %pad_maximum_fusion.refs_0_), channel_id=1, source_target_pairs={{0,128},{64,192},{128,0},{192,64},{1,129},{65,193},{129,1},{193,65... | collective-permute-start | bytes 663560 | tf_op jit(solution)/shard_map/ppermute | solution.py:24
  11.3 0.7 compare_reduce_fusion.2
  12.0 3.7 %multiply_reduce_fusion = (f32[1280]{0:T(1024)S(1)}, f32[1280,768]{1,0:T(8,128)S(1)}) fusion(f32[768]{0:T(1024)S(1)} %get-tuple-element.50, f32[768]{0:T(1024)S(1)} %get-tuple-element.51, pred[1280]{0:T(1024)(128)(4,1)S(1)} %get-tuple-element.53, f32[768]{0:T(1024)S(1)} %get-tuple-element.49, pred[1280]{0:T(1024)(128)(4,1)S(1)} %get-tuple-element.54, ...), kind=kLoop, calls=%fused_computation.1 | loop fusion | flops 6880000 | bytes 5919488 | tf_op jit(solution)/shard_map/reduce_sum | solution.py:252
  15.7 0.0 copy-start.1
  15.8 0.0 collective-permute-done.1.refs_1_
  15.8 0.0 collective-permute-done.2.refs_2_
  15.8 0.0 collective-permute-done.3.refs_4_
  15.8 4.5 %collective-permute-done.4.refs_6_ = bf16[2,3,48,384]{3,2,1,0:T(8,128)(2,1)S(1)} collective-permute-done((bf16[2,3,48,384]{3,2,1,0:T(8,128)(2,1)S(1)}, bf16[2,3,48,384]{3,2,1,0:T(8,128)(2,1)S(1)}, u32[]{:S(2)}, u32[]{:S(2)}) %collective-permute-start.4) | collective-permute-done | bytes 221216 | tf_op jit(solution)/shard_map/ppermute | solution.py:24
  20.3 0.4 multiply_convert_fusion.refs_8_
  20.7 0.0 copy-start.2
  20.8 1.6 %collective-permute-start.7 = (bf16[1280,768]{1,0:T(8,128)(2,1)S(1)}, bf16[1280,768]{1,0:T(8,128)(2,1)S(1)}, u32[]{:S(2)}, u32[]{:S(2)}) collective-permute-start(bf16[1280,768]{1,0:T(8,128)(2,1)S(1)} %multiply_convert_fusion.refs_8_), channel_id=1, source_target_pairs={{0,16},{16,0},{1,17},{17,1},{2,18},{18,2},{3,19},{19,3},{4,20},{20... | collective-permute-start | bytes 5898248 | tf_op jit(solution)/shard_map/ppermute | solution.py:28
  22.4 0.1 constant_dynamic-slice_fusion.2
  22.5 0.1 collective-permute-start.8
  22.6 0.9 collective-permute-start.5
  23.5 1.8 %collective-permute-start.6 = (bf16[2,3,48,384]{3,2,1,0:T(8,128)(2,1)S(1)}, bf16[2,3,48,384]{3,2,1,0:T(8,128)(2,1)S(1)}, u32[]{:S(2)}, u32[]{:S(2)}) collective-permute-start(bf16[2,3,48,384]{3,2,1,0:T(8,128)(2,1)S(1)} %collective-permute-done.1.refs_1_), channel_id=1, source_target_pairs={{0,192},{64,0},{128,64},{192,128},{1,193},{65,1},{129,65},{193,129... | collective-permute-start | bytes 663560 | tf_op jit(solution)/shard_map/ppermute | solution.py:24
  25.4 5.1 %collective-permute-done.5.refs_3_ = bf16[2,3,48,384]{3,2,1,0:T(8,128)(2,1)S(1)} collective-permute-done((bf16[2,3,48,384]{3,2,1,0:T(8,128)(2,1)S(1)}, bf16[2,3,48,384]{3,2,1,0:T(8,128)(2,1)S(1)}, u32[]{:S(2)}, u32[]{:S(2)}) %collective-permute-start.5) | collective-permute-done | bytes 221216 | tf_op jit(solution)/shard_map/ppermute | solution.py:24
  30.5 0.0 collective-permute-done.6.refs_5_
  30.5 0.0 collective-permute-done.8.refs_13_
  30.5 0.0 collective-permute-done.7.refs_9_
  30.6 1.2 copy-done.3
  31.9 1.3 %collective-permute-start.11 = (bf16[160,768]{1,0:T(8,128)(2,1)S(1)}, bf16[160,768]{1,0:T(8,128)(2,1)S(1)}, u32[]{:S(2)}, u32[]{:S(2)}) collective-permute-start(bf16[160,768]{1,0:T(8,128)(2,1)S(1)} %maximum_maximum_fusion.1), channel_id=1, source_target_pairs={{1,0},{2,1},{3,2},{4,3},{5,4},{6,5},{7,6},{8,7},{9,8},{10,9},{11,1... | collective-permute-start | bytes 737288 | tf_op jit(solution)/shard_map/ppermute | solution.py:277
  33.2 4.2 %collective-permute-start.10 = (bf16[160,768]{1,0:T(8,128)(2,1)S(1)}, bf16[160,768]{1,0:T(8,128)(2,1)S(1)}, u32[]{:S(2)}, u32[]{:S(2)}) collective-permute-start(bf16[160,768]{1,0:T(8,128)(2,1)S(1)} %maximum_maximum_fusion), channel_id=1, source_target_pairs={{0,1},{1,2},{2,3},{3,4},{4,5},{5,6},{6,7},{7,8},{8,9},{9,10},{10,1... | collective-permute-start | bytes 737288 | tf_op jit(solution)/shard_map/ppermute | solution.py:272
  37.4 1.6 %collective-permute-start.9 = (bf16[2,3,48,384]{3,2,1,0:T(8,128)(2,1)S(1)}, bf16[2,3,48,384]{3,2,1,0:T(8,128)(2,1)S(1)}, u32[]{:S(2)}, u32[]{:S(2)}) collective-permute-start(bf16[2,3,48,384]{3,2,1,0:T(8,128)(2,1)S(1)} %collective-permute-done.1.refs_1_), channel_id=1, source_target_pairs={{0,128},{64,192},{128,0},{192,64},{1,129},{65,193},{129,1},{193,65... | collective-permute-start | bytes 663560 | tf_op jit(solution)/shard_map/ppermute | solution.py:24
  39.0 0.6 pad_add_fusion.position
  39.6 4.8 %collective-permute-done.9.refs_7_ = bf16[2,3,48,384]{3,2,1,0:T(8,128)(2,1)S(1)} collective-permute-done((bf16[2,3,48,384]{3,2,1,0:T(8,128)(2,1)S(1)}, bf16[2,3,48,384]{3,2,1,0:T(8,128)(2,1)S(1)}, u32[]{:S(2)}, u32[]{:S(2)}) %collective-permute-start.9) | collective-permute-done | bytes 221216 | tf_op jit(solution)/shard_map/ppermute | solution.py:24
  44.5 0.0 collective-permute-done.11.refs_11_
  44.5 0.0 collective-permute-done.10.refs_10_
  44.5 0.7 copy-done.16
  45.2 0.1 copy-done.8
  45.3 0.7 copy-done.9
  45.9 18.4 %forward.1 = (bf16[3,768,384]{2,1,0:T(8,128)(2,1)}, bf16[1344,384]{1,0:T(8,128)(2,1)}, bf16[1344,384]{1,0:T(8,128)(2,1)}, bf16[16,3,48,384]{3,2,1,0:T(8,128)(2,1)}) custom-call(s32[4]{0:T(128)} %pad_add_fusion.position, bf16[2,3,48,384]{3,2,1,0:T(8,128)(2,1)} %copy-done.7, bf16[2,3,48,384]{3,2,1,0:T(8,128)(2,1)} %copy-done.10, ...), custom_call_target="tpu_custom_call" | custom-call | tf_op jit(solution)/shard_map/forward/pallas_call | solution.py:156
  64.3 2.7 %collective-permute-start.13 = (bf16[3,768,384]{2,1,0:T(8,128)(2,1)}, bf16[3,768,384]{2,1,0:T(8,128)(2,1)S(1)}, u32[]{:S(2)}, u32[]{:S(2)}) collective-permute-start(bf16[3,768,384]{2,1,0:T(8,128)(2,1)} %get-tuple-element.44.weight_a), channel_id=1, source_target_pairs={{0,16},{16,0},{1,17},{17,1},{2,18},{18,2},{3,19},{19,3},{4,20},{20... | collective-permute-start | bytes 5308424 | tf_op jit(solution)/shard_map/ppermute | solution.py:28
  67.0 8.6 %all-to-all-start = ((bf16[16,3,48,384]{3,2,1,0:T(8,128)(2,1)}), bf16[16,3,48,384]{3,2,1,0:T(8,128)(2,1)S(1)}, u32[]{:S(2)}, u32[]{:S(2)}) async-start(bf16[16,3,48,384]{3,2,1,0:T(8,128)(2,1)} %get-tuple-element.45), calls=%async_computation | async-start | bytes 3538944 | tf_op jit(solution)/shard_map/all_to_all | solution.py:293
  75.6 0.4 collective-permute-start.12
  76.0 0.6 broadcast_in_dim.80.gain
  76.5 1.1 broadcast_in_dim.82.scale
  77.6 0.9 collective-permute-done.12.back_b
  78.5 0.0 collective-permute-done.13.weight_b
  78.5 1.0 copy-done.6
  79.5 0.6 copy-done.4
  80.1 10.8 %backward.1 = bf16[1280,768]{1,0:T(8,128)(2,1)} custom-call(bf16[1344,384]{1,0:T(8,128)(2,1)} %get-tuple-element.42.back_a, bf16[1344,384]{1,0:T(8,128)(2,1)} %copy-done.6, bf16[3,768,384]{2,1,0:T(8,128)(2,1)} %get-tuple-element.44.weight_a, bf16[3,768,384]{2,1,0:T(8,128)(2,1)} %copy-done.4, f32[1280,768]{1,0:T(8,128)} %copy-done, ...), custom_call_target="tpu_custom_call" | custom-call | tf_op jit(solution)/shard_map/backward/pallas_call | solution.py:206
  90.8 10.5 %all-to-all-done = bf16[16,3,48,384]{3,2,1,0:T(8,128)(2,1)S(1)} async-done(((bf16[16,3,48,384]{3,2,1,0:T(8,128)(2,1)}), bf16[16,3,48,384]{3,2,1,0:T(8,128)(2,1)S(1)}, u32[]{:S(2)}, u32[]{:S(2)}) %all-to-all-start) | async-done | bytes 1769504 | tf_op jit(solution)/shard_map/all_to_all | solution.py:293
  101.3 0.2 reduce_sum.22
  101.5 0.1 collective-permute-start.14
  101.6 1.0 collective-permute-start.15
  102.7 2.5 %collective-permute-start.16 = (bf16[3,48,384]{2,1,0:T(8,128)(2,1)S(1)}, bf16[3,48,384]{2,1,0:T(8,128)(2,1)S(1)}, u32[]{:S(2)}, u32[]{:S(2)}) collective-permute-start(bf16[3,48,384]{2,1,0:T(8,128)(2,1)S(1)} %reduce_sum.22), channel_id=1, source_target_pairs={{0,3},{1,2},{2,1},{3,0},{4,7},{5,6},{6,5},{7,4},{8,11},{9,10},{10,... | collective-permute-start | bytes 331784 | tf_op jit(solution)/shard_map/ppermute | solution.py:28
  105.2 1.5 %collective-permute-done.14 = bf16[3,48,384]{2,1,0:T(8,128)(2,1)S(1)} collective-permute-done((bf16[3,48,384]{2,1,0:T(8,128)(2,1)S(1)}, bf16[3,48,384]{2,1,0:T(8,128)(2,1)S(1)}, u32[]{:S(2)}, u32[]{:S(2)}) %collective-permute-start.14) | collective-permute-done | bytes 110624 | tf_op jit(solution)/shard_map/ppermute | solution.py:28
  106.7 0.0 collective-permute-done.15
  106.7 2.3 %collective-permute-done.16 = bf16[3,48,384]{2,1,0:T(8,128)(2,1)S(1)} collective-permute-done((bf16[3,48,384]{2,1,0:T(8,128)(2,1)S(1)}, bf16[3,48,384]{2,1,0:T(8,128)(2,1)S(1)}, u32[]{:S(2)}, u32[]{:S(2)}) %collective-permute-start.16) | collective-permute-done | bytes 110624 | tf_op jit(solution)/shard_map/ppermute | solution.py:28
  109.0 0.1 add_convert_fusion.1
  109.1 2.7 %collective-permute-start.17 = (bf16[3,48,384]{2,1,0:T(8,128)(2,1)S(1)}, bf16[3,48,384]{2,1,0:T(8,128)(2,1)S(1)}, u32[]{:S(2)}, u32[]{:S(2)}) collective-permute-start(bf16[3,48,384]{2,1,0:T(8,128)(2,1)S(1)} %add_convert_fusion.1), channel_id=1, source_target_pairs={{0,7},{1,6},{2,5},{3,4},{4,3},{5,2},{6,1},{7,0},{8,15},{9,14},{10,... | collective-permute-start | bytes 331784 | tf_op jit(solution)/shard_map/ppermute | solution.py:28
  111.8 2.2 %collective-permute-done.17 = bf16[3,48,384]{2,1,0:T(8,128)(2,1)S(1)} collective-permute-done((bf16[3,48,384]{2,1,0:T(8,128)(2,1)S(1)}, bf16[3,48,384]{2,1,0:T(8,128)(2,1)S(1)}, u32[]{:S(2)}, u32[]{:S(2)}) %collective-permute-start.17) | collective-permute-done | bytes 110624 | tf_op jit(solution)/shard_map/ppermute | solution.py:28
  114.0 6.9 %collective-permute-start.18 = (bf16[3,48,384]{2,1,0:T(8,128)(2,1)S(1)}, bf16[3,48,384]{2,1,0:T(8,128)(2,1)S(1)}, u32[]{:S(2)}, u32[]{:S(2)}) collective-permute-start(bf16[3,48,384]{2,1,0:T(8,128)(2,1)S(1)} %add_convert_fusion), channel_id=1, source_target_pairs={{16,0},{8,24},{0,8},{24,16},{17,1},{9,25},{1,9},{25,17},{18,2},{10... | collective-permute-start | bytes 331784 | tf_op jit(solution)/shard_map/ppermute | solution.py:224
  120.9 2.1 %collective-permute-start.19 = (bf16[3,48,384]{2,1,0:T(8,128)(2,1)S(1)}, bf16[3,48,384]{2,1,0:T(8,128)(2,1)S(1)}, u32[]{:S(2)}, u32[]{:S(2)}) collective-permute-start(bf16[3,48,384]{2,1,0:T(8,128)(2,1)S(1)} %add_convert_fusion), channel_id=1, source_target_pairs={{16,8},{8,16},{17,9},{9,17},{18,10},{10,18},{19,11},{11,19},{20,12... | collective-permute-start | bytes 331784 | tf_op jit(solution)/shard_map/ppermute | solution.py:225
  123.0 0.0 collective-permute-done.18
  123.0 3.9 %collective-permute-done.19 = bf16[3,48,384]{2,1,0:T(8,128)(2,1)S(1)} collective-permute-done((bf16[3,48,384]{2,1,0:T(8,128)(2,1)S(1)}, bf16[3,48,384]{2,1,0:T(8,128)(2,1)S(1)}, u32[]{:S(2)}, u32[]{:S(2)}) %collective-permute-start.19) | collective-permute-done | bytes 110624 | tf_op jit(solution)/shard_map/ppermute | solution.py:225
  127.0 0.8 convert_multiply_fusion
  (40 shorter events, 0.3 us)
Async XLA Ops:
  0.6 19.7 %copy-start.17 = (f32[768]{0:T(1024)S(1)}, f32[768]{0:T(1024)}, u32[]{:S(2)}) copy-start(f32[768]{0:T(1024)} %param.9) | copy-start | bytes 9220
  1.6 4.3 %collective-permute-start = (bf16[3,48,384]{2,1,0:T(8,128)(2,1)S(1)}, bf16[3,48,384]{2,1,0:T(8,128)(2,1)S(1)}, u32[]{:S(2)}, u32[]{:S(2)}) collective-permute-start(bf16[3,48,384]{2,1,0:T(8,128)(2,1)S(1)} %get-tuple-element.68), channel_id=1, source_target_pairs={{0,16},{16,0},{1,17},{17,1},{2,18},{18,2},{3,19},{19,3},{4,20},{20... | collective-permute-start | bytes 331784 | tf_op jit(solution)/shard_map/ppermute | solution.py:28
  6.0 14.8 %copy-start.7 = (bf16[2,3,48,384]{3,2,1,0:T(8,128)(2,1)}, bf16[2,3,48,384]{3,2,1,0:T(8,128)(2,1)S(1)}, u32[]{:S(2)}) copy-start(bf16[2,3,48,384]{3,2,1,0:T(8,128)(2,1)S(1)} %pad_maximum_fusion.refs_0_) | copy-start | bytes 663556
  6.0 9.8 %collective-permute-start.1 = (bf16[2,3,48,384]{3,2,1,0:T(8,128)(2,1)S(1)}, bf16[2,3,48,384]{3,2,1,0:T(8,128)(2,1)S(1)}, u32[]{:S(2)}, u32[]{:S(2)}) collective-permute-start(bf16[2,3,48,384]{3,2,1,0:T(8,128)(2,1)S(1)} %pad_maximum_fusion.refs_0_), channel_id=1, source_target_pairs={{0,40},{8,32},{32,8},{40,0},{1,41},{9,33},{33,9},{41,1},{2,42},{10... | collective-permute-start | bytes 663560 | tf_op jit(solution)/shard_map/ppermute | solution.py:28
  7.0 8.7 %collective-permute-start.2 = (bf16[2,3,48,384]{3,2,1,0:T(8,128)(2,1)S(1)}, bf16[2,3,48,384]{3,2,1,0:T(8,128)(2,1)S(1)}, u32[]{:S(2)}, u32[]{:S(2)}) collective-permute-start(bf16[2,3,48,384]{3,2,1,0:T(8,128)(2,1)S(1)} %pad_maximum_fusion.refs_0_), channel_id=1, source_target_pairs={{0,64},{64,128},{128,192},{192,0},{1,65},{65,129},{129,193},{193,1... | collective-permute-start | bytes 663560 | tf_op jit(solution)/shard_map/ppermute | solution.py:24
  8.3 7.5 %collective-permute-start.3 = (bf16[2,3,48,384]{3,2,1,0:T(8,128)(2,1)S(1)}, bf16[2,3,48,384]{3,2,1,0:T(8,128)(2,1)S(1)}, u32[]{:S(2)}, u32[]{:S(2)}) collective-permute-start(bf16[2,3,48,384]{3,2,1,0:T(8,128)(2,1)S(1)} %pad_maximum_fusion.refs_0_), channel_id=1, source_target_pairs={{0,192},{64,0},{128,64},{192,128},{1,193},{65,1},{129,65},{193,129... | collective-permute-start | bytes 663560 | tf_op jit(solution)/shard_map/ppermute | solution.py:24
  9.7 10.6 %collective-permute-start.4 = (bf16[2,3,48,384]{3,2,1,0:T(8,128)(2,1)S(1)}, bf16[2,3,48,384]{3,2,1,0:T(8,128)(2,1)S(1)}, u32[]{:S(2)}, u32[]{:S(2)}) collective-permute-start(bf16[2,3,48,384]{3,2,1,0:T(8,128)(2,1)S(1)} %pad_maximum_fusion.refs_0_), channel_id=1, source_target_pairs={{0,128},{64,192},{128,0},{192,64},{1,129},{65,193},{129,1},{193,65... | collective-permute-start | bytes 663560 | tf_op jit(solution)/shard_map/ppermute | solution.py:24
  15.7 6.7 %copy-start = (f32[1280,768]{1,0:T(8,128)}, f32[1280,768]{1,0:T(8,128)S(1)}, u32[]{:S(2)}) copy-start(f32[1280,768]{1,0:T(8,128)S(1)} %get-tuple-element.31.inputs) | copy-start | bytes 11796484
  15.7 6.6 %copy-start.1 = (bf16[1,1280,768]{2,1,0:T(8,128)(2,1)S(1)}, bf16[1,1280,768]{2,1,0:T(8,128)(2,1)}, u32[]{:S(2)}) copy-start(bf16[1,1280,768]{2,1,0:T(8,128)(2,1)} %param.11) | copy-start | bytes 5898244
  15.8 21.6 %copy-start.10 = (bf16[2,3,48,384]{3,2,1,0:T(8,128)(2,1)}, bf16[2,3,48,384]{3,2,1,0:T(8,128)(2,1)S(1)}, u32[]{:S(2)}) copy-start(bf16[2,3,48,384]{3,2,1,0:T(8,128)(2,1)S(1)} %collective-permute-done.1.refs_1_) | copy-start | bytes 663556
  15.8 6.7 %copy-start.11 = (bf16[2,3,48,384]{3,2,1,0:T(8,128)(2,1)}, bf16[2,3,48,384]{3,2,1,0:T(8,128)(2,1)S(1)}, u32[]{:S(2)}) copy-start(bf16[2,3,48,384]{3,2,1,0:T(8,128)(2,1)S(1)} %collective-permute-done.2.refs_2_) | copy-start | bytes 663556
  15.8 6.7 %copy-start.12 = (bf16[2,3,48,384]{3,2,1,0:T(8,128)(2,1)}, bf16[2,3,48,384]{3,2,1,0:T(8,128)(2,1)S(1)}, u32[]{:S(2)}) copy-start(bf16[2,3,48,384]{3,2,1,0:T(8,128)(2,1)S(1)} %collective-permute-done.3.refs_4_) | copy-start | bytes 663556
  20.3 2.2 %copy-start.13 = (bf16[2,3,48,384]{3,2,1,0:T(8,128)(2,1)}, bf16[2,3,48,384]{3,2,1,0:T(8,128)(2,1)S(1)}, u32[]{:S(2)}) copy-start(bf16[2,3,48,384]{3,2,1,0:T(8,128)(2,1)S(1)} %collective-permute-done.4.refs_6_) | copy-start | bytes 663556
  20.7 9.8 %copy-start.2 = (bf16[1280,768]{1,0:T(8,128)(2,1)}, bf16[1280,768]{1,0:T(8,128)(2,1)S(1)}, u32[]{:S(2)}) copy-start(bf16[1280,768]{1,0:T(8,128)(2,1)S(1)} %multiply_convert_fusion.refs_8_) | copy-start | bytes 5898244
  20.8 9.7 %collective-permute-start.7 = (bf16[1280,768]{1,0:T(8,128)(2,1)S(1)}, bf16[1280,768]{1,0:T(8,128)(2,1)S(1)}, u32[]{:S(2)}, u32[]{:S(2)}) collective-permute-start(bf16[1280,768]{1,0:T(8,128)(2,1)S(1)} %multiply_convert_fusion.refs_8_), channel_id=1, source_target_pairs={{0,16},{16,0},{1,17},{17,1},{2,18},{18,2},{3,19},{19,3},{4,20},{20... | collective-permute-start | bytes 5898248 | tf_op jit(solution)/shard_map/ppermute | solution.py:28
  22.5 8.0 %collective-permute-start.8 = (bf16[1280,384]{1,0:T(8,128)(2,1)S(1)}, bf16[1280,384]{1,0:T(8,128)(2,1)S(1)}, u32[]{:S(2)}, u32[]{:S(2)}) collective-permute-start(bf16[1280,384]{1,0:T(8,128)(2,1)S(1)} %constant_dynamic-slice_fusion.2), channel_id=1, source_target_pairs={{0,16},{16,0},{1,17},{17,1},{2,18},{18,2},{3,19},{19,3},{4,20},{20... | collective-permute-start | bytes 2949128 | tf_op jit(solution)/shard_map/ppermute | solution.py:28
  22.6 7.8 %collective-permute-start.5 = (bf16[2,3,48,384]{3,2,1,0:T(8,128)(2,1)S(1)}, bf16[2,3,48,384]{3,2,1,0:T(8,128)(2,1)S(1)}, u32[]{:S(2)}, u32[]{:S(2)}) collective-permute-start(bf16[2,3,48,384]{3,2,1,0:T(8,128)(2,1)S(1)} %collective-permute-done.1.refs_1_), channel_id=1, source_target_pairs={{0,64},{64,128},{128,192},{192,0},{1,65},{65,129},{129,193},{193,1... | collective-permute-start | bytes 663560 | tf_op jit(solution)/shard_map/ppermute | solution.py:24
  23.5 6.9 %collective-permute-start.6 = (bf16[2,3,48,384]{3,2,1,0:T(8,128)(2,1)S(1)}, bf16[2,3,48,384]{3,2,1,0:T(8,128)(2,1)S(1)}, u32[]{:S(2)}, u32[]{:S(2)}) collective-permute-start(bf16[2,3,48,384]{3,2,1,0:T(8,128)(2,1)S(1)} %collective-permute-done.1.refs_1_), channel_id=1, source_target_pairs={{0,192},{64,0},{128,64},{192,128},{1,193},{65,1},{129,65},{193,129... | collective-permute-start | bytes 663560 | tf_op jit(solution)/shard_map/ppermute | solution.py:24
  30.5 14.0 %copy-start.14 = (bf16[2,3,48,384]{3,2,1,0:T(8,128)(2,1)}, bf16[2,3,48,384]{3,2,1,0:T(8,128)(2,1)S(1)}, u32[]{:S(2)}) copy-start(bf16[2,3,48,384]{3,2,1,0:T(8,128)(2,1)S(1)} %collective-permute-done.5.refs_3_) | copy-start | bytes 663556
  30.5 14.0 %copy-start.15 = (bf16[2,3,48,384]{3,2,1,0:T(8,128)(2,1)}, bf16[2,3,48,384]{3,2,1,0:T(8,128)(2,1)S(1)}, u32[]{:S(2)}) copy-start(bf16[2,3,48,384]{3,2,1,0:T(8,128)(2,1)S(1)} %collective-permute-done.6.refs_5_) | copy-start | bytes 663556
  30.5 14.0 %copy-start.5 = (bf16[1280,384]{1,0:T(8,128)(2,1)}, bf16[1280,384]{1,0:T(8,128)(2,1)S(1)}, u32[]{:S(2)}) copy-start(bf16[1280,384]{1,0:T(8,128)(2,1)S(1)} %collective-permute-done.8.refs_13_) | copy-start | bytes 2949124
  30.5 1.3 %copy-start.3 = (bf16[1280,768]{1,0:T(8,128)(2,1)}, bf16[1280,768]{1,0:T(8,128)(2,1)S(1)}, u32[]{:S(2)}) copy-start(bf16[1280,768]{1,0:T(8,128)(2,1)S(1)} %collective-permute-done.7.refs_9_) | copy-start | bytes 5898244
  31.9 12.6 %collective-permute-start.11 = (bf16[160,768]{1,0:T(8,128)(2,1)S(1)}, bf16[160,768]{1,0:T(8,128)(2,1)S(1)}, u32[]{:S(2)}, u32[]{:S(2)}) collective-permute-start(bf16[160,768]{1,0:T(8,128)(2,1)S(1)} %maximum_maximum_fusion.1), channel_id=1, source_target_pairs={{1,0},{2,1},{3,2},{4,3},{5,4},{6,5},{7,6},{8,7},{9,8},{10,9},{11,1... | collective-permute-start | bytes 737288 | tf_op jit(solution)/shard_map/ppermute | solution.py:277
  33.2 11.3 %collective-permute-start.10 = (bf16[160,768]{1,0:T(8,128)(2,1)S(1)}, bf16[160,768]{1,0:T(8,128)(2,1)S(1)}, u32[]{:S(2)}, u32[]{:S(2)}) collective-permute-start(bf16[160,768]{1,0:T(8,128)(2,1)S(1)} %maximum_maximum_fusion), channel_id=1, source_target_pairs={{0,1},{1,2},{2,3},{3,4},{4,5},{5,6},{6,7},{7,8},{8,9},{9,10},{10,1... | collective-permute-start | bytes 737288 | tf_op jit(solution)/shard_map/ppermute | solution.py:272
  37.4 7.1 %collective-permute-start.9 = (bf16[2,3,48,384]{3,2,1,0:T(8,128)(2,1)S(1)}, bf16[2,3,48,384]{3,2,1,0:T(8,128)(2,1)S(1)}, u32[]{:S(2)}, u32[]{:S(2)}) collective-permute-start(bf16[2,3,48,384]{3,2,1,0:T(8,128)(2,1)S(1)} %collective-permute-done.1.refs_1_), channel_id=1, source_target_pairs={{0,128},{64,192},{128,0},{192,64},{1,129},{65,193},{129,1},{193,65... | collective-permute-start | bytes 663560 | tf_op jit(solution)/shard_map/ppermute | solution.py:24
  44.5 0.7 copy-start.16
  44.5 0.8 copy-start.8
  45.3 0.7 copy-start.9
  64.3 14.2 %collective-permute-start.13 = (bf16[3,768,384]{2,1,0:T(8,128)(2,1)}, bf16[3,768,384]{2,1,0:T(8,128)(2,1)S(1)}, u32[]{:S(2)}, u32[]{:S(2)}) collective-permute-start(bf16[3,768,384]{2,1,0:T(8,128)(2,1)} %get-tuple-element.44.weight_a), channel_id=1, source_target_pairs={{0,16},{16,0},{1,17},{17,1},{2,18},{18,2},{3,19},{19,3},{4,20},{20... | collective-permute-start | bytes 5308424 | tf_op jit(solution)/shard_map/ppermute | solution.py:28
  67.0 34.3 %all-to-all-start = ((bf16[16,3,48,384]{3,2,1,0:T(8,128)(2,1)}), bf16[16,3,48,384]{3,2,1,0:T(8,128)(2,1)S(1)}, u32[]{:S(2)}, u32[]{:S(2)}) async-start(bf16[16,3,48,384]{3,2,1,0:T(8,128)(2,1)} %get-tuple-element.45), calls=%async_computation | async-start | bytes 3538944 | tf_op jit(solution)/shard_map/all_to_all | solution.py:293
  75.6 2.9 %collective-permute-start.12 = (bf16[1344,384]{1,0:T(8,128)(2,1)}, bf16[1344,384]{1,0:T(8,128)(2,1)S(1)}, u32[]{:S(2)}, u32[]{:S(2)}) collective-permute-start(bf16[1344,384]{1,0:T(8,128)(2,1)} %get-tuple-element.43), channel_id=1, source_target_pairs={{0,16},{16,0},{1,17},{17,1},{2,18},{18,2},{3,19},{19,3},{4,20},{20... | collective-permute-start | bytes 3096584 | tf_op jit(solution)/shard_map/ppermute | solution.py:28
  78.5 1.0 copy-start.6
  78.5 1.6 %copy-start.4 = (bf16[3,768,384]{2,1,0:T(8,128)(2,1)}, bf16[3,768,384]{2,1,0:T(8,128)(2,1)S(1)}, u32[]{:S(2)}) copy-start(bf16[3,768,384]{2,1,0:T(8,128)(2,1)S(1)} %collective-permute-done.13.weight_b) | copy-start | bytes 5308420
  101.5 5.1 %collective-permute-start.14 = (bf16[3,48,384]{2,1,0:T(8,128)(2,1)S(1)}, bf16[3,48,384]{2,1,0:T(8,128)(2,1)S(1)}, u32[]{:S(2)}, u32[]{:S(2)}) collective-permute-start(bf16[3,48,384]{2,1,0:T(8,128)(2,1)S(1)} %reduce_sum.22), channel_id=1, source_target_pairs={{0,1},{1,0},{2,3},{3,2},{4,5},{5,4},{6,7},{7,6},{8,9},{9,8},{10,11... | collective-permute-start | bytes 331784 | tf_op jit(solution)/shard_map/ppermute | solution.py:28
  101.6 5.1 %collective-permute-start.15 = (bf16[3,48,384]{2,1,0:T(8,128)(2,1)S(1)}, bf16[3,48,384]{2,1,0:T(8,128)(2,1)S(1)}, u32[]{:S(2)}, u32[]{:S(2)}) collective-permute-start(bf16[3,48,384]{2,1,0:T(8,128)(2,1)S(1)} %reduce_sum.22), channel_id=1, source_target_pairs={{0,2},{1,3},{2,0},{3,1},{4,6},{5,7},{6,4},{7,5},{8,10},{9,11},{10,... | collective-permute-start | bytes 331784 | tf_op jit(solution)/shard_map/ppermute | solution.py:28
  102.7 6.4 %collective-permute-start.16 = (bf16[3,48,384]{2,1,0:T(8,128)(2,1)S(1)}, bf16[3,48,384]{2,1,0:T(8,128)(2,1)S(1)}, u32[]{:S(2)}, u32[]{:S(2)}) collective-permute-start(bf16[3,48,384]{2,1,0:T(8,128)(2,1)S(1)} %reduce_sum.22), channel_id=1, source_target_pairs={{0,3},{1,2},{2,1},{3,0},{4,7},{5,6},{6,5},{7,4},{8,11},{9,10},{10,... | collective-permute-start | bytes 331784 | tf_op jit(solution)/shard_map/ppermute | solution.py:28
  109.1 4.9 %collective-permute-start.17 = (bf16[3,48,384]{2,1,0:T(8,128)(2,1)S(1)}, bf16[3,48,384]{2,1,0:T(8,128)(2,1)S(1)}, u32[]{:S(2)}, u32[]{:S(2)}) collective-permute-start(bf16[3,48,384]{2,1,0:T(8,128)(2,1)S(1)} %add_convert_fusion.1), channel_id=1, source_target_pairs={{0,7},{1,6},{2,5},{3,4},{4,3},{5,2},{6,1},{7,0},{8,15},{9,14},{10,... | collective-permute-start | bytes 331784 | tf_op jit(solution)/shard_map/ppermute | solution.py:28
  114.0 9.0 %collective-permute-start.18 = (bf16[3,48,384]{2,1,0:T(8,128)(2,1)S(1)}, bf16[3,48,384]{2,1,0:T(8,128)(2,1)S(1)}, u32[]{:S(2)}, u32[]{:S(2)}) collective-permute-start(bf16[3,48,384]{2,1,0:T(8,128)(2,1)S(1)} %add_convert_fusion), channel_id=1, source_target_pairs={{16,0},{8,24},{0,8},{24,16},{17,1},{9,25},{1,9},{25,17},{18,2},{10... | collective-permute-start | bytes 331784 | tf_op jit(solution)/shard_map/ppermute | solution.py:224
  120.9 6.1 %collective-permute-start.19 = (bf16[3,48,384]{2,1,0:T(8,128)(2,1)S(1)}, bf16[3,48,384]{2,1,0:T(8,128)(2,1)S(1)}, u32[]{:S(2)}, u32[]{:S(2)}) collective-permute-start(bf16[3,48,384]{2,1,0:T(8,128)(2,1)S(1)} %add_convert_fusion), channel_id=1, source_target_pairs={{16,8},{8,16},{17,9},{9,17},{18,10},{10,18},{19,11},{11,19},{20,12... | collective-permute-start | bytes 331784 | tf_op jit(solution)/shard_map/ppermute | solution.py:225

commit v5 on v4

--- a/solution.py
+++ b/solution.py
@@ -45,8 +45,9 @@
     x, yh, core = position[0], position[1], position[2]
     rows = pieces[0].shape[2]
     steps = [(0, 0), (0, 1), (3, 0), (3, 1), (1, 0), (1, 1), (2, 0), (2, 1)]
+    blocks = list(pieces[:6]) + [pieces[6].at[0], pieces[6].at[1]]
     copies = []
-    for block, (step_x, step_y) in zip(pieces, steps):
+    for block, (step_x, step_y) in zip(blocks, steps):
         for side in range(2):
             owner = ((x + step_x) % 4) * 4 + ((yh + step_y) % 2) * 2 + (core + side) % 2
             place = pl.multiple_of(owner * rows, 16)
@@ -59,7 +60,7 @@
 
 
 def forward_kernel(position, *refs):
-    pieces, refs = refs[:8], refs[8:]
+    pieces, refs = refs[:7], refs[7:]
     normed_hbm, edges, upstream_hbm = refs[0:2], refs[2:4], refs[4:6]
     weight_out, back_out, grad_out = refs[6], refs[7:9], refs[9]
     weight, normed, upstream, back, grad = refs[10:15]
@@ -75,15 +76,15 @@
         center = upstream_hbm[index]
         if index == 0:
             center = center.at[:, pl.ds(lane, half)]
-        rows, lanes = slice(index * wide, (index + 1) * wide), slice(index * half, (index + 1) * half)
+        rows, lanes = pl.ds(index * wide, wide), pl.ds(index * half, half)
         moves = [
             (normed_hbm[index], normed.at[index, wide : wide + count]),
             (center, upstream.at[index, REACH : REACH + count]),
+            (edges[0].at[rows], normed.at[index, :wide]),
+            (edges[1].at[rows], normed.at[index, wide + count :]),
+            (edges[0].at[2 * wide :, lanes], upstream.at[index, :REACH]),
+            (edges[1].at[2 * wide :, lanes], upstream.at[index, REACH + count :]),
         ]
-        for edge, place in zip(edges, (0, wide + count)):
-            moves.append((edge.at[rows], normed.at[index, place : place + wide]))
-        for edge, place in zip(edges, (0, REACH + count)):
-            moves.append((edge.at[2 * wide :, lanes], upstream.at[index, place : place + REACH]))
         loads.append(
             [
                 pltpu.make_async_copy(source, target, load_sem.at[index, place])
@@ -158,7 +159,7 @@
         out_shape=[jax.ShapeDtypeStruct((FILTER_TAPS, channels, half), BF16)]
         + [jax.ShapeDtypeStruct((length, half), BF16)] * 2
         + [jax.ShapeDtypeStruct((16, FILTER_TAPS, channels // 16, half), BF16)],
-        in_specs=[pl.BlockSpec(memory_space=pltpu.SMEM)] + [anywhere] * 14,
+        in_specs=[pl.BlockSpec(memory_space=pltpu.SMEM)] + [anywhere] * 13,
         out_specs=[anywhere] * 4,
         scratch_shapes=[
             pltpu.VMEM((FILTER_TAPS, channels, half), BF16),
@@ -172,7 +173,7 @@
             dma,
             dma((16,)),
         ],
-        compiler_params=pltpu.CompilerParams(vmem_limit_bytes=56 * 1024 * 1024),
+        compiler_params=pltpu.CompilerParams(vmem_limit_bytes=26 * 1024 * 1024),
         name="forward",
     )(position, *pieces, *normed, *edges, *upstream)
 
@@ -210,7 +211,7 @@
         in_specs=[whole(back[0]), whole(back[1]), whole(weight[0]), whole(weight[1]), part]
         + [pl.BlockSpec((block, 1), lambda i: (i, 0)), whole(gain), part],
         out_specs=part,
-        compiler_params=pltpu.CompilerParams(vmem_limit_bytes=56 * 1024 * 1024),
+        compiler_params=pltpu.CompilerParams(vmem_limit_bytes=26 * 1024 * 1024),
         name="backward",
     )(*back, *weight, inputs, scale, gain, incoming)
 
@@ -243,48 +244,40 @@
     own, tokens, nucleotides, incoming = join(own, tokens, nucleotides, incoming)
 
     across = swap(own, RING_Y, 4, 3)
-    around_own = [shift(own, "x", 4, step) for step in (1, -1, 2)]
+    up_own, down_own = shift(own, "x", 4, 1), shift(own, "x", 4, -1)
     bases = nucleotides[0][:, None]
     row = base_table[3][None]
     for base in (2, 1, 0):
         row = jnp.where(bases == base, base_table[base][None], row)
     inputs = tokens.astype(F32) + row
-    square = jnp.mean(inputs * inputs, axis=-1)
-    across, inputs, square, incoming, *around_own = join(
-        across, inputs, square, incoming, *around_own
-    )
-
-    around_across = [shift(across, "x", 4, step) for step in (1, -1, 2)]
-    scale_inv = lax.rsqrt(square + 1e-06)[:, None]
+    scale_inv = lax.rsqrt(jnp.mean(inputs * inputs, axis=-1, keepdims=True) + 1e-06)
     normed = (inputs * scale_inv * norm_gain).astype(BF16)
+    own, across, up_own, down_own, normed, incoming = join(
+        own, across, up_own, down_own, normed, incoming
+    )
+
+    far = shift(jnp.stack([own, across]), "x", 4, 2)
+    up_across, down_across = shift(across, "x", 4, 1), shift(across, "x", 4, -1)
     upstream_sent = lax.dynamic_slice_in_dim(incoming, (1 - core) * half, half, axis=1)
     normed_other = swap(normed, "core", 2, 1)
     upstream_other = swap(upstream_sent, "core", 2, 1)
-    around_across[0], around_across[1], normed, normed_other, upstream_other, incoming = join(
-        around_across[0], around_across[1], normed, normed_other, upstream_other, incoming
-    )
 
     def edge(rows, reach_rows):
         upstream_edge = lax.dynamic_slice_in_dim(incoming[reach_rows], core * half, half, axis=1)
         upstream_edge = jnp.concatenate([upstream_edge, upstream_other[reach_rows]], axis=1)
         return jnp.concatenate([normed[rows], normed_other[rows], upstream_edge])
 
-    low = lax.ppermute(
-        edge(slice(count - 2 * REACH, count), slice(count - REACH, count)),
-        SEQ,
-        [(i, i + 1) for i in range(15)],
-    )
-    high = lax.ppermute(
-        edge(slice(0, 2 * REACH), slice(0, REACH)), SEQ, [(i + 1, i) for i in range(15)]
-    )
-    pieces = [own, across]
-    for pair in zip(around_own, around_across):
-        pieces += pair
+    last = edge(slice(count - 2 * REACH, count), slice(count - REACH, count))
+    first = edge(slice(0, 2 * REACH), slice(0, REACH))
+    edges = (
+        lax.ppermute(last, SEQ, [(i, i + 1) for i in range(15)]),
+        lax.ppermute(first, SEQ, [(i + 1, i) for i in range(15)]),
+    )
     weight, back, back_other, grads = forward(
         position,
-        pieces,
+        [own, across, up_own, up_across, down_own, down_across, far],
         (normed, normed_other),
-        (low, high),
+        edges,
         (incoming, upstream_other),
     )
 

time: 129 us -> 131 us (1.016)
  local copies, waits for them, and re-layouts: 7.97 us -> 15.1 us
  waiting for transfers between devices: 35.8 us -> 29.2 us
  other arithmetic: 6.75 us -> 9.88 us
  Pallas kernels: 29.1 us -> 27.7 us
    ppermute x6 -> x5, waiting for transfers between devices: 14.4 us -> 4.78 us  [shift(): return lax.ppermute(value, axis, pairs)]
    unnamed x36 -> x32, local copies, waits for them, and re-layouts: 4.27 us -> 12.9 us
    ppermute x10, waiting for transfers between devices: 6.98 us -> 9.47 us  [swap(): return lax.ppermute(value, axis, [(i, i ^ mask) for i in range(count)])]
    ppermute x10, starting transfers between devices: 15.5 us -> 17.6 us  [swap(): return lax.ppermute(value, axis, [(i, i ^ mask) for i in range(count)])]
    ppermute x6 -> x5, starting transfers between devices: 8.53 us -> 6.89 us  [shift(): return lax.ppermute(value, axis, pairs)]
    reduce_sum x1, other arithmetic: 0.25 us -> 1.73 us  [on_device(): total = jnp.sum(arrived.astype(F32), axis=0)]
    concatenate x2, other arithmetic: 0.04 us -> 1.44 us  [edge(): return jnp.concatenate([normed[rows], normed_other[rows], upstream_edge])]
    ppermute x1, starting transfers between devices: 6.9 us -> 5.55 us  [share_weight_grad(): first = lax.ppermute(mine, pair, [(2, 0), (1, 3), (0, 1), (3, 2)])]
  transfers between devices with their start and end apart: 21 -> 20, of which waited for: 10 -> 9; matrix products, arithmetic and copies ran while one was open for 6% -> 6% of each run, Pallas kernels for 8% -> 7%
where the time goes in v5:
time: 131 us; the launch traced here: 130 us
  starting transfers between devices  47.4 us (36%)
  waiting for transfers between devices  29.2 us (22%)
  Pallas kernels  27.7 us (21%)
  local copies, waits for them, and re-layouts  15.1 us (12%)
  other arithmetic  9.88 us (8%)
    pallas_call x1, Pallas kernels, forward(): pl.pallas_call(forward_kernel, out_shape=[jax.ShapeDtypeStruct((FILTER_TA...  18 us
    ppermute x10, starting transfers between devices, swap(): return lax.ppermute(value, axis, [(i, i ^ mask) for i in range(count)])  17.6 us
    unnamed x32, local copies, waits for them, and re-layouts  12.9 us
    all_to_all x1, waiting for transfers between devices, on_device(): arrived = lax.all_to_all(grads, ('x', 'yh', 'yl'), 0, 0, tiled=True)  11 us
    pallas_call x1, Pallas kernels, backward(): pl.pallas_call(backward_kernel, grid=(count // block,), out_shape=jax.Sha...  9.73 us
    ppermute x10, waiting for transfers between devices, swap(): return lax.ppermute(value, axis, [(i, i ^ mask) for i in range(count)])  9.47 us
    all_to_all x1, starting transfers between devices, on_device(): arrived = lax.all_to_all(grads, ('x', 'yh', 'yl'), 0, 0, tiled=True)  9.14 us
    ppermute x5, starting transfers between devices, shift(): return lax.ppermute(value, axis, pairs)  6.89 us
  transfers between devices with their start and end apart: 20, of which 9 were waited for; matrix products, arithmetic and copies ran while one was open for 6% of the time, Pallas kernels for 7%

profile of v5, /device:TPU:1, one launch (start us, length us, event | category | flops | bytes accessed | tf_op | source)
XLA Modules:
  0.0 130.3 jit_solution(1621318528047218724)
XLA Ops:
  0.6 1.0 dynamic-slice_bitcast_fusion
  1.6 3.3 %collective-permute-start = (bf16[3,48,384]{2,1,0:T(8,128)(2,1)S(1)}, bf16[3,48,384]{2,1,0:T(8,128)(2,1)S(1)}, u32[]{:S(2)}, u32[]{:S(2)}) collective-permute-start(bf16[3,48,384]{2,1,0:T(8,128)(2,1)S(1)} %get-tuple-element.54), channel_id=1, source_target_pairs={{0,16},{16,0},{1,17},{17,1},{2,18},{18,2},{3,19},{19,3},{4,20},{20... | collective-permute-start | bytes 331784 | tf_op jit(solution)/shard_map/ppermute | solution.py:28
  5.0 0.9 slice_reduce_fusion.3
  5.9 0.1 collective-permute-done
  6.0 1.1 collective-permute-start.1
  7.0 1.2 collective-permute-start.2
  8.2 1.5 %collective-permute-start.3 = (bf16[2,3,48,384]{3,2,1,0:T(8,128)(2,1)S(1)}, bf16[2,3,48,384]{3,2,1,0:T(8,128)(2,1)S(1)}, u32[]{:S(2)}, u32[]{:S(2)}) collective-permute-start(bf16[2,3,48,384]{3,2,1,0:T(8,128)(2,1)S(1)} %pad_maximum_fusion.1.refs_0_), channel_id=1, source_target_pairs={{0,192},{64,0},{128,64},{192,128},{1,193},{65,1},{129,65},{193,129... | collective-permute-start | bytes 663560 | tf_op jit(solution)/shard_map/ppermute | solution.py:24
  9.7 0.7 compare_reduce_fusion.2
  10.5 3.7 %multiply_reduce_fusion = (f32[1280]{0:T(1024)S(1)}, f32[1280,768]{1,0:T(8,128)S(1)}) fusion(f32[768]{0:T(1024)S(1)} %get-tuple-element.36, f32[768]{0:T(1024)S(1)} %get-tuple-element.37, pred[1280]{0:T(1024)(128)(4,1)S(1)} %get-tuple-element.39, f32[768]{0:T(1024)S(1)} %get-tuple-element.35, pred[1280]{0:T(1024)(128)(4,1)S(1)} %get-tuple-element.40, ...), kind=kLoop, calls=%fused_computation.1 | loop fusion | flops 6880000 | bytes 5919488 | tf_op jit(solution)/shard_map/reduce_sum | solution.py:253
  14.2 0.0 copy-start.2
  14.2 0.4 multiply_convert_fusion.refs_7_
  14.6 0.0 copy-start.3
  14.6 0.0 collective-permute-done.1.refs_1_
  14.7 0.7 copy-done.10
  15.3 0.0 collective-permute-done.3.refs_4_
  15.3 0.7 copy-done.12
  16.0 1.4 %collective-permute-start.7 = (bf16[1280,768]{1,0:T(8,128)(2,1)S(1)}, bf16[1280,768]{1,0:T(8,128)(2,1)S(1)}, u32[]{:S(2)}, u32[]{:S(2)}) collective-permute-start(bf16[1280,768]{1,0:T(8,128)(2,1)S(1)} %multiply_convert_fusion.refs_7_), channel_id=1, source_target_pairs={{0,16},{16,0},{1,17},{17,1},{2,18},{18,2},{3,19},{19,3},{4,20},{20... | collective-permute-start | bytes 5898248 | tf_op jit(solution)/shard_map/ppermute | solution.py:28
  17.5 0.1 constant_dynamic-slice_fusion.1
  17.6 1.0 collective-permute-start.8
  18.6 0.8 pad_maximum_fusion
  19.4 1.5 %collective-permute-start.6 = (bf16[2,2,3,48,384]{4,3,2,1,0:T(8,128)(2,1)}, bf16[2,2,3,48,384]{4,3,2,1,0:T(8,128)(2,1)}, u32[]{:S(2)}, u32[]{:S(2)}) collective-permute-start(bf16[2,2,3,48,384]{4,3,2,1,0:T(8,128)(2,1)} %pad_maximum_fusion), channel_id=1, source_target_pairs={{0,128},{64,192},{128,0},{192,64},{1,129},{65,193},{129,1},{193,65... | collective-permute-start | bytes 1327112 | tf_op jit(solution)/shard_map/ppermute | solution.py:24
  21.0 1.4 %collective-permute-done.8.refs_12_ = bf16[1280,384]{1,0:T(8,128)(2,1)S(1)} collective-permute-done((bf16[1280,384]{1,0:T(8,128)(2,1)S(1)}, bf16[1280,384]{1,0:T(8,128)(2,1)S(1)}, u32[]{:S(2)}, u32[]{:S(2)}) %collective-permute-start.8) | collective-permute-done | bytes 983072 | tf_op jit(solution)/shard_map/ppermute | solution.py:28
  22.5 0.0 collective-permute-done.7.refs_8_
  22.5 1.3 copy-done.5
  23.8 0.7 maximum_maximum_fusion.1
  24.5 1.3 collective-permute-start.10
  25.8 0.7 maximum_maximum_fusion
  26.5 4.9 %collective-permute-start.9 = (bf16[160,768]{1,0:T(8,128)(2,1)}, bf16[160,768]{1,0:T(8,128)(2,1)}, u32[]{:S(2)}, u32[]{:S(2)}) collective-permute-start(bf16[160,768]{1,0:T(8,128)(2,1)} %maximum_maximum_fusion), channel_id=1, source_target_pairs={{0,1},{1,2},{2,3},{3,4},{4,5},{5,6},{6,7},{7,8},{8,9},{9,10},{10,1... | collective-permute-start | bytes 737288 | tf_op jit(solution)/shard_map/ppermute | solution.py:273
  31.4 0.5 collective-permute-start.4
  31.9 2.1 %collective-permute-start.5 = (bf16[2,3,48,384]{3,2,1,0:T(8,128)(2,1)S(1)}, bf16[2,3,48,384]{3,2,1,0:T(8,128)(2,1)}, u32[]{:S(2)}, u32[]{:S(2)}) collective-permute-start(bf16[2,3,48,384]{3,2,1,0:T(8,128)(2,1)S(1)} %collective-permute-done.1.refs_1_), channel_id=1, source_target_pairs={{0,192},{64,0},{128,64},{192,128},{1,193},{65,1},{129,65},{193,129... | collective-permute-start | bytes 663560 | tf_op jit(solution)/shard_map/ppermute | solution.py:24
  34.1 0.1 pad_add_fusion.position
  34.1 4.8 %collective-permute-done.4.refs_3_ = bf16[2,3,48,384]{3,2,1,0:T(8,128)(2,1)} collective-permute-done((bf16[2,3,48,384]{3,2,1,0:T(8,128)(2,1)S(1)}, bf16[2,3,48,384]{3,2,1,0:T(8,128)(2,1)}, u32[]{:S(2)}, u32[]{:S(2)}) %collective-permute-start.4) | collective-permute-done | bytes 221216 | tf_op jit(solution)/shard_map/ppermute | solution.py:24
  38.9 0.0 collective-permute-done.5.refs_5_
  38.9 0.0 collective-permute-done.6.refs_6_
  38.9 0.0 copy-start.4
  38.9 1.5 %copy-done.4 = bf16[1280,768]{1,0:T(8,128)(2,1)S(1)} copy-done((bf16[1280,768]{1,0:T(8,128)(2,1)S(1)}, bf16[1280,768]{1,0:T(8,128)(2,1)}, u32[]{:S(2)}) %copy-start.4) | copy-done | bytes 1966104
  40.5 1.5 %copy-done.6 = bf16[1280,768]{1,0:T(8,128)(2,1)S(1)} copy-done((bf16[1280,768]{1,0:T(8,128)(2,1)S(1)}, bf16[1280,768]{1,0:T(8,128)(2,1)}, u32[]{:S(2)}) %copy-start.6) | copy-done | bytes 1966104
  42.0 0.9 copy-done.11
  43.0 0.9 copy-done.13
  43.9 18.0 %forward.1 = (bf16[3,768,384]{2,1,0:T(8,128)(2,1)}, bf16[1344,384]{1,0:T(8,128)(2,1)S(1)}, bf16[1344,384]{1,0:T(8,128)(2,1)S(1)}, bf16[16,3,48,384]{3,2,1,0:T(8,128)(2,1)S(1)}) custom-call(s32[4]{0:T(128)S(1)} %pad_add_fusion.position, bf16[2,3,48,384]{3,2,1,0:T(8,128)(2,1)S(1)} %pad_maximum_fusion.1.refs_0_, ...), custom_call_target="tpu_custom_call" | custom-call | tf_op jit(solution)/shard_map/forward/pallas_call | solution.py:157
  61.9 1.2 copy-done.7
  63.2 1.0 copy-done.8
  64.1 0.9 copy-done.14
  65.1 1.6 %collective-permute-start.12 = (bf16[3,768,384]{2,1,0:T(8,128)(2,1)}, bf16[3,768,384]{2,1,0:T(8,128)(2,1)}, u32[]{:S(2)}, u32[]{:S(2)}) collective-permute-start(bf16[3,768,384]{2,1,0:T(8,128)(2,1)} %get-tuple-element.30.weight_a), channel_id=1, source_target_pairs={{0,16},{16,0},{1,17},{17,1},{2,18},{18,2},{3,19},{19,3},{4,20},{20... | collective-permute-start | bytes 5308424 | tf_op jit(solution)/shard_map/ppermute | solution.py:28
  66.7 9.1 %all-to-all-start = ((bf16[16,3,48,384]{3,2,1,0:T(8,128)(2,1)}), bf16[16,3,48,384]{3,2,1,0:T(8,128)(2,1)}, u32[]{:S(2)}, u32[]{:S(2)}) async-start(bf16[16,3,48,384]{3,2,1,0:T(8,128)(2,1)} %copy-done.7), calls=%async_computation | async-start | bytes 3538944 | tf_op jit(solution)/shard_map/all_to_all | solution.py:286
  75.9 0.5 collective-permute-start.11
  76.4 0.2 rsqrt.7.scale
  76.6 2.2 %collective-permute-done.11.back_b = bf16[1344,384]{1,0:T(8,128)(2,1)S(1)} collective-permute-done((bf16[1344,384]{1,0:T(8,128)(2,1)}, bf16[1344,384]{1,0:T(8,128)(2,1)S(1)}, u32[]{:S(2)}, u32[]{:S(2)}) %collective-permute-start.11) | collective-permute-done | bytes 1032224 | tf_op jit(solution)/shard_map/ppermute | solution.py:28
  78.9 2.1 %copy-done.1 = f32[1280,768]{1,0:T(8,128)S(1)} copy-done((f32[1280,768]{1,0:T(8,128)S(1)}, f32[1280,768]{1,0:T(8,128)}, u32[]{:S(2)}) %copy-start.1) | copy-done | bytes 3932184
  81.0 9.7 %backward.1 = bf16[1280,768]{1,0:T(8,128)(2,1)} custom-call(bf16[1344,384]{1,0:T(8,128)(2,1)S(1)} %copy-done.9, bf16[1344,384]{1,0:T(8,128)(2,1)S(1)} %collective-permute-done.11.back_b, bf16[3,768,384]{2,1,0:T(8,128)(2,1)} %get-tuple-element.30.weight_a, bf16[3,768,384]{2,1,0:T(8,128)(2,1)} %collective-permute-done.12.weight_b, f32[1280,768]{1,0:T(8,128)S(1)} %copy-done.1, ...), custom_call_target="tpu_custom_call" | custom-call | tf_op jit(solution)/shard_map/backward/pallas_call | solution.py:207
  90.7 11.0 %all-to-all-done = bf16[16,3,48,384]{3,2,1,0:T(8,128)(2,1)} async-done(((bf16[16,3,48,384]{3,2,1,0:T(8,128)(2,1)}), bf16[16,3,48,384]{3,2,1,0:T(8,128)(2,1)}, u32[]{:S(2)}, u32[]{:S(2)}) %all-to-all-start) | async-done | bytes 1769504 | tf_op jit(solution)/shard_map/all_to_all | solution.py:286
  101.7 1.7 %reduce_sum.22 = bf16[3,48,384]{2,1,0:T(8,128)(2,1)S(1)} reduce(bf16[16,3,48,384]{3,2,1,0:T(8,128)(2,1)} %all-to-all-done, bf16[]{:T(256)} %constant.41.clone.1), dimensions={0}, to_apply=%region_1.2 | reduce | flops 829440 | bytes 1880066 | tf_op jit(solution)/shard_map/reduce_sum | solution.py:291
  103.4 0.3 collective-permute-start.13
  103.7 0.5 collective-permute-start.14
  104.2 3.0 %collective-permute-start.15 = (bf16[3,48,384]{2,1,0:T(8,128)(2,1)S(1)}, bf16[3,48,384]{2,1,0:T(8,128)(2,1)S(1)}, u32[]{:S(2)}, u32[]{:S(2)}) collective-permute-start(bf16[3,48,384]{2,1,0:T(8,128)(2,1)S(1)} %reduce_sum.22), channel_id=1, source_target_pairs={{0,3},{1,2},{2,1},{3,0},{4,7},{5,6},{6,5},{7,4},{8,11},{9,10},{10,... | collective-permute-start | bytes 331784 | tf_op jit(solution)/shard_map/ppermute | solution.py:28
  107.3 1.2 collective-permute-done.13
  108.5 2.4 %collective-permute-done.14 = bf16[3,48,384]{2,1,0:T(8,128)(2,1)S(1)} collective-permute-done((bf16[3,48,384]{2,1,0:T(8,128)(2,1)S(1)}, bf16[3,48,384]{2,1,0:T(8,128)(2,1)S(1)}, u32[]{:S(2)}, u32[]{:S(2)}) %collective-permute-start.14) | collective-permute-done | bytes 110624 | tf_op jit(solution)/shard_map/ppermute | solution.py:28
  110.9 0.1 add_convert_fusion.1
  110.9 4.7 %collective-permute-start.16 = (bf16[3,48,384]{2,1,0:T(8,128)(2,1)S(1)}, bf16[3,48,384]{2,1,0:T(8,128)(2,1)S(1)}, u32[]{:S(2)}, u32[]{:S(2)}) collective-permute-start(bf16[3,48,384]{2,1,0:T(8,128)(2,1)S(1)} %add_convert_fusion.1), channel_id=1, source_target_pairs={{0,7},{1,6},{2,5},{3,4},{4,3},{5,2},{6,1},{7,0},{8,15},{9,14},{10,... | collective-permute-start | bytes 331784 | tf_op jit(solution)/shard_map/ppermute | solution.py:28
  115.7 2.1 %collective-permute-done.16 = bf16[3,48,384]{2,1,0:T(8,128)(2,1)S(1)} collective-permute-done((bf16[3,48,384]{2,1,0:T(8,128)(2,1)S(1)}, bf16[3,48,384]{2,1,0:T(8,128)(2,1)S(1)}, u32[]{:S(2)}, u32[]{:S(2)}) %collective-permute-start.16) | collective-permute-done | bytes 110624 | tf_op jit(solution)/shard_map/ppermute | solution.py:28
  117.8 5.5 %collective-permute-start.17 = (bf16[3,48,384]{2,1,0:T(8,128)(2,1)S(1)}, bf16[3,48,384]{2,1,0:T(8,128)(2,1)S(1)}, u32[]{:S(2)}, u32[]{:S(2)}) collective-permute-start(bf16[3,48,384]{2,1,0:T(8,128)(2,1)S(1)} %add_convert_fusion), channel_id=1, source_target_pairs={{16,0},{8,24},{0,8},{24,16},{17,1},{9,25},{1,9},{25,17},{18,2},{10... | collective-permute-start | bytes 331784 | tf_op jit(solution)/shard_map/ppermute | solution.py:225
  123.4 2.1 %collective-permute-start.18 = (bf16[3,48,384]{2,1,0:T(8,128)(2,1)S(1)}, bf16[3,48,384]{2,1,0:T(8,128)(2,1)S(1)}, u32[]{:S(2)}, u32[]{:S(2)}) collective-permute-start(bf16[3,48,384]{2,1,0:T(8,128)(2,1)S(1)} %add_convert_fusion), channel_id=1, source_target_pairs={{16,8},{8,16},{17,9},{9,17},{18,10},{10,18},{19,11},{11,19},{20,12... | collective-permute-start | bytes 331784 | tf_op jit(solution)/shard_map/ppermute | solution.py:226
  125.5 3.9 %collective-permute-done.18 = bf16[3,48,384]{2,1,0:T(8,128)(2,1)S(1)} collective-permute-done((bf16[3,48,384]{2,1,0:T(8,128)(2,1)S(1)}, bf16[3,48,384]{2,1,0:T(8,128)(2,1)S(1)}, u32[]{:S(2)}, u32[]{:S(2)}) %collective-permute-start.18) | collective-permute-done | bytes 110624 | tf_op jit(solution)/shard_map/ppermute | solution.py:226
  129.5 0.8 convert_multiply_fusion
  (35 shorter events, 0.2 us)
Async XLA Ops:
  0.6 13.6 %copy-start.15 = (f32[768]{0:T(1024)S(1)}, f32[768]{0:T(1024)}, u32[]{:S(2)}) copy-start(f32[768]{0:T(1024)} %param.9) | copy-start | bytes 9220
  1.6 4.3 %collective-permute-start = (bf16[3,48,384]{2,1,0:T(8,128)(2,1)S(1)}, bf16[3,48,384]{2,1,0:T(8,128)(2,1)S(1)}, u32[]{:S(2)}, u32[]{:S(2)}) collective-permute-start(bf16[3,48,384]{2,1,0:T(8,128)(2,1)S(1)} %get-tuple-element.54), channel_id=1, source_target_pairs={{0,16},{16,0},{1,17},{17,1},{2,18},{18,2},{3,19},{19,3},{4,20},{20... | collective-permute-start | bytes 331784 | tf_op jit(solution)/shard_map/ppermute | solution.py:28
  6.0 8.7 %collective-permute-start.1 = (bf16[2,3,48,384]{3,2,1,0:T(8,128)(2,1)S(1)}, bf16[2,3,48,384]{3,2,1,0:T(8,128)(2,1)S(1)}, u32[]{:S(2)}, u32[]{:S(2)}) collective-permute-start(bf16[2,3,48,384]{3,2,1,0:T(8,128)(2,1)S(1)} %pad_maximum_fusion.1.refs_0_), channel_id=1, source_target_pairs={{0,40},{8,32},{32,8},{40,0},{1,41},{9,33},{33,9},{41,1},{2,42},{10... | collective-permute-start | bytes 663560 | tf_op jit(solution)/shard_map/ppermute | solution.py:28
  7.0 7.6 %collective-permute-start.2 = (bf16[2,3,48,384]{3,2,1,0:T(8,128)(2,1)S(1)}, bf16[2,3,48,384]{3,2,1,0:T(8,128)(2,1)S(1)}, u32[]{:S(2)}, u32[]{:S(2)}) collective-permute-start(bf16[2,3,48,384]{3,2,1,0:T(8,128)(2,1)S(1)} %pad_maximum_fusion.1.refs_0_), channel_id=1, source_target_pairs={{0,64},{64,128},{128,192},{192,0},{1,65},{65,129},{129,193},{193,1... | collective-permute-start | bytes 663560 | tf_op jit(solution)/shard_map/ppermute | solution.py:24
  8.2 7.1 %collective-permute-start.3 = (bf16[2,3,48,384]{3,2,1,0:T(8,128)(2,1)S(1)}, bf16[2,3,48,384]{3,2,1,0:T(8,128)(2,1)S(1)}, u32[]{:S(2)}, u32[]{:S(2)}) collective-permute-start(bf16[2,3,48,384]{3,2,1,0:T(8,128)(2,1)S(1)} %pad_maximum_fusion.1.refs_0_), channel_id=1, source_target_pairs={{0,192},{64,0},{128,64},{192,128},{1,193},{65,1},{129,65},{193,129... | collective-permute-start | bytes 663560 | tf_op jit(solution)/shard_map/ppermute | solution.py:24
  14.2 3.4 %copy-start = (f32[1280,768]{1,0:T(8,128)}, f32[1280,768]{1,0:T(8,128)S(1)}, u32[]{:S(2)}) copy-start(f32[1280,768]{1,0:T(8,128)S(1)} %get-tuple-element.42.inputs) | copy-start | bytes 11796484
  14.2 3.3 %copy-start.2 = (bf16[1,1280,768]{2,1,0:T(8,128)(2,1)S(1)}, bf16[1,1280,768]{2,1,0:T(8,128)(2,1)}, u32[]{:S(2)}) copy-start(bf16[1,1280,768]{2,1,0:T(8,128)(2,1)} %param.11) | copy-start | bytes 5898244
  14.6 6.4 %copy-start.3 = (bf16[1280,768]{1,0:T(8,128)(2,1)}, bf16[1280,768]{1,0:T(8,128)(2,1)S(1)}, u32[]{:S(2)}) copy-start(bf16[1280,768]{1,0:T(8,128)(2,1)S(1)} %multiply_convert_fusion.refs_7_) | copy-start | bytes 5898244
  14.7 0.7 copy-start.10
  15.3 0.7 copy-start.12
  16.0 6.4 %collective-permute-start.7 = (bf16[1280,768]{1,0:T(8,128)(2,1)S(1)}, bf16[1280,768]{1,0:T(8,128)(2,1)S(1)}, u32[]{:S(2)}, u32[]{:S(2)}) collective-permute-start(bf16[1280,768]{1,0:T(8,128)(2,1)S(1)} %multiply_convert_fusion.refs_7_), channel_id=1, source_target_pairs={{0,16},{16,0},{1,17},{17,1},{2,18},{18,2},{3,19},{19,3},{4,20},{20... | collective-permute-start | bytes 5898248 | tf_op jit(solution)/shard_map/ppermute | solution.py:28
  17.6 4.9 %collective-permute-start.8 = (bf16[1280,384]{1,0:T(8,128)(2,1)S(1)}, bf16[1280,384]{1,0:T(8,128)(2,1)S(1)}, u32[]{:S(2)}, u32[]{:S(2)}) collective-permute-start(bf16[1280,384]{1,0:T(8,128)(2,1)S(1)} %constant_dynamic-slice_fusion.1), channel_id=1, source_target_pairs={{0,16},{16,0},{1,17},{17,1},{2,18},{18,2},{3,19},{19,3},{4,20},{20... | collective-permute-start | bytes 2949128 | tf_op jit(solution)/shard_map/ppermute | solution.py:28
  19.4 19.5 %collective-permute-start.6 = (bf16[2,2,3,48,384]{4,3,2,1,0:T(8,128)(2,1)}, bf16[2,2,3,48,384]{4,3,2,1,0:T(8,128)(2,1)}, u32[]{:S(2)}, u32[]{:S(2)}) collective-permute-start(bf16[2,2,3,48,384]{4,3,2,1,0:T(8,128)(2,1)} %pad_maximum_fusion), channel_id=1, source_target_pairs={{0,128},{64,192},{128,0},{192,64},{1,129},{65,193},{129,1},{193,65... | collective-permute-start | bytes 1327112 | tf_op jit(solution)/shard_map/ppermute | solution.py:24
  22.5 1.3 copy-start.5
  24.5 14.4 %collective-permute-start.10 = (bf16[160,768]{1,0:T(8,128)(2,1)}, bf16[160,768]{1,0:T(8,128)(2,1)}, u32[]{:S(2)}, u32[]{:S(2)}) collective-permute-start(bf16[160,768]{1,0:T(8,128)(2,1)} %maximum_maximum_fusion.1), channel_id=1, source_target_pairs={{1,0},{2,1},{3,2},{4,3},{5,4},{6,5},{7,6},{8,7},{9,8},{10,9},{11,1... | collective-permute-start | bytes 737288 | tf_op jit(solution)/shard_map/ppermute | solution.py:274
  26.5 12.4 %collective-permute-start.9 = (bf16[160,768]{1,0:T(8,128)(2,1)}, bf16[160,768]{1,0:T(8,128)(2,1)}, u32[]{:S(2)}, u32[]{:S(2)}) collective-permute-start(bf16[160,768]{1,0:T(8,128)(2,1)} %maximum_maximum_fusion), channel_id=1, source_target_pairs={{0,1},{1,2},{2,3},{3,4},{4,5},{5,6},{6,7},{7,8},{8,9},{9,10},{10,1... | collective-permute-start | bytes 737288 | tf_op jit(solution)/shard_map/ppermute | solution.py:273
  31.4 7.5 %collective-permute-start.4 = (bf16[2,3,48,384]{3,2,1,0:T(8,128)(2,1)S(1)}, bf16[2,3,48,384]{3,2,1,0:T(8,128)(2,1)}, u32[]{:S(2)}, u32[]{:S(2)}) collective-permute-start(bf16[2,3,48,384]{3,2,1,0:T(8,128)(2,1)S(1)} %collective-permute-done.1.refs_1_), channel_id=1, source_target_pairs={{0,64},{64,128},{128,192},{192,0},{1,65},{65,129},{129,193},{193,1... | collective-permute-start | bytes 663560 | tf_op jit(solution)/shard_map/ppermute | solution.py:24
  31.9 7.0 %collective-permute-start.5 = (bf16[2,3,48,384]{3,2,1,0:T(8,128)(2,1)S(1)}, bf16[2,3,48,384]{3,2,1,0:T(8,128)(2,1)}, u32[]{:S(2)}, u32[]{:S(2)}) collective-permute-start(bf16[2,3,48,384]{3,2,1,0:T(8,128)(2,1)S(1)} %collective-permute-done.1.refs_1_), channel_id=1, source_target_pairs={{0,192},{64,0},{128,64},{192,128},{1,193},{65,1},{129,65},{193,129... | collective-permute-start | bytes 663560 | tf_op jit(solution)/shard_map/ppermute | solution.py:24
  38.9 1.5 %copy-start.4 = (bf16[1280,768]{1,0:T(8,128)(2,1)S(1)}, bf16[1280,768]{1,0:T(8,128)(2,1)}, u32[]{:S(2)}) copy-start(bf16[1280,768]{1,0:T(8,128)(2,1)} %copy-done.3) | copy-start | bytes 5898244
  40.5 1.5 %copy-start.6 = (bf16[1280,768]{1,0:T(8,128)(2,1)S(1)}, bf16[1280,768]{1,0:T(8,128)(2,1)}, u32[]{:S(2)}) copy-start(bf16[1280,768]{1,0:T(8,128)(2,1)} %copy-done.5) | copy-start | bytes 5898244
  42.0 0.9 copy-start.11
  43.0 0.9 copy-start.13
  61.9 1.2 copy-start.7
  63.2 1.0 copy-start.8
  64.1 1.0 copy-start.14
  65.1 13.8 %copy-start.9 = (bf16[1344,384]{1,0:T(8,128)(2,1)S(1)}, bf16[1344,384]{1,0:T(8,128)(2,1)}, u32[]{:S(2)}) copy-start(bf16[1344,384]{1,0:T(8,128)(2,1)} %copy-done.8) | copy-start | bytes 3096580
  65.1 13.8 %collective-permute-start.12 = (bf16[3,768,384]{2,1,0:T(8,128)(2,1)}, bf16[3,768,384]{2,1,0:T(8,128)(2,1)}, u32[]{:S(2)}, u32[]{:S(2)}) collective-permute-start(bf16[3,768,384]{2,1,0:T(8,128)(2,1)} %get-tuple-element.30.weight_a), channel_id=1, source_target_pairs={{0,16},{16,0},{1,17},{17,1},{2,18},{18,2},{3,19},{19,3},{4,20},{20... | collective-permute-start | bytes 5308424 | tf_op jit(solution)/shard_map/ppermute | solution.py:28
  66.7 35.0 %all-to-all-start = ((bf16[16,3,48,384]{3,2,1,0:T(8,128)(2,1)}), bf16[16,3,48,384]{3,2,1,0:T(8,128)(2,1)}, u32[]{:S(2)}, u32[]{:S(2)}) async-start(bf16[16,3,48,384]{3,2,1,0:T(8,128)(2,1)} %copy-done.7), calls=%async_computation | async-start | bytes 3538944 | tf_op jit(solution)/shard_map/all_to_all | solution.py:286
  75.9 3.0 %collective-permute-start.11 = (bf16[1344,384]{1,0:T(8,128)(2,1)}, bf16[1344,384]{1,0:T(8,128)(2,1)S(1)}, u32[]{:S(2)}, u32[]{:S(2)}) collective-permute-start(bf16[1344,384]{1,0:T(8,128)(2,1)} %copy-done.14), channel_id=1, source_target_pairs={{0,16},{16,0},{1,17},{17,1},{2,18},{18,2},{3,19},{19,3},{4,20},{20... | collective-permute-start | bytes 3096584 | tf_op jit(solution)/shard_map/ppermute | solution.py:28
  78.9 2.1 %copy-start.1 = (f32[1280,768]{1,0:T(8,128)S(1)}, f32[1280,768]{1,0:T(8,128)}, u32[]{:S(2)}) copy-start(f32[1280,768]{1,0:T(8,128)} %copy-done) | copy-start | bytes 11796484
  103.4 5.0 %collective-permute-start.13 = (bf16[3,48,384]{2,1,0:T(8,128)(2,1)S(1)}, bf16[3,48,384]{2,1,0:T(8,128)(2,1)S(1)}, u32[]{:S(2)}, u32[]{:S(2)}) collective-permute-start(bf16[3,48,384]{2,1,0:T(8,128)(2,1)S(1)} %reduce_sum.22), channel_id=1, source_target_pairs={{0,1},{1,0},{2,3},{3,2},{4,5},{5,4},{6,7},{7,6},{8,9},{9,8},{10,11... | collective-permute-start | bytes 331784 | tf_op jit(solution)/shard_map/ppermute | solution.py:28
  103.7 7.1 %collective-permute-start.14 = (bf16[3,48,384]{2,1,0:T(8,128)(2,1)S(1)}, bf16[3,48,384]{2,1,0:T(8,128)(2,1)S(1)}, u32[]{:S(2)}, u32[]{:S(2)}) collective-permute-start(bf16[3,48,384]{2,1,0:T(8,128)(2,1)S(1)} %reduce_sum.22), channel_id=1, source_target_pairs={{0,2},{1,3},{2,0},{3,1},{4,6},{5,7},{6,4},{7,5},{8,10},{9,11},{10,... | collective-permute-start | bytes 331784 | tf_op jit(solution)/shard_map/ppermute | solution.py:28
  104.2 6.6 %collective-permute-start.15 = (bf16[3,48,384]{2,1,0:T(8,128)(2,1)S(1)}, bf16[3,48,384]{2,1,0:T(8,128)(2,1)S(1)}, u32[]{:S(2)}, u32[]{:S(2)}) collective-permute-start(bf16[3,48,384]{2,1,0:T(8,128)(2,1)S(1)} %reduce_sum.22), channel_id=1, source_target_pairs={{0,3},{1,2},{2,1},{3,0},{4,7},{5,6},{6,5},{7,4},{8,11},{9,10},{10,... | collective-permute-start | bytes 331784 | tf_op jit(solution)/shard_map/ppermute | solution.py:28
  110.9 6.9 %collective-permute-start.16 = (bf16[3,48,384]{2,1,0:T(8,128)(2,1)S(1)}, bf16[3,48,384]{2,1,0:T(8,128)(2,1)S(1)}, u32[]{:S(2)}, u32[]{:S(2)}) collective-permute-start(bf16[3,48,384]{2,1,0:T(8,128)(2,1)S(1)} %add_convert_fusion.1), channel_id=1, source_target_pairs={{0,7},{1,6},{2,5},{3,4},{4,3},{5,2},{6,1},{7,0},{8,15},{9,14},{10,... | collective-permute-start | bytes 331784 | tf_op jit(solution)/shard_map/ppermute | solution.py:28
  117.8 7.7 %collective-permute-start.17 = (bf16[3,48,384]{2,1,0:T(8,128)(2,1)S(1)}, bf16[3,48,384]{2,1,0:T(8,128)(2,1)S(1)}, u32[]{:S(2)}, u32[]{:S(2)}) collective-permute-start(bf16[3,48,384]{2,1,0:T(8,128)(2,1)S(1)} %add_convert_fusion), channel_id=1, source_target_pairs={{16,0},{8,24},{0,8},{24,16},{17,1},{9,25},{1,9},{25,17},{18,2},{10... | collective-permute-start | bytes 331784 | tf_op jit(solution)/shard_map/ppermute | solution.py:225
  123.4 6.1 %collective-permute-start.18 = (bf16[3,48,384]{2,1,0:T(8,128)(2,1)S(1)}, bf16[3,48,384]{2,1,0:T(8,128)(2,1)S(1)}, u32[]{:S(2)}, u32[]{:S(2)}) collective-permute-start(bf16[3,48,384]{2,1,0:T(8,128)(2,1)S(1)} %add_convert_fusion), channel_id=1, source_target_pairs={{16,8},{8,16},{17,9},{9,17},{18,10},{10,18},{19,11},{11,19},{20,12... | collective-permute-start | bytes 331784 | tf_op jit(solution)/shard_map/ppermute | solution.py:226

commit v6 on v5

--- a/solution.py
+++ b/solution.py
@@ -62,10 +62,10 @@
 def forward_kernel(position, *refs):
     pieces, refs = refs[:7], refs[7:]
     normed_hbm, edges, upstream_hbm = refs[0:2], refs[2:4], refs[4:6]
-    weight_out, back_out, grad_out = refs[6], refs[7:9], refs[9]
-    weight, normed, upstream, back, grad = refs[10:15]
-    piece_sem, load_sem, back_sem, weight_sem, grad_sem = refs[15:]
-    core = position[2]
+    weight_out, back_out, grad_out = refs[6], refs[7:9], refs[9:13]
+    weight, normed, upstream, back, grad = refs[13:18]
+    piece_sem, load_sem, back_sem, weight_sem, grad_sem = refs[18:]
+    x, core = position[0], position[2]
     channels, half = weight.shape[1:]
     count = normed_hbm[0].shape[0]
     lane = pl.multiple_of(core * half, 128)
@@ -135,12 +135,11 @@
         total = part if total is None else total + part
     for tap in range(FILTER_TAPS):
         grad[tap] = total[:, tap * half : (tap + 1) * half].astype(BF16)
-    owners, _, rows, _ = grad_out.shape
-    for owner in range(owners):
+    quarter = channels // 4
+    for step in range(4):
+        place = pl.multiple_of(((x + step) % 4) * quarter, 16)
         grad_save = pltpu.make_async_copy(
-            grad.at[:, owner * rows : (owner + 1) * rows, :],
-            grad_out.at[owner],
-            grad_sem.at[owner],
+            grad.at[:, pl.ds(place, quarter), :], grad_out[step], grad_sem.at[step]
         )
         grad_save.start()
         saves.append(grad_save)
@@ -158,9 +157,9 @@
         forward_kernel,
         out_shape=[jax.ShapeDtypeStruct((FILTER_TAPS, channels, half), BF16)]
         + [jax.ShapeDtypeStruct((length, half), BF16)] * 2
-        + [jax.ShapeDtypeStruct((16, FILTER_TAPS, channels // 16, half), BF16)],
+        + [jax.ShapeDtypeStruct((FILTER_TAPS, channels // 4, half), BF16)] * 4,
         in_specs=[pl.BlockSpec(memory_space=pltpu.SMEM)] + [anywhere] * 13,
-        out_specs=[anywhere] * 4,
+        out_specs=[anywhere] * 7,
         scratch_shapes=[
             pltpu.VMEM((FILTER_TAPS, channels, half), BF16),
             pltpu.VMEM((2, length + 2 * REACH, channels), BF16),
@@ -171,7 +170,7 @@
             dma((2, 6)),
             dma((2,)),
             dma,
-            dma((16,)),
+            dma((4,)),
         ],
         compiler_params=pltpu.CompilerParams(vmem_limit_bytes=26 * 1024 * 1024),
         name="forward",
@@ -233,6 +232,7 @@
 
 def on_device(activations, nucleotides, base_table, norm_gain, filter_weight, upstream):
     x, yh, core, yl = (lax.axis_index(name) for name in ("x", "yh", "core", "yl"))
+    y = yh * 2 + yl
     position = jnp.stack([x, yh, core, yl]).astype(jnp.int32)
     tokens, incoming = activations[0], upstream[0]
     count, channels = tokens.shape
@@ -273,7 +273,7 @@
         lax.ppermute(last, SEQ, [(i, i + 1) for i in range(15)]),
         lax.ppermute(first, SEQ, [(i + 1, i) for i in range(15)]),
     )
-    weight, back, back_other, grads = forward(
+    weight, back, back_other, *grads = forward(
         position,
         [own, across, up_own, up_across, down_own, down_across, far],
         (normed, normed_other),
@@ -283,12 +283,21 @@
 
     back_rest = swap(back_other, "core", 2, 1)
     weight_rest = swap(weight, "core", 2, 1)
-    arrived = lax.all_to_all(grads, ("x", "yh", "yl"), 0, 0, tiled=True)
+    along_x = [grads[0]] + [shift(grads[step], "x", 4, step) for step in (1, 3, 2)]
     result = backward(
         (back, back_rest), (weight, weight_rest), inputs, scale_inv, norm_gain[None], incoming
     )
-    result, arrived = join(result, arrived)
-    total = jnp.sum(arrived.astype(F32), axis=0)
+    result, *along_x = join(result, *along_x)
+
+    rows = channels // 16
+    by_y = []
+    for step in range(4):
+        start = ((y + step) % 4) * rows
+        parts = [lax.dynamic_slice_in_dim(part, start, rows, axis=1) for part in along_x]
+        by_y.append(sum(part.astype(F32) for part in parts))
+    total = by_y[0]
+    for step in (1, 3, 2):
+        total = total + shift(by_y[step].astype(BF16), RING_Y, 4, step).astype(F32)
     weight_grad = share_weight_grad(total, yl, core)
     total_rows = 16 * 16 * count
     return (result[None], weight_grad / math.sqrt(total_rows))

time: 131 us -> 129 us (0.985)
  waiting for transfers between devices: 29.2 us -> 27.4 us
    ppermute x5 -> x11, starting transfers between devices: 6.89 us -> 18 us  [shift(): return lax.ppermute(value, axis, pairs)]
    all_to_all x1 -> x0, waiting for transfers between devices: 11 us -> none  [on_device(): arrived = lax.all_to_all(grads, ('x', 'yh', 'yl'), 0, 0, tiled=True)]
    all_to_all x1 -> x0, starting transfers between devices: 9.14 us -> none  [on_device(): arrived = lax.all_to_all(grads, ('x', 'yh', 'yl'), 0, 0, tiled=True)]
    ppermute x5 -> x11, waiting for transfers between devices: 4.78 us -> 13.8 us  [shift(): return lax.ppermute(value, axis, pairs)]
    convert_element_type x0 -> x2, other arithmetic: none -> 2.57 us  [the longest x1 1.46 us: on_device(): total = total + shift(by_y[step].astype(BF16), RING_Y, 4, step).astype(F32)]
    ppermute x10, starting transfers between devices: 17.6 us -> 15.3 us  [swap(): return lax.ppermute(value, axis, [(i, i ^ mask) for i in range(count)])]
    reduce_sum x1 -> x0, other arithmetic: 1.73 us -> none  [on_device(): total = jnp.sum(arrived.astype(F32), axis=0)]
  transfers between devices with their start and end apart: 20 -> 25, of which waited for: 9 -> 13; matrix products, arithmetic and copies ran while one was open for 6% -> 7% of each run, Pallas kernels for 7% -> 7%
where the time goes in v6:
time: 129 us; the launch traced here: 128 us
  starting transfers between devices  47.3 us (37%)
  waiting for transfers between devices  27.4 us (21%)
  Pallas kernels  26.7 us (21%)
  local copies, waits for them, and re-layouts  15.1 us (12%)
  other arithmetic  10.7 us (8%)
    ppermute x11, starting transfers between devices, shift(): return lax.ppermute(value, axis, pairs)  18 us
    pallas_call x1, Pallas kernels, forward(): pl.pallas_call(forward_kernel, out_shape=[jax.ShapeDtypeStruct((FILTER_TA...  17.2 us
    ppermute x10, starting transfers between devices, swap(): return lax.ppermute(value, axis, [(i, i ^ mask) for i in range(count)])  15.3 us
    ppermute x11, waiting for transfers between devices, shift(): return lax.ppermute(value, axis, pairs)  13.8 us
    unnamed x32, local copies, waits for them, and re-layouts  12.8 us
    ppermute x10, waiting for transfers between devices, swap(): return lax.ppermute(value, axis, [(i, i ^ mask) for i in range(count)])  10.1 us
    pallas_call x1, Pallas kernels, backward(): pl.pallas_call(backward_kernel, grid=(count // block,), out_shape=jax.Sha...  9.51 us
    ppermute x1, starting transfers between devices, share_weight_grad(): first = lax.ppermute(mine, pair, [(2, 0), (1, 3), (0, 1), (3, 2)])  5.3 us
  transfers between devices with their start and end apart: 25, of which 13 were waited for; matrix products, arithmetic and copies ran while one was open for 7% of the time, Pallas kernels for 7%

profile of v6, /device:TPU:1, one launch (start us, length us, event | category | flops | bytes accessed | tf_op | source)
XLA Modules:
  0.0 128.1 jit_solution(3373587602378127956)
XLA Ops:
  0.6 1.0 dynamic-slice_bitcast_fusion
  1.6 3.3 %collective-permute-start = (bf16[3,48,384]{2,1,0:T(8,128)(2,1)S(1)}, bf16[3,48,384]{2,1,0:T(8,128)(2,1)S(1)}, u32[]{:S(2)}, u32[]{:S(2)}) collective-permute-start(bf16[3,48,384]{2,1,0:T(8,128)(2,1)S(1)} %get-tuple-element.69), channel_id=1, source_target_pairs={{0,16},{16,0},{1,17},{17,1},{2,18},{18,2},{3,19},{19,3},{4,20},{20... | collective-permute-start | bytes 331784 | tf_op jit(solution)/shard_map/ppermute | solution.py:28
  5.0 0.9 slice_reduce_fusion.3
  5.9 0.1 collective-permute-done
  6.0 1.1 collective-permute-start.1
  7.0 1.2 collective-permute-start.2
  8.2 1.5 %collective-permute-start.3 = (bf16[2,3,48,384]{3,2,1,0:T(8,128)(2,1)S(1)}, bf16[2,3,48,384]{3,2,1,0:T(8,128)(2,1)S(1)}, u32[]{:S(2)}, u32[]{:S(2)}) collective-permute-start(bf16[2,3,48,384]{3,2,1,0:T(8,128)(2,1)S(1)} %pad_maximum_fusion.1.refs_0_), channel_id=1, source_target_pairs={{0,192},{64,0},{128,64},{192,128},{1,193},{65,1},{129,65},{193,129... | collective-permute-start | bytes 663560 | tf_op jit(solution)/shard_map/ppermute | solution.py:24
  9.7 0.7 compare_reduce_fusion.2
  10.5 3.7 %multiply_reduce_fusion = (f32[1280]{0:T(1024)S(1)}, f32[1280,768]{1,0:T(8,128)S(1)}) fusion(f32[768]{0:T(1024)S(1)} %get-tuple-element.48, f32[768]{0:T(1024)S(1)} %get-tuple-element.49, pred[1280]{0:T(1024)(128)(4,1)S(1)} %get-tuple-element.51, f32[768]{0:T(1024)S(1)} %get-tuple-element.47, pred[1280]{0:T(1024)(128)(4,1)S(1)} %get-tuple-element.52, ...), kind=kLoop, calls=%fused_computation.1 | loop fusion | flops 6880000 | bytes 5919488 | tf_op jit(solution)/shard_map/reduce_sum | solution.py:253
  14.2 0.4 multiply_convert_fusion.refs_7_
  14.7 0.7 copy-done.11
  15.3 0.7 copy-done.13
  16.1 1.4 %collective-permute-start.7 = (bf16[1280,768]{1,0:T(8,128)(2,1)S(1)}, bf16[1280,768]{1,0:T(8,128)(2,1)S(1)}, u32[]{:S(2)}, u32[]{:S(2)}) collective-permute-start(bf16[1280,768]{1,0:T(8,128)(2,1)S(1)} %multiply_convert_fusion.refs_7_), channel_id=1, source_target_pairs={{0,16},{16,0},{1,17},{17,1},{2,18},{18,2},{3,19},{19,3},{4,20},{20... | collective-permute-start | bytes 5898248 | tf_op jit(solution)/shard_map/ppermute | solution.py:28
  17.5 0.1 constant_dynamic-slice_fusion.1
  17.6 1.0 collective-permute-start.8
  18.6 0.8 pad_maximum_fusion
  19.4 1.5 %collective-permute-start.6 = (bf16[2,2,3,48,384]{4,3,2,1,0:T(8,128)(2,1)}, bf16[2,2,3,48,384]{4,3,2,1,0:T(8,128)(2,1)}, u32[]{:S(2)}, u32[]{:S(2)}) collective-permute-start(bf16[2,2,3,48,384]{4,3,2,1,0:T(8,128)(2,1)} %pad_maximum_fusion), channel_id=1, source_target_pairs={{0,128},{64,192},{128,0},{192,64},{1,129},{65,193},{129,1},{193,65... | collective-permute-start | bytes 1327112 | tf_op jit(solution)/shard_map/ppermute | solution.py:24
  21.0 1.5 %collective-permute-done.8.refs_12_ = bf16[1280,384]{1,0:T(8,128)(2,1)S(1)} collective-permute-done((bf16[1280,384]{1,0:T(8,128)(2,1)S(1)}, bf16[1280,384]{1,0:T(8,128)(2,1)S(1)}, u32[]{:S(2)}, u32[]{:S(2)}) %collective-permute-start.8) | collective-permute-done | bytes 983072 | tf_op jit(solution)/shard_map/ppermute | solution.py:28
  22.6 1.3 copy-done.5
  23.8 0.7 maximum_maximum_fusion.1
  24.6 1.3 collective-permute-start.10
  25.8 0.7 maximum_maximum_fusion
  26.6 4.9 %collective-permute-start.9 = (bf16[160,768]{1,0:T(8,128)(2,1)}, bf16[160,768]{1,0:T(8,128)(2,1)}, u32[]{:S(2)}, u32[]{:S(2)}) collective-permute-start(bf16[160,768]{1,0:T(8,128)(2,1)} %maximum_maximum_fusion), channel_id=1, source_target_pairs={{0,1},{1,2},{2,3},{3,4},{4,5},{5,6},{6,7},{7,8},{8,9},{9,10},{10,1... | collective-permute-start | bytes 737288 | tf_op jit(solution)/shard_map/ppermute | solution.py:273
  31.4 0.5 collective-permute-start.4
  32.0 2.1 %collective-permute-start.5 = (bf16[2,3,48,384]{3,2,1,0:T(8,128)(2,1)S(1)}, bf16[2,3,48,384]{3,2,1,0:T(8,128)(2,1)}, u32[]{:S(2)}, u32[]{:S(2)}) collective-permute-start(bf16[2,3,48,384]{3,2,1,0:T(8,128)(2,1)S(1)} %collective-permute-done.1.refs_1_), channel_id=1, source_target_pairs={{0,192},{64,0},{128,64},{192,128},{1,193},{65,1},{129,65},{193,129... | collective-permute-start | bytes 663560 | tf_op jit(solution)/shard_map/ppermute | solution.py:24
  34.1 0.1 pad_add_fusion.position
  34.2 4.8 %collective-permute-done.4.refs_3_ = bf16[2,3,48,384]{3,2,1,0:T(8,128)(2,1)} collective-permute-done((bf16[2,3,48,384]{3,2,1,0:T(8,128)(2,1)S(1)}, bf16[2,3,48,384]{3,2,1,0:T(8,128)(2,1)}, u32[]{:S(2)}, u32[]{:S(2)}) %collective-permute-start.4) | collective-permute-done | bytes 221216 | tf_op jit(solution)/shard_map/ppermute | solution.py:24
  39.0 1.5 %copy-done.4 = bf16[1280,768]{1,0:T(8,128)(2,1)S(1)} copy-done((bf16[1280,768]{1,0:T(8,128)(2,1)S(1)}, bf16[1280,768]{1,0:T(8,128)(2,1)}, u32[]{:S(2)}) %copy-start.4) | copy-done | bytes 1966104
  40.5 1.5 %copy-done.6 = bf16[1280,768]{1,0:T(8,128)(2,1)S(1)} copy-done((bf16[1280,768]{1,0:T(8,128)(2,1)S(1)}, bf16[1280,768]{1,0:T(8,128)(2,1)}, u32[]{:S(2)}) %copy-start.6) | copy-done | bytes 1966104
  42.1 0.9 copy-done.12
  43.0 0.9 copy-done.14
  43.9 17.2 %forward.1 = (bf16[3,768,384]{2,1,0:T(8,128)(2,1)}, bf16[1344,384]{1,0:T(8,128)(2,1)S(1)}, bf16[1344,384]{1,0:T(8,128)(2,1)}, bf16[3,192,384]{2,1,0:T(8,128)(2,1...) custom-call(s32[4]{0:T(128)S(1)} %pad_add_fusion.position, ...), custom_call_target="tpu_custom_call" | custom-call | tf_op jit(solution)/shard_map/forward/pallas_call | solution.py:156
  61.1 1.1 copy-done.7
  62.2 0.8 copy-done.9
  63.0 1.6 %collective-permute-start.12 = (bf16[3,768,384]{2,1,0:T(8,128)(2,1)}, bf16[3,768,384]{2,1,0:T(8,128)(2,1)}, u32[]{:S(2)}, u32[]{:S(2)}) collective-permute-start(bf16[3,768,384]{2,1,0:T(8,128)(2,1)} %get-tuple-element.36.weight_a), channel_id=1, source_target_pairs={{0,16},{16,0},{1,17},{17,1},{2,18},{18,2},{3,19},{19,3},{4,20},{20... | collective-permute-start | bytes 5308424 | tf_op jit(solution)/shard_map/ppermute | solution.py:28
  64.6 0.2 collective-permute-start.13
  64.8 2.4 %collective-permute-start.14 = (bf16[3,192,384]{2,1,0:T(8,128)(2,1)}, bf16[3,192,384]{2,1,0:T(8,128)(2,1)}, u32[]{:S(2)}, u32[]{:S(2)}) collective-permute-start(bf16[3,192,384]{2,1,0:T(8,128)(2,1)} %get-tuple-element.39), channel_id=1, source_target_pairs={{0,192},{64,0},{128,64},{192,128},{1,193},{65,1},{129,65},{193,129... | collective-permute-start | bytes 1327112 | tf_op jit(solution)/shard_map/ppermute | solution.py:24
  67.3 1.2 collective-permute-start.15
  68.5 0.2 rsqrt.7.scale
  68.7 0.8 collective-permute-done.11.back_b
  69.5 0.3 collective-permute-done.12.weight_b
  69.8 2.1 %copy-done.1 = f32[1280,768]{1,0:T(8,128)S(1)} copy-done((f32[1280,768]{1,0:T(8,128)S(1)}, f32[1280,768]{1,0:T(8,128)}, u32[]{:S(2)}) %copy-start.1) | copy-done | bytes 3932184
  71.9 1.2 copy-done.8
  73.1 9.5 %backward.1 = bf16[1280,768]{1,0:T(8,128)(2,1)} custom-call(bf16[1344,384]{1,0:T(8,128)(2,1)S(1)} %copy-done.8, bf16[1344,384]{1,0:T(8,128)(2,1)S(1)} %collective-permute-done.11.back_b, bf16[3,768,384]{2,1,0:T(8,128)(2,1)} %get-tuple-element.36.weight_a, bf16[3,768,384]{2,1,0:T(8,128)(2,1)} %collective-permute-done.12.weight_b, f32[1280,768]{1,0:T(8,128)S(1)} %copy-done.1, ...), custom_call_target="tpu_custom_call" | custom-call | tf_op jit(solution)/shard_map/backward/pallas_call | solution.py:206
  82.6 5.4 %collective-permute-done.15 = bf16[3,192,384]{2,1,0:T(8,128)(2,1)} collective-permute-done((bf16[3,192,384]{2,1,0:T(8,128)(2,1)}, bf16[3,192,384]{2,1,0:T(8,128)(2,1)}, u32[]{:S(2)}, u32[]{:S(2)}) %collective-permute-start.15) | collective-permute-done | bytes 442400 | tf_op jit(solution)/shard_map/ppermute | solution.py:24
  88.0 1.5 %add_convert_fusion.5 = (bf16[3,48,384]{2,1,0:T(8,128)(2,1)S(1)}, bf16[3,48,384]{2,1,0:T(8,128)(2,1)S(1)}, bf16[3,48,384]{2,1,0:T(8,128)(2,1)S(1)}) fusion(bf16[3,192,384]{2,1,0:T(8,128)(2,1)} %collective-permute-done.15, s32[]{:T(128)S(6)} %select_n.95, bf16[3,192,384]{2,1,0:T(8,128)(2,1)} %collective-permute-done.14, ...), kind=kLoop, calls=%fused_computation.13 | loop fusion | flops 1327104 | bytes 1658892 | tf_op jit(solution)/shard_map/convert_element_type | solution.py:300
  89.5 5.4 %collective-permute-start.16 = (bf16[3,48,384]{2,1,0:T(8,128)(2,1)S(1)}, bf16[3,48,384]{2,1,0:T(8,128)(2,1)S(1)}, u32[]{:S(2)}, u32[]{:S(2)}) collective-permute-start(bf16[3,48,384]{2,1,0:T(8,128)(2,1)S(1)} %get-tuple-element.61), channel_id=1, source_target_pairs={{0,8},{8,32},{32,40},{40,0},{1,9},{9,33},{33,41},{41,1},{2,10},{10... | collective-permute-start | bytes 331784 | tf_op jit(solution)/shard_map/ppermute | solution.py:24
  94.9 1.9 %collective-permute-start.18 = (bf16[3,48,384]{2,1,0:T(8,128)(2,1)S(1)}, bf16[3,48,384]{2,1,0:T(8,128)(2,1)S(1)}, u32[]{:S(2)}, u32[]{:S(2)}) collective-permute-start(bf16[3,48,384]{2,1,0:T(8,128)(2,1)S(1)} %get-tuple-element.62), channel_id=1, source_target_pairs={{0,32},{8,40},{32,0},{40,8},{1,33},{9,41},{33,1},{41,9},{2,34},{10... | collective-permute-start | bytes 331784 | tf_op jit(solution)/shard_map/ppermute | solution.py:24
  96.8 1.7 %collective-permute-done.17 = bf16[3,48,384]{2,1,0:T(8,128)(2,1)S(1)} collective-permute-done((bf16[3,48,384]{2,1,0:T(8,128)(2,1)S(1)}, bf16[3,48,384]{2,1,0:T(8,128)(2,1)S(1)}, u32[]{:S(2)}, u32[]{:S(2)}) %collective-permute-start.17) | collective-permute-done | bytes 110624 | tf_op jit(solution)/shard_map/ppermute | solution.py:24
  98.5 1.9 %collective-permute-done.18 = bf16[3,48,384]{2,1,0:T(8,128)(2,1)S(1)} collective-permute-done((bf16[3,48,384]{2,1,0:T(8,128)(2,1)S(1)}, bf16[3,48,384]{2,1,0:T(8,128)(2,1)S(1)}, u32[]{:S(2)}, u32[]{:S(2)}) %collective-permute-start.18) | collective-permute-done | bytes 110624 | tf_op jit(solution)/shard_map/ppermute | solution.py:24
  100.4 1.1 add_convert_fusion.2
  101.5 0.1 collective-permute-start.19
  101.6 2.2 %collective-permute-start.20 = (bf16[3,48,384]{2,1,0:T(8,128)(2,1)S(1)}, bf16[3,48,384]{2,1,0:T(8,128)(2,1)S(1)}, u32[]{:S(2)}, u32[]{:S(2)}) collective-permute-start(bf16[3,48,384]{2,1,0:T(8,128)(2,1)S(1)} %add_convert_fusion.2), channel_id=1, source_target_pairs={{0,2},{1,3},{2,0},{3,1},{4,6},{5,7},{6,4},{7,5},{8,10},{9,11},{10,... | collective-permute-start | bytes 331784 | tf_op jit(solution)/shard_map/ppermute | solution.py:28
  103.8 1.3 %collective-permute-start.21 = (bf16[3,48,384]{2,1,0:T(8,128)(2,1)S(1)}, bf16[3,48,384]{2,1,0:T(8,128)(2,1)S(1)}, u32[]{:S(2)}, u32[]{:S(2)}) collective-permute-start(bf16[3,48,384]{2,1,0:T(8,128)(2,1)S(1)} %add_convert_fusion.2), channel_id=1, source_target_pairs={{0,3},{1,2},{2,1},{3,0},{4,7},{5,6},{6,5},{7,4},{8,11},{9,10},{10,... | collective-permute-start | bytes 331784 | tf_op jit(solution)/shard_map/ppermute | solution.py:28
  105.1 1.2 collective-permute-done.19
  106.3 1.2 collective-permute-done.20
  107.5 3.0 %collective-permute-done.21 = bf16[3,48,384]{2,1,0:T(8,128)(2,1)S(1)} collective-permute-done((bf16[3,48,384]{2,1,0:T(8,128)(2,1)S(1)}, bf16[3,48,384]{2,1,0:T(8,128)(2,1)S(1)}, u32[]{:S(2)}, u32[]{:S(2)}) %collective-permute-start.21) | collective-permute-done | bytes 110624 | tf_op jit(solution)/shard_map/ppermute | solution.py:28
  110.5 0.1 add_convert_fusion.1
  110.5 3.2 %collective-permute-start.22 = (bf16[3,48,384]{2,1,0:T(8,128)(2,1)S(1)}, bf16[3,48,384]{2,1,0:T(8,128)(2,1)S(1)}, u32[]{:S(2)}, u32[]{:S(2)}) collective-permute-start(bf16[3,48,384]{2,1,0:T(8,128)(2,1)S(1)} %add_convert_fusion.1), channel_id=1, source_target_pairs={{0,7},{1,6},{2,5},{3,4},{4,3},{5,2},{6,1},{7,0},{8,15},{9,14},{10,... | collective-permute-start | bytes 331784 | tf_op jit(solution)/shard_map/ppermute | solution.py:28
  113.8 2.1 %collective-permute-done.22 = bf16[3,48,384]{2,1,0:T(8,128)(2,1)S(1)} collective-permute-done((bf16[3,48,384]{2,1,0:T(8,128)(2,1)S(1)}, bf16[3,48,384]{2,1,0:T(8,128)(2,1)S(1)}, u32[]{:S(2)}, u32[]{:S(2)}) %collective-permute-start.22) | collective-permute-done | bytes 110624 | tf_op jit(solution)/shard_map/ppermute | solution.py:28
  115.9 5.3 %collective-permute-start.23 = (bf16[3,48,384]{2,1,0:T(8,128)(2,1)S(1)}, bf16[3,48,384]{2,1,0:T(8,128)(2,1)S(1)}, u32[]{:S(2)}, u32[]{:S(2)}) collective-permute-start(bf16[3,48,384]{2,1,0:T(8,128)(2,1)S(1)} %add_convert_fusion), channel_id=1, source_target_pairs={{16,0},{8,24},{0,8},{24,16},{17,1},{9,25},{1,9},{25,17},{18,2},{10... | collective-permute-start | bytes 331784 | tf_op jit(solution)/shard_map/ppermute | solution.py:224
  121.2 2.6 %collective-permute-start.24 = (bf16[3,48,384]{2,1,0:T(8,128)(2,1)S(1)}, bf16[3,48,384]{2,1,0:T(8,128)(2,1)S(1)}, u32[]{:S(2)}, u32[]{:S(2)}) collective-permute-start(bf16[3,48,384]{2,1,0:T(8,128)(2,1)S(1)} %add_convert_fusion), channel_id=1, source_target_pairs={{16,8},{8,16},{17,9},{9,17},{18,10},{10,18},{19,11},{11,19},{20,12... | collective-permute-start | bytes 331784 | tf_op jit(solution)/shard_map/ppermute | solution.py:225
  123.8 3.5 %collective-permute-done.24 = bf16[3,48,384]{2,1,0:T(8,128)(2,1)S(1)} collective-permute-done((bf16[3,48,384]{2,1,0:T(8,128)(2,1)S(1)}, bf16[3,48,384]{2,1,0:T(8,128)(2,1)S(1)}, u32[]{:S(2)}, u32[]{:S(2)}) %collective-permute-start.24) | collective-permute-done | bytes 110624 | tf_op jit(solution)/shard_map/ppermute | solution.py:225
  127.3 0.8 convert_multiply_fusion
  (46 shorter events, 0.3 us)
Async XLA Ops:
  0.6 13.6 %copy-start.15 = (f32[768]{0:T(1024)S(1)}, f32[768]{0:T(1024)}, u32[]{:S(2)}) copy-start(f32[768]{0:T(1024)} %param.9) | copy-start | bytes 9220
  1.6 4.3 %collective-permute-start = (bf16[3,48,384]{2,1,0:T(8,128)(2,1)S(1)}, bf16[3,48,384]{2,1,0:T(8,128)(2,1)S(1)}, u32[]{:S(2)}, u32[]{:S(2)}) collective-permute-start(bf16[3,48,384]{2,1,0:T(8,128)(2,1)S(1)} %get-tuple-element.69), channel_id=1, source_target_pairs={{0,16},{16,0},{1,17},{17,1},{2,18},{18,2},{3,19},{19,3},{4,20},{20... | collective-permute-start | bytes 331784 | tf_op jit(solution)/shard_map/ppermute | solution.py:28
  6.0 8.7 %collective-permute-start.1 = (bf16[2,3,48,384]{3,2,1,0:T(8,128)(2,1)S(1)}, bf16[2,3,48,384]{3,2,1,0:T(8,128)(2,1)S(1)}, u32[]{:S(2)}, u32[]{:S(2)}) collective-permute-start(bf16[2,3,48,384]{3,2,1,0:T(8,128)(2,1)S(1)} %pad_maximum_fusion.1.refs_0_), channel_id=1, source_target_pairs={{0,40},{8,32},{32,8},{40,0},{1,41},{9,33},{33,9},{41,1},{2,42},{10... | collective-permute-start | bytes 663560 | tf_op jit(solution)/shard_map/ppermute | solution.py:28
  7.0 7.6 %collective-permute-start.2 = (bf16[2,3,48,384]{3,2,1,0:T(8,128)(2,1)S(1)}, bf16[2,3,48,384]{3,2,1,0:T(8,128)(2,1)S(1)}, u32[]{:S(2)}, u32[]{:S(2)}) collective-permute-start(bf16[2,3,48,384]{3,2,1,0:T(8,128)(2,1)S(1)} %pad_maximum_fusion.1.refs_0_), channel_id=1, source_target_pairs={{0,64},{64,128},{128,192},{192,0},{1,65},{65,129},{129,193},{193,1... | collective-permute-start | bytes 663560 | tf_op jit(solution)/shard_map/ppermute | solution.py:24
  8.2 7.1 %collective-permute-start.3 = (bf16[2,3,48,384]{3,2,1,0:T(8,128)(2,1)S(1)}, bf16[2,3,48,384]{3,2,1,0:T(8,128)(2,1)S(1)}, u32[]{:S(2)}, u32[]{:S(2)}) collective-permute-start(bf16[2,3,48,384]{3,2,1,0:T(8,128)(2,1)S(1)} %pad_maximum_fusion.1.refs_0_), channel_id=1, source_target_pairs={{0,192},{64,0},{128,64},{192,128},{1,193},{65,1},{129,65},{193,129... | collective-permute-start | bytes 663560 | tf_op jit(solution)/shard_map/ppermute | solution.py:24
  14.2 3.4 %copy-start = (f32[1280,768]{1,0:T(8,128)}, f32[1280,768]{1,0:T(8,128)S(1)}, u32[]{:S(2)}) copy-start(f32[1280,768]{1,0:T(8,128)S(1)} %get-tuple-element.54.inputs) | copy-start | bytes 11796484
  14.2 3.3 %copy-start.2 = (bf16[1,1280,768]{2,1,0:T(8,128)(2,1)S(1)}, bf16[1,1280,768]{2,1,0:T(8,128)(2,1)}, u32[]{:S(2)}) copy-start(bf16[1,1280,768]{2,1,0:T(8,128)(2,1)} %param.11) | copy-start | bytes 5898244
  14.6 6.4 %copy-start.3 = (bf16[1280,768]{1,0:T(8,128)(2,1)}, bf16[1280,768]{1,0:T(8,128)(2,1)S(1)}, u32[]{:S(2)}) copy-start(bf16[1280,768]{1,0:T(8,128)(2,1)S(1)} %multiply_convert_fusion.refs_7_) | copy-start | bytes 5898244
  14.7 0.7 copy-start.11
  15.3 0.7 copy-start.13
  16.1 6.4 %collective-permute-start.7 = (bf16[1280,768]{1,0:T(8,128)(2,1)S(1)}, bf16[1280,768]{1,0:T(8,128)(2,1)S(1)}, u32[]{:S(2)}, u32[]{:S(2)}) collective-permute-start(bf16[1280,768]{1,0:T(8,128)(2,1)S(1)} %multiply_convert_fusion.refs_7_), channel_id=1, source_target_pairs={{0,16},{16,0},{1,17},{17,1},{2,18},{18,2},{3,19},{19,3},{4,20},{20... | collective-permute-start | bytes 5898248 | tf_op jit(solution)/shard_map/ppermute | solution.py:28
  17.6 4.9 %collective-permute-start.8 = (bf16[1280,384]{1,0:T(8,128)(2,1)S(1)}, bf16[1280,384]{1,0:T(8,128)(2,1)S(1)}, u32[]{:S(2)}, u32[]{:S(2)}) collective-permute-start(bf16[1280,384]{1,0:T(8,128)(2,1)S(1)} %constant_dynamic-slice_fusion.1), channel_id=1, source_target_pairs={{0,16},{16,0},{1,17},{17,1},{2,18},{18,2},{3,19},{19,3},{4,20},{20... | collective-permute-start | bytes 2949128 | tf_op jit(solution)/shard_map/ppermute | solution.py:28
  19.4 19.5 %collective-permute-start.6 = (bf16[2,2,3,48,384]{4,3,2,1,0:T(8,128)(2,1)}, bf16[2,2,3,48,384]{4,3,2,1,0:T(8,128)(2,1)}, u32[]{:S(2)}, u32[]{:S(2)}) collective-permute-start(bf16[2,2,3,48,384]{4,3,2,1,0:T(8,128)(2,1)} %pad_maximum_fusion), channel_id=1, source_target_pairs={{0,128},{64,192},{128,0},{192,64},{1,129},{65,193},{129,1},{193,65... | collective-permute-start | bytes 1327112 | tf_op jit(solution)/shard_map/ppermute | solution.py:24
  22.6 1.3 %copy-start.5 = (bf16[1280,768]{1,0:T(8,128)(2,1)}, bf16[1280,768]{1,0:T(8,128)(2,1)S(1)}, u32[]{:S(2)}) copy-start(bf16[1280,768]{1,0:T(8,128)(2,1)S(1)} %collective-permute-done.7.refs_8_) | copy-start | bytes 5898244
  24.6 14.4 %collective-permute-start.10 = (bf16[160,768]{1,0:T(8,128)(2,1)}, bf16[160,768]{1,0:T(8,128)(2,1)}, u32[]{:S(2)}, u32[]{:S(2)}) collective-permute-start(bf16[160,768]{1,0:T(8,128)(2,1)} %maximum_maximum_fusion.1), channel_id=1, source_target_pairs={{1,0},{2,1},{3,2},{4,3},{5,4},{6,5},{7,6},{8,7},{9,8},{10,9},{11,1... | collective-permute-start | bytes 737288 | tf_op jit(solution)/shard_map/ppermute | solution.py:274
  26.6 12.4 %collective-permute-start.9 = (bf16[160,768]{1,0:T(8,128)(2,1)}, bf16[160,768]{1,0:T(8,128)(2,1)}, u32[]{:S(2)}, u32[]{:S(2)}) collective-permute-start(bf16[160,768]{1,0:T(8,128)(2,1)} %maximum_maximum_fusion), channel_id=1, source_target_pairs={{0,1},{1,2},{2,3},{3,4},{4,5},{5,6},{6,7},{7,8},{8,9},{9,10},{10,1... | collective-permute-start | bytes 737288 | tf_op jit(solution)/shard_map/ppermute | solution.py:273
  31.4 7.5 %collective-permute-start.4 = (bf16[2,3,48,384]{3,2,1,0:T(8,128)(2,1)S(1)}, bf16[2,3,48,384]{3,2,1,0:T(8,128)(2,1)}, u32[]{:S(2)}, u32[]{:S(2)}) collective-permute-start(bf16[2,3,48,384]{3,2,1,0:T(8,128)(2,1)S(1)} %collective-permute-done.1.refs_1_), channel_id=1, source_target_pairs={{0,64},{64,128},{128,192},{192,0},{1,65},{65,129},{129,193},{193,1... | collective-permute-start | bytes 663560 | tf_op jit(solution)/shard_map/ppermute | solution.py:24
  32.0 7.0 %collective-permute-start.5 = (bf16[2,3,48,384]{3,2,1,0:T(8,128)(2,1)S(1)}, bf16[2,3,48,384]{3,2,1,0:T(8,128)(2,1)}, u32[]{:S(2)}, u32[]{:S(2)}) collective-permute-start(bf16[2,3,48,384]{3,2,1,0:T(8,128)(2,1)S(1)} %collective-permute-done.1.refs_1_), channel_id=1, source_target_pairs={{0,192},{64,0},{128,64},{192,128},{1,193},{65,1},{129,65},{193,129... | collective-permute-start | bytes 663560 | tf_op jit(solution)/shard_map/ppermute | solution.py:24
  39.0 1.5 %copy-start.4 = (bf16[1280,768]{1,0:T(8,128)(2,1)S(1)}, bf16[1280,768]{1,0:T(8,128)(2,1)}, u32[]{:S(2)}) copy-start(bf16[1280,768]{1,0:T(8,128)(2,1)} %copy-done.3) | copy-start | bytes 5898244
  40.5 1.5 %copy-start.6 = (bf16[1280,768]{1,0:T(8,128)(2,1)S(1)}, bf16[1280,768]{1,0:T(8,128)(2,1)}, u32[]{:S(2)}) copy-start(bf16[1280,768]{1,0:T(8,128)(2,1)} %copy-done.5) | copy-start | bytes 5898244
  42.1 0.9 copy-start.12
  43.0 0.9 copy-start.14
  61.1 1.1 copy-start.7
  62.2 0.8 copy-start.9
  63.0 6.8 %collective-permute-start.12 = (bf16[3,768,384]{2,1,0:T(8,128)(2,1)}, bf16[3,768,384]{2,1,0:T(8,128)(2,1)}, u32[]{:S(2)}, u32[]{:S(2)}) collective-permute-start(bf16[3,768,384]{2,1,0:T(8,128)(2,1)} %get-tuple-element.36.weight_a), channel_id=1, source_target_pairs={{0,16},{16,0},{1,17},{17,1},{2,18},{18,2},{3,19},{19,3},{4,20},{20... | collective-permute-start | bytes 5308424 | tf_op jit(solution)/shard_map/ppermute | solution.py:28
  64.6 4.9 %collective-permute-start.11 = (bf16[1344,384]{1,0:T(8,128)(2,1)}, bf16[1344,384]{1,0:T(8,128)(2,1)S(1)}, u32[]{:S(2)}, u32[]{:S(2)}) collective-permute-start(bf16[1344,384]{1,0:T(8,128)(2,1)} %get-tuple-element.35), channel_id=1, source_target_pairs={{0,16},{16,0},{1,17},{17,1},{2,18},{18,2},{3,19},{19,3},{4,20},{20... | collective-permute-start | bytes 3096584 | tf_op jit(solution)/shard_map/ppermute | solution.py:28
  64.6 18.0 %collective-permute-start.13 = (bf16[3,192,384]{2,1,0:T(8,128)(2,1)}, bf16[3,192,384]{2,1,0:T(8,128)(2,1)}, u32[]{:S(2)}, u32[]{:S(2)}) collective-permute-start(bf16[3,192,384]{2,1,0:T(8,128)(2,1)} %get-tuple-element.38), channel_id=1, source_target_pairs={{0,64},{64,128},{128,192},{192,0},{1,65},{65,129},{129,193},{193,1... | collective-permute-start | bytes 1327112 | tf_op jit(solution)/shard_map/ppermute | solution.py:24
  64.8 17.8 %collective-permute-start.14 = (bf16[3,192,384]{2,1,0:T(8,128)(2,1)}, bf16[3,192,384]{2,1,0:T(8,128)(2,1)}, u32[]{:S(2)}, u32[]{:S(2)}) collective-permute-start(bf16[3,192,384]{2,1,0:T(8,128)(2,1)} %get-tuple-element.39), channel_id=1, source_target_pairs={{0,192},{64,0},{128,64},{192,128},{1,193},{65,1},{129,65},{193,129... | collective-permute-start | bytes 1327112 | tf_op jit(solution)/shard_map/ppermute | solution.py:24
  67.3 20.7 %collective-permute-start.15 = (bf16[3,192,384]{2,1,0:T(8,128)(2,1)}, bf16[3,192,384]{2,1,0:T(8,128)(2,1)}, u32[]{:S(2)}, u32[]{:S(2)}) collective-permute-start(bf16[3,192,384]{2,1,0:T(8,128)(2,1)} %get-tuple-element.40), channel_id=1, source_target_pairs={{0,128},{64,192},{128,0},{192,64},{1,129},{65,193},{129,1},{193,65... | collective-permute-start | bytes 1327112 | tf_op jit(solution)/shard_map/ppermute | solution.py:24
  69.8 2.1 %copy-start.1 = (f32[1280,768]{1,0:T(8,128)S(1)}, f32[1280,768]{1,0:T(8,128)}, u32[]{:S(2)}) copy-start(f32[1280,768]{1,0:T(8,128)} %copy-done) | copy-start | bytes 11796484
  71.9 1.2 copy-start.8
  73.1 14.9 %copy-start.10 = (bf16[3,192,384]{2,1,0:T(8,128)(2,1)S(1)}, bf16[3,192,384]{2,1,0:T(8,128)(2,1)}, u32[]{:S(2)}) copy-start(bf16[3,192,384]{2,1,0:T(8,128)(2,1)} %copy-done.9) | copy-start | bytes 1327108
  89.5 7.3 %collective-permute-start.16 = (bf16[3,48,384]{2,1,0:T(8,128)(2,1)S(1)}, bf16[3,48,384]{2,1,0:T(8,128)(2,1)S(1)}, u32[]{:S(2)}, u32[]{:S(2)}) collective-permute-start(bf16[3,48,384]{2,1,0:T(8,128)(2,1)S(1)} %get-tuple-element.61), channel_id=1, source_target_pairs={{0,8},{8,32},{32,40},{40,0},{1,9},{9,33},{33,41},{41,1},{2,10},{10... | collective-permute-start | bytes 331784 | tf_op jit(solution)/shard_map/ppermute | solution.py:24
  94.9 3.6 %collective-permute-start.17 = (bf16[3,48,384]{2,1,0:T(8,128)(2,1)S(1)}, bf16[3,48,384]{2,1,0:T(8,128)(2,1)S(1)}, u32[]{:S(2)}, u32[]{:S(2)}) collective-permute-start(bf16[3,48,384]{2,1,0:T(8,128)(2,1)S(1)} %get-tuple-element.63), channel_id=1, source_target_pairs={{0,40},{8,0},{32,8},{40,32},{1,41},{9,1},{33,9},{41,33},{2,42},{10... | collective-permute-start | bytes 331784 | tf_op jit(solution)/shard_map/ppermute | solution.py:24
  94.9 5.5 %collective-permute-start.18 = (bf16[3,48,384]{2,1,0:T(8,128)(2,1)S(1)}, bf16[3,48,384]{2,1,0:T(8,128)(2,1)S(1)}, u32[]{:S(2)}, u32[]{:S(2)}) collective-permute-start(bf16[3,48,384]{2,1,0:T(8,128)(2,1)S(1)} %get-tuple-element.62), channel_id=1, source_target_pairs={{0,32},{8,40},{32,0},{40,8},{1,33},{9,41},{33,1},{41,9},{2,34},{10... | collective-permute-start | bytes 331784 | tf_op jit(solution)/shard_map/ppermute | solution.py:24
  101.5 4.8 %collective-permute-start.19 = (bf16[3,48,384]{2,1,0:T(8,128)(2,1)S(1)}, bf16[3,48,384]{2,1,0:T(8,128)(2,1)S(1)}, u32[]{:S(2)}, u32[]{:S(2)}) collective-permute-start(bf16[3,48,384]{2,1,0:T(8,128)(2,1)S(1)} %add_convert_fusion.2), channel_id=1, source_target_pairs={{0,1},{1,0},{2,3},{3,2},{4,5},{5,4},{6,7},{7,6},{8,9},{9,8},{10,11... | collective-permute-start | bytes 331784 | tf_op jit(solution)/shard_map/ppermute | solution.py:28
  101.6 5.9 %collective-permute-start.20 = (bf16[3,48,384]{2,1,0:T(8,128)(2,1)S(1)}, bf16[3,48,384]{2,1,0:T(8,128)(2,1)S(1)}, u32[]{:S(2)}, u32[]{:S(2)}) collective-permute-start(bf16[3,48,384]{2,1,0:T(8,128)(2,1)S(1)} %add_convert_fusion.2), channel_id=1, source_target_pairs={{0,2},{1,3},{2,0},{3,1},{4,6},{5,7},{6,4},{7,5},{8,10},{9,11},{10,... | collective-permute-start | bytes 331784 | tf_op jit(solution)/shard_map/ppermute | solution.py:28
  103.8 6.7 %collective-permute-start.21 = (bf16[3,48,384]{2,1,0:T(8,128)(2,1)S(1)}, bf16[3,48,384]{2,1,0:T(8,128)(2,1)S(1)}, u32[]{:S(2)}, u32[]{:S(2)}) collective-permute-start(bf16[3,48,384]{2,1,0:T(8,128)(2,1)S(1)} %add_convert_fusion.2), channel_id=1, source_target_pairs={{0,3},{1,2},{2,1},{3,0},{4,7},{5,6},{6,5},{7,4},{8,11},{9,10},{10,... | collective-permute-start | bytes 331784 | tf_op jit(solution)/shard_map/ppermute | solution.py:28
  110.5 5.3 %collective-permute-start.22 = (bf16[3,48,384]{2,1,0:T(8,128)(2,1)S(1)}, bf16[3,48,384]{2,1,0:T(8,128)(2,1)S(1)}, u32[]{:S(2)}, u32[]{:S(2)}) collective-permute-start(bf16[3,48,384]{2,1,0:T(8,128)(2,1)S(1)} %add_convert_fusion.1), channel_id=1, source_target_pairs={{0,7},{1,6},{2,5},{3,4},{4,3},{5,2},{6,1},{7,0},{8,15},{9,14},{10,... | collective-permute-start | bytes 331784 | tf_op jit(solution)/shard_map/ppermute | solution.py:28
  115.9 7.9 %collective-permute-start.23 = (bf16[3,48,384]{2,1,0:T(8,128)(2,1)S(1)}, bf16[3,48,384]{2,1,0:T(8,128)(2,1)S(1)}, u32[]{:S(2)}, u32[]{:S(2)}) collective-permute-start(bf16[3,48,384]{2,1,0:T(8,128)(2,1)S(1)} %add_convert_fusion), channel_id=1, source_target_pairs={{16,0},{8,24},{0,8},{24,16},{17,1},{9,25},{1,9},{25,17},{18,2},{10... | collective-permute-start | bytes 331784 | tf_op jit(solution)/shard_map/ppermute | solution.py:224
  121.2 6.1 %collective-permute-start.24 = (bf16[3,48,384]{2,1,0:T(8,128)(2,1)S(1)}, bf16[3,48,384]{2,1,0:T(8,128)(2,1)S(1)}, u32[]{:S(2)}, u32[]{:S(2)}) collective-permute-start(bf16[3,48,384]{2,1,0:T(8,128)(2,1)S(1)} %add_convert_fusion), channel_id=1, source_target_pairs={{16,8},{8,16},{17,9},{9,17},{18,10},{10,18},{19,11},{11,19},{20,12... | collective-permute-start | bytes 331784 | tf_op jit(solution)/shard_map/ppermute | solution.py:225

commit v7 on v6

--- a/solution.py
+++ b/solution.py
@@ -91,27 +91,44 @@
                 for place, (source, target) in enumerate(moves)
             ]
         )
-    for copy in copies + loads[0] + loads[1]:
+    for copy in copies + loads[0]:
         copy.start()
     for copy in copies:
         copy.wait()
+    for copy in loads[1]:
+        copy.start()
     save = pltpu.make_async_copy(weight, weight_out, weight_sem)
     save.start()
     length = back.shape[1]
     block = length // 3
+    wide_lanes = half // 384 * 256
     saves = [save]
     for index in range(2):
         for copy in loads[index]:
             copy.wait()
+        narrow = jnp.concatenate([weight[tap, :, wide_lanes:] for tap in range(FILTER_TAPS)], axis=1)
         for start in range(0, length, block):
             conv = jnp.dot(
-                normed[index, start : start + block, :], weight[0], preferred_element_type=F32
+                normed[index, start : start + block, :],
+                weight[0, :, :wide_lanes],
+                preferred_element_type=F32,
             )
             for tap in range(1, FILTER_TAPS):
                 low = start + tap * DILATION_STEP
                 conv = conv + jnp.dot(
-                    normed[index, low : low + block, :], weight[tap], preferred_element_type=F32
+                    normed[index, low : low + block, :],
+                    weight[tap, :, :wide_lanes],
+                    preferred_element_type=F32,
                 )
+            every = jnp.dot(
+                normed[index, start : start + block + wide, :], narrow, preferred_element_type=F32
+            )
+            lanes_left = half - wide_lanes
+            rest = every[:block, :lanes_left]
+            for tap in range(1, FILTER_TAPS):
+                low = tap * DILATION_STEP
+                rest = rest + every[low : low + block, tap * lanes_left : (tap + 1) * lanes_left]
+            conv = jnp.concatenate([conv, rest], axis=1)
             incoming = upstream[index, start : start + block, :].astype(F32)
             back[index, start : start + block, :] = (incoming * gelu_slope(conv)).astype(BF16)
         back_save = pltpu.make_async_copy(back.at[index], back_out[index], back_sem.at[index])
@@ -172,7 +189,7 @@
             dma,
             dma((4,)),
         ],
-        compiler_params=pltpu.CompilerParams(vmem_limit_bytes=26 * 1024 * 1024),
+        compiler_params=pltpu.CompilerParams(vmem_limit_bytes=56 * 1024 * 1024),
         name="forward",
     )(position, *pieces, *normed, *edges, *upstream)
 
@@ -210,7 +227,7 @@
         in_specs=[whole(back[0]), whole(back[1]), whole(weight[0]), whole(weight[1]), part]
         + [pl.BlockSpec((block, 1), lambda i: (i, 0)), whole(gain), part],
         out_specs=part,
-        compiler_params=pltpu.CompilerParams(vmem_limit_bytes=26 * 1024 * 1024),
+        compiler_params=pltpu.CompilerParams(vmem_limit_bytes=56 * 1024 * 1024),
         name="backward",
     )(*back, *weight, inputs, scale, gain, incoming)
 
@@ -261,6 +278,9 @@
     upstream_sent = lax.dynamic_slice_in_dim(incoming, (1 - core) * half, half, axis=1)
     normed_other = swap(normed, "core", 2, 1)
     upstream_other = swap(upstream_sent, "core", 2, 1)
+    normed, incoming, normed_other, upstream_other = join(
+        normed, incoming, normed_other, upstream_other
+    )
 
     def edge(rows, reach_rows):
         upstream_edge = lax.dynamic_slice_in_dim(incoming[reach_rows], core * half, half, axis=1)

time: 129 us -> 121 us (0.938)
  local copies, waits for them, and re-layouts: 15.1 us -> 9.06 us
  starting transfers between devices: 47.3 us -> 45 us
    unnamed x32 -> x34, local copies, waits for them, and re-layouts: 12.8 us -> 5.32 us
    ppermute x10, waiting for transfers between devices: 10.1 us -> 8.44 us  [swap(): return lax.ppermute(value, axis, [(i, i ^ mask) for i in range(count)])]
    concatenate x2, other arithmetic: 1.43 us -> 0.04 us  [edge(): return jnp.concatenate([normed[rows], normed_other[rows], upstream_edge])]
    pallas_call x1, Pallas kernels: 9.51 us -> 10.8 us  [backward(): pl.pallas_call(backward_kernel, grid=(count // block,), out_shape=jax.Sha...]
  transfers between devices with their start and end apart: 25 -> 25, of which waited for: 13 -> 12; matrix products, arithmetic and copies ran while one was open for 7% -> 8% of each run, Pallas kernels for 7% -> 9%
where the time goes in v7:
time: 121 us; the launch traced here: 120 us
  starting transfers between devices  45 us (37%)
  waiting for transfers between devices  27.5 us (23%)
  Pallas kernels  27.5 us (23%)
  other arithmetic  9.9 us (8%)
  local copies, waits for them, and re-layouts  9.06 us (7%)
    ppermute x11, starting transfers between devices, shift(): return lax.ppermute(value, axis, pairs)  17.5 us
    pallas_call x1, Pallas kernels, forward(): pl.pallas_call(forward_kernel, out_shape=[jax.ShapeDtypeStruct((FILTER_TA...  16.7 us
    ppermute x11, waiting for transfers between devices, shift(): return lax.ppermute(value, axis, pairs)  14.9 us
    ppermute x10, starting transfers between devices, swap(): return lax.ppermute(value, axis, [(i, i ^ mask) for i in range(count)])  14.8 us
    pallas_call x1, Pallas kernels, backward(): pl.pallas_call(backward_kernel, grid=(count // block,), out_shape=jax.Sha...  10.8 us
    ppermute x10, waiting for transfers between devices, swap(): return lax.ppermute(value, axis, [(i, i ^ mask) for i in range(count)])  8.44 us
    unnamed x34, local copies, waits for them, and re-layouts  5.32 us
    ppermute x1, starting transfers between devices, share_weight_grad(): first = lax.ppermute(mine, pair, [(2, 0), (1, 3), (0, 1), (3, 2)])  5.3 us
  transfers between devices with their start and end apart: 25, of which 12 were waited for; matrix products, arithmetic and copies ran while one was open for 8% of the time, Pallas kernels for 9%

profile of v7, /device:TPU:1, one launch (start us, length us, event | category | flops | bytes accessed | tf_op | source)
XLA Modules:
  0.0 120.0 jit_solution(13715113905528524575)
XLA Ops:
  0.6 1.0 dynamic-slice_bitcast_fusion
  1.6 3.3 %collective-permute-start = (bf16[3,48,384]{2,1,0:T(8,128)(2,1)S(1)}, bf16[3,48,384]{2,1,0:T(8,128)(2,1)S(1)}, u32[]{:S(2)}, u32[]{:S(2)}) collective-permute-start(bf16[3,48,384]{2,1,0:T(8,128)(2,1)S(1)} %get-tuple-element.77), channel_id=1, source_target_pairs={{0,16},{16,0},{1,17},{17,1},{2,18},{18,2},{3,19},{19,3},{4,20},{20... | collective-permute-start | bytes 331784 | tf_op jit(solution)/shard_map/ppermute | solution.py:28
  5.0 0.9 slice_reduce_fusion.3
  5.9 0.1 collective-permute-done
  6.0 1.1 collective-permute-start.1
  7.0 1.2 %collective-permute-start.2 = (bf16[2,3,48,384]{3,2,1,0:T(8,128)(2,1)S(1)}, bf16[2,3,48,384]{3,2,1,0:T(8,128)(2,1)S(1)}, u32[]{:S(2)}, u32[]{:S(2)}) collective-permute-start(bf16[2,3,48,384]{3,2,1,0:T(8,128)(2,1)S(1)} %pad_maximum_fusion.1.refs_0_), channel_id=1, source_target_pairs={{0,64},{64,128},{128,192},{192,0},{1,65},{65,129},{129,193},{193,1... | collective-permute-start | bytes 663560 | tf_op jit(solution)/shard_map/ppermute | solution.py:24
  8.3 1.5 %collective-permute-start.3 = (bf16[2,3,48,384]{3,2,1,0:T(8,128)(2,1)S(1)}, bf16[2,3,48,384]{3,2,1,0:T(8,128)(2,1)S(1)}, u32[]{:S(2)}, u32[]{:S(2)}) collective-permute-start(bf16[2,3,48,384]{3,2,1,0:T(8,128)(2,1)S(1)} %pad_maximum_fusion.1.refs_0_), channel_id=1, source_target_pairs={{0,192},{64,0},{128,64},{192,128},{1,193},{65,1},{129,65},{193,129... | collective-permute-start | bytes 663560 | tf_op jit(solution)/shard_map/ppermute | solution.py:24
  9.7 0.7 compare_reduce_fusion.2
  10.5 3.7 %multiply_reduce_fusion = (f32[1280]{0:T(1024)S(1)}, f32[1280,768]{1,0:T(8,128)S(1)}) fusion(f32[768]{0:T(1024)S(1)} %get-tuple-element.56, f32[768]{0:T(1024)S(1)} %get-tuple-element.57, pred[1280]{0:T(1024)(128)(4,1)S(1)} %get-tuple-element.59, f32[768]{0:T(1024)S(1)} %get-tuple-element.55, pred[1280]{0:T(1024)(128)(4,1)S(1)} %get-tuple-element.60, ...), kind=kLoop, calls=%fused_computation.1 | loop fusion | flops 6880000 | bytes 5919488 | tf_op jit(solution)/shard_map/reduce_sum | solution.py:270
  14.2 0.0 copy-start.1
  14.2 0.4 multiply_convert_fusion.refs_7_
  14.6 0.0 copy-start.2
  14.7 0.0 collective-permute-done.2.refs_2_
  14.7 1.5 %collective-permute-start.7 = (bf16[1280,768]{1,0:T(8,128)(2,1)S(1)}, bf16[1280,768]{1,0:T(8,128)(2,1)S(1)}, u32[]{:S(2)}, u32[]{:S(2)}) collective-permute-start(bf16[1280,768]{1,0:T(8,128)(2,1)S(1)} %multiply_convert_fusion.refs_7_), channel_id=1, source_target_pairs={{0,16},{16,0},{1,17},{17,1},{2,18},{18,2},{3,19},{19,3},{4,20},{20... | collective-permute-start | bytes 5898248 | tf_op jit(solution)/shard_map/ppermute | solution.py:28
  16.2 1.0 copy-done.1
  17.2 0.1 constant_dynamic-slice_fusion.2
  17.3 1.3 %collective-permute-start.8 = (bf16[1280,384]{1,0:T(8,128)(2,1)S(1)}, bf16[1280,384]{1,0:T(8,128)(2,1)S(1)}, u32[]{:S(2)}, u32[]{:S(2)}) collective-permute-start(bf16[1280,384]{1,0:T(8,128)(2,1)S(1)} %constant_dynamic-slice_fusion.2), channel_id=1, source_target_pairs={{0,16},{16,0},{1,17},{17,1},{2,18},{18,2},{3,19},{19,3},{4,20},{20... | collective-permute-start | bytes 2949128 | tf_op jit(solution)/shard_map/ppermute | solution.py:28
  18.6 0.8 pad_maximum_fusion
  19.4 1.5 %collective-permute-start.6 = (bf16[2,2,3,48,384]{4,3,2,1,0:T(8,128)(2,1)}, bf16[2,2,3,48,384]{4,3,2,1,0:T(8,128)(2,1)}, u32[]{:S(2)}, u32[]{:S(2)}) collective-permute-start(bf16[2,2,3,48,384]{4,3,2,1,0:T(8,128)(2,1)} %pad_maximum_fusion), channel_id=1, source_target_pairs={{0,128},{64,192},{128,0},{192,64},{1,129},{65,193},{129,1},{193,65... | collective-permute-start | bytes 1327112 | tf_op jit(solution)/shard_map/ppermute | solution.py:24
  21.0 0.2 collective-permute-done.8.refs_12_
  21.2 0.0 collective-permute-done.7.refs_8_
  21.3 1.2 %copy-done.3 = bf16[1280,768]{1,0:T(8,128)(2,1)} copy-done((bf16[1280,768]{1,0:T(8,128)(2,1)}, bf16[1280,768]{1,0:T(8,128)(2,1)S(1)}, u32[]{:S(2)}) %copy-start.3) | copy-done | bytes 1966104
  22.5 1.3 %collective-permute-start.10 = (bf16[160,768]{1,0:T(8,128)(2,1)S(1)}, bf16[160,768]{1,0:T(8,128)(2,1)S(1)}, u32[]{:S(2)}, u32[]{:S(2)}) collective-permute-start(bf16[160,768]{1,0:T(8,128)(2,1)S(1)} %maximum_maximum_fusion.1), channel_id=1, source_target_pairs={{1,0},{2,1},{3,2},{4,3},{5,4},{6,5},{7,6},{8,7},{9,8},{10,9},{11,1... | collective-permute-start | bytes 737288 | tf_op jit(solution)/shard_map/ppermute | solution.py:294
  23.9 4.2 %collective-permute-start.9 = (bf16[160,768]{1,0:T(8,128)(2,1)S(1)}, bf16[160,768]{1,0:T(8,128)(2,1)S(1)}, u32[]{:S(2)}, u32[]{:S(2)}) collective-permute-start(bf16[160,768]{1,0:T(8,128)(2,1)S(1)} %maximum_maximum_fusion), channel_id=1, source_target_pairs={{0,1},{1,2},{2,3},{3,4},{4,5},{5,6},{6,7},{7,8},{8,9},{9,10},{10,1... | collective-permute-start | bytes 737288 | tf_op jit(solution)/shard_map/ppermute | solution.py:293
  28.1 1.2 %collective-permute-start.4 = (bf16[2,3,48,384]{3,2,1,0:T(8,128)(2,1)S(1)}, bf16[2,3,48,384]{3,2,1,0:T(8,128)(2,1)S(1)}, u32[]{:S(2)}, u32[]{:S(2)}) collective-permute-start(bf16[2,3,48,384]{3,2,1,0:T(8,128)(2,1)S(1)} %collective-permute-done.1.refs_1_), channel_id=1, source_target_pairs={{0,64},{64,128},{128,192},{192,0},{1,65},{65,129},{129,193},{193,1... | collective-permute-start | bytes 663560 | tf_op jit(solution)/shard_map/ppermute | solution.py:24
  29.3 1.7 %collective-permute-start.5 = (bf16[2,3,48,384]{3,2,1,0:T(8,128)(2,1)S(1)}, bf16[2,3,48,384]{3,2,1,0:T(8,128)(2,1)S(1)}, u32[]{:S(2)}, u32[]{:S(2)}) collective-permute-start(bf16[2,3,48,384]{3,2,1,0:T(8,128)(2,1)S(1)} %collective-permute-done.1.refs_1_), channel_id=1, source_target_pairs={{0,192},{64,0},{128,64},{192,128},{1,193},{65,1},{129,65},{193,129... | collective-permute-start | bytes 663560 | tf_op jit(solution)/shard_map/ppermute | solution.py:24
  31.0 0.7 pad_add_fusion.position
  31.7 6.3 %collective-permute-done.4.refs_3_ = bf16[2,3,48,384]{3,2,1,0:T(8,128)(2,1)S(1)} collective-permute-done((bf16[2,3,48,384]{3,2,1,0:T(8,128)(2,1)S(1)}, bf16[2,3,48,384]{3,2,1,0:T(8,128)(2,1)S(1)}, u32[]{:S(2)}, u32[]{:S(2)}) %collective-permute-start.4) | collective-permute-done | bytes 221216 | tf_op jit(solution)/shard_map/ppermute | solution.py:24
  38.0 0.6 copy-done.14
  38.7 0.1 copy-done.15
  38.7 0.1 copy-done.10
  38.8 0.7 copy-done.11
  39.5 16.7 %forward.1 = (bf16[3,768,384]{2,1,0:T(8,128)(2,1)}, bf16[1344,384]{1,0:T(8,128)(2,1)}, bf16[1344,384]{1,0:T(8,128)(2,1)}, bf16[3,192,384]{2,1,0:T(8,128)(2,1)}, ...) custom-call(s32[4]{0:T(128)} %pad_add_fusion.position, ...), custom_call_target="tpu_custom_call" | custom-call | tf_op jit(solution)/shard_map/forward/pallas_call | solution.py:173
  56.3 0.6 collective-permute-start.12
  56.8 0.1 collective-permute-start.11
  56.9 0.0 collective-permute-start.13
  57.0 2.6 %collective-permute-start.14 = (bf16[3,192,384]{2,1,0:T(8,128)(2,1)}, bf16[3,192,384]{2,1,0:T(8,128)(2,1)}, u32[]{:S(2)}, u32[]{:S(2)}) collective-permute-start(bf16[3,192,384]{2,1,0:T(8,128)(2,1)} %get-tuple-element.47), channel_id=1, source_target_pairs={{0,192},{64,0},{128,64},{192,128},{1,193},{65,1},{129,65},{193,129... | collective-permute-start | bytes 1327112 | tf_op jit(solution)/shard_map/ppermute | solution.py:24
  59.6 0.3 collective-permute-start.15
  60.0 0.6 broadcast_in_dim.77.gain
  60.5 1.1 rsqrt.7.scale
  61.6 0.2 collective-permute-done.11.back_b
  61.9 1.0 copy-done.7
  62.8 0.6 copy-done.5
  63.4 10.8 %backward.1 = bf16[1280,768]{1,0:T(8,128)(2,1)} custom-call(bf16[1344,384]{1,0:T(8,128)(2,1)} %get-tuple-element.42.back_a, bf16[1344,384]{1,0:T(8,128)(2,1)} %copy-done.7, bf16[3,768,384]{2,1,0:T(8,128)(2,1)} %get-tuple-element.44.weight_a, bf16[3,768,384]{2,1,0:T(8,128)(2,1)} %copy-done.5, f32[1280,768]{1,0:T(8,128)} %copy-done, f32[1280,1]{1,0:T(8,128)} %rsqrt.7.scale, ...), custom_call_target="tpu_custom_call" | custom-call | tf_op jit(solution)/shard_map/backward/pallas_call | solution.py:223
  74.2 5.1 %collective-permute-done.15 = bf16[3,192,384]{2,1,0:T(8,128)(2,1)} collective-permute-done((bf16[3,192,384]{2,1,0:T(8,128)(2,1)}, bf16[3,192,384]{2,1,0:T(8,128)(2,1)}, u32[]{:S(2)}, u32[]{:S(2)}) %collective-permute-start.15) | collective-permute-done | bytes 442400 | tf_op jit(solution)/shard_map/ppermute | solution.py:24
  79.3 1.5 %add_convert_fusion.5 = (bf16[3,48,384]{2,1,0:T(8,128)(2,1)S(1)}, bf16[3,48,384]{2,1,0:T(8,128)(2,1)S(1)}, bf16[3,48,384]{2,1,0:T(8,128)(2,1)S(1)}) fusion(bf16[3,192,384]{2,1,0:T(8,128)(2,1)} %collective-permute-done.15, s32[]{:T(128)S(6)} %select_n.95, bf16[3,192,384]{2,1,0:T(8,128)(2,1)} %collective-permute-done.14, ...), kind=kLoop, calls=%fused_computation.13 | loop fusion | flops 1327104 | bytes 1658892 | tf_op jit(solution)/shard_map/convert_element_type | solution.py:320
  80.8 5.5 %collective-permute-start.16 = (bf16[3,48,384]{2,1,0:T(8,128)(2,1)S(1)}, bf16[3,48,384]{2,1,0:T(8,128)(2,1)S(1)}, u32[]{:S(2)}, u32[]{:S(2)}) collective-permute-start(bf16[3,48,384]{2,1,0:T(8,128)(2,1)S(1)} %get-tuple-element.69), channel_id=1, source_target_pairs={{0,8},{8,32},{32,40},{40,0},{1,9},{9,33},{33,41},{41,1},{2,10},{10... | collective-permute-start | bytes 331784 | tf_op jit(solution)/shard_map/ppermute | solution.py:24
  86.3 1.9 %collective-permute-start.18 = (bf16[3,48,384]{2,1,0:T(8,128)(2,1)S(1)}, bf16[3,48,384]{2,1,0:T(8,128)(2,1)S(1)}, u32[]{:S(2)}, u32[]{:S(2)}) collective-permute-start(bf16[3,48,384]{2,1,0:T(8,128)(2,1)S(1)} %get-tuple-element.70), channel_id=1, source_target_pairs={{0,32},{8,40},{32,0},{40,8},{1,33},{9,41},{33,1},{41,9},{2,34},{10... | collective-permute-start | bytes 331784 | tf_op jit(solution)/shard_map/ppermute | solution.py:24
  88.2 1.7 %collective-permute-done.17 = bf16[3,48,384]{2,1,0:T(8,128)(2,1)S(1)} collective-permute-done((bf16[3,48,384]{2,1,0:T(8,128)(2,1)S(1)}, bf16[3,48,384]{2,1,0:T(8,128)(2,1)S(1)}, u32[]{:S(2)}, u32[]{:S(2)}) %collective-permute-start.17) | collective-permute-done | bytes 110624 | tf_op jit(solution)/shard_map/ppermute | solution.py:24
  89.9 1.8 %collective-permute-done.18 = bf16[3,48,384]{2,1,0:T(8,128)(2,1)S(1)} collective-permute-done((bf16[3,48,384]{2,1,0:T(8,128)(2,1)S(1)}, bf16[3,48,384]{2,1,0:T(8,128)(2,1)S(1)}, u32[]{:S(2)}, u32[]{:S(2)}) %collective-permute-start.18) | collective-permute-done | bytes 110624 | tf_op jit(solution)/shard_map/ppermute | solution.py:24
  91.7 1.1 add_convert_fusion.2
  92.8 0.1 collective-permute-start.19
  92.9 2.8 %collective-permute-start.20 = (bf16[3,48,384]{2,1,0:T(8,128)(2,1)S(1)}, bf16[3,48,384]{2,1,0:T(8,128)(2,1)S(1)}, u32[]{:S(2)}, u32[]{:S(2)}) collective-permute-start(bf16[3,48,384]{2,1,0:T(8,128)(2,1)S(1)} %add_convert_fusion.2), channel_id=1, source_target_pairs={{0,2},{1,3},{2,0},{3,1},{4,6},{5,7},{6,4},{7,5},{8,10},{9,11},{10,... | collective-permute-start | bytes 331784 | tf_op jit(solution)/shard_map/ppermute | solution.py:28
  95.7 0.7 collective-permute-start.21
  96.4 0.1 collective-permute-done.19
  96.5 2.7 %collective-permute-done.20 = bf16[3,48,384]{2,1,0:T(8,128)(2,1)S(1)} collective-permute-done((bf16[3,48,384]{2,1,0:T(8,128)(2,1)S(1)}, bf16[3,48,384]{2,1,0:T(8,128)(2,1)S(1)}, u32[]{:S(2)}, u32[]{:S(2)}) %collective-permute-start.20) | collective-permute-done | bytes 110624 | tf_op jit(solution)/shard_map/ppermute | solution.py:28
  99.1 3.1 %collective-permute-done.21 = bf16[3,48,384]{2,1,0:T(8,128)(2,1)S(1)} collective-permute-done((bf16[3,48,384]{2,1,0:T(8,128)(2,1)S(1)}, bf16[3,48,384]{2,1,0:T(8,128)(2,1)S(1)}, u32[]{:S(2)}, u32[]{:S(2)}) %collective-permute-start.21) | collective-permute-done | bytes 110624 | tf_op jit(solution)/shard_map/ppermute | solution.py:28
  102.2 0.1 add_convert_fusion.1
  102.3 3.4 %collective-permute-start.22 = (bf16[3,48,384]{2,1,0:T(8,128)(2,1)S(1)}, bf16[3,48,384]{2,1,0:T(8,128)(2,1)S(1)}, u32[]{:S(2)}, u32[]{:S(2)}) collective-permute-start(bf16[3,48,384]{2,1,0:T(8,128)(2,1)S(1)} %add_convert_fusion.1), channel_id=1, source_target_pairs={{0,7},{1,6},{2,5},{3,4},{4,3},{5,2},{6,1},{7,0},{8,15},{9,14},{10,... | collective-permute-start | bytes 331784 | tf_op jit(solution)/shard_map/ppermute | solution.py:28
  105.6 2.1 %collective-permute-done.22 = bf16[3,48,384]{2,1,0:T(8,128)(2,1)S(1)} collective-permute-done((bf16[3,48,384]{2,1,0:T(8,128)(2,1)S(1)}, bf16[3,48,384]{2,1,0:T(8,128)(2,1)S(1)}, u32[]{:S(2)}, u32[]{:S(2)}) %collective-permute-start.22) | collective-permute-done | bytes 110624 | tf_op jit(solution)/shard_map/ppermute | solution.py:28
  107.8 5.3 %collective-permute-start.23 = (bf16[3,48,384]{2,1,0:T(8,128)(2,1)S(1)}, bf16[3,48,384]{2,1,0:T(8,128)(2,1)S(1)}, u32[]{:S(2)}, u32[]{:S(2)}) collective-permute-start(bf16[3,48,384]{2,1,0:T(8,128)(2,1)S(1)} %add_convert_fusion), channel_id=1, source_target_pairs={{16,0},{8,24},{0,8},{24,16},{17,1},{9,25},{1,9},{25,17},{18,2},{10... | collective-permute-start | bytes 331784 | tf_op jit(solution)/shard_map/ppermute | solution.py:241
  113.1 1.9 %collective-permute-start.24 = (bf16[3,48,384]{2,1,0:T(8,128)(2,1)S(1)}, bf16[3,48,384]{2,1,0:T(8,128)(2,1)S(1)}, u32[]{:S(2)}, u32[]{:S(2)}) collective-permute-start(bf16[3,48,384]{2,1,0:T(8,128)(2,1)S(1)} %add_convert_fusion), channel_id=1, source_target_pairs={{16,8},{8,16},{17,9},{9,17},{18,10},{10,18},{19,11},{11,19},{20,12... | collective-permute-start | bytes 331784 | tf_op jit(solution)/shard_map/ppermute | solution.py:242
  115.0 4.1 %collective-permute-done.24 = bf16[3,48,384]{2,1,0:T(8,128)(2,1)S(1)} collective-permute-done((bf16[3,48,384]{2,1,0:T(8,128)(2,1)S(1)}, bf16[3,48,384]{2,1,0:T(8,128)(2,1)S(1)}, u32[]{:S(2)}, u32[]{:S(2)}) %collective-permute-start.24) | collective-permute-done | bytes 110624 | tf_op jit(solution)/shard_map/ppermute | solution.py:242
  119.2 0.8 convert_multiply_fusion
  (47 shorter events, 0.3 us)
Async XLA Ops:
  0.6 13.6 %copy-start.16 = (f32[768]{0:T(1024)S(1)}, f32[768]{0:T(1024)}, u32[]{:S(2)}) copy-start(f32[768]{0:T(1024)} %param.9) | copy-start | bytes 9220
  1.6 4.3 %collective-permute-start = (bf16[3,48,384]{2,1,0:T(8,128)(2,1)S(1)}, bf16[3,48,384]{2,1,0:T(8,128)(2,1)S(1)}, u32[]{:S(2)}, u32[]{:S(2)}) collective-permute-start(bf16[3,48,384]{2,1,0:T(8,128)(2,1)S(1)} %get-tuple-element.77), channel_id=1, source_target_pairs={{0,16},{16,0},{1,17},{17,1},{2,18},{18,2},{3,19},{19,3},{4,20},{20... | collective-permute-start | bytes 331784 | tf_op jit(solution)/shard_map/ppermute | solution.py:28
  6.0 12.7 %copy-start.4 = (bf16[2,3,48,384]{3,2,1,0:T(8,128)(2,1)}, bf16[2,3,48,384]{3,2,1,0:T(8,128)(2,1)S(1)}, u32[]{:S(2)}) copy-start(bf16[2,3,48,384]{3,2,1,0:T(8,128)(2,1)S(1)} %pad_maximum_fusion.1.refs_0_) | copy-start | bytes 663556
  6.0 8.7 %collective-permute-start.1 = (bf16[2,3,48,384]{3,2,1,0:T(8,128)(2,1)S(1)}, bf16[2,3,48,384]{3,2,1,0:T(8,128)(2,1)S(1)}, u32[]{:S(2)}, u32[]{:S(2)}) collective-permute-start(bf16[2,3,48,384]{3,2,1,0:T(8,128)(2,1)S(1)} %pad_maximum_fusion.1.refs_0_), channel_id=1, source_target_pairs={{0,40},{8,32},{32,8},{40,0},{1,41},{9,33},{33,9},{41,1},{2,42},{10... | collective-permute-start | bytes 663560 | tf_op jit(solution)/shard_map/ppermute | solution.py:28
  7.0 7.6 %collective-permute-start.2 = (bf16[2,3,48,384]{3,2,1,0:T(8,128)(2,1)S(1)}, bf16[2,3,48,384]{3,2,1,0:T(8,128)(2,1)S(1)}, u32[]{:S(2)}, u32[]{:S(2)}) collective-permute-start(bf16[2,3,48,384]{3,2,1,0:T(8,128)(2,1)S(1)} %pad_maximum_fusion.1.refs_0_), channel_id=1, source_target_pairs={{0,64},{64,128},{128,192},{192,0},{1,65},{65,129},{129,193},{193,1... | collective-permute-start | bytes 663560 | tf_op jit(solution)/shard_map/ppermute | solution.py:24
  8.3 6.4 %collective-permute-start.3 = (bf16[2,3,48,384]{3,2,1,0:T(8,128)(2,1)S(1)}, bf16[2,3,48,384]{3,2,1,0:T(8,128)(2,1)S(1)}, u32[]{:S(2)}, u32[]{:S(2)}) collective-permute-start(bf16[2,3,48,384]{3,2,1,0:T(8,128)(2,1)S(1)} %pad_maximum_fusion.1.refs_0_), channel_id=1, source_target_pairs={{0,192},{64,0},{128,64},{192,128},{1,193},{65,1},{129,65},{193,129... | collective-permute-start | bytes 663560 | tf_op jit(solution)/shard_map/ppermute | solution.py:24
  14.2 3.1 %copy-start = (f32[1280,768]{1,0:T(8,128)}, f32[1280,768]{1,0:T(8,128)S(1)}, u32[]{:S(2)}) copy-start(f32[1280,768]{1,0:T(8,128)S(1)} %get-tuple-element.62.inputs) | copy-start | bytes 11796484
  14.2 3.0 %copy-start.1 = (bf16[1,1280,768]{2,1,0:T(8,128)(2,1)S(1)}, bf16[1,1280,768]{2,1,0:T(8,128)(2,1)}, u32[]{:S(2)}) copy-start(bf16[1,1280,768]{2,1,0:T(8,128)(2,1)} %param.11) | copy-start | bytes 5898244
  14.6 6.6 %copy-start.2 = (bf16[1280,768]{1,0:T(8,128)(2,1)}, bf16[1280,768]{1,0:T(8,128)(2,1)S(1)}, u32[]{:S(2)}) copy-start(bf16[1280,768]{1,0:T(8,128)(2,1)S(1)} %multiply_convert_fusion.refs_7_) | copy-start | bytes 5898244
  14.7 23.3 %copy-start.8 = (bf16[2,3,48,384]{3,2,1,0:T(8,128)(2,1)}, bf16[2,3,48,384]{3,2,1,0:T(8,128)(2,1)S(1)}, u32[]{:S(2)}) copy-start(bf16[2,3,48,384]{3,2,1,0:T(8,128)(2,1)S(1)} %collective-permute-done.1.refs_1_) | copy-start | bytes 663556
  14.7 1.5 %copy-start.12 = (bf16[2,3,48,384]{3,2,1,0:T(8,128)(2,1)}, bf16[2,3,48,384]{3,2,1,0:T(8,128)(2,1)S(1)}, u32[]{:S(2)}) copy-start(bf16[2,3,48,384]{3,2,1,0:T(8,128)(2,1)S(1)} %collective-permute-done.2.refs_2_) | copy-start | bytes 663556
  14.7 1.5 %copy-start.13 = (bf16[2,3,48,384]{3,2,1,0:T(8,128)(2,1)}, bf16[2,3,48,384]{3,2,1,0:T(8,128)(2,1)S(1)}, u32[]{:S(2)}) copy-start(bf16[2,3,48,384]{3,2,1,0:T(8,128)(2,1)S(1)} %collective-permute-done.3.refs_4_) | copy-start | bytes 663556
  14.7 6.5 %collective-permute-start.7 = (bf16[1280,768]{1,0:T(8,128)(2,1)S(1)}, bf16[1280,768]{1,0:T(8,128)(2,1)S(1)}, u32[]{:S(2)}, u32[]{:S(2)}) collective-permute-start(bf16[1280,768]{1,0:T(8,128)(2,1)S(1)} %multiply_convert_fusion.refs_7_), channel_id=1, source_target_pairs={{0,16},{16,0},{1,17},{17,1},{2,18},{18,2},{3,19},{19,3},{4,20},{20... | collective-permute-start | bytes 5898248 | tf_op jit(solution)/shard_map/ppermute | solution.py:28
  17.3 3.9 %collective-permute-start.8 = (bf16[1280,384]{1,0:T(8,128)(2,1)S(1)}, bf16[1280,384]{1,0:T(8,128)(2,1)S(1)}, u32[]{:S(2)}, u32[]{:S(2)}) collective-permute-start(bf16[1280,384]{1,0:T(8,128)(2,1)S(1)} %constant_dynamic-slice_fusion.2), channel_id=1, source_target_pairs={{0,16},{16,0},{1,17},{17,1},{2,18},{18,2},{3,19},{19,3},{4,20},{20... | collective-permute-start | bytes 2949128 | tf_op jit(solution)/shard_map/ppermute | solution.py:28
  19.4 18.6 %collective-permute-start.6 = (bf16[2,2,3,48,384]{4,3,2,1,0:T(8,128)(2,1)}, bf16[2,2,3,48,384]{4,3,2,1,0:T(8,128)(2,1)}, u32[]{:S(2)}, u32[]{:S(2)}) collective-permute-start(bf16[2,2,3,48,384]{4,3,2,1,0:T(8,128)(2,1)} %pad_maximum_fusion), channel_id=1, source_target_pairs={{0,128},{64,192},{128,0},{192,64},{1,129},{65,193},{129,1},{193,65... | collective-permute-start | bytes 1327112 | tf_op jit(solution)/shard_map/ppermute | solution.py:24
  21.2 16.8 %copy-start.6 = (bf16[1280,384]{1,0:T(8,128)(2,1)}, bf16[1280,384]{1,0:T(8,128)(2,1)S(1)}, u32[]{:S(2)}) copy-start(bf16[1280,384]{1,0:T(8,128)(2,1)S(1)} %collective-permute-done.8.refs_12_) | copy-start | bytes 2949124
  21.2 1.3 %copy-start.3 = (bf16[1280,768]{1,0:T(8,128)(2,1)}, bf16[1280,768]{1,0:T(8,128)(2,1)S(1)}, u32[]{:S(2)}) copy-start(bf16[1280,768]{1,0:T(8,128)(2,1)S(1)} %collective-permute-done.7.refs_8_) | copy-start | bytes 5898244
  22.5 15.4 %collective-permute-start.10 = (bf16[160,768]{1,0:T(8,128)(2,1)S(1)}, bf16[160,768]{1,0:T(8,128)(2,1)S(1)}, u32[]{:S(2)}, u32[]{:S(2)}) collective-permute-start(bf16[160,768]{1,0:T(8,128)(2,1)S(1)} %maximum_maximum_fusion.1), channel_id=1, source_target_pairs={{1,0},{2,1},{3,2},{4,3},{5,4},{6,5},{7,6},{8,7},{9,8},{10,9},{11,1... | collective-permute-start | bytes 737288 | tf_op jit(solution)/shard_map/ppermute | solution.py:294
  23.9 14.1 %collective-permute-start.9 = (bf16[160,768]{1,0:T(8,128)(2,1)S(1)}, bf16[160,768]{1,0:T(8,128)(2,1)S(1)}, u32[]{:S(2)}, u32[]{:S(2)}) collective-permute-start(bf16[160,768]{1,0:T(8,128)(2,1)S(1)} %maximum_maximum_fusion), channel_id=1, source_target_pairs={{0,1},{1,2},{2,3},{3,4},{4,5},{5,6},{6,7},{7,8},{8,9},{9,10},{10,1... | collective-permute-start | bytes 737288 | tf_op jit(solution)/shard_map/ppermute | solution.py:293
  28.1 9.9 %collective-permute-start.4 = (bf16[2,3,48,384]{3,2,1,0:T(8,128)(2,1)S(1)}, bf16[2,3,48,384]{3,2,1,0:T(8,128)(2,1)S(1)}, u32[]{:S(2)}, u32[]{:S(2)}) collective-permute-start(bf16[2,3,48,384]{3,2,1,0:T(8,128)(2,1)S(1)} %collective-permute-done.1.refs_1_), channel_id=1, source_target_pairs={{0,64},{64,128},{128,192},{192,0},{1,65},{65,129},{129,193},{193,1... | collective-permute-start | bytes 663560 | tf_op jit(solution)/shard_map/ppermute | solution.py:24
  29.3 8.7 %collective-permute-start.5 = (bf16[2,3,48,384]{3,2,1,0:T(8,128)(2,1)S(1)}, bf16[2,3,48,384]{3,2,1,0:T(8,128)(2,1)S(1)}, u32[]{:S(2)}, u32[]{:S(2)}) collective-permute-start(bf16[2,3,48,384]{3,2,1,0:T(8,128)(2,1)S(1)} %collective-permute-done.1.refs_1_), channel_id=1, source_target_pairs={{0,192},{64,0},{128,64},{192,128},{1,193},{65,1},{129,65},{193,129... | collective-permute-start | bytes 663560 | tf_op jit(solution)/shard_map/ppermute | solution.py:24
  38.0 0.7 copy-start.14
  38.0 0.7 copy-start.15
  38.0 0.8 copy-start.10
  38.8 0.7 copy-start.11
  56.3 5.6 %collective-permute-start.12 = (bf16[3,768,384]{2,1,0:T(8,128)(2,1)}, bf16[3,768,384]{2,1,0:T(8,128)(2,1)S(1)}, u32[]{:S(2)}, u32[]{:S(2)}) collective-permute-start(bf16[3,768,384]{2,1,0:T(8,128)(2,1)} %get-tuple-element.44.weight_a), channel_id=1, source_target_pairs={{0,16},{16,0},{1,17},{17,1},{2,18},{18,2},{3,19},{19,3},{4,20},{20... | collective-permute-start | bytes 5308424 | tf_op jit(solution)/shard_map/ppermute | solution.py:28
  56.8 5.0 %collective-permute-start.11 = (bf16[1344,384]{1,0:T(8,128)(2,1)}, bf16[1344,384]{1,0:T(8,128)(2,1)S(1)}, u32[]{:S(2)}, u32[]{:S(2)}) collective-permute-start(bf16[1344,384]{1,0:T(8,128)(2,1)} %get-tuple-element.43), channel_id=1, source_target_pairs={{0,16},{16,0},{1,17},{17,1},{2,18},{18,2},{3,19},{19,3},{4,20},{20... | collective-permute-start | bytes 3096584 | tf_op jit(solution)/shard_map/ppermute | solution.py:28
  56.9 17.3 %collective-permute-start.13 = (bf16[3,192,384]{2,1,0:T(8,128)(2,1)}, bf16[3,192,384]{2,1,0:T(8,128)(2,1)}, u32[]{:S(2)}, u32[]{:S(2)}) collective-permute-start(bf16[3,192,384]{2,1,0:T(8,128)(2,1)} %get-tuple-element.46), channel_id=1, source_target_pairs={{0,64},{64,128},{128,192},{192,0},{1,65},{65,129},{129,193},{193,1... | collective-permute-start | bytes 1327112 | tf_op jit(solution)/shard_map/ppermute | solution.py:24
  57.0 17.2 %collective-permute-start.14 = (bf16[3,192,384]{2,1,0:T(8,128)(2,1)}, bf16[3,192,384]{2,1,0:T(8,128)(2,1)}, u32[]{:S(2)}, u32[]{:S(2)}) collective-permute-start(bf16[3,192,384]{2,1,0:T(8,128)(2,1)} %get-tuple-element.47), channel_id=1, source_target_pairs={{0,192},{64,0},{128,64},{192,128},{1,193},{65,1},{129,65},{193,129... | collective-permute-start | bytes 1327112 | tf_op jit(solution)/shard_map/ppermute | solution.py:24
  59.6 19.7 %collective-permute-start.15 = (bf16[3,192,384]{2,1,0:T(8,128)(2,1)}, bf16[3,192,384]{2,1,0:T(8,128)(2,1)}, u32[]{:S(2)}, u32[]{:S(2)}) collective-permute-start(bf16[3,192,384]{2,1,0:T(8,128)(2,1)} %get-tuple-element.48), channel_id=1, source_target_pairs={{0,128},{64,192},{128,0},{192,64},{1,129},{65,193},{129,1},{193,65... | collective-permute-start | bytes 1327112 | tf_op jit(solution)/shard_map/ppermute | solution.py:24
  61.9 1.0 copy-start.7
  61.9 1.5 %copy-start.5 = (bf16[3,768,384]{2,1,0:T(8,128)(2,1)}, bf16[3,768,384]{2,1,0:T(8,128)(2,1)S(1)}, u32[]{:S(2)}) copy-start(bf16[3,768,384]{2,1,0:T(8,128)(2,1)S(1)} %collective-permute-done.12.weight_b) | copy-start | bytes 5308420
  63.4 15.9 %copy-start.9 = (bf16[3,192,384]{2,1,0:T(8,128)(2,1)S(1)}, bf16[3,192,384]{2,1,0:T(8,128)(2,1)}, u32[]{:S(2)}) copy-start(bf16[3,192,384]{2,1,0:T(8,128)(2,1)} %get-tuple-element.50) | copy-start | bytes 1327108
  80.8 7.4 %collective-permute-start.16 = (bf16[3,48,384]{2,1,0:T(8,128)(2,1)S(1)}, bf16[3,48,384]{2,1,0:T(8,128)(2,1)S(1)}, u32[]{:S(2)}, u32[]{:S(2)}) collective-permute-start(bf16[3,48,384]{2,1,0:T(8,128)(2,1)S(1)} %get-tuple-element.69), channel_id=1, source_target_pairs={{0,8},{8,32},{32,40},{40,0},{1,9},{9,33},{33,41},{41,1},{2,10},{10... | collective-permute-start | bytes 331784 | tf_op jit(solution)/shard_map/ppermute | solution.py:24
  86.3 3.6 %collective-permute-start.17 = (bf16[3,48,384]{2,1,0:T(8,128)(2,1)S(1)}, bf16[3,48,384]{2,1,0:T(8,128)(2,1)S(1)}, u32[]{:S(2)}, u32[]{:S(2)}) collective-permute-start(bf16[3,48,384]{2,1,0:T(8,128)(2,1)S(1)} %get-tuple-element.71), channel_id=1, source_target_pairs={{0,40},{8,0},{32,8},{40,32},{1,41},{9,1},{33,9},{41,33},{2,42},{10... | collective-permute-start | bytes 331784 | tf_op jit(solution)/shard_map/ppermute | solution.py:24
  86.3 5.4 %collective-permute-start.18 = (bf16[3,48,384]{2,1,0:T(8,128)(2,1)S(1)}, bf16[3,48,384]{2,1,0:T(8,128)(2,1)S(1)}, u32[]{:S(2)}, u32[]{:S(2)}) collective-permute-start(bf16[3,48,384]{2,1,0:T(8,128)(2,1)S(1)} %get-tuple-element.70), channel_id=1, source_target_pairs={{0,32},{8,40},{32,0},{40,8},{1,33},{9,41},{33,1},{41,9},{2,34},{10... | collective-permute-start | bytes 331784 | tf_op jit(solution)/shard_map/ppermute | solution.py:24
  92.8 3.7 %collective-permute-start.19 = (bf16[3,48,384]{2,1,0:T(8,128)(2,1)S(1)}, bf16[3,48,384]{2,1,0:T(8,128)(2,1)S(1)}, u32[]{:S(2)}, u32[]{:S(2)}) collective-permute-start(bf16[3,48,384]{2,1,0:T(8,128)(2,1)S(1)} %add_convert_fusion.2), channel_id=1, source_target_pairs={{0,1},{1,0},{2,3},{3,2},{4,5},{5,4},{6,7},{7,6},{8,9},{9,8},{10,11... | collective-permute-start | bytes 331784 | tf_op jit(solution)/shard_map/ppermute | solution.py:28
  92.9 6.2 %collective-permute-start.20 = (bf16[3,48,384]{2,1,0:T(8,128)(2,1)S(1)}, bf16[3,48,384]{2,1,0:T(8,128)(2,1)S(1)}, u32[]{:S(2)}, u32[]{:S(2)}) collective-permute-start(bf16[3,48,384]{2,1,0:T(8,128)(2,1)S(1)} %add_convert_fusion.2), channel_id=1, source_target_pairs={{0,2},{1,3},{2,0},{3,1},{4,6},{5,7},{6,4},{7,5},{8,10},{9,11},{10,... | collective-permute-start | bytes 331784 | tf_op jit(solution)/shard_map/ppermute | solution.py:28
  95.7 6.5 %collective-permute-start.21 = (bf16[3,48,384]{2,1,0:T(8,128)(2,1)S(1)}, bf16[3,48,384]{2,1,0:T(8,128)(2,1)S(1)}, u32[]{:S(2)}, u32[]{:S(2)}) collective-permute-start(bf16[3,48,384]{2,1,0:T(8,128)(2,1)S(1)} %add_convert_fusion.2), channel_id=1, source_target_pairs={{0,3},{1,2},{2,1},{3,0},{4,7},{5,6},{6,5},{7,4},{8,11},{9,10},{10,... | collective-permute-start | bytes 331784 | tf_op jit(solution)/shard_map/ppermute | solution.py:28
  102.3 5.5 %collective-permute-start.22 = (bf16[3,48,384]{2,1,0:T(8,128)(2,1)S(1)}, bf16[3,48,384]{2,1,0:T(8,128)(2,1)S(1)}, u32[]{:S(2)}, u32[]{:S(2)}) collective-permute-start(bf16[3,48,384]{2,1,0:T(8,128)(2,1)S(1)} %add_convert_fusion.1), channel_id=1, source_target_pairs={{0,7},{1,6},{2,5},{3,4},{4,3},{5,2},{6,1},{7,0},{8,15},{9,14},{10,... | collective-permute-start | bytes 331784 | tf_op jit(solution)/shard_map/ppermute | solution.py:28
  107.8 7.2 %collective-permute-start.23 = (bf16[3,48,384]{2,1,0:T(8,128)(2,1)S(1)}, bf16[3,48,384]{2,1,0:T(8,128)(2,1)S(1)}, u32[]{:S(2)}, u32[]{:S(2)}) collective-permute-start(bf16[3,48,384]{2,1,0:T(8,128)(2,1)S(1)} %add_convert_fusion), channel_id=1, source_target_pairs={{16,0},{8,24},{0,8},{24,16},{17,1},{9,25},{1,9},{25,17},{18,2},{10... | collective-permute-start | bytes 331784 | tf_op jit(solution)/shard_map/ppermute | solution.py:241
  113.1 6.1 %collective-permute-start.24 = (bf16[3,48,384]{2,1,0:T(8,128)(2,1)S(1)}, bf16[3,48,384]{2,1,0:T(8,128)(2,1)S(1)}, u32[]{:S(2)}, u32[]{:S(2)}) collective-permute-start(bf16[3,48,384]{2,1,0:T(8,128)(2,1)S(1)} %add_convert_fusion), channel_id=1, source_target_pairs={{16,8},{8,16},{17,9},{9,17},{18,10},{10,18},{19,11},{11,19},{20,12... | collective-permute-start | bytes 331784 | tf_op jit(solution)/shard_map/ppermute | solution.py:242

commit v8 on v7

--- a/solution.py
+++ b/solution.py
@@ -44,8 +44,9 @@
 def load_weight(position, pieces, weight, sem):
     x, yh, core = position[0], position[1], position[2]
     rows = pieces[0].shape[2]
+    own, across, up, down, far_own, far_across = pieces
     steps = [(0, 0), (0, 1), (3, 0), (3, 1), (1, 0), (1, 1), (2, 0), (2, 1)]
-    blocks = list(pieces[:6]) + [pieces[6].at[0], pieces[6].at[1]]
+    blocks = [own, across, up.at[0], up.at[1], down.at[0], down.at[1], far_own, far_across]
     copies = []
     for block, (step_x, step_y) in zip(blocks, steps):
         for side in range(2):
@@ -60,7 +61,7 @@
 
 
 def forward_kernel(position, *refs):
-    pieces, refs = refs[:7], refs[7:]
+    pieces, refs = refs[:6], refs[6:]
     normed_hbm, edges, upstream_hbm = refs[0:2], refs[2:4], refs[4:6]
     weight_out, back_out, grad_out = refs[6], refs[7:9], refs[9:13]
     weight, normed, upstream, back, grad = refs[13:18]
@@ -175,7 +176,7 @@
         out_shape=[jax.ShapeDtypeStruct((FILTER_TAPS, channels, half), BF16)]
         + [jax.ShapeDtypeStruct((length, half), BF16)] * 2
         + [jax.ShapeDtypeStruct((FILTER_TAPS, channels // 4, half), BF16)] * 4,
-        in_specs=[pl.BlockSpec(memory_space=pltpu.SMEM)] + [anywhere] * 13,
+        in_specs=[pl.BlockSpec(memory_space=pltpu.SMEM)] + [anywhere] * 12,
         out_specs=[anywhere] * 7,
         scratch_shapes=[
             pltpu.VMEM((FILTER_TAPS, channels, half), BF16),
@@ -227,7 +228,7 @@
         in_specs=[whole(back[0]), whole(back[1]), whole(weight[0]), whole(weight[1]), part]
         + [pl.BlockSpec((block, 1), lambda i: (i, 0)), whole(gain), part],
         out_specs=part,
-        compiler_params=pltpu.CompilerParams(vmem_limit_bytes=56 * 1024 * 1024),
+        compiler_params=pltpu.CompilerParams(vmem_limit_bytes=36 * 1024 * 1024),
         name="backward",
     )(*back, *weight, inputs, scale, gain, incoming)
 
@@ -261,20 +262,16 @@
     own, tokens, nucleotides, incoming = join(own, tokens, nucleotides, incoming)
 
     across = swap(own, RING_Y, 4, 3)
-    up_own, down_own = shift(own, "x", 4, 1), shift(own, "x", 4, -1)
-    bases = nucleotides[0][:, None]
-    row = base_table[3][None]
-    for base in (2, 1, 0):
-        row = jnp.where(bases == base, base_table[base][None], row)
-    inputs = tokens.astype(F32) + row
+    far_own = shift(own, "x", 4, 2)
+    hot = (nucleotides[0][:, None] == jnp.arange(4, dtype=jnp.int32)[None, :]).astype(F32)
+    inputs = tokens.astype(F32) + jnp.dot(hot, base_table, precision=lax.Precision.HIGHEST)
     scale_inv = lax.rsqrt(jnp.mean(inputs * inputs, axis=-1, keepdims=True) + 1e-06)
     normed = (inputs * scale_inv * norm_gain).astype(BF16)
-    own, across, up_own, down_own, normed, incoming = join(
-        own, across, up_own, down_own, normed, incoming
-    )
-
-    far = shift(jnp.stack([own, across]), "x", 4, 2)
-    up_across, down_across = shift(across, "x", 4, 1), shift(across, "x", 4, -1)
+    own, across, far_own, normed, incoming = join(own, across, far_own, normed, incoming)
+
+    pair = jnp.stack([own, across])
+    up, down = shift(pair, "x", 4, 1), shift(pair, "x", 4, -1)
+    far_across = shift(across, "x", 4, 2)
     upstream_sent = lax.dynamic_slice_in_dim(incoming, (1 - core) * half, half, axis=1)
     normed_other = swap(normed, "core", 2, 1)
     upstream_other = swap(upstream_sent, "core", 2, 1)
@@ -295,7 +292,7 @@
     )
     weight, back, back_other, *grads = forward(
         position,
-        [own, across, up_own, up_across, down_own, down_across, far],
+        [own, across, up, down, far_own, far_across],
         (normed, normed_other),
         edges,
         (incoming, upstream_other),

time: 121 us -> 120 us (level)
  other arithmetic: 9.9 us -> 6.09 us
  matrix products: 0 us -> 3.59 us
  Pallas kernels: 27.5 us -> 26 us
    reduce_sum x1 -> x0, other arithmetic: 3.71 us -> none  [on_device(): jnp.mean(inputs * inputs, axis=-1, keepdims=True) + 1e-06]
    dot_general x0 -> x1, matrix products: none -> 3.59 us  [on_device(): jnp.dot(hot, base_table, precision=lax.Precision.HIGHEST)]
    unnamed x34, local copies, waits for them, and re-layouts: 5.32 us -> 8.41 us
    ppermute x11 -> x10, waiting for transfers between devices: 14.9 us -> 12.3 us  [shift(): return lax.ppermute(value, axis, pairs)]
    ppermute x10, waiting for transfers between devices: 8.44 us -> 10.8 us  [swap(): return lax.ppermute(value, axis, [(i, i ^ mask) for i in range(count)])]
    pallas_call x1, Pallas kernels: 10.8 us -> 9.08 us  [backward(): pl.pallas_call(backward_kernel, grid=(count // block,), out_shape=jax.Sha...]
    ppermute x11 -> x10, starting transfers between devices: 17.5 us -> 17.7 us  [shift(): return lax.ppermute(value, axis, pairs)]
  transfers between devices with their start and end apart: 25 -> 24, of which waited for: 12 -> 13; matrix products, arithmetic and copies ran while one was open for 8% -> 5% of each run, Pallas kernels for 9% -> 8%
where the time goes in v8:
time: 120 us
  starting transfers between devices  46.2 us (38%)
  waiting for transfers between devices  27.2 us (23%)
  Pallas kernels  26 us (22%)
  local copies, waits for them, and re-layouts  9.78 us (8%)
  other arithmetic  6.09 us (5%)
  matrix products  3.59 us (3%)
    ppermute x10, starting transfers between devices, shift(): return lax.ppermute(value, axis, pairs)  17.7 us
    pallas_call x1, Pallas kernels, forward(): pl.pallas_call(forward_kernel, out_shape=[jax.ShapeDtypeStruct((FILTER_TA...  16.9 us
    ppermute x10, starting transfers between devices, swap(): return lax.ppermute(value, axis, [(i, i ^ mask) for i in range(count)])  15.2 us
    ppermute x10, waiting for transfers between devices, shift(): return lax.ppermute(value, axis, pairs)  12.3 us
    ppermute x10, waiting for transfers between devices, swap(): return lax.ppermute(value, axis, [(i, i ^ mask) for i in range(count)])  10.8 us
    pallas_call x1, Pallas kernels, backward(): pl.pallas_call(backward_kernel, grid=(count // block,), out_shape=jax.Sha...  9.08 us
    unnamed x34, local copies, waits for them, and re-layouts  8.41 us
    ppermute x1, starting transfers between devices, share_weight_grad(): first = lax.ppermute(mine, pair, [(2, 0), (1, 3), (0, 1), (3, 2)])  5.3 us
  transfers between devices with their start and end apart: 24, of which 13 were waited for; matrix products, arithmetic and copies ran while one was open for 5% of the time, Pallas kernels for 8%

profile of v8, /device:TPU:1, one launch (start us, length us, event | category | flops | bytes accessed | tf_op | source)
XLA Modules:
  0.0 119.8 jit_solution(11951232388666075802)
XLA Ops:
  0.6 0.0 copy-start
  0.7 1.0 dynamic-slice_bitcast_fusion
  1.6 3.3 %collective-permute-start = (bf16[3,48,384]{2,1,0:T(8,128)(2,1)S(1)}, bf16[3,48,384]{2,1,0:T(8,128)(2,1)S(1)}, u32[]{:S(2)}, u32[]{:S(2)}) collective-permute-start(bf16[3,48,384]{2,1,0:T(8,128)(2,1)S(1)} %get-tuple-element.66), channel_id=1, source_target_pairs={{0,16},{16,0},{1,17},{17,1},{2,18},{18,2},{3,19},{19,3},{4,20},{20... | collective-permute-start | bytes 331784 | tf_op jit(solution)/shard_map/ppermute | solution.py:28
  5.0 1.0 collective-permute-done
  6.0 1.1 collective-permute-start.1
  7.1 2.7 %collective-permute-start.2 = (bf16[2,3,48,384]{3,2,1,0:T(8,128)(2,1)S(1)}, bf16[2,3,48,384]{3,2,1,0:T(8,128)(2,1)S(1)}, u32[]{:S(2)}, u32[]{:S(2)}) collective-permute-start(bf16[2,3,48,384]{3,2,1,0:T(8,128)(2,1)S(1)} %pad_maximum_fusion.1.refs_0_), channel_id=1, source_target_pairs={{0,128},{64,192},{128,0},{192,64},{1,129},{65,193},{129,1},{193,65... | collective-permute-start | bytes 663560 | tf_op jit(solution)/shard_map/ppermute | solution.py:24
  9.8 0.7 reduce
  10.5 0.0 copy-start.16
  10.5 3.6 %multiply_reduce_fusion = (f32[1280]{0:T(1024)S(1)}, f32[1280,768]{1,0:T(8,128)S(1)}) fusion(f32[4,768]{1,0:T(4,128)S(1)} %copy-done, s32[1280]{0:T(1024)S(1)} %reduce, bf16[1280,768]{1,0:T(8,128)(2,1)} %bitcast.18), kind=kOutput, calls=%fused_computation.2 | convolution fusion | flops 51121920 | bytes 5920768 | tf_op jit(solution)/shard_map/dot_general | solution.py:267
  14.2 0.0 copy-start.3
  14.2 0.4 multiply_convert_fusion.refs_6_
  14.6 1.6 %copy-done.1 = f32[1280,768]{1,0:T(8,128)} copy-done((f32[1280,768]{1,0:T(8,128)}, f32[1280,768]{1,0:T(8,128)S(1)}, u32[]{:S(2)}) %copy-start.1) | copy-done | bytes 3932184
  16.1 0.0 collective-permute-done.1.refs_1_
  16.1 0.0 collective-permute-done.2.refs_4_
  16.1 1.0 collective-permute-start.6
  17.2 0.1 constant_dynamic-slice_fusion.2
  17.3 1.0 collective-permute-start.7
  18.2 0.8 pad_maximum_fusion
  19.1 0.3 collective-permute-start.3
  19.4 2.4 %collective-permute-start.4 = (bf16[2,2,3,48,384]{4,3,2,1,0:T(8,128)(2,1)}, bf16[2,2,3,48,384]{4,3,2,1,0:T(8,128)(2,1)}, u32[]{:S(2)}, u32[]{:S(2)}) collective-permute-start(bf16[2,2,3,48,384]{4,3,2,1,0:T(8,128)(2,1)} %pad_maximum_fusion), channel_id=1, source_target_pairs={{0,192},{64,0},{128,64},{192,128},{1,193},{65,1},{129,65},{193,129... | collective-permute-start | bytes 1327112 | tf_op jit(solution)/shard_map/ppermute | solution.py:24
  21.7 0.4 collective-permute-done.7.refs_11_
  22.2 0.0 collective-permute-done.6.refs_7_
  22.3 1.2 %copy-done.8 = bf16[1280,768]{1,0:T(8,128)(2,1)} copy-done((bf16[1280,768]{1,0:T(8,128)(2,1)}, bf16[1280,768]{1,0:T(8,128)(2,1)S(1)}, u32[]{:S(2)}) %copy-start.8) | copy-done | bytes 1966104
  23.5 1.3 %collective-permute-start.9 = (bf16[160,768]{1,0:T(8,128)(2,1)S(1)}, bf16[160,768]{1,0:T(8,128)(2,1)S(1)}, u32[]{:S(2)}, u32[]{:S(2)}) collective-permute-start(bf16[160,768]{1,0:T(8,128)(2,1)S(1)} %maximum_maximum_fusion.1), channel_id=1, source_target_pairs={{1,0},{2,1},{3,2},{4,3},{5,4},{6,5},{7,6},{8,7},{9,8},{10,9},{11,1... | collective-permute-start | bytes 737288 | tf_op jit(solution)/shard_map/ppermute | solution.py:291
  24.9 4.9 %collective-permute-start.8 = (bf16[160,768]{1,0:T(8,128)(2,1)S(1)}, bf16[160,768]{1,0:T(8,128)(2,1)}, u32[]{:S(2)}, u32[]{:S(2)}) collective-permute-start(bf16[160,768]{1,0:T(8,128)(2,1)S(1)} %maximum_maximum_fusion), channel_id=1, source_target_pairs={{0,1},{1,2},{2,3},{3,4},{4,5},{5,6},{6,7},{7,8},{8,9},{9,10},{10,1... | collective-permute-start | bytes 737288 | tf_op jit(solution)/shard_map/ppermute | solution.py:290
  29.7 2.0 %collective-permute-start.5 = (bf16[2,3,48,384]{3,2,1,0:T(8,128)(2,1)S(1)}, bf16[2,3,48,384]{3,2,1,0:T(8,128)(2,1)S(1)}, u32[]{:S(2)}, u32[]{:S(2)}) collective-permute-start(bf16[2,3,48,384]{3,2,1,0:T(8,128)(2,1)S(1)} %collective-permute-done.1.refs_1_), channel_id=1, source_target_pairs={{0,128},{64,192},{128,0},{192,64},{1,129},{65,193},{129,1},{193,65... | collective-permute-start | bytes 663560 | tf_op jit(solution)/shard_map/ppermute | solution.py:24
  31.7 0.6 pad_add_fusion.position
  32.3 5.1 %collective-permute-done.5.refs_5_ = bf16[2,3,48,384]{3,2,1,0:T(8,128)(2,1)S(1)} collective-permute-done((bf16[2,3,48,384]{3,2,1,0:T(8,128)(2,1)S(1)}, bf16[2,3,48,384]{3,2,1,0:T(8,128)(2,1)S(1)}, u32[]{:S(2)}, u32[]{:S(2)}) %collective-permute-start.5) | collective-permute-done | bytes 221216 | tf_op jit(solution)/shard_map/ppermute | solution.py:24
  37.5 0.0 collective-permute-done.3.refs_2_
  37.5 0.7 copy-done.13
  38.2 0.0 copy-done.15
  38.2 16.9 %forward.1 = (bf16[3,768,384]{2,1,0:T(8,128)(2,1)}, bf16[1344,384]{1,0:T(8,128)(2,1)}, bf16[1344,384]{1,0:T(8,128)(2,1)}, bf16[3,192,384]{2,1,0:T(8,128)(2,1)}, ...) custom-call(s32[4]{0:T(128)} %pad_add_fusion.position, ...), custom_call_target="tpu_custom_call" | custom-call | tf_op jit(solution)/shard_map/forward/pallas_call | solution.py:174
  55.1 1.7 %collective-permute-start.11 = (bf16[3,768,384]{2,1,0:T(8,128)(2,1)}, bf16[3,768,384]{2,1,0:T(8,128)(2,1)}, u32[]{:S(2)}, u32[]{:S(2)}) collective-permute-start(bf16[3,768,384]{2,1,0:T(8,128)(2,1)} %get-tuple-element.42.weight_a), channel_id=1, source_target_pairs={{0,16},{16,0},{1,17},{17,1},{2,18},{18,2},{3,19},{19,3},{4,20},{20... | collective-permute-start | bytes 5308424 | tf_op jit(solution)/shard_map/ppermute | solution.py:28
  56.9 0.1 collective-permute-start.10
  57.0 0.5 collective-permute-start.12
  57.4 2.2 %collective-permute-start.13 = (bf16[3,192,384]{2,1,0:T(8,128)(2,1)}, bf16[3,192,384]{2,1,0:T(8,128)(2,1)}, u32[]{:S(2)}, u32[]{:S(2)}) collective-permute-start(bf16[3,192,384]{2,1,0:T(8,128)(2,1)} %get-tuple-element.45), channel_id=1, source_target_pairs={{0,192},{64,0},{128,64},{192,128},{1,193},{65,1},{129,65},{193,129... | collective-permute-start | bytes 1327112 | tf_op jit(solution)/shard_map/ppermute | solution.py:24
  59.6 0.8 collective-permute-start.14
  60.4 0.2 rsqrt.7.scale
  60.6 1.2 collective-permute-done.10.back_b
  61.8 0.2 collective-permute-done.11.weight_b
  62.0 2.1 %copy-done.2 = f32[1280,768]{1,0:T(8,128)S(1)} copy-done((f32[1280,768]{1,0:T(8,128)S(1)}, f32[1280,768]{1,0:T(8,128)}, u32[]{:S(2)}) %copy-start.2) | copy-done | bytes 3932184
  64.1 1.5 %copy-done.5 = bf16[3,768,384]{2,1,0:T(8,128)(2,1)S(1)} copy-done((bf16[3,768,384]{2,1,0:T(8,128)(2,1)S(1)}, bf16[3,768,384]{2,1,0:T(8,128)(2,1)}, u32[]{:S(2)}) %copy-start.5) | copy-done | bytes 1769496
  65.6 1.2 %copy-done.6 = bf16[1344,384]{1,0:T(8,128)(2,1)S(1)} copy-done((bf16[1344,384]{1,0:T(8,128)(2,1)S(1)}, bf16[1344,384]{1,0:T(8,128)(2,1)}, u32[]{:S(2)}) %copy-start.6) | copy-done | bytes 1032216
  66.8 9.1 %backward.1 = bf16[1280,768]{1,0:T(8,128)(2,1)} custom-call(bf16[1344,384]{1,0:T(8,128)(2,1)S(1)} %copy-done.6, bf16[1344,384]{1,0:T(8,128)(2,1)S(1)} %collective-permute-done.10.back_b, bf16[3,768,384]{2,1,0:T(8,128)(2,1)S(1)} %copy-done.5, bf16[3,768,384]{2,1,0:T(8,128)(2,1)} %collective-permute-done.11.weight_b, f32[1280,768]{1,0:T(8,128)S(1)} %copy-done.2, ...), custom_call_target="tpu_custom_call" | custom-call | tf_op jit(solution)/shard_map/backward/pallas_call | solution.py:224
  75.9 3.6 %collective-permute-done.14 = bf16[3,192,384]{2,1,0:T(8,128)(2,1)} collective-permute-done((bf16[3,192,384]{2,1,0:T(8,128)(2,1)}, bf16[3,192,384]{2,1,0:T(8,128)(2,1)}, u32[]{:S(2)}, u32[]{:S(2)}) %collective-permute-start.14) | collective-permute-done | bytes 442400 | tf_op jit(solution)/shard_map/ppermute | solution.py:24
  79.5 1.5 %add_convert_fusion.5 = (bf16[3,48,384]{2,1,0:T(8,128)(2,1)S(1)}, bf16[3,48,384]{2,1,0:T(8,128)(2,1)S(1)}, bf16[3,48,384]{2,1,0:T(8,128)(2,1)S(1)}) fusion(bf16[3,192,384]{2,1,0:T(8,128)(2,1)} %collective-permute-done.14, s32[]{:T(128)S(6)} %select_n.81, bf16[3,192,384]{2,1,0:T(8,128)(2,1)} %collective-permute-done.13, ...), kind=kLoop, calls=%fused_computation.15 | loop fusion | flops 1327104 | bytes 1658892 | tf_op jit(solution)/shard_map/convert_element_type | solution.py:317
  81.0 4.9 %collective-permute-start.15 = (bf16[3,48,384]{2,1,0:T(8,128)(2,1)S(1)}, bf16[3,48,384]{2,1,0:T(8,128)(2,1)S(1)}, u32[]{:S(2)}, u32[]{:S(2)}) collective-permute-start(bf16[3,48,384]{2,1,0:T(8,128)(2,1)S(1)} %get-tuple-element.58), channel_id=1, source_target_pairs={{0,8},{8,32},{32,40},{40,0},{1,9},{9,33},{33,41},{41,1},{2,10},{10... | collective-permute-start | bytes 331784 | tf_op jit(solution)/shard_map/ppermute | solution.py:24
  85.9 1.9 %collective-permute-start.17 = (bf16[3,48,384]{2,1,0:T(8,128)(2,1)S(1)}, bf16[3,48,384]{2,1,0:T(8,128)(2,1)S(1)}, u32[]{:S(2)}, u32[]{:S(2)}) collective-permute-start(bf16[3,48,384]{2,1,0:T(8,128)(2,1)S(1)} %get-tuple-element.59), channel_id=1, source_target_pairs={{0,32},{8,40},{32,0},{40,8},{1,33},{9,41},{33,1},{41,9},{2,34},{10... | collective-permute-start | bytes 331784 | tf_op jit(solution)/shard_map/ppermute | solution.py:24
  87.8 1.7 %collective-permute-done.16 = bf16[3,48,384]{2,1,0:T(8,128)(2,1)S(1)} collective-permute-done((bf16[3,48,384]{2,1,0:T(8,128)(2,1)S(1)}, bf16[3,48,384]{2,1,0:T(8,128)(2,1)S(1)}, u32[]{:S(2)}, u32[]{:S(2)}) %collective-permute-start.16) | collective-permute-done | bytes 110624 | tf_op jit(solution)/shard_map/ppermute | solution.py:24
  89.5 1.8 %collective-permute-done.17 = bf16[3,48,384]{2,1,0:T(8,128)(2,1)S(1)} collective-permute-done((bf16[3,48,384]{2,1,0:T(8,128)(2,1)S(1)}, bf16[3,48,384]{2,1,0:T(8,128)(2,1)S(1)}, u32[]{:S(2)}, u32[]{:S(2)}) %collective-permute-start.17) | collective-permute-done | bytes 110624 | tf_op jit(solution)/shard_map/ppermute | solution.py:24
  91.3 1.1 add_convert_fusion.2
  92.4 0.1 collective-permute-start.18
  92.5 3.0 %collective-permute-start.19 = (bf16[3,48,384]{2,1,0:T(8,128)(2,1)S(1)}, bf16[3,48,384]{2,1,0:T(8,128)(2,1)S(1)}, u32[]{:S(2)}, u32[]{:S(2)}) collective-permute-start(bf16[3,48,384]{2,1,0:T(8,128)(2,1)S(1)} %add_convert_fusion.2), channel_id=1, source_target_pairs={{0,2},{1,3},{2,0},{3,1},{4,6},{5,7},{6,4},{7,5},{8,10},{9,11},{10,... | collective-permute-start | bytes 331784 | tf_op jit(solution)/shard_map/ppermute | solution.py:28
  95.5 0.6 collective-permute-start.20
  96.0 0.1 collective-permute-done.18
  96.1 2.8 %collective-permute-done.19 = bf16[3,48,384]{2,1,0:T(8,128)(2,1)S(1)} collective-permute-done((bf16[3,48,384]{2,1,0:T(8,128)(2,1)S(1)}, bf16[3,48,384]{2,1,0:T(8,128)(2,1)S(1)}, u32[]{:S(2)}, u32[]{:S(2)}) %collective-permute-start.19) | collective-permute-done | bytes 110624 | tf_op jit(solution)/shard_map/ppermute | solution.py:28
  98.9 3.1 %collective-permute-done.20 = bf16[3,48,384]{2,1,0:T(8,128)(2,1)S(1)} collective-permute-done((bf16[3,48,384]{2,1,0:T(8,128)(2,1)S(1)}, bf16[3,48,384]{2,1,0:T(8,128)(2,1)S(1)}, u32[]{:S(2)}, u32[]{:S(2)}) %collective-permute-start.20) | collective-permute-done | bytes 110624 | tf_op jit(solution)/shard_map/ppermute | solution.py:28
  102.0 0.1 add_convert_fusion.1
  102.0 3.4 %collective-permute-start.21 = (bf16[3,48,384]{2,1,0:T(8,128)(2,1)S(1)}, bf16[3,48,384]{2,1,0:T(8,128)(2,1)S(1)}, u32[]{:S(2)}, u32[]{:S(2)}) collective-permute-start(bf16[3,48,384]{2,1,0:T(8,128)(2,1)S(1)} %add_convert_fusion.1), channel_id=1, source_target_pairs={{0,7},{1,6},{2,5},{3,4},{4,3},{5,2},{6,1},{7,0},{8,15},{9,14},{10,... | collective-permute-start | bytes 331784 | tf_op jit(solution)/shard_map/ppermute | solution.py:28
  105.4 2.1 %collective-permute-done.21 = bf16[3,48,384]{2,1,0:T(8,128)(2,1)S(1)} collective-permute-done((bf16[3,48,384]{2,1,0:T(8,128)(2,1)S(1)}, bf16[3,48,384]{2,1,0:T(8,128)(2,1)S(1)}, u32[]{:S(2)}, u32[]{:S(2)}) %collective-permute-start.21) | collective-permute-done | bytes 110624 | tf_op jit(solution)/shard_map/ppermute | solution.py:28
  107.6 5.3 %collective-permute-start.22 = (bf16[3,48,384]{2,1,0:T(8,128)(2,1)S(1)}, bf16[3,48,384]{2,1,0:T(8,128)(2,1)S(1)}, u32[]{:S(2)}, u32[]{:S(2)}) collective-permute-start(bf16[3,48,384]{2,1,0:T(8,128)(2,1)S(1)} %add_convert_fusion), channel_id=1, source_target_pairs={{16,0},{8,24},{0,8},{24,16},{17,1},{9,25},{1,9},{25,17},{18,2},{10... | collective-permute-start | bytes 331784 | tf_op jit(solution)/shard_map/ppermute | solution.py:242
  112.9 1.9 %collective-permute-start.23 = (bf16[3,48,384]{2,1,0:T(8,128)(2,1)S(1)}, bf16[3,48,384]{2,1,0:T(8,128)(2,1)S(1)}, u32[]{:S(2)}, u32[]{:S(2)}) collective-permute-start(bf16[3,48,384]{2,1,0:T(8,128)(2,1)S(1)} %add_convert_fusion), channel_id=1, source_target_pairs={{16,8},{8,16},{17,9},{9,17},{18,10},{10,18},{19,11},{11,19},{20,12... | collective-permute-start | bytes 331784 | tf_op jit(solution)/shard_map/ppermute | solution.py:243
  114.8 4.1 %collective-permute-done.23 = bf16[3,48,384]{2,1,0:T(8,128)(2,1)S(1)} collective-permute-done((bf16[3,48,384]{2,1,0:T(8,128)(2,1)S(1)}, bf16[3,48,384]{2,1,0:T(8,128)(2,1)S(1)}, u32[]{:S(2)}, u32[]{:S(2)}) %collective-permute-start.23) | collective-permute-done | bytes 110624 | tf_op jit(solution)/shard_map/ppermute | solution.py:243
  119.0 0.8 convert_multiply_fusion
  (44 shorter events, 0.3 us)
Async XLA Ops:
  0.6 9.9 %copy-start = (f32[4,768]{1,0:T(4,128)S(1)}, f32[4,768]{1,0:T(4,128)}, u32[]{:S(2)}) copy-start(f32[4,768]{1,0:T(4,128)} %param.8) | copy-start | bytes 36868
  1.6 4.3 %collective-permute-start = (bf16[3,48,384]{2,1,0:T(8,128)(2,1)S(1)}, bf16[3,48,384]{2,1,0:T(8,128)(2,1)S(1)}, u32[]{:S(2)}, u32[]{:S(2)}) collective-permute-start(bf16[3,48,384]{2,1,0:T(8,128)(2,1)S(1)} %get-tuple-element.66), channel_id=1, source_target_pairs={{0,16},{16,0},{1,17},{17,1},{2,18},{18,2},{3,19},{19,3},{4,20},{20... | collective-permute-start | bytes 331784 | tf_op jit(solution)/shard_map/ppermute | solution.py:28
  6.0 12.3 %copy-start.9 = (bf16[2,3,48,384]{3,2,1,0:T(8,128)(2,1)}, bf16[2,3,48,384]{3,2,1,0:T(8,128)(2,1)S(1)}, u32[]{:S(2)}) copy-start(bf16[2,3,48,384]{3,2,1,0:T(8,128)(2,1)S(1)} %pad_maximum_fusion.1.refs_0_) | copy-start | bytes 663556
  6.0 10.2 %collective-permute-start.1 = (bf16[2,3,48,384]{3,2,1,0:T(8,128)(2,1)S(1)}, bf16[2,3,48,384]{3,2,1,0:T(8,128)(2,1)S(1)}, u32[]{:S(2)}, u32[]{:S(2)}) collective-permute-start(bf16[2,3,48,384]{3,2,1,0:T(8,128)(2,1)S(1)} %pad_maximum_fusion.1.refs_0_), channel_id=1, source_target_pairs={{0,40},{8,32},{32,8},{40,0},{1,41},{9,33},{33,9},{41,1},{2,42},{10... | collective-permute-start | bytes 663560 | tf_op jit(solution)/shard_map/ppermute | solution.py:28
  7.1 9.1 %collective-permute-start.2 = (bf16[2,3,48,384]{3,2,1,0:T(8,128)(2,1)S(1)}, bf16[2,3,48,384]{3,2,1,0:T(8,128)(2,1)S(1)}, u32[]{:S(2)}, u32[]{:S(2)}) collective-permute-start(bf16[2,3,48,384]{3,2,1,0:T(8,128)(2,1)S(1)} %pad_maximum_fusion.1.refs_0_), channel_id=1, source_target_pairs={{0,128},{64,192},{128,0},{192,64},{1,129},{65,193},{129,1},{193,65... | collective-permute-start | bytes 663560 | tf_op jit(solution)/shard_map/ppermute | solution.py:24
  10.5 3.6 %copy-start.16 = (f32[768]{0:T(1024)S(1)}, f32[768]{0:T(1024)}, u32[]{:S(2)}) copy-start(f32[768]{0:T(1024)} %param.9) | copy-start | bytes 9220
  14.1 2.0 %copy-start.1 = (f32[1280,768]{1,0:T(8,128)}, f32[1280,768]{1,0:T(8,128)S(1)}, u32[]{:S(2)}) copy-start(f32[1280,768]{1,0:T(8,128)S(1)} %get-tuple-element.68.inputs) | copy-start | bytes 11796484
  14.2 3.0 %copy-start.3 = (bf16[1,1280,768]{2,1,0:T(8,128)(2,1)S(1)}, bf16[1,1280,768]{2,1,0:T(8,128)(2,1)}, u32[]{:S(2)}) copy-start(bf16[1,1280,768]{2,1,0:T(8,128)(2,1)} %param.11) | copy-start | bytes 5898244
  16.1 6.1 %copy-start.7 = (bf16[1280,768]{1,0:T(8,128)(2,1)}, bf16[1280,768]{1,0:T(8,128)(2,1)S(1)}, u32[]{:S(2)}) copy-start(bf16[1280,768]{1,0:T(8,128)(2,1)S(1)} %multiply_convert_fusion.refs_6_) | copy-start | bytes 5898244
  16.1 13.6 %copy-start.11 = (bf16[2,3,48,384]{3,2,1,0:T(8,128)(2,1)}, bf16[2,3,48,384]{3,2,1,0:T(8,128)(2,1)S(1)}, u32[]{:S(2)}) copy-start(bf16[2,3,48,384]{3,2,1,0:T(8,128)(2,1)S(1)} %collective-permute-done.1.refs_1_) | copy-start | bytes 663556
  16.1 1.0 copy-start.14
  16.1 6.0 %collective-permute-start.6 = (bf16[1280,768]{1,0:T(8,128)(2,1)S(1)}, bf16[1280,768]{1,0:T(8,128)(2,1)S(1)}, u32[]{:S(2)}, u32[]{:S(2)}) collective-permute-start(bf16[1280,768]{1,0:T(8,128)(2,1)S(1)} %multiply_convert_fusion.refs_6_), channel_id=1, source_target_pairs={{0,16},{16,0},{1,17},{17,1},{2,18},{18,2},{3,19},{19,3},{4,20},{20... | collective-permute-start | bytes 5898248 | tf_op jit(solution)/shard_map/ppermute | solution.py:28
  17.3 4.9 %collective-permute-start.7 = (bf16[1280,384]{1,0:T(8,128)(2,1)S(1)}, bf16[1280,384]{1,0:T(8,128)(2,1)S(1)}, u32[]{:S(2)}, u32[]{:S(2)}) collective-permute-start(bf16[1280,384]{1,0:T(8,128)(2,1)S(1)} %constant_dynamic-slice_fusion.2), channel_id=1, source_target_pairs={{0,16},{16,0},{1,17},{17,1},{2,18},{18,2},{3,19},{19,3},{4,20},{20... | collective-permute-start | bytes 2949128 | tf_op jit(solution)/shard_map/ppermute | solution.py:28
  19.1 18.4 %collective-permute-start.3 = (bf16[2,2,3,48,384]{4,3,2,1,0:T(8,128)(2,1)}, bf16[2,2,3,48,384]{4,3,2,1,0:T(8,128)(2,1)}, u32[]{:S(2)}, u32[]{:S(2)}) collective-permute-start(bf16[2,2,3,48,384]{4,3,2,1,0:T(8,128)(2,1)} %pad_maximum_fusion), channel_id=1, source_target_pairs={{0,64},{64,128},{128,192},{192,0},{1,65},{65,129},{129,193},{193,1... | collective-permute-start | bytes 1327112 | tf_op jit(solution)/shard_map/ppermute | solution.py:24
  19.4 18.1 %collective-permute-start.4 = (bf16[2,2,3,48,384]{4,3,2,1,0:T(8,128)(2,1)}, bf16[2,2,3,48,384]{4,3,2,1,0:T(8,128)(2,1)}, u32[]{:S(2)}, u32[]{:S(2)}) collective-permute-start(bf16[2,2,3,48,384]{4,3,2,1,0:T(8,128)(2,1)} %pad_maximum_fusion), channel_id=1, source_target_pairs={{0,192},{64,0},{128,64},{192,128},{1,193},{65,1},{129,65},{193,129... | collective-permute-start | bytes 1327112 | tf_op jit(solution)/shard_map/ppermute | solution.py:24
  22.2 16.1 %copy-start.10 = (bf16[1280,384]{1,0:T(8,128)(2,1)}, bf16[1280,384]{1,0:T(8,128)(2,1)S(1)}, u32[]{:S(2)}) copy-start(bf16[1280,384]{1,0:T(8,128)(2,1)S(1)} %collective-permute-done.7.refs_11_) | copy-start | bytes 2949124
  22.2 1.3 %copy-start.8 = (bf16[1280,768]{1,0:T(8,128)(2,1)}, bf16[1280,768]{1,0:T(8,128)(2,1)S(1)}, u32[]{:S(2)}) copy-start(bf16[1280,768]{1,0:T(8,128)(2,1)S(1)} %collective-permute-done.6.refs_7_) | copy-start | bytes 5898244
  23.5 13.9 %collective-permute-start.9 = (bf16[160,768]{1,0:T(8,128)(2,1)S(1)}, bf16[160,768]{1,0:T(8,128)(2,1)S(1)}, u32[]{:S(2)}, u32[]{:S(2)}) collective-permute-start(bf16[160,768]{1,0:T(8,128)(2,1)S(1)} %maximum_maximum_fusion.1), channel_id=1, source_target_pairs={{1,0},{2,1},{3,2},{4,3},{5,4},{6,5},{7,6},{8,7},{9,8},{10,9},{11,1... | collective-permute-start | bytes 737288 | tf_op jit(solution)/shard_map/ppermute | solution.py:291
  24.9 13.3 %collective-permute-start.8 = (bf16[160,768]{1,0:T(8,128)(2,1)S(1)}, bf16[160,768]{1,0:T(8,128)(2,1)}, u32[]{:S(2)}, u32[]{:S(2)}) collective-permute-start(bf16[160,768]{1,0:T(8,128)(2,1)S(1)} %maximum_maximum_fusion), channel_id=1, source_target_pairs={{0,1},{1,2},{2,3},{3,4},{4,5},{5,6},{6,7},{7,8},{8,9},{9,10},{10,1... | collective-permute-start | bytes 737288 | tf_op jit(solution)/shard_map/ppermute | solution.py:290
  29.7 7.7 %collective-permute-start.5 = (bf16[2,3,48,384]{3,2,1,0:T(8,128)(2,1)S(1)}, bf16[2,3,48,384]{3,2,1,0:T(8,128)(2,1)S(1)}, u32[]{:S(2)}, u32[]{:S(2)}) collective-permute-start(bf16[2,3,48,384]{3,2,1,0:T(8,128)(2,1)S(1)} %collective-permute-done.1.refs_1_), channel_id=1, source_target_pairs={{0,128},{64,192},{128,0},{192,64},{1,129},{65,193},{129,1},{193,65... | collective-permute-start | bytes 663560 | tf_op jit(solution)/shard_map/ppermute | solution.py:24
  37.5 0.8 copy-start.15
  37.5 0.7 copy-start.13
  38.2 23.7 %copy-start.4 = (bf16[1,1280,768]{2,1,0:T(8,128)(2,1)S(1)}, bf16[1,1280,768]{2,1,0:T(8,128)(2,1)}, u32[]{:S(2)}) copy-start(bf16[1,1280,768]{2,1,0:T(8,128)(2,1)} %param.11) | copy-start | bytes 5898244
  55.1 6.9 %collective-permute-start.11 = (bf16[3,768,384]{2,1,0:T(8,128)(2,1)}, bf16[3,768,384]{2,1,0:T(8,128)(2,1)}, u32[]{:S(2)}, u32[]{:S(2)}) collective-permute-start(bf16[3,768,384]{2,1,0:T(8,128)(2,1)} %get-tuple-element.42.weight_a), channel_id=1, source_target_pairs={{0,16},{16,0},{1,17},{17,1},{2,18},{18,2},{3,19},{19,3},{4,20},{20... | collective-permute-start | bytes 5308424 | tf_op jit(solution)/shard_map/ppermute | solution.py:28
  56.9 5.0 %collective-permute-start.10 = (bf16[1344,384]{1,0:T(8,128)(2,1)}, bf16[1344,384]{1,0:T(8,128)(2,1)S(1)}, u32[]{:S(2)}, u32[]{:S(2)}) collective-permute-start(bf16[1344,384]{1,0:T(8,128)(2,1)} %get-tuple-element.41), channel_id=1, source_target_pairs={{0,16},{16,0},{1,17},{17,1},{2,18},{18,2},{3,19},{19,3},{4,20},{20... | collective-permute-start | bytes 3096584 | tf_op jit(solution)/shard_map/ppermute | solution.py:28
  57.0 18.9 %collective-permute-start.12 = (bf16[3,192,384]{2,1,0:T(8,128)(2,1)}, bf16[3,192,384]{2,1,0:T(8,128)(2,1)}, u32[]{:S(2)}, u32[]{:S(2)}) collective-permute-start(bf16[3,192,384]{2,1,0:T(8,128)(2,1)} %get-tuple-element.44), channel_id=1, source_target_pairs={{0,64},{64,128},{128,192},{192,0},{1,65},{65,129},{129,193},{193,1... | collective-permute-start | bytes 1327112 | tf_op jit(solution)/shard_map/ppermute | solution.py:24
  57.4 18.5 %collective-permute-start.13 = (bf16[3,192,384]{2,1,0:T(8,128)(2,1)}, bf16[3,192,384]{2,1,0:T(8,128)(2,1)}, u32[]{:S(2)}, u32[]{:S(2)}) collective-permute-start(bf16[3,192,384]{2,1,0:T(8,128)(2,1)} %get-tuple-element.45), channel_id=1, source_target_pairs={{0,192},{64,0},{128,64},{192,128},{1,193},{65,1},{129,65},{193,129... | collective-permute-start | bytes 1327112 | tf_op jit(solution)/shard_map/ppermute | solution.py:24
  59.6 19.9 %collective-permute-start.14 = (bf16[3,192,384]{2,1,0:T(8,128)(2,1)}, bf16[3,192,384]{2,1,0:T(8,128)(2,1)}, u32[]{:S(2)}, u32[]{:S(2)}) collective-permute-start(bf16[3,192,384]{2,1,0:T(8,128)(2,1)} %get-tuple-element.46), channel_id=1, source_target_pairs={{0,128},{64,192},{128,0},{192,64},{1,129},{65,193},{129,1},{193,65... | collective-permute-start | bytes 1327112 | tf_op jit(solution)/shard_map/ppermute | solution.py:24
  62.0 2.1 %copy-start.2 = (f32[1280,768]{1,0:T(8,128)S(1)}, f32[1280,768]{1,0:T(8,128)}, u32[]{:S(2)}) copy-start(f32[1280,768]{1,0:T(8,128)} %copy-done.1) | copy-start | bytes 11796484
  64.1 1.5 %copy-start.5 = (bf16[3,768,384]{2,1,0:T(8,128)(2,1)S(1)}, bf16[3,768,384]{2,1,0:T(8,128)(2,1)}, u32[]{:S(2)}) copy-start(bf16[3,768,384]{2,1,0:T(8,128)(2,1)} %get-tuple-element.42.weight_a) | copy-start | bytes 5308420
  65.6 1.2 %copy-start.6 = (bf16[1344,384]{1,0:T(8,128)(2,1)S(1)}, bf16[1344,384]{1,0:T(8,128)(2,1)}, u32[]{:S(2)}) copy-start(bf16[1344,384]{1,0:T(8,128)(2,1)} %get-tuple-element.40.back_a) | copy-start | bytes 3096580
  66.8 12.7 %copy-start.12 = (bf16[3,192,384]{2,1,0:T(8,128)(2,1)S(1)}, bf16[3,192,384]{2,1,0:T(8,128)(2,1)}, u32[]{:S(2)}) copy-start(bf16[3,192,384]{2,1,0:T(8,128)(2,1)} %get-tuple-element.48) | copy-start | bytes 1327108
  81.0 6.8 %collective-permute-start.15 = (bf16[3,48,384]{2,1,0:T(8,128)(2,1)S(1)}, bf16[3,48,384]{2,1,0:T(8,128)(2,1)S(1)}, u32[]{:S(2)}, u32[]{:S(2)}) collective-permute-start(bf16[3,48,384]{2,1,0:T(8,128)(2,1)S(1)} %get-tuple-element.58), channel_id=1, source_target_pairs={{0,8},{8,32},{32,40},{40,0},{1,9},{9,33},{33,41},{41,1},{2,10},{10... | collective-permute-start | bytes 331784 | tf_op jit(solution)/shard_map/ppermute | solution.py:24
  85.9 3.6 %collective-permute-start.16 = (bf16[3,48,384]{2,1,0:T(8,128)(2,1)S(1)}, bf16[3,48,384]{2,1,0:T(8,128)(2,1)S(1)}, u32[]{:S(2)}, u32[]{:S(2)}) collective-permute-start(bf16[3,48,384]{2,1,0:T(8,128)(2,1)S(1)} %get-tuple-element.60), channel_id=1, source_target_pairs={{0,40},{8,0},{32,8},{40,32},{1,41},{9,1},{33,9},{41,33},{2,42},{10... | collective-permute-start | bytes 331784 | tf_op jit(solution)/shard_map/ppermute | solution.py:24
  85.9 5.4 %collective-permute-start.17 = (bf16[3,48,384]{2,1,0:T(8,128)(2,1)S(1)}, bf16[3,48,384]{2,1,0:T(8,128)(2,1)S(1)}, u32[]{:S(2)}, u32[]{:S(2)}) collective-permute-start(bf16[3,48,384]{2,1,0:T(8,128)(2,1)S(1)} %get-tuple-element.59), channel_id=1, source_target_pairs={{0,32},{8,40},{32,0},{40,8},{1,33},{9,41},{33,1},{41,9},{2,34},{10... | collective-permute-start | bytes 331784 | tf_op jit(solution)/shard_map/ppermute | solution.py:24
  92.4 3.7 %collective-permute-start.18 = (bf16[3,48,384]{2,1,0:T(8,128)(2,1)S(1)}, bf16[3,48,384]{2,1,0:T(8,128)(2,1)S(1)}, u32[]{:S(2)}, u32[]{:S(2)}) collective-permute-start(bf16[3,48,384]{2,1,0:T(8,128)(2,1)S(1)} %add_convert_fusion.2), channel_id=1, source_target_pairs={{0,1},{1,0},{2,3},{3,2},{4,5},{5,4},{6,7},{7,6},{8,9},{9,8},{10,11... | collective-permute-start | bytes 331784 | tf_op jit(solution)/shard_map/ppermute | solution.py:28
  92.5 6.4 %collective-permute-start.19 = (bf16[3,48,384]{2,1,0:T(8,128)(2,1)S(1)}, bf16[3,48,384]{2,1,0:T(8,128)(2,1)S(1)}, u32[]{:S(2)}, u32[]{:S(2)}) collective-permute-start(bf16[3,48,384]{2,1,0:T(8,128)(2,1)S(1)} %add_convert_fusion.2), channel_id=1, source_target_pairs={{0,2},{1,3},{2,0},{3,1},{4,6},{5,7},{6,4},{7,5},{8,10},{9,11},{10,... | collective-permute-start | bytes 331784 | tf_op jit(solution)/shard_map/ppermute | solution.py:28
  95.5 6.5 %collective-permute-start.20 = (bf16[3,48,384]{2,1,0:T(8,128)(2,1)S(1)}, bf16[3,48,384]{2,1,0:T(8,128)(2,1)S(1)}, u32[]{:S(2)}, u32[]{:S(2)}) collective-permute-start(bf16[3,48,384]{2,1,0:T(8,128)(2,1)S(1)} %add_convert_fusion.2), channel_id=1, source_target_pairs={{0,3},{1,2},{2,1},{3,0},{4,7},{5,6},{6,5},{7,4},{8,11},{9,10},{10,... | collective-permute-start | bytes 331784 | tf_op jit(solution)/shard_map/ppermute | solution.py:28
  102.0 5.5 %collective-permute-start.21 = (bf16[3,48,384]{2,1,0:T(8,128)(2,1)S(1)}, bf16[3,48,384]{2,1,0:T(8,128)(2,1)S(1)}, u32[]{:S(2)}, u32[]{:S(2)}) collective-permute-start(bf16[3,48,384]{2,1,0:T(8,128)(2,1)S(1)} %add_convert_fusion.1), channel_id=1, source_target_pairs={{0,7},{1,6},{2,5},{3,4},{4,3},{5,2},{6,1},{7,0},{8,15},{9,14},{10,... | collective-permute-start | bytes 331784 | tf_op jit(solution)/shard_map/ppermute | solution.py:28
  107.6 7.2 %collective-permute-start.22 = (bf16[3,48,384]{2,1,0:T(8,128)(2,1)S(1)}, bf16[3,48,384]{2,1,0:T(8,128)(2,1)S(1)}, u32[]{:S(2)}, u32[]{:S(2)}) collective-permute-start(bf16[3,48,384]{2,1,0:T(8,128)(2,1)S(1)} %add_convert_fusion), channel_id=1, source_target_pairs={{16,0},{8,24},{0,8},{24,16},{17,1},{9,25},{1,9},{25,17},{18,2},{10... | collective-permute-start | bytes 331784 | tf_op jit(solution)/shard_map/ppermute | solution.py:242
  112.9 6.1 %collective-permute-start.23 = (bf16[3,48,384]{2,1,0:T(8,128)(2,1)S(1)}, bf16[3,48,384]{2,1,0:T(8,128)(2,1)S(1)}, u32[]{:S(2)}, u32[]{:S(2)}) collective-permute-start(bf16[3,48,384]{2,1,0:T(8,128)(2,1)S(1)} %add_convert_fusion), channel_id=1, source_target_pairs={{16,8},{8,16},{17,9},{9,17},{18,10},{10,18},{19,11},{11,19},{20,12... | collective-permute-start | bytes 331784 | tf_op jit(solution)/shard_map/ppermute | solution.py:243

commit v9 on v8

--- a/solution.py
+++ b/solution.py
@@ -151,16 +151,18 @@
             preferred_element_type=F32,
         )
         total = part if total is None else total + part
+    quarter = channels // 4
     for tap in range(FILTER_TAPS):
         grad[tap] = total[:, tap * half : (tap + 1) * half].astype(BF16)
-    quarter = channels // 4
-    for step in range(4):
-        place = pl.multiple_of(((x + step) % 4) * quarter, 16)
-        grad_save = pltpu.make_async_copy(
-            grad.at[:, pl.ds(place, quarter), :], grad_out[step], grad_sem.at[step]
-        )
-        grad_save.start()
-        saves.append(grad_save)
+        for step in range(4):
+            place = pl.multiple_of(((x + step) % 4) * quarter, 16)
+            grad_save = pltpu.make_async_copy(
+                grad.at[tap, pl.ds(place, quarter), :],
+                grad_out[step].at[tap],
+                grad_sem.at[tap, step],
+            )
+            grad_save.start()
+            saves.append(grad_save)
     for copy in saves:
         copy.wait()
 
@@ -188,7 +190,7 @@
             dma((2, 6)),
             dma((2,)),
             dma,
-            dma((4,)),
+            dma((FILTER_TAPS, 4)),
         ],
         compiler_params=pltpu.CompilerParams(vmem_limit_bytes=56 * 1024 * 1024),
         name="forward",
@@ -218,7 +220,7 @@
 
 def backward(back, weight, inputs, scale, gain, incoming):
     count, channels = inputs.shape
-    block = 256
+    block = 320
     whole = lambda array: pl.BlockSpec(array.shape, lambda i: (0,) * array.ndim)
     part = pl.BlockSpec((block, channels), lambda i: (i, 0))
     return pl.pallas_call(

time: 120 us -> 120 us (level)
  transfers between devices with their start and end apart: 24 -> 24, of which waited for: 13 -> 13; matrix products, arithmetic and copies ran while one was open for 5% -> 5% of each run, Pallas kernels for 8% -> 7%
where the time goes in v9:
time: 120 us
  starting transfers between devices  46.2 us (38%)
  waiting for transfers between devices  27.5 us (23%)
  Pallas kernels  25.4 us (21%)
  local copies, waits for them, and re-layouts  9.78 us (8%)
  other arithmetic  6.09 us (5%)
  matrix products  3.59 us (3%)
    ppermute x10, starting transfers between devices, shift(): return lax.ppermute(value, axis, pairs)  17.7 us
    pallas_call x1, Pallas kernels, forward(): pl.pallas_call(forward_kernel, out_shape=[jax.ShapeDtypeStruct((FILTER_TA...  16.6 us
    ppermute x10, starting transfers between devices, swap(): return lax.ppermute(value, axis, [(i, i ^ mask) for i in range(count)])  15.2 us
    ppermute x10, waiting for transfers between devices, shift(): return lax.ppermute(value, axis, pairs)  12.6 us
    ppermute x10, waiting for transfers between devices, swap(): return lax.ppermute(value, axis, [(i, i ^ mask) for i in range(count)])  10.8 us
    pallas_call x1, Pallas kernels, backward(): pl.pallas_call(backward_kernel, grid=(count // block,), out_shape=jax.Sha...  8.78 us
    unnamed x34, local copies, waits for them, and re-layouts  8.41 us
    ppermute x1, starting transfers between devices, share_weight_grad(): first = lax.ppermute(mine, pair, [(2, 0), (1, 3), (0, 1), (3, 2)])  5.3 us
  transfers between devices with their start and end apart: 24, of which 13 were waited for; matrix products, arithmetic and copies ran while one was open for 5% of the time, Pallas kernels for 7%

profile of v9, /device:TPU:1, one launch (start us, length us, event | category | flops | bytes accessed | tf_op | source)
XLA Modules:
  0.0 119.5 jit_solution(4675608775017200135)
XLA Ops:
  0.6 0.0 copy-start
  0.7 1.0 dynamic-slice_bitcast_fusion
  1.6 3.3 %collective-permute-start = (bf16[3,48,384]{2,1,0:T(8,128)(2,1)S(1)}, bf16[3,48,384]{2,1,0:T(8,128)(2,1)S(1)}, u32[]{:S(2)}, u32[]{:S(2)}) collective-permute-start(bf16[3,48,384]{2,1,0:T(8,128)(2,1)S(1)} %get-tuple-element.66), channel_id=1, source_target_pairs={{0,16},{16,0},{1,17},{17,1},{2,18},{18,2},{3,19},{19,3},{4,20},{20... | collective-permute-start | bytes 331784 | tf_op jit(solution)/shard_map/ppermute | solution.py:28
  5.0 1.0 collective-permute-done
  6.0 1.1 collective-permute-start.1
  7.1 2.7 %collective-permute-start.2 = (bf16[2,3,48,384]{3,2,1,0:T(8,128)(2,1)S(1)}, bf16[2,3,48,384]{3,2,1,0:T(8,128)(2,1)S(1)}, u32[]{:S(2)}, u32[]{:S(2)}) collective-permute-start(bf16[2,3,48,384]{3,2,1,0:T(8,128)(2,1)S(1)} %pad_maximum_fusion.1.refs_0_), channel_id=1, source_target_pairs={{0,128},{64,192},{128,0},{192,64},{1,129},{65,193},{129,1},{193,65... | collective-permute-start | bytes 663560 | tf_op jit(solution)/shard_map/ppermute | solution.py:24
  9.8 0.7 reduce
  10.5 0.0 copy-start.16
  10.5 3.6 %multiply_reduce_fusion = (f32[1280]{0:T(1024)S(1)}, f32[1280,768]{1,0:T(8,128)S(1)}) fusion(f32[4,768]{1,0:T(4,128)S(1)} %copy-done, s32[1280]{0:T(1024)S(1)} %reduce, bf16[1280,768]{1,0:T(8,128)(2,1)} %bitcast.18), kind=kOutput, calls=%fused_computation.2 | convolution fusion | flops 51121920 | bytes 5920768 | tf_op jit(solution)/shard_map/dot_general | solution.py:269
  14.2 0.0 copy-start.3
  14.2 0.4 multiply_convert_fusion.refs_6_
  14.6 1.6 %copy-done.1 = f32[1280,768]{1,0:T(8,128)} copy-done((f32[1280,768]{1,0:T(8,128)}, f32[1280,768]{1,0:T(8,128)S(1)}, u32[]{:S(2)}) %copy-start.1) | copy-done | bytes 3932184
  16.1 0.0 collective-permute-done.1.refs_1_
  16.1 0.0 collective-permute-done.2.refs_4_
  16.1 1.0 collective-permute-start.6
  17.2 0.1 constant_dynamic-slice_fusion.2
  17.3 1.0 collective-permute-start.7
  18.2 0.8 pad_maximum_fusion
  19.1 0.3 collective-permute-start.3
  19.4 2.4 %collective-permute-start.4 = (bf16[2,2,3,48,384]{4,3,2,1,0:T(8,128)(2,1)}, bf16[2,2,3,48,384]{4,3,2,1,0:T(8,128)(2,1)}, u32[]{:S(2)}, u32[]{:S(2)}) collective-permute-start(bf16[2,2,3,48,384]{4,3,2,1,0:T(8,128)(2,1)} %pad_maximum_fusion), channel_id=1, source_target_pairs={{0,192},{64,0},{128,64},{192,128},{1,193},{65,1},{129,65},{193,129... | collective-permute-start | bytes 1327112 | tf_op jit(solution)/shard_map/ppermute | solution.py:24
  21.7 0.4 collective-permute-done.7.refs_11_
  22.2 0.0 collective-permute-done.6.refs_7_
  22.3 1.2 %copy-done.8 = bf16[1280,768]{1,0:T(8,128)(2,1)} copy-done((bf16[1280,768]{1,0:T(8,128)(2,1)}, bf16[1280,768]{1,0:T(8,128)(2,1)S(1)}, u32[]{:S(2)}) %copy-start.8) | copy-done | bytes 1966104
  23.5 1.3 %collective-permute-start.9 = (bf16[160,768]{1,0:T(8,128)(2,1)S(1)}, bf16[160,768]{1,0:T(8,128)(2,1)S(1)}, u32[]{:S(2)}, u32[]{:S(2)}) collective-permute-start(bf16[160,768]{1,0:T(8,128)(2,1)S(1)} %maximum_maximum_fusion.1), channel_id=1, source_target_pairs={{1,0},{2,1},{3,2},{4,3},{5,4},{6,5},{7,6},{8,7},{9,8},{10,9},{11,1... | collective-permute-start | bytes 737288 | tf_op jit(solution)/shard_map/ppermute | solution.py:293
  24.9 4.9 %collective-permute-start.8 = (bf16[160,768]{1,0:T(8,128)(2,1)S(1)}, bf16[160,768]{1,0:T(8,128)(2,1)}, u32[]{:S(2)}, u32[]{:S(2)}) collective-permute-start(bf16[160,768]{1,0:T(8,128)(2,1)S(1)} %maximum_maximum_fusion), channel_id=1, source_target_pairs={{0,1},{1,2},{2,3},{3,4},{4,5},{5,6},{6,7},{7,8},{8,9},{9,10},{10,1... | collective-permute-start | bytes 737288 | tf_op jit(solution)/shard_map/ppermute | solution.py:292
  29.7 2.0 %collective-permute-start.5 = (bf16[2,3,48,384]{3,2,1,0:T(8,128)(2,1)S(1)}, bf16[2,3,48,384]{3,2,1,0:T(8,128)(2,1)S(1)}, u32[]{:S(2)}, u32[]{:S(2)}) collective-permute-start(bf16[2,3,48,384]{3,2,1,0:T(8,128)(2,1)S(1)} %collective-permute-done.1.refs_1_), channel_id=1, source_target_pairs={{0,128},{64,192},{128,0},{192,64},{1,129},{65,193},{129,1},{193,65... | collective-permute-start | bytes 663560 | tf_op jit(solution)/shard_map/ppermute | solution.py:24
  31.7 0.6 pad_add_fusion.position
  32.3 5.1 %collective-permute-done.5.refs_5_ = bf16[2,3,48,384]{3,2,1,0:T(8,128)(2,1)S(1)} collective-permute-done((bf16[2,3,48,384]{3,2,1,0:T(8,128)(2,1)S(1)}, bf16[2,3,48,384]{3,2,1,0:T(8,128)(2,1)S(1)}, u32[]{:S(2)}, u32[]{:S(2)}) %collective-permute-start.5) | collective-permute-done | bytes 221216 | tf_op jit(solution)/shard_map/ppermute | solution.py:24
  37.5 0.0 collective-permute-done.3.refs_2_
  37.5 0.7 copy-done.13
  38.2 0.0 copy-done.15
  38.2 16.6 %forward.1 = (bf16[3,768,384]{2,1,0:T(8,128)(2,1)}, bf16[1344,384]{1,0:T(8,128)(2,1)}, bf16[1344,384]{1,0:T(8,128)(2,1)}, bf16[3,192,384]{2,1,0:T(8,128)(2,1)}, ...) custom-call(s32[4]{0:T(128)} %pad_add_fusion.position, ...), custom_call_target="tpu_custom_call" | custom-call | tf_op jit(solution)/shard_map/forward/pallas_call | solution.py:176
  54.9 1.7 %collective-permute-start.11 = (bf16[3,768,384]{2,1,0:T(8,128)(2,1)}, bf16[3,768,384]{2,1,0:T(8,128)(2,1)}, u32[]{:S(2)}, u32[]{:S(2)}) collective-permute-start(bf16[3,768,384]{2,1,0:T(8,128)(2,1)} %get-tuple-element.42.weight_a), channel_id=1, source_target_pairs={{0,16},{16,0},{1,17},{17,1},{2,18},{18,2},{3,19},{19,3},{4,20},{20... | collective-permute-start | bytes 5308424 | tf_op jit(solution)/shard_map/ppermute | solution.py:28
  56.6 0.1 collective-permute-start.10
  56.7 0.5 collective-permute-start.12
  57.2 2.2 %collective-permute-start.13 = (bf16[3,192,384]{2,1,0:T(8,128)(2,1)}, bf16[3,192,384]{2,1,0:T(8,128)(2,1)}, u32[]{:S(2)}, u32[]{:S(2)}) collective-permute-start(bf16[3,192,384]{2,1,0:T(8,128)(2,1)} %get-tuple-element.45), channel_id=1, source_target_pairs={{0,192},{64,0},{128,64},{192,128},{1,193},{65,1},{129,65},{193,129... | collective-permute-start | bytes 1327112 | tf_op jit(solution)/shard_map/ppermute | solution.py:24
  59.4 0.8 collective-permute-start.14
  60.2 0.2 rsqrt.7.scale
  60.4 1.2 collective-permute-done.10.back_b
  61.6 0.2 collective-permute-done.11.weight_b
  61.7 2.1 %copy-done.2 = f32[1280,768]{1,0:T(8,128)S(1)} copy-done((f32[1280,768]{1,0:T(8,128)S(1)}, f32[1280,768]{1,0:T(8,128)}, u32[]{:S(2)}) %copy-start.2) | copy-done | bytes 3932184
  63.8 1.5 %copy-done.5 = bf16[3,768,384]{2,1,0:T(8,128)(2,1)S(1)} copy-done((bf16[3,768,384]{2,1,0:T(8,128)(2,1)S(1)}, bf16[3,768,384]{2,1,0:T(8,128)(2,1)}, u32[]{:S(2)}) %copy-start.5) | copy-done | bytes 1769496
  65.3 1.2 %copy-done.6 = bf16[1344,384]{1,0:T(8,128)(2,1)S(1)} copy-done((bf16[1344,384]{1,0:T(8,128)(2,1)S(1)}, bf16[1344,384]{1,0:T(8,128)(2,1)}, u32[]{:S(2)}) %copy-start.6) | copy-done | bytes 1032216
  66.5 8.8 %backward.1 = bf16[1280,768]{1,0:T(8,128)(2,1)} custom-call(bf16[1344,384]{1,0:T(8,128)(2,1)S(1)} %copy-done.6, bf16[1344,384]{1,0:T(8,128)(2,1)S(1)} %collective-permute-done.10.back_b, bf16[3,768,384]{2,1,0:T(8,128)(2,1)S(1)} %copy-done.5, bf16[3,768,384]{2,1,0:T(8,128)(2,1)} %collective-permute-done.11.weight_b, f32[1280,768]{1,0:T(8,128)S(1)} %copy-done.2, ...), custom_call_target="tpu_custom_call" | custom-call | tf_op jit(solution)/shard_map/backward/pallas_call | solution.py:226
  75.3 3.9 %collective-permute-done.14 = bf16[3,192,384]{2,1,0:T(8,128)(2,1)} collective-permute-done((bf16[3,192,384]{2,1,0:T(8,128)(2,1)}, bf16[3,192,384]{2,1,0:T(8,128)(2,1)}, u32[]{:S(2)}, u32[]{:S(2)}) %collective-permute-start.14) | collective-permute-done | bytes 442400 | tf_op jit(solution)/shard_map/ppermute | solution.py:24
  79.3 1.5 %add_convert_fusion.5 = (bf16[3,48,384]{2,1,0:T(8,128)(2,1)S(1)}, bf16[3,48,384]{2,1,0:T(8,128)(2,1)S(1)}, bf16[3,48,384]{2,1,0:T(8,128)(2,1)S(1)}) fusion(bf16[3,192,384]{2,1,0:T(8,128)(2,1)} %collective-permute-done.14, s32[]{:T(128)S(6)} %select_n.81, bf16[3,192,384]{2,1,0:T(8,128)(2,1)} %collective-permute-done.13, ...), kind=kLoop, calls=%fused_computation.15 | loop fusion | flops 1327104 | bytes 1658892 | tf_op jit(solution)/shard_map/convert_element_type | solution.py:319
  80.7 4.9 %collective-permute-start.15 = (bf16[3,48,384]{2,1,0:T(8,128)(2,1)S(1)}, bf16[3,48,384]{2,1,0:T(8,128)(2,1)S(1)}, u32[]{:S(2)}, u32[]{:S(2)}) collective-permute-start(bf16[3,48,384]{2,1,0:T(8,128)(2,1)S(1)} %get-tuple-element.58), channel_id=1, source_target_pairs={{0,8},{8,32},{32,40},{40,0},{1,9},{9,33},{33,41},{41,1},{2,10},{10... | collective-permute-start | bytes 331784 | tf_op jit(solution)/shard_map/ppermute | solution.py:24
  85.7 1.9 %collective-permute-start.17 = (bf16[3,48,384]{2,1,0:T(8,128)(2,1)S(1)}, bf16[3,48,384]{2,1,0:T(8,128)(2,1)S(1)}, u32[]{:S(2)}, u32[]{:S(2)}) collective-permute-start(bf16[3,48,384]{2,1,0:T(8,128)(2,1)S(1)} %get-tuple-element.59), channel_id=1, source_target_pairs={{0,32},{8,40},{32,0},{40,8},{1,33},{9,41},{33,1},{41,9},{2,34},{10... | collective-permute-start | bytes 331784 | tf_op jit(solution)/shard_map/ppermute | solution.py:24
  87.5 1.7 %collective-permute-done.16 = bf16[3,48,384]{2,1,0:T(8,128)(2,1)S(1)} collective-permute-done((bf16[3,48,384]{2,1,0:T(8,128)(2,1)S(1)}, bf16[3,48,384]{2,1,0:T(8,128)(2,1)S(1)}, u32[]{:S(2)}, u32[]{:S(2)}) %collective-permute-start.16) | collective-permute-done | bytes 110624 | tf_op jit(solution)/shard_map/ppermute | solution.py:24
  89.3 1.8 %collective-permute-done.17 = bf16[3,48,384]{2,1,0:T(8,128)(2,1)S(1)} collective-permute-done((bf16[3,48,384]{2,1,0:T(8,128)(2,1)S(1)}, bf16[3,48,384]{2,1,0:T(8,128)(2,1)S(1)}, u32[]{:S(2)}, u32[]{:S(2)}) %collective-permute-start.17) | collective-permute-done | bytes 110624 | tf_op jit(solution)/shard_map/ppermute | solution.py:24
  91.0 1.1 add_convert_fusion.2
  92.1 0.1 collective-permute-start.18
  92.2 3.0 %collective-permute-start.19 = (bf16[3,48,384]{2,1,0:T(8,128)(2,1)S(1)}, bf16[3,48,384]{2,1,0:T(8,128)(2,1)S(1)}, u32[]{:S(2)}, u32[]{:S(2)}) collective-permute-start(bf16[3,48,384]{2,1,0:T(8,128)(2,1)S(1)} %add_convert_fusion.2), channel_id=1, source_target_pairs={{0,2},{1,3},{2,0},{3,1},{4,6},{5,7},{6,4},{7,5},{8,10},{9,11},{10,... | collective-permute-start | bytes 331784 | tf_op jit(solution)/shard_map/ppermute | solution.py:28
  95.2 0.6 collective-permute-start.20
  95.8 0.1 collective-permute-done.18
  95.8 2.8 %collective-permute-done.19 = bf16[3,48,384]{2,1,0:T(8,128)(2,1)S(1)} collective-permute-done((bf16[3,48,384]{2,1,0:T(8,128)(2,1)S(1)}, bf16[3,48,384]{2,1,0:T(8,128)(2,1)S(1)}, u32[]{:S(2)}, u32[]{:S(2)}) %collective-permute-start.19) | collective-permute-done | bytes 110624 | tf_op jit(solution)/shard_map/ppermute | solution.py:28
  98.6 3.1 %collective-permute-done.20 = bf16[3,48,384]{2,1,0:T(8,128)(2,1)S(1)} collective-permute-done((bf16[3,48,384]{2,1,0:T(8,128)(2,1)S(1)}, bf16[3,48,384]{2,1,0:T(8,128)(2,1)S(1)}, u32[]{:S(2)}, u32[]{:S(2)}) %collective-permute-start.20) | collective-permute-done | bytes 110624 | tf_op jit(solution)/shard_map/ppermute | solution.py:28
  101.7 0.1 add_convert_fusion.1
  101.8 3.4 %collective-permute-start.21 = (bf16[3,48,384]{2,1,0:T(8,128)(2,1)S(1)}, bf16[3,48,384]{2,1,0:T(8,128)(2,1)S(1)}, u32[]{:S(2)}, u32[]{:S(2)}) collective-permute-start(bf16[3,48,384]{2,1,0:T(8,128)(2,1)S(1)} %add_convert_fusion.1), channel_id=1, source_target_pairs={{0,7},{1,6},{2,5},{3,4},{4,3},{5,2},{6,1},{7,0},{8,15},{9,14},{10,... | collective-permute-start | bytes 331784 | tf_op jit(solution)/shard_map/ppermute | solution.py:28
  105.1 2.1 %collective-permute-done.21 = bf16[3,48,384]{2,1,0:T(8,128)(2,1)S(1)} collective-permute-done((bf16[3,48,384]{2,1,0:T(8,128)(2,1)S(1)}, bf16[3,48,384]{2,1,0:T(8,128)(2,1)S(1)}, u32[]{:S(2)}, u32[]{:S(2)}) %collective-permute-start.21) | collective-permute-done | bytes 110624 | tf_op jit(solution)/shard_map/ppermute | solution.py:28
  107.3 5.3 %collective-permute-start.22 = (bf16[3,48,384]{2,1,0:T(8,128)(2,1)S(1)}, bf16[3,48,384]{2,1,0:T(8,128)(2,1)S(1)}, u32[]{:S(2)}, u32[]{:S(2)}) collective-permute-start(bf16[3,48,384]{2,1,0:T(8,128)(2,1)S(1)} %add_convert_fusion), channel_id=1, source_target_pairs={{16,0},{8,24},{0,8},{24,16},{17,1},{9,25},{1,9},{25,17},{18,2},{10... | collective-permute-start | bytes 331784 | tf_op jit(solution)/shard_map/ppermute | solution.py:244
  112.6 1.9 %collective-permute-start.23 = (bf16[3,48,384]{2,1,0:T(8,128)(2,1)S(1)}, bf16[3,48,384]{2,1,0:T(8,128)(2,1)S(1)}, u32[]{:S(2)}, u32[]{:S(2)}) collective-permute-start(bf16[3,48,384]{2,1,0:T(8,128)(2,1)S(1)} %add_convert_fusion), channel_id=1, source_target_pairs={{16,8},{8,16},{17,9},{9,17},{18,10},{10,18},{19,11},{11,19},{20,12... | collective-permute-start | bytes 331784 | tf_op jit(solution)/shard_map/ppermute | solution.py:245
  114.5 4.1 %collective-permute-done.23 = bf16[3,48,384]{2,1,0:T(8,128)(2,1)S(1)} collective-permute-done((bf16[3,48,384]{2,1,0:T(8,128)(2,1)S(1)}, bf16[3,48,384]{2,1,0:T(8,128)(2,1)S(1)}, u32[]{:S(2)}, u32[]{:S(2)}) %collective-permute-start.23) | collective-permute-done | bytes 110624 | tf_op jit(solution)/shard_map/ppermute | solution.py:245
  118.7 0.8 convert_multiply_fusion
  (44 shorter events, 0.3 us)
Async XLA Ops:
  0.6 9.9 %copy-start = (f32[4,768]{1,0:T(4,128)S(1)}, f32[4,768]{1,0:T(4,128)}, u32[]{:S(2)}) copy-start(f32[4,768]{1,0:T(4,128)} %param.8) | copy-start | bytes 36868
  1.6 4.3 %collective-permute-start = (bf16[3,48,384]{2,1,0:T(8,128)(2,1)S(1)}, bf16[3,48,384]{2,1,0:T(8,128)(2,1)S(1)}, u32[]{:S(2)}, u32[]{:S(2)}) collective-permute-start(bf16[3,48,384]{2,1,0:T(8,128)(2,1)S(1)} %get-tuple-element.66), channel_id=1, source_target_pairs={{0,16},{16,0},{1,17},{17,1},{2,18},{18,2},{3,19},{19,3},{4,20},{20... | collective-permute-start | bytes 331784 | tf_op jit(solution)/shard_map/ppermute | solution.py:28
  6.0 12.3 %copy-start.9 = (bf16[2,3,48,384]{3,2,1,0:T(8,128)(2,1)}, bf16[2,3,48,384]{3,2,1,0:T(8,128)(2,1)S(1)}, u32[]{:S(2)}) copy-start(bf16[2,3,48,384]{3,2,1,0:T(8,128)(2,1)S(1)} %pad_maximum_fusion.1.refs_0_) | copy-start | bytes 663556
  6.0 10.2 %collective-permute-start.1 = (bf16[2,3,48,384]{3,2,1,0:T(8,128)(2,1)S(1)}, bf16[2,3,48,384]{3,2,1,0:T(8,128)(2,1)S(1)}, u32[]{:S(2)}, u32[]{:S(2)}) collective-permute-start(bf16[2,3,48,384]{3,2,1,0:T(8,128)(2,1)S(1)} %pad_maximum_fusion.1.refs_0_), channel_id=1, source_target_pairs={{0,40},{8,32},{32,8},{40,0},{1,41},{9,33},{33,9},{41,1},{2,42},{10... | collective-permute-start | bytes 663560 | tf_op jit(solution)/shard_map/ppermute | solution.py:28
  7.1 9.1 %collective-permute-start.2 = (bf16[2,3,48,384]{3,2,1,0:T(8,128)(2,1)S(1)}, bf16[2,3,48,384]{3,2,1,0:T(8,128)(2,1)S(1)}, u32[]{:S(2)}, u32[]{:S(2)}) collective-permute-start(bf16[2,3,48,384]{3,2,1,0:T(8,128)(2,1)S(1)} %pad_maximum_fusion.1.refs_0_), channel_id=1, source_target_pairs={{0,128},{64,192},{128,0},{192,64},{1,129},{65,193},{129,1},{193,65... | collective-permute-start | bytes 663560 | tf_op jit(solution)/shard_map/ppermute | solution.py:24
  10.5 3.6 %copy-start.16 = (f32[768]{0:T(1024)S(1)}, f32[768]{0:T(1024)}, u32[]{:S(2)}) copy-start(f32[768]{0:T(1024)} %param.9) | copy-start | bytes 9220
  14.1 2.0 %copy-start.1 = (f32[1280,768]{1,0:T(8,128)}, f32[1280,768]{1,0:T(8,128)S(1)}, u32[]{:S(2)}) copy-start(f32[1280,768]{1,0:T(8,128)S(1)} %get-tuple-element.68.inputs) | copy-start | bytes 11796484
  14.2 3.0 %copy-start.3 = (bf16[1,1280,768]{2,1,0:T(8,128)(2,1)S(1)}, bf16[1,1280,768]{2,1,0:T(8,128)(2,1)}, u32[]{:S(2)}) copy-start(bf16[1,1280,768]{2,1,0:T(8,128)(2,1)} %param.11) | copy-start | bytes 5898244
  16.1 6.1 %copy-start.7 = (bf16[1280,768]{1,0:T(8,128)(2,1)}, bf16[1280,768]{1,0:T(8,128)(2,1)S(1)}, u32[]{:S(2)}) copy-start(bf16[1280,768]{1,0:T(8,128)(2,1)S(1)} %multiply_convert_fusion.refs_6_) | copy-start | bytes 5898244
  16.1 13.6 %copy-start.11 = (bf16[2,3,48,384]{3,2,1,0:T(8,128)(2,1)}, bf16[2,3,48,384]{3,2,1,0:T(8,128)(2,1)S(1)}, u32[]{:S(2)}) copy-start(bf16[2,3,48,384]{3,2,1,0:T(8,128)(2,1)S(1)} %collective-permute-done.1.refs_1_) | copy-start | bytes 663556
  16.1 1.0 copy-start.14
  16.1 6.0 %collective-permute-start.6 = (bf16[1280,768]{1,0:T(8,128)(2,1)S(1)}, bf16[1280,768]{1,0:T(8,128)(2,1)S(1)}, u32[]{:S(2)}, u32[]{:S(2)}) collective-permute-start(bf16[1280,768]{1,0:T(8,128)(2,1)S(1)} %multiply_convert_fusion.refs_6_), channel_id=1, source_target_pairs={{0,16},{16,0},{1,17},{17,1},{2,18},{18,2},{3,19},{19,3},{4,20},{20... | collective-permute-start | bytes 5898248 | tf_op jit(solution)/shard_map/ppermute | solution.py:28
  17.3 4.9 %collective-permute-start.7 = (bf16[1280,384]{1,0:T(8,128)(2,1)S(1)}, bf16[1280,384]{1,0:T(8,128)(2,1)S(1)}, u32[]{:S(2)}, u32[]{:S(2)}) collective-permute-start(bf16[1280,384]{1,0:T(8,128)(2,1)S(1)} %constant_dynamic-slice_fusion.2), channel_id=1, source_target_pairs={{0,16},{16,0},{1,17},{17,1},{2,18},{18,2},{3,19},{19,3},{4,20},{20... | collective-permute-start | bytes 2949128 | tf_op jit(solution)/shard_map/ppermute | solution.py:28
  19.1 18.4 %collective-permute-start.3 = (bf16[2,2,3,48,384]{4,3,2,1,0:T(8,128)(2,1)}, bf16[2,2,3,48,384]{4,3,2,1,0:T(8,128)(2,1)}, u32[]{:S(2)}, u32[]{:S(2)}) collective-permute-start(bf16[2,2,3,48,384]{4,3,2,1,0:T(8,128)(2,1)} %pad_maximum_fusion), channel_id=1, source_target_pairs={{0,64},{64,128},{128,192},{192,0},{1,65},{65,129},{129,193},{193,1... | collective-permute-start | bytes 1327112 | tf_op jit(solution)/shard_map/ppermute | solution.py:24
  19.4 18.1 %collective-permute-start.4 = (bf16[2,2,3,48,384]{4,3,2,1,0:T(8,128)(2,1)}, bf16[2,2,3,48,384]{4,3,2,1,0:T(8,128)(2,1)}, u32[]{:S(2)}, u32[]{:S(2)}) collective-permute-start(bf16[2,2,3,48,384]{4,3,2,1,0:T(8,128)(2,1)} %pad_maximum_fusion), channel_id=1, source_target_pairs={{0,192},{64,0},{128,64},{192,128},{1,193},{65,1},{129,65},{193,129... | collective-permute-start | bytes 1327112 | tf_op jit(solution)/shard_map/ppermute | solution.py:24
  22.2 16.1 %copy-start.10 = (bf16[1280,384]{1,0:T(8,128)(2,1)}, bf16[1280,384]{1,0:T(8,128)(2,1)S(1)}, u32[]{:S(2)}) copy-start(bf16[1280,384]{1,0:T(8,128)(2,1)S(1)} %collective-permute-done.7.refs_11_) | copy-start | bytes 2949124
  22.2 1.3 %copy-start.8 = (bf16[1280,768]{1,0:T(8,128)(2,1)}, bf16[1280,768]{1,0:T(8,128)(2,1)S(1)}, u32[]{:S(2)}) copy-start(bf16[1280,768]{1,0:T(8,128)(2,1)S(1)} %collective-permute-done.6.refs_7_) | copy-start | bytes 5898244
  23.5 13.9 %collective-permute-start.9 = (bf16[160,768]{1,0:T(8,128)(2,1)S(1)}, bf16[160,768]{1,0:T(8,128)(2,1)S(1)}, u32[]{:S(2)}, u32[]{:S(2)}) collective-permute-start(bf16[160,768]{1,0:T(8,128)(2,1)S(1)} %maximum_maximum_fusion.1), channel_id=1, source_target_pairs={{1,0},{2,1},{3,2},{4,3},{5,4},{6,5},{7,6},{8,7},{9,8},{10,9},{11,1... | collective-permute-start | bytes 737288 | tf_op jit(solution)/shard_map/ppermute | solution.py:293
  24.9 13.3 %collective-permute-start.8 = (bf16[160,768]{1,0:T(8,128)(2,1)S(1)}, bf16[160,768]{1,0:T(8,128)(2,1)}, u32[]{:S(2)}, u32[]{:S(2)}) collective-permute-start(bf16[160,768]{1,0:T(8,128)(2,1)S(1)} %maximum_maximum_fusion), channel_id=1, source_target_pairs={{0,1},{1,2},{2,3},{3,4},{4,5},{5,6},{6,7},{7,8},{8,9},{9,10},{10,1... | collective-permute-start | bytes 737288 | tf_op jit(solution)/shard_map/ppermute | solution.py:292
  29.7 7.7 %collective-permute-start.5 = (bf16[2,3,48,384]{3,2,1,0:T(8,128)(2,1)S(1)}, bf16[2,3,48,384]{3,2,1,0:T(8,128)(2,1)S(1)}, u32[]{:S(2)}, u32[]{:S(2)}) collective-permute-start(bf16[2,3,48,384]{3,2,1,0:T(8,128)(2,1)S(1)} %collective-permute-done.1.refs_1_), channel_id=1, source_target_pairs={{0,128},{64,192},{128,0},{192,64},{1,129},{65,193},{129,1},{193,65... | collective-permute-start | bytes 663560 | tf_op jit(solution)/shard_map/ppermute | solution.py:24
  37.5 0.8 copy-start.15
  37.5 0.7 copy-start.13
  38.2 23.5 %copy-start.4 = (bf16[1,1280,768]{2,1,0:T(8,128)(2,1)S(1)}, bf16[1,1280,768]{2,1,0:T(8,128)(2,1)}, u32[]{:S(2)}) copy-start(bf16[1,1280,768]{2,1,0:T(8,128)(2,1)} %param.11) | copy-start | bytes 5898244
  54.9 6.9 %collective-permute-start.11 = (bf16[3,768,384]{2,1,0:T(8,128)(2,1)}, bf16[3,768,384]{2,1,0:T(8,128)(2,1)}, u32[]{:S(2)}, u32[]{:S(2)}) collective-permute-start(bf16[3,768,384]{2,1,0:T(8,128)(2,1)} %get-tuple-element.42.weight_a), channel_id=1, source_target_pairs={{0,16},{16,0},{1,17},{17,1},{2,18},{18,2},{3,19},{19,3},{4,20},{20... | collective-permute-start | bytes 5308424 | tf_op jit(solution)/shard_map/ppermute | solution.py:28
  56.6 5.0 %collective-permute-start.10 = (bf16[1344,384]{1,0:T(8,128)(2,1)}, bf16[1344,384]{1,0:T(8,128)(2,1)S(1)}, u32[]{:S(2)}, u32[]{:S(2)}) collective-permute-start(bf16[1344,384]{1,0:T(8,128)(2,1)} %get-tuple-element.41), channel_id=1, source_target_pairs={{0,16},{16,0},{1,17},{17,1},{2,18},{18,2},{3,19},{19,3},{4,20},{20... | collective-permute-start | bytes 3096584 | tf_op jit(solution)/shard_map/ppermute | solution.py:28
  56.7 18.6 %collective-permute-start.12 = (bf16[3,192,384]{2,1,0:T(8,128)(2,1)}, bf16[3,192,384]{2,1,0:T(8,128)(2,1)}, u32[]{:S(2)}, u32[]{:S(2)}) collective-permute-start(bf16[3,192,384]{2,1,0:T(8,128)(2,1)} %get-tuple-element.44), channel_id=1, source_target_pairs={{0,64},{64,128},{128,192},{192,0},{1,65},{65,129},{129,193},{193,1... | collective-permute-start | bytes 1327112 | tf_op jit(solution)/shard_map/ppermute | solution.py:24
  57.2 18.2 %collective-permute-start.13 = (bf16[3,192,384]{2,1,0:T(8,128)(2,1)}, bf16[3,192,384]{2,1,0:T(8,128)(2,1)}, u32[]{:S(2)}, u32[]{:S(2)}) collective-permute-start(bf16[3,192,384]{2,1,0:T(8,128)(2,1)} %get-tuple-element.45), channel_id=1, source_target_pairs={{0,192},{64,0},{128,64},{192,128},{1,193},{65,1},{129,65},{193,129... | collective-permute-start | bytes 1327112 | tf_op jit(solution)/shard_map/ppermute | solution.py:24
  59.4 19.9 %collective-permute-start.14 = (bf16[3,192,384]{2,1,0:T(8,128)(2,1)}, bf16[3,192,384]{2,1,0:T(8,128)(2,1)}, u32[]{:S(2)}, u32[]{:S(2)}) collective-permute-start(bf16[3,192,384]{2,1,0:T(8,128)(2,1)} %get-tuple-element.46), channel_id=1, source_target_pairs={{0,128},{64,192},{128,0},{192,64},{1,129},{65,193},{129,1},{193,65... | collective-permute-start | bytes 1327112 | tf_op jit(solution)/shard_map/ppermute | solution.py:24
  61.7 2.1 %copy-start.2 = (f32[1280,768]{1,0:T(8,128)S(1)}, f32[1280,768]{1,0:T(8,128)}, u32[]{:S(2)}) copy-start(f32[1280,768]{1,0:T(8,128)} %copy-done.1) | copy-start | bytes 11796484
  63.8 1.5 %copy-start.5 = (bf16[3,768,384]{2,1,0:T(8,128)(2,1)S(1)}, bf16[3,768,384]{2,1,0:T(8,128)(2,1)}, u32[]{:S(2)}) copy-start(bf16[3,768,384]{2,1,0:T(8,128)(2,1)} %get-tuple-element.42.weight_a) | copy-start | bytes 5308420
  65.3 1.2 %copy-start.6 = (bf16[1344,384]{1,0:T(8,128)(2,1)S(1)}, bf16[1344,384]{1,0:T(8,128)(2,1)}, u32[]{:S(2)}) copy-start(bf16[1344,384]{1,0:T(8,128)(2,1)} %get-tuple-element.40.back_a) | copy-start | bytes 3096580
  66.5 12.7 %copy-start.12 = (bf16[3,192,384]{2,1,0:T(8,128)(2,1)S(1)}, bf16[3,192,384]{2,1,0:T(8,128)(2,1)}, u32[]{:S(2)}) copy-start(bf16[3,192,384]{2,1,0:T(8,128)(2,1)} %get-tuple-element.48) | copy-start | bytes 1327108
  80.7 6.8 %collective-permute-start.15 = (bf16[3,48,384]{2,1,0:T(8,128)(2,1)S(1)}, bf16[3,48,384]{2,1,0:T(8,128)(2,1)S(1)}, u32[]{:S(2)}, u32[]{:S(2)}) collective-permute-start(bf16[3,48,384]{2,1,0:T(8,128)(2,1)S(1)} %get-tuple-element.58), channel_id=1, source_target_pairs={{0,8},{8,32},{32,40},{40,0},{1,9},{9,33},{33,41},{41,1},{2,10},{10... | collective-permute-start | bytes 331784 | tf_op jit(solution)/shard_map/ppermute | solution.py:24
  85.7 3.6 %collective-permute-start.16 = (bf16[3,48,384]{2,1,0:T(8,128)(2,1)S(1)}, bf16[3,48,384]{2,1,0:T(8,128)(2,1)S(1)}, u32[]{:S(2)}, u32[]{:S(2)}) collective-permute-start(bf16[3,48,384]{2,1,0:T(8,128)(2,1)S(1)} %get-tuple-element.60), channel_id=1, source_target_pairs={{0,40},{8,0},{32,8},{40,32},{1,41},{9,1},{33,9},{41,33},{2,42},{10... | collective-permute-start | bytes 331784 | tf_op jit(solution)/shard_map/ppermute | solution.py:24
  85.7 5.4 %collective-permute-start.17 = (bf16[3,48,384]{2,1,0:T(8,128)(2,1)S(1)}, bf16[3,48,384]{2,1,0:T(8,128)(2,1)S(1)}, u32[]{:S(2)}, u32[]{:S(2)}) collective-permute-start(bf16[3,48,384]{2,1,0:T(8,128)(2,1)S(1)} %get-tuple-element.59), channel_id=1, source_target_pairs={{0,32},{8,40},{32,0},{40,8},{1,33},{9,41},{33,1},{41,9},{2,34},{10... | collective-permute-start | bytes 331784 | tf_op jit(solution)/shard_map/ppermute | solution.py:24
  92.1 3.7 %collective-permute-start.18 = (bf16[3,48,384]{2,1,0:T(8,128)(2,1)S(1)}, bf16[3,48,384]{2,1,0:T(8,128)(2,1)S(1)}, u32[]{:S(2)}, u32[]{:S(2)}) collective-permute-start(bf16[3,48,384]{2,1,0:T(8,128)(2,1)S(1)} %add_convert_fusion.2), channel_id=1, source_target_pairs={{0,1},{1,0},{2,3},{3,2},{4,5},{5,4},{6,7},{7,6},{8,9},{9,8},{10,11... | collective-permute-start | bytes 331784 | tf_op jit(solution)/shard_map/ppermute | solution.py:28
  92.2 6.4 %collective-permute-start.19 = (bf16[3,48,384]{2,1,0:T(8,128)(2,1)S(1)}, bf16[3,48,384]{2,1,0:T(8,128)(2,1)S(1)}, u32[]{:S(2)}, u32[]{:S(2)}) collective-permute-start(bf16[3,48,384]{2,1,0:T(8,128)(2,1)S(1)} %add_convert_fusion.2), channel_id=1, source_target_pairs={{0,2},{1,3},{2,0},{3,1},{4,6},{5,7},{6,4},{7,5},{8,10},{9,11},{10,... | collective-permute-start | bytes 331784 | tf_op jit(solution)/shard_map/ppermute | solution.py:28
  95.2 6.5 %collective-permute-start.20 = (bf16[3,48,384]{2,1,0:T(8,128)(2,1)S(1)}, bf16[3,48,384]{2,1,0:T(8,128)(2,1)S(1)}, u32[]{:S(2)}, u32[]{:S(2)}) collective-permute-start(bf16[3,48,384]{2,1,0:T(8,128)(2,1)S(1)} %add_convert_fusion.2), channel_id=1, source_target_pairs={{0,3},{1,2},{2,1},{3,0},{4,7},{5,6},{6,5},{7,4},{8,11},{9,10},{10,... | collective-permute-start | bytes 331784 | tf_op jit(solution)/shard_map/ppermute | solution.py:28
  101.8 5.5 %collective-permute-start.21 = (bf16[3,48,384]{2,1,0:T(8,128)(2,1)S(1)}, bf16[3,48,384]{2,1,0:T(8,128)(2,1)S(1)}, u32[]{:S(2)}, u32[]{:S(2)}) collective-permute-start(bf16[3,48,384]{2,1,0:T(8,128)(2,1)S(1)} %add_convert_fusion.1), channel_id=1, source_target_pairs={{0,7},{1,6},{2,5},{3,4},{4,3},{5,2},{6,1},{7,0},{8,15},{9,14},{10,... | collective-permute-start | bytes 331784 | tf_op jit(solution)/shard_map/ppermute | solution.py:28
  107.3 7.2 %collective-permute-start.22 = (bf16[3,48,384]{2,1,0:T(8,128)(2,1)S(1)}, bf16[3,48,384]{2,1,0:T(8,128)(2,1)S(1)}, u32[]{:S(2)}, u32[]{:S(2)}) collective-permute-start(bf16[3,48,384]{2,1,0:T(8,128)(2,1)S(1)} %add_convert_fusion), channel_id=1, source_target_pairs={{16,0},{8,24},{0,8},{24,16},{17,1},{9,25},{1,9},{25,17},{18,2},{10... | collective-permute-start | bytes 331784 | tf_op jit(solution)/shard_map/ppermute | solution.py:244
  112.6 6.1 %collective-permute-start.23 = (bf16[3,48,384]{2,1,0:T(8,128)(2,1)S(1)}, bf16[3,48,384]{2,1,0:T(8,128)(2,1)S(1)}, u32[]{:S(2)}, u32[]{:S(2)}) collective-permute-start(bf16[3,48,384]{2,1,0:T(8,128)(2,1)S(1)} %add_convert_fusion), channel_id=1, source_target_pairs={{16,8},{8,16},{17,9},{9,17},{18,10},{10,18},{19,11},{11,19},{20,12... | collective-permute-start | bytes 331784 | tf_op jit(solution)/shard_map/ppermute | solution.py:245
